TPU v7x, 32 devices: a whole 2x2x4 slice. The times are simulated.
32 devices in a mesh: heads: 8 (over y, x, core), keys: 4 (over z).
Axes of the slice: x: 2, y: 2, z: 4, core: 2. Of those that a mesh axis runs over, the one named last changes fastest.
Arguments:
- main_query: bfloat16 [128, 128, 576], P(None, 'heads'), may hold values from -5 to 5
- latent_keys: bfloat16 [8192, 576], P('keys'), may hold values from -16 to 16
- index_query: bfloat16 [128, 64, 128], P('heads'), may hold values from -1 to 1
- index_keys: bfloat16 [8192, 128], P('keys'), may hold values from -20 to 20
- index_weight: float32 [128, 64], P('heads'), may hold values from -0.15 to 1
- query_pos: int32 [128], replicated, may hold values from 1024 to 8191, as said below
- kl_weight: float32 [128], P('heads'), may hold values from 2 to 16
Outputs:
- index_query_grad: float32 [128, 64, 128], P('heads')
- index_key_grad: float32 [8192, 128], P('keys')
- index_weight_grad: float32 [128, 64], P('heads')
Inputs may be any that keep to these rules, and one draw needn't show every extreme that they name: Query q sees the keys at positions 0 to query_pos[q]; some query sees all 8192 keys and some sees exactly the first 1025.
All inputs are finite; a program needn't handle non-finite values.
Results may differ from a plain program's by a relative error of at most 0.005.
Values sent between devices are 32-bit elements; how exact they have to be, the bound alone decides.
No kernel may reach another device: no remote copies, remote signals or barrier semaphores. Data moves between devices by JAX's collectives and lax.ppermute only.
A program may use at most 128 MiB of HBM per device.

v0:
```python
import jax
import jax.numpy as jnp
from jax import lax
from jax.sharding import PartitionSpec as P

H = 128


softmax_scale = 192.0 ** (-0.5)
masked_fill = -1e30


def contract_last(left_side, right_side):
    return lax.dot_general(
        left_side, right_side, (((1,), (1,)), ((), ())), preferred_element_type=jnp.float32
    )


def shards(main_query, latent_keys, index_query, index_keys, index_weight, query_pos, kl_weight):
    query_count, head_local, feature_width = main_query.shape
    key_local = latent_keys.shape[0]
    row_local, index_heads, index_width = index_query.shape
    key_first = lax.axis_index("keys") * key_local
    key_index = key_first + lax.iota(jnp.int32, key_local)
    visible = key_index[None, :] <= query_pos[:, None]
    row_first = lax.axis_index("heads") * row_local
    row_pos = lax.dynamic_slice_in_dim(query_pos, row_first, row_local)
    row_visible = key_index[None, :] <= row_pos[:, None]
    main_scores = contract_last(
        main_query.reshape(query_count * head_local, feature_width), latent_keys
    )
    main_scores = main_scores.reshape(query_count, head_local, key_local) * softmax_scale
    main_scores = jnp.where(visible[:, None, :], main_scores, masked_fill)
    index_logits = contract_last(
        index_query.reshape(row_local * index_heads, index_width), index_keys
    )
    index_logits = index_logits.reshape(row_local, index_heads, key_local)
    active = jnp.maximum(index_logits, 0.0)
    index_scores = jnp.einsum("qj,qjk->qk", index_weight, active, precision=lax.Precision.HIGHEST)
    index_scores = jnp.where(row_visible, index_scores, masked_fill)
    main_local = jnp.max(main_scores, axis=2)
    index_local = jnp.max(index_scores, axis=1)
    main_maxima, index_maxima = lax.pmax((main_local, index_local), "keys")
    main_sum = jnp.sum(
        jnp.where(visible[:, None, :], jnp.exp(main_scores - main_maxima[:, :, None]), 0.0), axis=2
    )
    index_sum = jnp.sum(
        jnp.where(row_visible, jnp.exp(index_scores - index_maxima[:, None]), 0.0), axis=1
    )
    main_totals, index_totals = lax.psum((main_sum, index_sum), "keys")
    main_probs = (
        jnp.where(visible[:, None, :], jnp.exp(main_scores - main_maxima[:, :, None]), 0.0)
        / main_totals[:, :, None]
    )
    partial_value = jnp.sum(main_probs, axis=1)
    target = lax.psum_scatter(partial_value, "heads", scatter_dimension=0, tiled=True)
    target = target / H
    index_probs = (
        jnp.where(row_visible, jnp.exp(index_scores - index_maxima[:, None]), 0.0)
        / index_totals[:, None]
    )
    index_delta = kl_weight[:, None] * (index_probs - target)
    weight_grad = jnp.einsum("qk,qjk->qj", index_delta, active, precision=lax.Precision.HIGHEST)
    slopes = jnp.where(
        index_logits > 0.0, index_delta[:, None, :] * index_weight[:, :, None], 0.0
    ).astype(jnp.bfloat16)
    flattened = slopes.reshape(row_local * index_heads, key_local)
    query_grad = jnp.dot(flattened, index_keys, preferred_element_type=jnp.float32).reshape(
        row_local, index_heads, index_width
    )
    key_grad = lax.dot_general(
        flattened,
        index_query.reshape(row_local * index_heads, index_width),
        (((0,), (0,)), ((), ())),
        preferred_element_type=jnp.float32,
    )
    query_grad, weight_grad = lax.psum((query_grad, weight_grad), "keys")
    key_grad = lax.psum(key_grad, "heads")
    return (query_grad, key_grad, weight_grad)


def solution(mesh):
    placed = (
        P(None, "heads", None),
        P("keys", None),
        P("heads", None, None),
        P("keys", None),
        P("heads", None),
        P(),
        P("heads"),
    )
    return jax.shard_map(
        shards,
        mesh=mesh,
        in_specs=placed,
        out_specs=(P("heads", None, None), P("keys", None), P("heads", None)),
        check_vma=False,
    )
```

profile of v0, /device:TPU:0, one launch (start us, length us, event | category | flops | bytes accessed | tf_op | source)
XLA Modules:
  0.0 222.2 jit_solution(17105415036770436941)
XLA Ops:
  7.2 0.0 copy-start
  7.2 0.0 copy-start.4
  7.2 0.0 reduce-scatter.2.cloned.1.call-start
  7.3 0.9 dynamic_slice.3
  8.1 0.9 broadcast_compare_fusion
  9.0 2.6 %fusion.8 = (u16[64,2048]{1,0:T(8,128)(2,1)S(1)}, f32[16,64,2048]{2,1,0:T(8,128)S(1)}) fusion(bf16[16,64,128]{2,1,0:T(8,128)(2,1)} %param.9, bf16[2048,128]{1,0:T(8,128)(2,1)} %param.10), kind=kOutput, calls=%fused_computation.14 | convolution fusion | flops 547225600 | bytes 9437184 | tf_op jit(solution)/shard_map/dot_general | solution.py:14
  11.6 3.2 %copy-done.1 = f32[16,64,2048]{2,1,0:T(8,128)} copy-done((f32[16,64,2048]{2,1,0:T(8,128)}, f32[16,64,2048]{2,1,0:T(8,128)S(1)}, u32[]{:S(2)}) %copy-start.1) | copy-done | bytes 8388632
  14.8 4.6 %fusion.4 = f32[16,1,2048]{2,1,0:T(1,128)S(1)} fusion(f32[16,64,1]{1,2,0:T(1,128)S(1)} %bitcast.36, f32[16,64,2048]{2,1,0:T(8,128)S(1)} %get-tuple-element.10), kind=kOutput, calls=%fused_computation.10 | convolution fusion | flops 27262976 | bytes 8523776 | tf_op jit(solution)/shard_map/qj,qjk->qk/dot_general | solution.py:39
  19.4 0.2 fusion.28
  19.6 11.5 %fusion = (f32[128,16]{0,1:T(8,128)S(1)}, f32[128,16,2048]{2,0,1:T(8,128)}) fusion(pred[128,2048]{1,0:T(8,128)(4,1)S(1)} %broadcast_compare_fusion, bf16[128,16,576]{0,2,1:T(8,128)(2,1)S(1)} %copy-done, bf16[2048,576]{0,1:T(8,128)(2,1)S(1)} %copy-done.8), kind=kOutput, calls=%fused_computation.3 | convolution fusion | flops 4844419072 | bytes 21766144 | tf_op jit(solution)/shard_map/dot_general | solution.py:14
  31.2 14.1 %all-reduce.1 = (f32[128,16]{0,1:T(8,128)S(1)}, f32[16]{0:T(128)S(1)}) all-reduce(f32[128,16]{0,1:T(8,128)S(1)} %get-tuple-element.7, f32[16]{0:T(128)S(1)} %fusion.28), channel_id=1, replica_groups=mesh['heads'=8,'keys'=4] {'keys'}, use_global_device_ids=true, to_apply=%region_5.6 | all-reduce | flops 2064 | bytes 16512 | tf_op jit(solution)/shard_map/pmax | solution.py:43
  45.3 0.2 fusion.29
  45.5 8.4 %fusion.1 = f32[128,16]{0,1:T(8,128)S(1)} fusion(f32[128,16,2048]{2,0,1:T(8,128)} %get-tuple-element.8, f32[128,16]{0,1:T(8,128)S(1)} %get-tuple-element.5, pred[128,2048]{1,0:T(8,128)(4,1)S(1)} %broadcast_compare_fusion), kind=kLoop, calls=%fused_computation.4 | loop fusion | flops 20969472 | bytes 17055744 | tf_op jit(solution)/shard_map/reduce_sum | solution.py:44
  53.9 9.3 %all-reduce = (f32[128,16]{0,1:T(8,128)}, f32[16]{0:T(128)}) all-reduce(f32[128,16]{0,1:T(8,128)S(1)} %fusion.1, f32[16]{0:T(128)S(1)} %fusion.29), channel_id=1, replica_groups=mesh['heads'=8,'keys'=4] {'keys'}, use_global_device_ids=true, to_apply=%region_7.8 | all-reduce | flops 2064 | bytes 16512 | tf_op jit(solution)/shard_map/psum | solution.py:50
  63.1 9.6 %divide_reduce_fusion = f32[128,2048]{1,0:T(8,128)} fusion(f32[128,16,2048]{2,0,1:T(8,128)} %get-tuple-element.8, f32[128,16]{0,1:T(8,128)} %get-tuple-element.3, f32[128,16]{0,1:T(8,128)S(1)} %get-tuple-element.5, pred[128,2048]{1,0:T(8,128)(4,1)S(1)} %broadcast_compare_fusion), kind=kLoop, calls=%fused_computation.2 | loop fusion | flops 24903680 | bytes 18104320 | tf_op jit(solution)/shard_map/reduce_sum | solution.py:55
  72.7 0.0 reduce-scatter.2.cloned.1.call-update
  72.7 0.0 all-reduce.5.cloned.1.call-start
  72.8 35.8 %reduce-scatter.2.cloned.1.call-done = f32[16,2048]{1,0:T(8,128)} async-done(((f32[128,2048]{1,0:T(8,128)}), f32[16,2048]{1,0:T(8,128)}) %reduce-scatter.2.cloned.1.call-update) | async-done | bytes 131088 | tf_op jit(solution)/shard_map/reduce_scatter | solution.py:56
  108.6 1.1 subtract_multiply_fusion
  109.6 0.0 copy-start.3
  109.7 0.0 copy-start.5
  109.7 2.9 %fusion.7 = f32[16,64,128]{2,1,0:T(8,128)} fusion(f32[16,64]{1,0:T(8,128)} %param.11, f32[16,2048]{1,0:T(8,128)S(1)} %subtract_multiply_fusion, u16[64,2048]{1,0:T(8,128)(2,1)S(1)} %get-tuple-element.9, bf16[2048,128]{1,0:T(8,128)(2,1)S(1)} %copy-done.2), kind=kOutput, calls=%fused_computation.13 | convolution fusion | flops 551550976 | bytes 1445888 | tf_op jit(solution)/shard_map/dot_general | solution.py:68
  112.5 0.0 all-reduce.5.cloned.1.call-update
  112.6 0.0 all-reduce.7.cloned.1.call-start
  112.6 2.6 %fusion.19 = f32[2048,128]{1,0:T(8,128)} fusion(bf16[16,64,128]{2,1,0:T(8,128)(2,1)S(1)} %copy-done.3, f32[16,64]{1,0:T(8,128)S(1)} %copy-done.5, f32[16,2048]{1,0:T(8,128)S(1)} %subtract_multiply_fusion, u16[64,2048]{1,0:T(8,128)(2,1)S(1)} %get-tuple-element.9), kind=kOutput, calls=%fused_computation.25 | convolution fusion | flops 551550976 | bytes 1708032 | tf_op jit(solution)/shard_map/dot_general | solution.py:71
  115.3 0.0 all-reduce.7.cloned.1.call-update
  115.3 9.0 %fusion.2 = f32[16,1,64]{2,1,0:T(1,128)S(1)} fusion(f32[16,64,2048]{2,1,0:T(8,128)} %copy-done.1, f32[16,2048,1]{1,0,2:T(8,128)S(1)} %bitcast.34), kind=kOutput, calls=%fused_computation.8 | convolution fusion | flops 27262976 | bytes 8523776 | tf_op jit(solution)/shard_map/qk,qjk->qj/dot_general | solution.py:63
  124.2 12.4 %psum.39 = f32[16,64]{1,0:T(8,128)} all-reduce(f32[16,64]{1,0:T(8,128)S(1)} %bitcast.35), channel_id=1, replica_groups=mesh['heads'=8,'keys'=4] {'keys'}, use_global_device_ids=true, to_apply=%region_12.13 | all-reduce | flops 1024 | bytes 8192 | tf_op jit(solution)/shard_map/psum | solution.py:77
  136.7 14.4 %all-reduce.5.cloned.1.call-done = f32[16,64,128]{2,1,0:T(8,128)} async-done(((f32[16,64,128]{2,1,0:T(8,128)}), f32[16,64,128]{2,1,0:T(8,128)}) %all-reduce.5.cloned.1.call-update) | async-done | bytes 524304 | tf_op jit(solution)/shard_map/psum | solution.py:77
  151.1 60.4 %all-reduce.7.cloned.1.call-done = f32[2048,128]{1,0:T(8,128)} async-done(((f32[2048,128]{1,0:T(8,128)}), f32[2048,128]{1,0:T(8,128)}) %all-reduce.7.cloned.1.call-update) | async-done | bytes 1048592 | tf_op jit(solution)/shard_map/psum | solution.py:78
  211.5 1.9 copy.27
  213.4 2.3 %copy.28 = f32[2048,128]{1,0:T(8,128)} copy(f32[2048,128]{1,0:T(8,128)} %all-reduce.7.cloned.1.call-done) | data formatting | bytes 2097152
  (14 shorter events, 0.0 us)
Async XLA Ops:
  7.2 12.5 %copy-start = (bf16[128,16,576]{0,2,1:T(8,128)(2,1)S(1)}, bf16[128,16,576]{0,2,1:T(8,128)(2,1)}, u32[]{:S(2)}) copy-start(bf16[128,16,576]{0,2,1:T(8,128)(2,1)} %param.7) | copy-start | bytes 7077892
  7.2 7.6 %copy-start.4 = (f32[16,64]{1,0:T(8,128)S(1)}, f32[16,64]{1,0:T(8,128)}, u32[]{:S(2)}) copy-start(f32[16,64]{1,0:T(8,128)} %param.11) | copy-start | bytes 12292
  7.2 101.4 %reduce-scatter.2.cloned.1.call-start = ((), (), s32[]{:S(2)}) async-start(), calls=%async_computation.1 | async-start | bytes 1179648 | tf_op jit(solution)/shard_map/reduce_scatter | solution.py:56
  8.1 37.1 %copy-start.6 = (s32[16]{0:T(128)}, s32[16]{0:T(128)S(1)}, u32[]{:S(2)}) copy-start(s32[16]{0:T(128)S(1)} %dynamic_slice.3) | copy-start | bytes 196
  9.0 10.6 %copy-start.8 = (bf16[2048,576]{0,1:T(8,128)(2,1)S(1)}, bf16[2048,576]{0,1:T(8,128)(2,1)}, u32[]{:S(2)}) copy-start(bf16[2048,576]{0,1:T(8,128)(2,1)} %param.8) | copy-start | bytes 7077892
  11.6 3.2 %copy-start.1 = (f32[16,64,2048]{2,1,0:T(8,128)}, f32[16,64,2048]{2,1,0:T(8,128)S(1)}, u32[]{:S(2)}) copy-start(f32[16,64,2048]{2,1,0:T(8,128)S(1)} %get-tuple-element.10) | copy-start | bytes 25165828
  45.2 8.6 %copy-start.7 = (f32[16]{0:T(128)}, f32[16]{0:T(128)S(1)}, u32[]{:S(2)}) copy-start(f32[16]{0:T(128)S(1)} %get-tuple-element.6) | copy-start | bytes 196
  63.1 46.5 %copy-start.2 = (bf16[2048,128]{1,0:T(8,128)(2,1)S(1)}, bf16[2048,128]{1,0:T(8,128)(2,1)}, u32[]{:S(2)}) copy-start(bf16[2048,128]{1,0:T(8,128)(2,1)} %param.10) | copy-start | bytes 1572868
  72.7 78.4 %all-reduce.5.cloned.1.call-start = ((), (), s32[]{:S(2)}) async-start(), calls=%async_computation.2 | async-start | bytes 1048576 | tf_op jit(solution)/shard_map/psum | solution.py:77
  109.6 3.0 %copy-start.3 = (bf16[16,64,128]{2,1,0:T(8,128)(2,1)S(1)}, bf16[16,64,128]{2,1,0:T(8,128)(2,1)}, u32[]{:S(2)}) copy-start(bf16[16,64,128]{2,1,0:T(8,128)(2,1)} %param.9) | copy-start | bytes 786436
  109.7 3.0 %copy-start.5 = (f32[16,64]{1,0:T(8,128)S(1)}, f32[16,64]{1,0:T(8,128)}, u32[]{:S(2)}) copy-start(f32[16,64]{1,0:T(8,128)} %param.11) | copy-start | bytes 12292
  112.6 98.9 %all-reduce.7.cloned.1.call-start = ((), (), s32[]{:S(2)}) async-start(), calls=%async_computation.3 | async-start | bytes 2097152 | tf_op jit(solution)/shard_map/psum | solution.py:78
Sparse Core Ops, SparseCore 0:
  72.9 35.6 reduce-scatter.1
  112.7 38.4 all-reduce.4
  154.9 56.5 all-reduce.6
where the time goes:
time: 223 us; the launch traced here: 222 us
  waiting for transfers between devices  111 us (50%)
  blocking collectives  35.8 us (16%)
  matrix products  33.1 us (15%)
  other arithmetic  20.3 us (9%)
  between operations  13.9 us (6%)
  local copies, waits for them, and re-layouts  8.29 us (4%)
    psum x1, waiting for transfers between devices, shards(): key_grad = lax.psum(key_grad, 'heads')  60.4 us
    reduce_scatter x1, waiting for transfers between devices, shards(): lax.psum_scatter(partial_value, 'heads', scatter_dimension=0, tiled=True)  35.8 us
    psum x1, waiting for transfers between devices, shards(): query_grad, weight_grad = lax.psum((query_grad, weight_grad), 'keys')  14.4 us
    dot_general x2, matrix products, contract_last(): lax.dot_general(left_side, right_side, (((1,), (1,)), ((), ())), preferre...  14.1 us
    pmax x1, blocking collectives, shards(): main_maxima, index_maxima = lax.pmax((main_local, index_local), 'keys')  14.1 us
    psum x1, blocking collectives, shards(): query_grad, weight_grad = lax.psum((query_grad, weight_grad), 'keys')  12.4 us
    reduce_sum x1, other arithmetic, shards(): partial_value = jnp.sum(main_probs, axis=1)  9.57 us
    psum x1, blocking collectives, shards(): main_totals, index_totals = lax.psum((main_sum, index_sum), 'keys')  9.27 us
  transfers between devices with their start and end apart: 3, of which 3 were waited for; matrix products, arithmetic and copies ran while one was open for 5% of the time, Pallas kernels for 0%

commit v1 on v0

v1 whole, which is shorter than its diff:
```python
import math

import jax
import jax.numpy as jnp
from jax import lax
from jax.experimental import pallas as pl
from jax.experimental.pallas import tpu as pltpu
from jax.sharding import PartitionSpec as P

H = 128

LOG2E = math.log2(math.e)
score_scale = 192.0 ** (-0.5) * LOG2E
masked_fill = -1e30
never_masked = 3e38

VMEM_LIMIT = 56 * 1024 * 1024
F32 = jnp.float32
BF16 = jnp.bfloat16


def params(**more):
    return pltpu.CompilerParams(vmem_limit_bytes=VMEM_LIMIT, **more)


def whole_spec(array):
    rank = len(array.shape)
    return pl.BlockSpec(array.shape, lambda *_: (0,) * rank)


def smem_spec():
    return pl.BlockSpec(memory_space=pltpu.SMEM)


def shape_of(dims, dtype=F32):
    return jax.ShapeDtypeStruct(dims, dtype)


def tile_of(extent, wanted):
    return wanted if extent % wanted == 0 else extent


def index_forward(place, row_pos, index_query, index_keys, index_weight, lanes):
    rows, heads, width = index_query.shape
    keys = index_keys.shape[0]
    tile = tile_of(keys, 512)

    def body(place_ref, pos_ref, query_ref, keys_ref, weight_ref, score_ref, lse_ref, wiq_ref):
        columns = weight_ref[...].T
        flat = query_ref[...].reshape(rows * heads, width)
        for row in range(rows):
            piece = query_ref[row].astype(F32) * columns[:, row : row + 1]
            wiq_ref[:, row * heads : (row + 1) * heads] = piece.T.astype(BF16)
        for at in range(0, keys, tile):
            logits = lax.dot_general(
                flat, keys_ref[at : at + tile, :], (((1,), (1,)), ((), ())), preferred_element_type=F32
            )
            index = place_ref[0] + at + lax.broadcasted_iota(jnp.int32, (1, tile), 1)
            for row in range(rows):
                active = jnp.maximum(logits[row * heads : (row + 1) * heads, :], 0.0)
                summed = jnp.sum(active * columns[:, row : row + 1], axis=0, keepdims=True)
                seen = index <= pos_ref[row]
                score_ref[row : row + 1, at : at + tile] = jnp.where(seen, summed * LOG2E, masked_fill)
        scores = score_ref[...]
        top = jnp.max(scores, axis=1, keepdims=True)
        total = jnp.sum(jnp.exp2(scores - top), axis=1, keepdims=True)
        lse_ref[...] = jnp.broadcast_to(top + jnp.log2(total), lse_ref.shape)

    operands = (place, row_pos, index_query, index_keys, index_weight)
    return pl.pallas_call(
        body,
        out_shape=(shape_of((rows, keys)), shape_of((rows, lanes)), shape_of((width, rows * heads), BF16)),
        in_specs=[smem_spec(), smem_spec()] + [whole_spec(a) for a in operands[2:]],
        out_specs=(
            pl.BlockSpec((rows, keys), lambda: (0, 0)),
            pl.BlockSpec((rows, lanes), lambda: (0, 0)),
            pl.BlockSpec((width, rows * heads), lambda: (0, 0)),
        ),
        compiler_params=params(),
        name="index_forward",
    )(*operands)


def main_scores(place, pos, query_t, keys_t, index_lse):
    head_local, feature, queries = query_t.shape
    keys = keys_t.shape[1]
    per = 256 // queries if queries < 256 and head_local % (256 // queries) == 0 else 1
    lanes = per * queries
    blocks = head_local // per
    tile = tile_of(keys, 512)
    tiles = keys // tile
    rows = index_lse.shape[0]

    def body(place_ref, pos_ref, query_ref, keys_ref, lse_ref, prob_ref, top_ref, stat_ref, key_rows, bias):
        step = pl.program_id(0)

        @pl.when(step == 0)
        def _():
            for at in range(0, keys, tile):
                key_rows[at : at + tile, :] = keys_ref[:, at : at + tile].T
            index = place_ref[0] + lax.broadcasted_iota(jnp.int32, (keys, queries), 0)
            bias[...] = jnp.where(index <= pos_ref[...], never_masked, masked_fill)
            stat_ref[blocks:, :] = lse_ref[...]

        weights = jnp.concatenate([query_ref[i] for i in range(per)], axis=1)
        tops, totals = [], []
        for t in range(tiles):
            span = slice(t * tile, (t + 1) * tile)
            scores = jnp.dot(key_rows[span, :], weights, preferred_element_type=F32)
            limit = bias[span, :]
            scores = jnp.minimum(scores, jnp.concatenate([limit] * per, axis=1))
            top = jnp.max(scores, axis=0, keepdims=True)
            prob = jnp.exp2((scores - top) * score_scale)
            tops.append(top * score_scale)
            totals.append(jnp.sum(prob, axis=0, keepdims=True))
            prob_ref[0, span, :] = prob.astype(BF16)
        best = tops[0]
        for top in tops[1:]:
            best = jnp.maximum(best, top)
        total = sum(s * jnp.exp2(top - best) for s, top in zip(totals, tops))
        for t in range(tiles):
            top_ref[0, t : t + 1, :] = tops[t]
        stat_ref[pl.ds(step, 1), :] = best + jnp.log2(total)

    return pl.pallas_call(
        body,
        grid=(blocks,),
        out_shape=(
            shape_of((blocks, keys, lanes), BF16),
            shape_of((blocks, tiles, lanes)),
            shape_of((blocks + rows, lanes)),
        ),
        in_specs=[
            smem_spec(),
            whole_spec(pos),
            pl.BlockSpec((per, feature, queries), lambda i: (i, 0, 0)),
            whole_spec(keys_t),
            whole_spec(index_lse),
        ],
        out_specs=(
            pl.BlockSpec((1, keys, lanes), lambda i: (i, 0, 0)),
            pl.BlockSpec((1, tiles, lanes), lambda i: (i, 0, 0)),
            pl.BlockSpec((blocks + rows, lanes), lambda i: (0, 0)),
        ),
        scratch_shapes=[pltpu.VMEM((keys, feature), BF16), pltpu.VMEM((keys, queries), F32)],
        compiler_params=params(),
        name="main_scores",
    )(place, pos, query_t, keys_t, index_lse)


def joined(stats):
    best = stats[0]
    for stat in stats[1:]:
        best = jnp.maximum(best, stat)
    return best + jnp.log2(sum(jnp.exp2(stat - best) for stat in stats))


def head_sum(place, probs, tops, stats, queries, row_local):
    blocks, keys, lanes = probs.shape
    tiles = tops.shape[1]
    tile = keys // tiles
    per = lanes // queries
    chips = queries // row_local // 2
    sub = tile_of(tile, 128)

    def body(place_ref, prob_ref, top_ref, *refs):
        stat_refs, (keep_ref, send_ref, summed) = refs[:-3], refs[-3:]
        step = pl.program_id(0)
        whole = joined([ref[:blocks, :] for ref in stat_refs])
        factors = [
            jnp.exp2(top_ref[b, pl.ds(step, 1), :] - whole[b : b + 1, :]) * (1.0 / H) for b in range(blocks)
        ]
        for at in range(0, tile, sub):
            total = None
            for b in range(blocks):
                part = prob_ref[b, at : at + sub, :].astype(F32) * factors[b]
                for i in range(per):
                    piece = part[:, i * queries : (i + 1) * queries]
                    total = piece if total is None else total + piece
            summed[:, at : at + sub] = total.T
        chip = place_ref[1] // 2
        core = place_ref[1] % 2
        for r in range(chips):
            first = (chip ^ r) * 2
            keep_ref[r] = summed[pl.ds(pl.multiple_of((first + core) * row_local, row_local), row_local), :]
            send_ref[r] = summed[pl.ds(pl.multiple_of((first + 1 - core) * row_local, row_local), row_local), :]

    half = shape_of((chips, row_local, keys))
    half_spec = pl.BlockSpec((chips, row_local, tile), lambda i: (0, 0, i))
    return pl.pallas_call(
        body,
        grid=(tiles,),
        out_shape=(half, half),
        in_specs=[smem_spec(), pl.BlockSpec((blocks, tile, lanes), lambda i: (0, i, 0)), whole_spec(tops)]
        + [whole_spec(s) for s in stats],
        out_specs=(half_spec, half_spec),
        scratch_shapes=[pltpu.VMEM((queries, tile), F32)],
        compiler_params=params(),
        name="head_sum",
    )(place, probs, tops, *stats)


def gradients(place, scores, stats, targets, kl, index_query, index_keys, wiq, key_devices, head_devices):
    rows, heads, width = index_query.shape
    keys = index_keys.shape[0]
    tile = tile_of(keys, 512)
    parts = len(targets)
    own = rows // key_devices
    chips = head_devices // 2
    chunk = keys // head_devices
    first_row = stats[0].shape[0] - rows

    def body(place_ref, score_ref, kl_ref, query_ref, keys_ref, wiq_ref, *refs):
        stat_refs, refs = refs[: len(stats)], refs[len(stats) :]
        target_refs, refs = refs[:parts], refs[parts:]
        query_outs, (keep_ref, send_ref, query_total, key_total) = refs[:key_devices], refs[key_devices:]
        whole = joined([ref[first_row:, :1] for ref in stat_refs])
        flat = query_ref[...].reshape(rows * heads, width)
        for at in range(0, keys, tile):
            span = slice(at, at + tile)
            target = target_refs[0][:, span]
            for ref in target_refs[1:]:
                target = target + ref[:, span]
            delta = kl_ref[...] * (jnp.exp2(score_ref[:, span] - whole) - target)
            logits = lax.dot_general(
                flat, keys_ref[span, :], (((1,), (1,)), ((), ())), preferred_element_type=F32
            ).astype(BF16)
            delta = delta.astype(BF16)
            pieces = []
            for row in range(rows):
                pieces.append(
                    jnp.where(
                        logits[row * heads : (row + 1) * heads, :] > 0,
                        jnp.broadcast_to(delta[row : row + 1, :], (heads, tile)),
                        jnp.zeros((), BF16),
                    )
                )
            slopes = jnp.concatenate(pieces, axis=0)
            part = jnp.dot(slopes, keys_ref[span, :], preferred_element_type=F32)
            if at == 0:
                query_total[...] = part
            else:
                query_total[...] += part
            key_part = jnp.dot(wiq_ref[...], slopes, preferred_element_type=F32)
            key_total[span, :] = key_part.T
        chip, core, z = place_ref[1] // 2, place_ref[1] % 2, place_ref[2]
        for r in range(chips):
            first = (chip ^ r) * 2
            keep_ref[r] = key_total[pl.ds(pl.multiple_of((first + core) * chunk, chunk), chunk), :]
            send_ref[r] = key_total[pl.ds(pl.multiple_of((first + 1 - core) * chunk, chunk), chunk), :]
        for r in range(key_devices):
            size = own * heads
            query_outs[r][...] = query_total[pl.ds(pl.multiple_of((z ^ r) * size, size), size), :]

    half = shape_of((chips, chunk, width))
    outs = tuple(shape_of((own * heads, width)) for _ in range(key_devices)) + (half, half)
    operands = (scores, kl, index_query, index_keys, wiq, *stats, *targets)
    return pl.pallas_call(
        body,
        out_shape=outs,
        in_specs=[smem_spec()] + [whole_spec(a) for a in operands],
        out_specs=tuple(whole_spec(o) for o in outs),
        scratch_shapes=[pltpu.VMEM((rows * heads, width), F32), pltpu.VMEM((keys, width), F32)],
        compiler_params=params(),
        name="gradients",
    )(place, *operands)


def finish_query(place, pieces, index_query, index_weight):
    rows, heads, width = index_query.shape
    own = rows // len(pieces)

    def body(place_ref, query_ref, weight_ref, *refs):
        piece_refs, (query_out, weight_out, columns) = refs[:-3], refs[-3:]
        z = place_ref[2]
        columns[...] = weight_ref[...].T
        weight_columns = columns[...]
        for r, ref in enumerate(piece_refs):
            first = (z ^ r) * own
            for i in range(own):
                row = first + i
                piece = ref[i * heads : (i + 1) * heads, :]
                picked = lax.broadcasted_iota(jnp.int32, (heads, rows), 1) == row
                column = jnp.sum(jnp.where(picked, weight_columns, 0.0), axis=1, keepdims=True)
                query_out[row] = piece * column
                summed = jnp.sum(piece * query_ref[row].astype(F32), axis=1, keepdims=True)
                weight_out[pl.ds(row, 1), :] = summed.T

    return pl.pallas_call(
        body,
        out_shape=(shape_of((rows, heads, width)), shape_of((rows, heads))),
        in_specs=[smem_spec(), whole_spec(index_query), whole_spec(index_weight)]
        + [whole_spec(p) for p in pieces],
        out_specs=(
            pl.BlockSpec((rows, heads, width), lambda: (0, 0, 0)),
            pl.BlockSpec((rows, heads), lambda: (0, 0)),
        ),
        scratch_shapes=[pltpu.VMEM((heads, rows), F32)],
        compiler_params=params(),
        name="finish_query",
    )(place, index_query, index_weight, *pieces)


def finish_keys(place, mine, others):
    chips = len(mine)
    chunk, width = mine[0].shape

    def body(place_ref, *refs):
        out_ref = refs[-1]
        chip, core = place_ref[1] // 2, place_ref[1] % 2
        for r in range(chips):
            first = (chip ^ r) * 2
            out_ref[pl.ds(pl.multiple_of((first + core) * chunk, chunk), chunk), :] = refs[r][...]
            out_ref[pl.ds(pl.multiple_of((first + 1 - core) * chunk, chunk), chunk), :] = refs[chips + r][...]

    out = shape_of((2 * chips * chunk, width))
    return pl.pallas_call(
        body,
        out_shape=out,
        in_specs=[smem_spec()] + [whole_spec(a) for a in (*mine, *others)],
        out_specs=whole_spec(out),
        compiler_params=params(),
        name="finish_keys",
    )(place, *mine, *others)


def shards(main_query, latent_keys, index_query, index_keys, index_weight, query_pos, kl_weight):
    queries = main_query.shape[0]
    key_local = latent_keys.shape[0]
    row_local = index_query.shape[0]
    head_devices = lax.axis_size("heads")
    key_devices = lax.axis_size("keys")
    chips = head_devices // 2
    at_head = lax.axis_index("heads")
    at_key = lax.axis_index("keys")
    place = jnp.stack([at_key * key_local, at_head, at_key]).astype(jnp.int32)
    row_pos = lax.dynamic_slice_in_dim(query_pos, at_head * row_local, row_local)

    def across(axis, count, value, bits):
        return lax.ppermute(value, axis, [(i, i ^ bits) for i in range(count)])

    def to_keys(value, bits):
        return across("keys", key_devices, value, bits)

    def to_heads(value, bits):
        return across("heads", head_devices, value, bits)

    lanes = 256 if queries < 256 else queries
    scores, index_lse, wiq = index_forward(place, row_pos, index_query, index_keys, index_weight, lanes)
    probs, tops, stat = main_scores(
        place, query_pos[None, :], main_query.transpose(1, 2, 0), latent_keys.T, index_lse
    )
    stats = [stat] + [to_keys(stat, bits) for bits in reversed(range(1, key_devices))]
    keep, send = head_sum(place, probs, tops, stats, queries, row_local)
    other = to_heads(send, 1)
    sums = [keep[r] + other[r] for r in range(chips)]
    targets = [sums[0]] + [to_heads(sums[r], 2 * r) for r in reversed(range(1, chips))]
    *query_parts, keep, send = gradients(
        place, scores, stats, targets, kl_weight[:, None], index_query, index_keys, wiq, key_devices, head_devices
    )
    other = to_heads(send, 1)
    query_own = query_parts[0]
    arrived = [to_keys(query_parts[r], r) for r in reversed(range(1, key_devices))]
    for part in arrived:
        query_own = query_own + part
    sums = [keep[r] + other[r] for r in range(chips)]
    key_own = sums[0]
    for part in [to_heads(sums[r], 2 * r) for r in reversed(range(1, chips))]:
        key_own = key_own + part
    query_pieces = [query_own] + [to_keys(query_own, r) for r in range(1, key_devices)]
    mine = [key_own] + [to_heads(key_own, 2 * r) for r in range(1, chips)]
    others = [to_heads(piece, 1) for piece in mine]
    query_grad, weight_grad = finish_query(place, query_pieces, index_query, index_weight)
    key_grad = finish_keys(place, mine, others)
    return query_grad, key_grad, weight_grad


def solution(mesh):
    placed = (
        P(None, "heads", None),
        P("keys", None),
        P("heads", None, None),
        P("keys", None),
        P("heads", None),
        P(),
        P("heads"),
    )
    return jax.shard_map(
        shards,
        mesh=mesh,
        in_specs=placed,
        out_specs=(P("heads", None, None), P("keys", None), P("heads", None)),
        check_vma=False,
    )
```

time: 223 us -> 95.4 us (0.43)
  waiting for transfers between devices: 111 us -> 21.4 us
  blocking collectives: 35.8 us -> 0 us
  Pallas kernels: 0 us -> 35.1 us
  matrix products: 33.1 us -> 0 us
  starting transfers between devices: 0.12 us -> 26.9 us
  other arithmetic: 20.3 us -> 5.47 us
  between operations: 13.9 us -> 0.81 us
  local copies, waits for them, and re-layouts: 8.29 us -> 5.22 us
    psum x2 -> x0, waiting for transfers between devices: 74.8 us -> none  [the longest x1 60.4 us: shards(): key_grad = lax.psum(key_grad, 'heads')]
    reduce_scatter x1 -> x0, waiting for transfers between devices: 35.8 us -> none  [shards(): lax.psum_scatter(partial_value, 'heads', scatter_dimension=0, tiled=True)]
    pallas_call x0 -> x6, Pallas kernels: none -> 35.1 us  [the longest x1 14.7 us: main_scores(): pl.pallas_call(body, grid=(blocks,), out_shape=(shape_of((blocks, keys, l...]
    dot_general x6 -> x0, matrix products: 33.1 us -> none  [the longest x2 14.1 us: contract_last(): lax.dot_general(left_side, right_side, (((1,), (1,)), ((), ())), preferre...]
    ppermute x0 -> x24, starting transfers between devices: none -> 26.9 us  [across(): return lax.ppermute(value, axis, [(i, i ^ bits) for i in range(count)])]
    psum x2 -> x0, blocking collectives: 21.7 us -> none  [the longest x1 12.4 us: shards(): query_grad, weight_grad = lax.psum((query_grad, weight_grad), 'keys')]
    ppermute x0 -> x24, waiting for transfers between devices: none -> 21.4 us  [across(): return lax.ppermute(value, axis, [(i, i ^ bits) for i in range(count)])]
    reduce_sum x3 -> x0, other arithmetic: 18.2 us -> none  [the longest x1 9.57 us: shards(): partial_value = jnp.sum(main_probs, axis=1)]
  transfers between devices with their start and end apart: 3 -> 24, of which waited for: 3 -> 12; matrix products, arithmetic and copies ran while one was open for 5% -> 4% of each run, Pallas kernels for 0% -> 3%
where the time goes in v1:
time: 95.4 us; the launch traced here: 95 us
  Pallas kernels  35.1 us (37%)
  starting transfers between devices  26.9 us (28%)
  waiting for transfers between devices  21.4 us (22%)
  other arithmetic  5.47 us (6%)
  local copies, waits for them, and re-layouts  5.22 us (5%)
    ppermute x24, starting transfers between devices, across(): return lax.ppermute(value, axis, [(i, i ^ bits) for i in range(count)])  26.9 us
    ppermute x24, waiting for transfers between devices, across(): return lax.ppermute(value, axis, [(i, i ^ bits) for i in range(count)])  21.4 us
    pallas_call x1, Pallas kernels, main_scores(): pl.pallas_call(body, grid=(blocks,), out_shape=(shape_of((blocks, keys, l...  14.7 us
    pallas_call x1, Pallas kernels, head_sum(): pl.pallas_call(body, grid=(tiles,), out_shape=(half, half), in_specs=[sme...  5.94 us
    pallas_call x1, Pallas kernels, gradients(): pl.pallas_call(body, out_shape=outs, in_specs=[smem_spec()] + [whole_spec...  5.64 us
    pallas_call x1, Pallas kernels, index_forward(): pl.pallas_call(body, out_shape=(shape_of((rows, keys)), shape_of((rows, l...  4 us
    unnamed x38, local copies, waits for them, and re-layouts  3.28 us
    add x2, other arithmetic, shards(): sums = [keep[r] + other[r] for r in range(chips)]  2.91 us
  transfers between devices with their start and end apart: 24, of which 12 were waited for; matrix products, arithmetic and copies ran while one was open for 4% of the time, Pallas kernels for 3%

profile of v1, /device:TPU:0, one launch (start us, length us, event | category | flops | bytes accessed | tf_op | source)
XLA Modules:
  0.0 95.0 jit_solution(15733778489955634837)
XLA Ops:
  0.6 1.3 %dynamic_slice.3.pos_ref = s32[16]{0:T(128)} dynamic-slice(s32[128]{0:T(128)} %param.12, s32[]{:T(128)S(6)} %select_n.3), dynamic_slice_sizes={16} | dynamic-slice | bytes 132 | tf_op jit(solution)/shard_map/dynamic_slice | solution.py:337
  2.6 4.0 %index_forward.1 = (f32[16,2048]{1,0:T(8,128)}, f32[16,256]{1,0:T(8,128)}, bf16[128,1024]{1,0:T(8,128)(2,1)}) custom-call(s32[3]{0:T(128)} %pad_add_fusion.place_ref, s32[16]{0:T(128)} %dynamic_slice.3.pos_ref, bf16[16,64,128]{2,1,0:T(8,128)(2,1)} %query_ref.5, bf16[2048,128]{1,0:T(8,128)(2,1)} %keys_ref.3, f32[16,64]{1,0:T(8,128)} %weight_ref.3), custom_call_target="tpu_custom_call" | custom-call | tf_op jit(solution)/shard_map/index_forward/pallas_call | solution.py:70
  6.6 14.7 %main_scores.1 = (bf16[8,2048,256]{2,1,0:T(8,128)(2,1)}, f32[8,4,256]{2,1,0:T(4,128)}, f32[24,256]{1,0:T(8,128)}) custom-call(s32[3]{0:T(128)} %pad_add_fusion.place_ref, s32[1,128]{1,0:T(1,128)} %bitcast.32, bf16[16,576,128]{2,1,0:T(8,128)(2,1)} %bitcast.29, bf16[576,2048]{1,0:T(8,128)(2,1)} %bitcast.30, f32[16,256]{1,0:T(8,128)} %get-tuple-element.21.lse_ref), custom_call_target="tpu_custom_call" | custom-call | tf_op jit(solution)/shard_map/main_scores/pallas_call | solution.py:125
  21.2 5.1 %collective-permute-start = (f32[24,256]{1,0:T(8,128)}, f32[24,256]{1,0:T(8,128)S(1)}, u32[]{:S(2)}, u32[]{:S(2)}) collective-permute-start(f32[24,256]{1,0:T(8,128)} %get-tuple-element.22.refs_0_), channel_id=1, source_target_pairs={{0,3},{1,2},{2,1},{3,0},{4,7},{5,6},{6,5},{7,4},{8,11},{9,10},{10,... | collective-permute-start | bytes 73736 | tf_op jit(solution)/shard_map/ppermute | solution.py:340
  27.0 1.4 %collective-permute-done.refs_1_ = f32[24,256]{1,0:T(8,128)S(1)} collective-permute-done((f32[24,256]{1,0:T(8,128)}, f32[24,256]{1,0:T(8,128)S(1)}, u32[]{:S(2)}, u32[]{:S(2)}) %collective-permute-start) | collective-permute-done | bytes 24608 | tf_op jit(solution)/shard_map/ppermute | solution.py:340
  28.4 2.9 %collective-permute-done.1.refs_2_ = f32[24,256]{1,0:T(8,128)S(1)} collective-permute-done((f32[24,256]{1,0:T(8,128)}, f32[24,256]{1,0:T(8,128)S(1)}, u32[]{:S(2)}, u32[]{:S(2)}) %collective-permute-start.1) | collective-permute-done | bytes 24608 | tf_op jit(solution)/shard_map/ppermute | solution.py:340
  31.9 5.9 %head_sum.1 = (f32[4,16,2048]{2,1,0:T(8,128)}, f32[4,16,2048]{2,1,0:T(8,128)}) custom-call(s32[3]{0:T(128)} %pad_add_fusion.place_ref, bf16[8,2048,256]{2,1,0:T(8,128)(2,1)} %get-tuple-element.23.prob_ref, f32[8,4,256]{2,1,0:T(4,128)} %get-tuple-element.24.top_ref, f32[24,256]{1,0:T(8,128)} %get-tuple-element.22.refs_0_, f32[24,256]{1,0:T(8,128)} %copy-done.15, ...), custom_call_target="tpu_custom_call" | custom-call | tf_op jit(solution)/shard_map/head_sum/pallas_call | solution.py:190
  37.8 2.1 %collective-permute-done.3 = f32[4,16,2048]{2,1,0:T(8,128)S(1)} collective-permute-done((f32[4,16,2048]{2,1,0:T(8,128)}, f32[4,16,2048]{2,1,0:T(8,128)S(1)}, u32[]{:S(2)}, u32[]{:S(2)}) %collective-permute-start.3) | collective-permute-done | bytes 524320 | tf_op jit(solution)/shard_map/ppermute | solution.py:340
  40.0 1.8 %fusion.7 = (f32[16,2048]{1,0:T(8,128)S(1)}, f32[16,2048]{1,0:T(8,128)S(1)}, f32[16,2048]{1,0:T(8,128)S(1)}, f32[16,2048]{1,0:T(8,128)}) fusion(f32[4,16,2048]{2,1,0:T(8,128)S(1)} %collective-permute-done.3, f32[4,16,2048]{2,1,0:T(8,128)} %get-tuple-element.25), kind=kLoop, calls=%fused_computation.12 | loop fusion | flops 131072 | bytes 1572864 | tf_op jit(solution)/shard_map/add | solution.py:356
  41.8 2.4 %collective-permute-start.4 = (f32[16,2048]{1,0:T(8,128)S(1)}, f32[16,2048]{1,0:T(8,128)S(1)}, u32[]{:S(2)}, u32[]{:S(2)}) collective-permute-start(f32[16,2048]{1,0:T(8,128)S(1)} %get-tuple-element.40), channel_id=1, source_target_pairs={{0,24},{4,28},{8,16},{12,20},{16,8},{20,12},{24,0},{28,4},{1,25},{... | collective-permute-start | bytes 393224 | tf_op jit(solution)/shard_map/ppermute | solution.py:340
  46.0 2.6 %collective-permute-done.4.refs_5_ = f32[16,2048]{1,0:T(8,128)S(1)} collective-permute-done((f32[16,2048]{1,0:T(8,128)S(1)}, f32[16,2048]{1,0:T(8,128)S(1)}, u32[]{:S(2)}, u32[]{:S(2)}) %collective-permute-start.4) | collective-permute-done | bytes 131104 | tf_op jit(solution)/shard_map/ppermute | solution.py:340
  48.5 2.5 %collective-permute-done.5.refs_6_ = f32[16,2048]{1,0:T(8,128)S(1)} collective-permute-done((f32[16,2048]{1,0:T(8,128)S(1)}, f32[16,2048]{1,0:T(8,128)S(1)}, u32[]{:S(2)}, u32[]{:S(2)}) %collective-permute-start.5) | collective-permute-done | bytes 131104 | tf_op jit(solution)/shard_map/ppermute | solution.py:340
  51.8 5.6 %gradients.1 = (f32[256,128]{1,0:T(8,128)}, f32[256,128]{1,0:T(8,128)}, f32[256,128]{1,0:T(8,128)}, f32[256,128]{1,0:T(8,128)}, f32[4,256,128]{2,1,0:T(8,128)}, /*index=5*/f32[4,256,128]{2,1,0:T(8,128)}) custom-call(s32[3]{0:T(128)} %pad_add_fusion.place_ref, f32[16,2048]{1,0:T(8,128)} %get-tuple-element.19.score_ref, f32[16,1]{1,0:T(8,128)} %copy.10.kl_ref, ...), custom_call_target="tpu_custom_call" | custom-call | tf_op jit(solution)/shard_map/gradients/pallas_call | solution.py:258
  57.4 1.5 %collective-permute-start.7 = (f32[256,128]{1,0:T(8,128)}, f32[256,128]{1,0:T(8,128)S(1)}, u32[]{:S(2)}, u32[]{:S(2)}) collective-permute-start(f32[256,128]{1,0:T(8,128)} %get-tuple-element.28), channel_id=1, source_target_pairs={{0,3},{1,2},{2,1},{3,0},{4,7},{5,6},{6,5},{7,4},{8,11},{9,10},{10,... | collective-permute-start | bytes 393224 | tf_op jit(solution)/shard_map/ppermute | solution.py:340
  59.6 2.3 %collective-permute-start.9 = (f32[256,128]{1,0:T(8,128)}, f32[256,128]{1,0:T(8,128)S(1)}, u32[]{:S(2)}, u32[]{:S(2)}) collective-permute-start(f32[256,128]{1,0:T(8,128)} %get-tuple-element.30), channel_id=1, source_target_pairs={{0,1},{1,0},{2,3},{3,2},{4,5},{5,4},{6,7},{7,6},{8,9},{9,8},{10,11... | collective-permute-start | bytes 393224 | tf_op jit(solution)/shard_map/ppermute | solution.py:340
  61.9 1.1 %fusion.2 = (f32[256,128]{1,0:T(8,128)S(1)}, f32[256,128]{1,0:T(8,128)S(1)}, f32[256,128]{1,0:T(8,128)S(1)}) fusion(f32[4,256,128]{2,1,0:T(8,128)S(1)} %collective-permute-done.13, f32[4,256,128]{2,1,0:T(8,128)} %get-tuple-element.32), kind=kLoop, calls=%fused_computation.5 | loop fusion | flops 98304 | bytes 1179648 | tf_op jit(solution)/shard_map/add | solution.py:366
  63.0 1.8 %collective-permute-start.14 = (f32[256,128]{1,0:T(8,128)S(1)}, f32[256,128]{1,0:T(8,128)S(1)}, u32[]{:S(2)}, u32[]{:S(2)}) collective-permute-start(f32[256,128]{1,0:T(8,128)S(1)} %get-tuple-element.35), channel_id=1, source_target_pairs={{0,24},{4,28},{8,16},{12,20},{16,8},{20,12},{24,0},{28,4},{1,25},{... | collective-permute-start | bytes 393224 | tf_op jit(solution)/shard_map/ppermute | solution.py:340
  64.8 1.2 %collective-permute-start.15 = (f32[256,128]{1,0:T(8,128)S(1)}, f32[256,128]{1,0:T(8,128)S(1)}, u32[]{:S(2)}, u32[]{:S(2)}) collective-permute-start(f32[256,128]{1,0:T(8,128)S(1)} %get-tuple-element.37), channel_id=1, source_target_pairs={{0,16},{4,20},{8,24},{12,28},{16,0},{20,4},{24,8},{28,12},{1,17},{... | collective-permute-start | bytes 393224 | tf_op jit(solution)/shard_map/ppermute | solution.py:340
  66.0 1.4 %collective-permute-start.16 = (f32[256,128]{1,0:T(8,128)S(1)}, f32[256,128]{1,0:T(8,128)S(1)}, u32[]{:S(2)}, u32[]{:S(2)}) collective-permute-start(f32[256,128]{1,0:T(8,128)S(1)} %get-tuple-element.36), channel_id=1, source_target_pairs={{0,8},{4,12},{8,0},{12,4},{16,24},{20,28},{24,16},{28,20},{1,9},{5... | collective-permute-start | bytes 393224 | tf_op jit(solution)/shard_map/ppermute | solution.py:340
  67.5 4.8 %collective-permute-done.8 = f32[256,128]{1,0:T(8,128)S(1)} collective-permute-done((f32[256,128]{1,0:T(8,128)}, f32[256,128]{1,0:T(8,128)S(1)}, u32[]{:S(2)}, u32[]{:S(2)}) %collective-permute-start.8) | collective-permute-done | bytes 131104 | tf_op jit(solution)/shard_map/ppermute | solution.py:340
  72.2 0.9 add_add_fusion.refs_0_
  73.3 3.2 %collective-permute-start.11 = (f32[256,128]{1,0:T(8,128)S(1)}, f32[256,128]{1,0:T(8,128)S(1)}, u32[]{:S(2)}, u32[]{:S(2)}) collective-permute-start(f32[256,128]{1,0:T(8,128)S(1)} %add_add_fusion.refs_0_), channel_id=1, source_target_pairs={{0,2},{1,3},{2,0},{3,1},{4,6},{5,7},{6,4},{7,5},{8,10},{9,11},{10,... | collective-permute-start | bytes 393224 | tf_op jit(solution)/shard_map/ppermute | solution.py:340
  76.5 0.9 fusion.6.refs_0_
  77.4 1.6 %collective-permute-start.17 = (f32[256,128]{1,0:T(8,128)S(1)}, f32[256,128]{1,0:T(8,128)S(1)}, u32[]{:S(2)}, u32[]{:S(2)}) collective-permute-start(f32[256,128]{1,0:T(8,128)S(1)} %fusion.6.refs_0_), channel_id=1, source_target_pairs={{0,8},{4,12},{8,0},{12,4},{16,24},{20,28},{24,16},{28,20},{1,9},{5... | collective-permute-start | bytes 393224 | tf_op jit(solution)/shard_map/ppermute | solution.py:340
  79.0 0.8 collective-permute-start.18
  79.8 1.2 %collective-permute-start.19 = (f32[256,128]{1,0:T(8,128)S(1)}, f32[256,128]{1,0:T(8,128)S(1)}, u32[]{:S(2)}, u32[]{:S(2)}) collective-permute-start(f32[256,128]{1,0:T(8,128)S(1)} %fusion.6.refs_0_), channel_id=1, source_target_pairs={{0,24},{4,28},{8,16},{12,20},{16,8},{20,12},{24,0},{28,4},{1,25},{... | collective-permute-start | bytes 393224 | tf_op jit(solution)/shard_map/ppermute | solution.py:340
  81.1 1.4 %collective-permute-start.12 = (f32[256,128]{1,0:T(8,128)S(1)}, f32[256,128]{1,0:T(8,128)S(1)}, u32[]{:S(2)}, u32[]{:S(2)}) collective-permute-start(f32[256,128]{1,0:T(8,128)S(1)} %add_add_fusion.refs_0_), channel_id=1, source_target_pairs={{0,3},{1,2},{2,1},{3,0},{4,7},{5,6},{6,5},{7,4},{8,11},{9,10},{10,... | collective-permute-start | bytes 393224 | tf_op jit(solution)/shard_map/ppermute | solution.py:340
  82.6 0.8 collective-permute-done.17.refs_1_
  83.4 3.0 %collective-permute-done.18.refs_2_ = f32[256,128]{1,0:T(8,128)S(1)} collective-permute-done((f32[256,128]{1,0:T(8,128)S(1)}, f32[256,128]{1,0:T(8,128)S(1)}, u32[]{:S(2)}, u32[]{:S(2)}) %collective-permute-start.18) | collective-permute-done | bytes 131104 | tf_op jit(solution)/shard_map/ppermute | solution.py:340
  86.9 1.1 %collective-permute-done.12.refs_3_ = f32[256,128]{1,0:T(8,128)S(1)} collective-permute-done((f32[256,128]{1,0:T(8,128)S(1)}, f32[256,128]{1,0:T(8,128)S(1)}, u32[]{:S(2)}, u32[]{:S(2)}) %collective-permute-start.12) | collective-permute-done | bytes 131104 | tf_op jit(solution)/shard_map/ppermute | solution.py:340
  88.6 2.6 %finish_query.1 = (f32[16,64,128]{2,1,0:T(8,128)}, f32[16,64]{1,0:T(8,128)}) custom-call(s32[3]{0:T(128)} %pad_add_fusion.place_ref, bf16[16,64,128]{2,1,0:T(8,128)(2,1)} %query_ref.5, f32[16,64]{1,0:T(8,128)} %weight_ref.3, f32[256,128]{1,0:T(8,128)} %copy-done, f32[256,128]{1,0:T(8,128)} %copy-done.9, f32[256,128]{1,0:T(8,128)} %copy-done.10, ...), custom_call_target="tpu_custom_call" | custom-call | tf_op jit(solution)/shard_map/finish_query/pallas_call | solution.py:289
  92.6 2.3 %finish_keys.1 = f32[2048,128]{1,0:T(8,128)} custom-call(s32[3]{0:T(128)} %pad_add_fusion.place_ref, f32[256,128]{1,0:T(8,128)} %copy-done.1, f32[256,128]{1,0:T(8,128)} %copy-done.2, f32[256,128]{1,0:T(8,128)} %copy-done.3, f32[256,128]{1,0:T(8,128)} %copy-done.4, f32[256,128]{1,0:T(8,128)} %copy-done.5, f32[256,128]{1,0:T(8,128)} %copy-done.6, ...), custom_call_target="tpu_custom_call" | custom-call | tf_op jit(solution)/shard_map/finish_keys/pallas_call | solution.py:317
  (67 shorter events, 7.8 us)
Async XLA Ops:
  21.2 7.1 %collective-permute-start = (f32[24,256]{1,0:T(8,128)}, f32[24,256]{1,0:T(8,128)S(1)}, u32[]{:S(2)}, u32[]{:S(2)}) collective-permute-start(f32[24,256]{1,0:T(8,128)} %get-tuple-element.22.refs_0_), channel_id=1, source_target_pairs={{0,3},{1,2},{2,1},{3,0},{4,7},{5,6},{6,5},{7,4},{8,11},{9,10},{10,... | collective-permute-start | bytes 73736 | tf_op jit(solution)/shard_map/ppermute | solution.py:340
  26.3 4.9 %collective-permute-start.1 = (f32[24,256]{1,0:T(8,128)}, f32[24,256]{1,0:T(8,128)S(1)}, u32[]{:S(2)}, u32[]{:S(2)}) collective-permute-start(f32[24,256]{1,0:T(8,128)} %get-tuple-element.22.refs_0_), channel_id=1, source_target_pairs={{0,2},{1,3},{2,0},{3,1},{4,6},{5,7},{6,4},{7,5},{8,10},{9,11},{10,... | collective-permute-start | bytes 73736 | tf_op jit(solution)/shard_map/ppermute | solution.py:340
  26.3 4.9 %collective-permute-start.2 = (f32[24,256]{1,0:T(8,128)}, f32[24,256]{1,0:T(8,128)S(1)}, u32[]{:S(2)}, u32[]{:S(2)}) collective-permute-start(f32[24,256]{1,0:T(8,128)} %get-tuple-element.22.refs_0_), channel_id=1, source_target_pairs={{0,1},{1,0},{2,3},{3,2},{4,5},{5,4},{6,7},{7,6},{8,9},{9,8},{10,11... | collective-permute-start | bytes 73736 | tf_op jit(solution)/shard_map/ppermute | solution.py:340
  31.9 13.4 %copy-start.18 = (f32[16]{0:T(128)S(1)}, f32[16]{0:T(128)}, u32[]{:S(2)}) copy-start(f32[16]{0:T(128)} %param.13) | copy-start | bytes 196
  37.8 2.1 %collective-permute-start.3 = (f32[4,16,2048]{2,1,0:T(8,128)}, f32[4,16,2048]{2,1,0:T(8,128)S(1)}, u32[]{:S(2)}, u32[]{:S(2)}) collective-permute-start(f32[4,16,2048]{2,1,0:T(8,128)} %get-tuple-element.26), channel_id=1, source_target_pairs={{0,4},{4,0},{8,12},{12,8},{16,20},{20,16},{24,28},{28,24},{1,5},{5... | collective-permute-start | bytes 1572872 | tf_op jit(solution)/shard_map/ppermute | solution.py:340
  41.8 6.7 %collective-permute-start.4 = (f32[16,2048]{1,0:T(8,128)S(1)}, f32[16,2048]{1,0:T(8,128)S(1)}, u32[]{:S(2)}, u32[]{:S(2)}) collective-permute-start(f32[16,2048]{1,0:T(8,128)S(1)} %get-tuple-element.40), channel_id=1, source_target_pairs={{0,24},{4,28},{8,16},{12,20},{16,8},{20,12},{24,0},{28,4},{1,25},{... | collective-permute-start | bytes 393224 | tf_op jit(solution)/shard_map/ppermute | solution.py:340
  44.2 6.8 %collective-permute-start.5 = (f32[16,2048]{1,0:T(8,128)S(1)}, f32[16,2048]{1,0:T(8,128)S(1)}, u32[]{:S(2)}, u32[]{:S(2)}) collective-permute-start(f32[16,2048]{1,0:T(8,128)S(1)} %get-tuple-element.39), channel_id=1, source_target_pairs={{0,16},{4,20},{8,24},{12,28},{16,0},{20,4},{24,8},{28,12},{1,17},{... | collective-permute-start | bytes 393224 | tf_op jit(solution)/shard_map/ppermute | solution.py:340
  44.7 6.4 %collective-permute-start.6 = (f32[16,2048]{1,0:T(8,128)S(1)}, f32[16,2048]{1,0:T(8,128)S(1)}, u32[]{:S(2)}, u32[]{:S(2)}) collective-permute-start(f32[16,2048]{1,0:T(8,128)S(1)} %get-tuple-element.38), channel_id=1, source_target_pairs={{0,8},{4,12},{8,0},{12,4},{16,24},{20,28},{24,16},{28,20},{1,9},{5... | collective-permute-start | bytes 393224 | tf_op jit(solution)/shard_map/ppermute | solution.py:340
  57.4 4.5 %collective-permute-start.13 = (f32[4,256,128]{2,1,0:T(8,128)}, f32[4,256,128]{2,1,0:T(8,128)S(1)}, u32[]{:S(2)}, u32[]{:S(2)}) collective-permute-start(f32[4,256,128]{2,1,0:T(8,128)} %get-tuple-element.33), channel_id=1, source_target_pairs={{0,4},{4,0},{8,12},{12,8},{16,20},{20,16},{24,28},{28,24},{1,5},{5... | collective-permute-start | bytes 1572872 | tf_op jit(solution)/shard_map/ppermute | solution.py:340
  57.4 8.6 %collective-permute-start.7 = (f32[256,128]{1,0:T(8,128)}, f32[256,128]{1,0:T(8,128)S(1)}, u32[]{:S(2)}, u32[]{:S(2)}) collective-permute-start(f32[256,128]{1,0:T(8,128)} %get-tuple-element.28), channel_id=1, source_target_pairs={{0,3},{1,2},{2,1},{3,0},{4,7},{5,6},{6,5},{7,4},{8,11},{9,10},{10,... | collective-permute-start | bytes 393224 | tf_op jit(solution)/shard_map/ppermute | solution.py:340
  59.0 13.3 %collective-permute-start.8 = (f32[256,128]{1,0:T(8,128)}, f32[256,128]{1,0:T(8,128)S(1)}, u32[]{:S(2)}, u32[]{:S(2)}) collective-permute-start(f32[256,128]{1,0:T(8,128)} %get-tuple-element.29), channel_id=1, source_target_pairs={{0,2},{1,3},{2,0},{3,1},{4,6},{5,7},{6,4},{7,5},{8,10},{9,11},{10,... | collective-permute-start | bytes 393224 | tf_op jit(solution)/shard_map/ppermute | solution.py:340
  59.6 12.6 %collective-permute-start.9 = (f32[256,128]{1,0:T(8,128)}, f32[256,128]{1,0:T(8,128)S(1)}, u32[]{:S(2)}, u32[]{:S(2)}) collective-permute-start(f32[256,128]{1,0:T(8,128)} %get-tuple-element.30), channel_id=1, source_target_pairs={{0,1},{1,0},{2,3},{3,2},{4,5},{5,4},{6,7},{7,6},{8,9},{9,8},{10,11... | collective-permute-start | bytes 393224 | tf_op jit(solution)/shard_map/ppermute | solution.py:340
  63.0 13.5 %collective-permute-start.14 = (f32[256,128]{1,0:T(8,128)S(1)}, f32[256,128]{1,0:T(8,128)S(1)}, u32[]{:S(2)}, u32[]{:S(2)}) collective-permute-start(f32[256,128]{1,0:T(8,128)S(1)} %get-tuple-element.35), channel_id=1, source_target_pairs={{0,24},{4,28},{8,16},{12,20},{16,8},{20,12},{24,0},{28,4},{1,25},{... | collective-permute-start | bytes 393224 | tf_op jit(solution)/shard_map/ppermute | solution.py:340
  64.8 11.7 %collective-permute-start.15 = (f32[256,128]{1,0:T(8,128)S(1)}, f32[256,128]{1,0:T(8,128)S(1)}, u32[]{:S(2)}, u32[]{:S(2)}) collective-permute-start(f32[256,128]{1,0:T(8,128)S(1)} %get-tuple-element.37), channel_id=1, source_target_pairs={{0,16},{4,20},{8,24},{12,28},{16,0},{20,4},{24,8},{28,12},{1,17},{... | collective-permute-start | bytes 393224 | tf_op jit(solution)/shard_map/ppermute | solution.py:340
  66.0 10.5 %collective-permute-start.16 = (f32[256,128]{1,0:T(8,128)S(1)}, f32[256,128]{1,0:T(8,128)S(1)}, u32[]{:S(2)}, u32[]{:S(2)}) collective-permute-start(f32[256,128]{1,0:T(8,128)S(1)} %get-tuple-element.36), channel_id=1, source_target_pairs={{0,8},{4,12},{8,0},{12,4},{16,24},{20,28},{24,16},{28,20},{1,9},{5... | collective-permute-start | bytes 393224 | tf_op jit(solution)/shard_map/ppermute | solution.py:340
  73.2 14.8 %copy-start = (f32[256,128]{1,0:T(8,128)}, f32[256,128]{1,0:T(8,128)S(1)}, u32[]{:S(2)}) copy-start(f32[256,128]{1,0:T(8,128)S(1)} %add_add_fusion.refs_0_) | copy-start | bytes 393220
  73.2 7.9 %collective-permute-start.10 = (f32[256,128]{1,0:T(8,128)S(1)}, f32[256,128]{1,0:T(8,128)S(1)}, u32[]{:S(2)}, u32[]{:S(2)}) collective-permute-start(f32[256,128]{1,0:T(8,128)S(1)} %add_add_fusion.refs_0_), channel_id=1, source_target_pairs={{0,1},{1,0},{2,3},{3,2},{4,5},{5,4},{6,7},{7,6},{8,9},{9,8},{10,11... | collective-permute-start | bytes 393224 | tf_op jit(solution)/shard_map/ppermute | solution.py:340
  73.3 9.3 %collective-permute-start.11 = (f32[256,128]{1,0:T(8,128)S(1)}, f32[256,128]{1,0:T(8,128)S(1)}, u32[]{:S(2)}, u32[]{:S(2)}) collective-permute-start(f32[256,128]{1,0:T(8,128)S(1)} %add_add_fusion.refs_0_), channel_id=1, source_target_pairs={{0,2},{1,3},{2,0},{3,1},{4,6},{5,7},{6,4},{7,5},{8,10},{9,11},{10,... | collective-permute-start | bytes 393224 | tf_op jit(solution)/shard_map/ppermute | solution.py:340
  77.4 13.8 %copy-start.1 = (f32[256,128]{1,0:T(8,128)}, f32[256,128]{1,0:T(8,128)S(1)}, u32[]{:S(2)}) copy-start(f32[256,128]{1,0:T(8,128)S(1)} %fusion.6.refs_0_) | copy-start | bytes 393220
  77.4 5.9 %collective-permute-start.17 = (f32[256,128]{1,0:T(8,128)S(1)}, f32[256,128]{1,0:T(8,128)S(1)}, u32[]{:S(2)}, u32[]{:S(2)}) collective-permute-start(f32[256,128]{1,0:T(8,128)S(1)} %fusion.6.refs_0_), channel_id=1, source_target_pairs={{0,8},{4,12},{8,0},{12,4},{16,24},{20,28},{24,16},{28,20},{1,9},{5... | collective-permute-start | bytes 393224 | tf_op jit(solution)/shard_map/ppermute | solution.py:340
  79.0 7.4 %collective-permute-start.18 = (f32[256,128]{1,0:T(8,128)S(1)}, f32[256,128]{1,0:T(8,128)S(1)}, u32[]{:S(2)}, u32[]{:S(2)}) collective-permute-start(f32[256,128]{1,0:T(8,128)S(1)} %fusion.6.refs_0_), channel_id=1, source_target_pairs={{0,16},{4,20},{8,24},{12,28},{16,0},{20,4},{24,8},{28,12},{1,17},{... | collective-permute-start | bytes 393224 | tf_op jit(solution)/shard_map/ppermute | solution.py:340
  79.8 6.6 %collective-permute-start.19 = (f32[256,128]{1,0:T(8,128)S(1)}, f32[256,128]{1,0:T(8,128)S(1)}, u32[]{:S(2)}, u32[]{:S(2)}) collective-permute-start(f32[256,128]{1,0:T(8,128)S(1)} %fusion.6.refs_0_), channel_id=1, source_target_pairs={{0,24},{4,28},{8,16},{12,20},{16,8},{20,12},{24,0},{28,4},{1,25},{... | collective-permute-start | bytes 393224 | tf_op jit(solution)/shard_map/ppermute | solution.py:340
  81.1 6.9 %copy-start.9 = (f32[256,128]{1,0:T(8,128)}, f32[256,128]{1,0:T(8,128)S(1)}, u32[]{:S(2)}) copy-start(f32[256,128]{1,0:T(8,128)S(1)} %collective-permute-done.10.refs_1_) | copy-start | bytes 393220
  81.1 6.9 %collective-permute-start.12 = (f32[256,128]{1,0:T(8,128)S(1)}, f32[256,128]{1,0:T(8,128)S(1)}, u32[]{:S(2)}, u32[]{:S(2)}) collective-permute-start(f32[256,128]{1,0:T(8,128)S(1)} %add_add_fusion.refs_0_), channel_id=1, source_target_pairs={{0,3},{1,2},{2,1},{3,0},{4,7},{5,6},{6,5},{7,4},{8,11},{9,10},{10,... | collective-permute-start | bytes 393224 | tf_op jit(solution)/shard_map/ppermute | solution.py:340
  82.6 5.4 %copy-start.10 = (f32[256,128]{1,0:T(8,128)}, f32[256,128]{1,0:T(8,128)S(1)}, u32[]{:S(2)}) copy-start(f32[256,128]{1,0:T(8,128)S(1)} %collective-permute-done.11.refs_2_) | copy-start | bytes 393220
  82.6 8.6 %collective-permute-start.20 = (f32[256,128]{1,0:T(8,128)S(1)}, f32[256,128]{1,0:T(8,128)S(1)}, u32[]{:S(2)}, u32[]{:S(2)}) collective-permute-start(f32[256,128]{1,0:T(8,128)S(1)} %fusion.6.refs_0_), channel_id=1, source_target_pairs={{0,4},{4,0},{8,12},{12,8},{16,20},{20,16},{24,28},{28,24},{1,5},{5... | collective-permute-start | bytes 393224 | tf_op jit(solution)/shard_map/ppermute | solution.py:340
  83.3 7.9 %copy-start.2 = (f32[256,128]{1,0:T(8,128)}, f32[256,128]{1,0:T(8,128)S(1)}, u32[]{:S(2)}) copy-start(f32[256,128]{1,0:T(8,128)S(1)} %collective-permute-done.17.refs_1_) | copy-start | bytes 393220
  83.4 7.9 %collective-permute-start.21 = (f32[256,128]{1,0:T(8,128)S(1)}, f32[256,128]{1,0:T(8,128)S(1)}, u32[]{:S(2)}, u32[]{:S(2)}) collective-permute-start(f32[256,128]{1,0:T(8,128)S(1)} %collective-permute-done.17.refs_1_), channel_id=1, source_target_pairs={{0,4},{4,0},{8,12},{12,8},{16,20},{20,16},{24,28},{28,24},{1,5},{5... | collective-permute-start | bytes 393224 | tf_op jit(solution)/shard_map/ppermute | solution.py:340
  86.4 4.9 %copy-start.3 = (f32[256,128]{1,0:T(8,128)}, f32[256,128]{1,0:T(8,128)S(1)}, u32[]{:S(2)}) copy-start(f32[256,128]{1,0:T(8,128)S(1)} %collective-permute-done.18.refs_2_) | copy-start | bytes 393220
  86.4 4.9 %collective-permute-start.22 = (f32[256,128]{1,0:T(8,128)S(1)}, f32[256,128]{1,0:T(8,128)S(1)}, u32[]{:S(2)}, u32[]{:S(2)}) collective-permute-start(f32[256,128]{1,0:T(8,128)S(1)} %collective-permute-done.18.refs_2_), channel_id=1, source_target_pairs={{0,4},{4,0},{8,12},{12,8},{16,20},{20,16},{24,28},{28,24},{1,5},{5... | collective-permute-start | bytes 393224 | tf_op jit(solution)/shard_map/ppermute | solution.py:340
  86.4 4.9 %copy-start.4 = (f32[256,128]{1,0:T(8,128)}, f32[256,128]{1,0:T(8,128)S(1)}, u32[]{:S(2)}) copy-start(f32[256,128]{1,0:T(8,128)S(1)} %collective-permute-done.19.refs_3_) | copy-start | bytes 393220
  86.4 4.9 %collective-permute-start.23 = (f32[256,128]{1,0:T(8,128)S(1)}, f32[256,128]{1,0:T(8,128)S(1)}, u32[]{:S(2)}, u32[]{:S(2)}) collective-permute-start(f32[256,128]{1,0:T(8,128)S(1)} %collective-permute-done.19.refs_3_), channel_id=1, source_target_pairs={{0,4},{4,0},{8,12},{12,8},{16,20},{20,16},{24,28},{28,24},{1,5},{5... | collective-permute-start | bytes 393224 | tf_op jit(solution)/shard_map/ppermute | solution.py:340
  (11 other events, 11.5 us)

commit v2 on v0

v2 whole, which is shorter than its diff:
```python
import math

import jax
import jax.numpy as jnp
from jax import lax
from jax.experimental import pallas as pl
from jax.experimental.pallas import tpu as pltpu
from jax.sharding import PartitionSpec as P

H = 128

LOG2E = math.log2(math.e)
score_scale = 192.0 ** (-0.5) * LOG2E
masked_fill = -1e30

F32 = jnp.float32
BF16 = jnp.bfloat16
MIB = 1024 * 1024

vmem_spec = pl.BlockSpec(memory_space=pltpu.VMEM)
any_spec = pl.BlockSpec(memory_space=pl.ANY)


def in_vmem(array):
    return pltpu.with_memory_space_constraint(array, pltpu.VMEM)


def in_hbm(array):
    return pltpu.with_memory_space_constraint(array, pltpu.HBM)


def vmem_call(body, name, outs, operands, scratch=(), out_specs=None, limit=32 * MIB, cost=0):
    several = isinstance(outs, (tuple, list))
    if out_specs is None:
        out_specs = tuple(vmem_spec for _ in outs) if several else vmem_spec
    return pl.pallas_call(
        body,
        out_shape=outs,
        in_specs=[vmem_spec] * len(operands),
        out_specs=out_specs,
        scratch_shapes=list(scratch),
        compiler_params=pltpu.CompilerParams(vmem_limit_bytes=limit),
        cost_estimate=pl.CostEstimate(flops=cost, bytes_accessed=0, transcendentals=0),
        name=name,
    )(*[in_vmem(a) for a in operands])


def tile_of(extent, wanted):
    return wanted if extent % wanted == 0 else extent


def rows_of(ref, first, count):
    return ref[pl.ds(pl.multiple_of(first, count), count)]


def head_place():
    at = lax.axis_index("heads")
    return at // 2, at % 2


def index_forward(query_pos, index_query, index_keys, index_weight, groups, after):
    rows, heads, width = index_query.shape
    keys = index_keys.shape[0]
    tile = tile_of(keys, 256)
    own = rows // groups

    def body(pos_ref, query_ref, keys_ref, weight_ref, _, score_ref, lse_ref, wiq_ref):
        columns = weight_ref[...].T
        flat = query_ref[...].reshape(rows * heads, width)
        for row in range(rows):
            piece = query_ref[row].astype(F32) * columns[:, row : row + 1]
            wiq_ref[row // own, :, (row % own) * heads : (row % own + 1) * heads] = piece.T.astype(BF16)
        first_key = lax.axis_index("keys") * keys
        first_row = lax.axis_index("heads") * rows
        for at in range(0, keys, tile):
            logits = lax.dot_general(
                flat, keys_ref[at : at + tile, :], (((1,), (1,)), ((), ())), preferred_element_type=F32
            )
            index = first_key + at + lax.broadcasted_iota(jnp.int32, (1, tile), 1)
            for row in range(rows):
                active = jnp.maximum(logits[row * heads : (row + 1) * heads, :], 0.0)
                summed = jnp.sum(active * columns[:, row : row + 1], axis=0, keepdims=True)
                seen = index <= pos_ref[first_row + row]
                score_ref[row : row + 1, at : at + tile] = jnp.where(seen, summed * LOG2E, masked_fill)
        scores = score_ref[...]
        top = jnp.max(scores, axis=1, keepdims=True)
        total = jnp.sum(jnp.exp2(scores - top), axis=1, keepdims=True)
        lse_ref[...] = jnp.broadcast_to(top + jnp.log2(total), lse_ref.shape)

    return pl.pallas_call(
        body,
        out_shape=(
            pltpu.VMEM((rows, keys), F32),
            pltpu.VMEM((rows, 128), F32),
            pltpu.VMEM((groups, width, own * heads), BF16),
        ),
        in_specs=[pl.BlockSpec(memory_space=pltpu.SMEM)] + [vmem_spec] * 4,
        out_specs=(vmem_spec,) * 3,
        compiler_params=pltpu.CompilerParams(vmem_limit_bytes=32 * MIB),
        cost_estimate=pl.CostEstimate(flops=10**9, bytes_accessed=0, transcendentals=0),
        name="index_forward",
    )(query_pos, *[in_vmem(a) for a in (index_query, index_keys, index_weight, after)])


def main_scores(pos, query_t, keys_t):
    head_local, feature, queries = query_t.shape
    keys = keys_t.shape[1]
    per = 256 // queries if queries < 256 and head_local % (256 // queries) == 0 else 1
    lanes = per * queries
    blocks = head_local // per
    tile = tile_of(keys, 128)
    tiles = keys // tile
    mask_at = -(-feature // 128) * 128
    depth = mask_at + -(-queries // 128) * 128

    def body(pos_ref, query_ref, keys_ref, prob_ref, top_ref, stat_ref, key_rows, weights):
        step = pl.program_id(0)

        @pl.when(step == 0)
        def _():
            chunk = tile_of(keys, 512)
            for at in range(0, keys, chunk):
                key_rows[at : at + chunk, :feature] = keys_ref[:, at : at + chunk].T
            if mask_at > feature:
                key_rows[:, feature:mask_at] = jnp.zeros((keys, mask_at - feature), BF16)
                weights[feature:mask_at, :] = jnp.zeros((mask_at - feature, lanes), BF16)
            index = lax.axis_index("keys") * keys + lax.broadcasted_iota(jnp.int32, (keys, queries), 0)
            hidden = jnp.where(index <= pos_ref[...], 0.0, masked_fill).astype(BF16)
            key_rows[:, mask_at : mask_at + queries] = hidden
            at_row = lax.broadcasted_iota(jnp.int32, (depth - mask_at, lanes), 0)
            at_lane = lax.broadcasted_iota(jnp.int32, (depth - mask_at, lanes), 1)
            weights[mask_at:, :] = jnp.where(at_row == at_lane % queries, 1.0, 0.0).astype(BF16)
            if depth > mask_at + queries:
                key_rows[:, mask_at + queries :] = jnp.zeros((keys, depth - mask_at - queries), BF16)

        for i in range(per):
            weights[:feature, i * queries : (i + 1) * queries] = query_ref[i]
        tops, totals = [], []
        for t in range(tiles):
            span = slice(t * tile, (t + 1) * tile)
            scores = jnp.dot(key_rows[span, :], weights[...], preferred_element_type=F32)
            top = jnp.max(scores, axis=0, keepdims=True)
            prob = jnp.exp2((scores - top) * score_scale)
            top = top * score_scale
            tops.append(top)
            totals.append(jnp.sum(prob, axis=0, keepdims=True))
            prob_ref[step, span, :] = prob.astype(prob_ref.dtype)
            top_ref[step, t : t + 1, :] = top
        best = tops[0]
        for top in tops[1:]:
            best = jnp.maximum(best, top)
        total = sum(s * jnp.exp2(top - best) for s, top in zip(totals, tops))
        stat_ref[pl.ds(step, 1), :] = best + jnp.log2(total)

    return pl.pallas_call(
        body,
        grid=(blocks,),
        out_shape=(
            pltpu.VMEM((blocks, keys, lanes), BF16),
            pltpu.VMEM((blocks, tiles, lanes), F32),
            pltpu.VMEM((blocks, lanes), F32),
        ),
        in_specs=[
            pl.BlockSpec((1, queries), lambda i: (0, 0)),
            pl.BlockSpec((per, feature, queries), lambda i: (i, 0, 0)),
            pl.BlockSpec((feature, keys), lambda i: (0, 0)),
        ],
        out_specs=(vmem_spec,) * 3,
        scratch_shapes=[pltpu.VMEM((keys, depth), BF16), pltpu.VMEM((depth, lanes), BF16)],
        compiler_params=pltpu.CompilerParams(vmem_limit_bytes=28 * MIB),
        name="main_scores",
    )(pos, in_hbm(query_t), in_hbm(keys_t))


def joined(stats):
    best = stats[0]
    for stat in stats[1:]:
        best = jnp.maximum(best, stat)
    return best + jnp.log2(sum(jnp.exp2(stat - best) for stat in stats))


def head_sum(probs, tops, stats, queries, row_local):
    blocks, keys, lanes = probs.shape
    tiles = tops.shape[1]
    tile = keys // tiles
    per = lanes // queries
    chips = queries // row_local // 2

    def body(prob_ref, top_ref, *refs):
        stat_refs, (keep_ref, send_ref, summed) = refs[:-3], refs[-3:]
        whole = joined([ref[...] for ref in stat_refs])
        factors = [jnp.exp2(top_ref[b] - whole[b : b + 1, :]) * (1.0 / H) for b in range(blocks)]
        for t in range(tiles):
            span = slice(t * tile, (t + 1) * tile)
            total = None
            for b in range(blocks):
                part = prob_ref[b, span, :].astype(F32) * factors[b][t : t + 1, :]
                for i in range(per):
                    piece = part[:, i * queries : (i + 1) * queries]
                    total = piece if total is None else total + piece
            summed[:, span] = total.T
        chip, core = head_place()
        for r in range(chips):
            first = (chip ^ r) * 2
            keep_ref[r] = rows_of(summed, (first + core) * row_local, row_local)
            send_ref[r] = rows_of(summed, (first + 1 - core) * row_local, row_local)

    half = pltpu.VMEM((chips, row_local, keys), F32)
    return vmem_call(
        body, "head_sum", (half, half), (probs, tops, *stats), [pltpu.VMEM((queries, keys), F32)], cost=10**9
    )


def add_stacks(left, right):
    count = left.shape[0]

    def body(left_ref, right_ref, *outs):
        for r in range(count):
            outs[r][...] = left_ref[r] + right_ref[r]

    return vmem_call(
        body, "add_stacks", tuple(pltpu.VMEM(left.shape[1:], F32) for _ in range(count)), (left, right)
    )


def add_all(parts):
    def body(*refs):
        total = refs[0][...]
        for ref in refs[1:-1]:
            total = total + ref[...]
        refs[-1][...] = total

    return vmem_call(body, "add_all", pltpu.VMEM(parts[0].shape, F32), parts)


def deltas(scores, stats, targets, kl, groups):
    rows, keys = scores.shape
    own = rows // groups

    def body(score_ref, kl_ref, *refs):
        stat_refs, target_refs, out_ref = refs[: len(stats)], refs[len(stats) : -1], refs[-1]
        whole = joined([ref[:, :1] for ref in stat_refs])
        target = target_refs[0][...]
        for ref in target_refs[1:]:
            target = target + ref[...]
        delta = kl_ref[...] * (jnp.exp2(score_ref[...] - whole) - target)
        for g in range(groups):
            out_ref[g] = delta[g * own : (g + 1) * own, :]

    return vmem_call(body, "deltas", pltpu.VMEM((groups, own, keys), F32), (scores, kl, *stats, *targets))


def query_part(r, delta, index_query, index_keys):
    groups, own, keys = delta.shape
    heads, width = index_query.shape[1:]
    tile = tile_of(keys, 512)

    def body(delta_ref, query_ref, keys_ref, slope_ref, out_ref):
        group = lax.axis_index("keys") ^ r
        flat = query_ref[pl.ds(group * own, own)].reshape(own * heads, width)
        for at in range(0, keys, tile):
            span = slice(at, at + tile)
            logits = lax.dot_general(
                flat, keys_ref[span, :], (((1,), (1,)), ((), ())), preferred_element_type=F32
            ).astype(BF16)
            delta_rows = delta_ref[group, :, span]
            for row in range(own):
                line = jnp.broadcast_to(delta_rows[row : row + 1, :], (heads, tile)).astype(BF16)
                part = slice(row * heads, (row + 1) * heads)
                slope_ref[part, span] = jnp.where(logits[part, :] > 0, line, jnp.zeros((), BF16))
        out_ref[...] = jnp.dot(slope_ref[...], keys_ref[...], preferred_element_type=F32)

    outs = (pltpu.VMEM((own * heads, keys), BF16), pltpu.VMEM((own * heads, width), F32))
    return vmem_call(body, "query_part", outs, (delta, index_query, index_keys), cost=3 * 10**8)


def key_part(slopes, wiq, head_devices):
    groups, width = wiq.shape[:2]
    keys = slopes[0].shape[1]
    tile = tile_of(keys, 512)
    chips = head_devices // 2
    chunk = keys // head_devices

    def body(wiq_ref, *refs):
        slope_refs, (keep_ref, send_ref, total) = refs[:groups], refs[groups:]
        z = lax.axis_index("keys")
        for at in range(0, keys, tile):
            span = slice(at, at + tile)
            summed = None
            for r in range(groups):
                part = jnp.dot(wiq_ref[z ^ r], slope_refs[r][:, span], preferred_element_type=F32)
                summed = part if summed is None else summed + part
            total[span, :] = summed.T
        chip, core = head_place()
        for r in range(chips):
            first = (chip ^ r) * 2
            keep_ref[r] = rows_of(total, (first + core) * chunk, chunk)
            send_ref[r] = rows_of(total, (first + 1 - core) * chunk, chunk)

    half = pltpu.VMEM((chips, chunk, width), F32)
    return vmem_call(
        body, "key_part", (half, half), (wiq, *slopes), [pltpu.VMEM((keys, width), F32)], cost=10**9
    )


def own_rows(parts, index_query, index_weight):
    rows, heads, width = index_query.shape
    size = parts[0].shape[0]
    own = size // heads
    extra = -(-own // 8) * 8

    def body(query_ref, weight_ref, *refs):
        first = lax.axis_index("keys") * own
        part_refs, out_ref = refs[:-1], refs[-1]
        columns = weight_ref[...].T
        lane = lax.broadcasted_iota(jnp.int32, (heads, rows), 1)
        for i in range(own):
            span = slice(i * heads, (i + 1) * heads)
            total = part_refs[0][span, :]
            for ref in part_refs[1:]:
                total = total + ref[span, :]
            column = jnp.sum(jnp.where(lane == first + i, columns, 0.0), axis=1, keepdims=True)
            out_ref[span, :] = total * column
            summed = jnp.sum(total * query_ref[first + i].astype(F32), axis=1, keepdims=True)
            line = summed.T
            out_ref[size + i : size + i + 1, :] = jnp.concatenate(
                [line, jnp.zeros((1, width - heads), F32)], axis=1
            )
        if extra > own:
            out_ref[size + own :, :] = jnp.zeros((extra - own, width), F32)

    return vmem_call(
        body, "own_rows", pltpu.VMEM((size + extra, width), F32), (index_query, index_weight, *parts)
    )


def place_query(pieces, rows, heads):
    own = rows // len(pieces)
    size = own * heads
    width = pieces[0].shape[1]

    def body(*refs):
        piece_refs, (query_out, weight_out, sems) = refs[: len(pieces)], refs[len(pieces) :]
        z = lax.axis_index("keys")
        copies = []
        for r, ref in enumerate(piece_refs):
            at = pl.multiple_of((z ^ r) * size, size)
            copies.append(pltpu.make_async_copy(ref.at[:size], query_out.at[pl.ds(at, size)], sems.at[r]))
            copies[-1].start()
        for r, ref in enumerate(piece_refs):
            weight_out[pl.ds((z ^ r) * own, own), :] = ref[size : size + own, :heads]
        for copy in copies:
            copy.wait()

    query, weight = vmem_call(
        body,
        "place_query",
        (jax.ShapeDtypeStruct((rows * heads, width), F32), jax.ShapeDtypeStruct((rows, heads), F32)),
        pieces,
        [pltpu.SemaphoreType.DMA((len(pieces),))],
        out_specs=(any_spec, vmem_spec),
    )
    return query.reshape(rows, heads, width), weight


def place_keys(mine, others):
    chips = len(mine)
    chunk, width = mine[0].shape

    def body(*refs):
        out_ref, sems = refs[-2:]
        chip, core = head_place()
        copies = []
        for r in range(chips):
            for side in range(2):
                at = pl.multiple_of(((chip ^ r) * 2 + (core ^ side)) * chunk, chunk)
                n = side * chips + r
                copies.append(pltpu.make_async_copy(refs[n], out_ref.at[pl.ds(at, chunk)], sems.at[n]))
                copies[-1].start()
        for copy in copies:
            copy.wait()

    return vmem_call(
        body,
        "place_keys",
        jax.ShapeDtypeStruct((2 * chips * chunk, width), F32),
        (*mine, *others),
        [pltpu.SemaphoreType.DMA((2 * chips,))],
        out_specs=any_spec,
    )


def shards(main_query, latent_keys, index_query, index_keys, index_weight, query_pos, kl_weight):
    queries = main_query.shape[0]
    row_local, index_heads, _ = index_query.shape
    head_devices = lax.axis_size("heads")
    key_devices = lax.axis_size("keys")
    chips = head_devices // 2

    def to_keys(value, bits):
        return lax.ppermute(value, "keys", [(i, i ^ bits) for i in range(key_devices)])

    def to_heads(value, bits):
        return lax.ppermute(value, "heads", [(i, i ^ bits) for i in range(head_devices)])

    far_first = list(reversed(range(1, key_devices)))
    chips_far_first = list(reversed(range(1, chips)))

    probs, tops, stat = main_scores(query_pos[None, :], main_query.transpose(1, 2, 0), latent_keys.T)
    stats = [stat] + [to_keys(stat, bits) for bits in far_first]
    scores, index_lse, wiq = index_forward(
        query_pos, index_query, index_keys, index_weight, key_devices, stat
    )
    keep, send = head_sum(probs, tops, stats, queries, row_local)
    sums = add_stacks(keep, to_heads(send, 1))
    targets = [sums[0]] + [to_heads(sums[r], 2 * r) for r in chips_far_first]
    index_lse, _ = lax.optimization_barrier((index_lse, sums[0]))
    index_stats = [index_lse] + [to_keys(index_lse, bits) for bits in far_first]
    delta = deltas(scores, index_stats, targets, kl_weight[:, None], key_devices)

    slopes, arrived = {}, []
    for r in far_first + [0]:
        slopes[r], part = query_part(r, delta, index_query, index_keys)
        arrived.append(to_keys(part, r) if r else part)
    keep, send = key_part([slopes[r] for r in range(key_devices)], wiq, head_devices)
    sums = add_stacks(keep, to_heads(send, 1))
    key_own = add_all([sums[0]] + [to_heads(sums[r], 2 * r) for r in chips_far_first])
    query_own = own_rows(arrived, index_query, index_weight)
    pieces = [query_own] + [to_keys(query_own, r) for r in range(1, key_devices)]
    mine = [key_own] + [to_heads(key_own, 2 * r) for r in range(1, chips)]
    others = [to_heads(piece, 1) for piece in mine]
    key_grad = place_keys(mine, others)
    query_grad, weight_grad = place_query(pieces, row_local, index_heads)
    return query_grad, key_grad, weight_grad


def solution(mesh):
    placed = (
        P(None, "heads", None),
        P("keys", None),
        P("heads", None, None),
        P("keys", None),
        P("heads", None),
        P(),
        P("heads"),
    )
    return jax.shard_map(
        shards,
        mesh=mesh,
        in_specs=placed,
        out_specs=(P("heads", None, None), P("keys", None), P("heads", None)),
        check_vma=False,
    )
```

time: 223 us -> 76.8 us (0.34)
  waiting for transfers between devices: 111 us -> 22.2 us
  blocking collectives: 35.8 us -> 0 us
  matrix products: 33.1 us -> 0 us
  starting transfers between devices: 0.12 us -> 29.7 us
  Pallas kernels: 0 us -> 23.1 us
  other arithmetic: 20.3 us -> 0 us
  between operations: 13.9 us -> 0.81 us
  local copies, waits for them, and re-layouts: 8.29 us -> 0.75 us
    psum x2 -> x0, waiting for transfers between devices: 74.8 us -> none  [the longest x1 60.4 us: shards(): key_grad = lax.psum(key_grad, 'heads')]
    reduce_scatter x1 -> x0, waiting for transfers between devices: 35.8 us -> none  [shards(): lax.psum_scatter(partial_value, 'heads', scatter_dimension=0, tiled=True)]
    dot_general x6 -> x0, matrix products: 33.1 us -> none  [the longest x2 14.1 us: contract_last(): lax.dot_general(left_side, right_side, (((1,), (1,)), ((), ())), preferre...]
    ppermute x0 -> x27, starting transfers between devices: none -> 29.7 us  [the longest x12 16.9 us: to_keys(): lax.ppermute(value, 'keys', [(i, i ^ bits) for i in range(key_devices)])]
    pallas_call x0 -> x15, Pallas kernels: none -> 23.1 us  [the longest x1 11.7 us: main_scores(): pl.pallas_call(body, grid=(blocks,), out_shape=(pltpu.VMEM((blocks, keys,...]
    ppermute x0 -> x27, waiting for transfers between devices: none -> 22.2 us  [the longest x12 19.5 us: to_keys(): lax.ppermute(value, 'keys', [(i, i ^ bits) for i in range(key_devices)])]
    psum x2 -> x0, blocking collectives: 21.7 us -> none  [the longest x1 12.4 us: shards(): query_grad, weight_grad = lax.psum((query_grad, weight_grad), 'keys')]
    reduce_sum x3 -> x0, other arithmetic: 18.2 us -> none  [the longest x1 9.57 us: shards(): partial_value = jnp.sum(main_probs, axis=1)]
  transfers between devices with their start and end apart: 3 -> 27, of which waited for: 3 -> 12; matrix products, arithmetic and copies ran while one was open for 5% -> 0% of each run, Pallas kernels for 0% -> 6%
where the time goes in v2:
time: 76.8 us; the launch traced here: 76.6 us
  starting transfers between devices  29.7 us (39%)
  Pallas kernels  23.1 us (30%)
  waiting for transfers between devices  22.2 us (29%)
  between operations  0.81 us (1%)
    ppermute x12, waiting for transfers between devices, to_keys(): lax.ppermute(value, 'keys', [(i, i ^ bits) for i in range(key_devices)])  19.5 us
    ppermute x12, starting transfers between devices, to_keys(): lax.ppermute(value, 'keys', [(i, i ^ bits) for i in range(key_devices)])  16.9 us
    ppermute x15, starting transfers between devices, to_heads(): lax.ppermute(value, 'heads', [(i, i ^ bits) for i in range(head_devices)])  12.8 us
    pallas_call x1, Pallas kernels, main_scores(): pl.pallas_call(body, grid=(blocks,), out_shape=(pltpu.VMEM((blocks, keys,...  11.7 us
    pallas_call x13, Pallas kernels, vmem_call(): pl.pallas_call(body, out_shape=outs, in_specs=[vmem_spec] * len(operands)...  8.66 us
    pallas_call x1, Pallas kernels, index_forward(): pl.pallas_call(body, out_shape=(pltpu.VMEM((rows, keys), F32), pltpu.VMEM...  2.73 us
    ppermute x15, waiting for transfers between devices, to_heads(): lax.ppermute(value, 'heads', [(i, i ^ bits) for i in range(head_devices)])  2.69 us
  transfers between devices with their start and end apart: 27, of which 12 were waited for; matrix products, arithmetic and copies ran while one was open for 0% of the time, Pallas kernels for 6%

profile of v2, /device:TPU:0, one launch (start us, length us, event | category | flops | bytes accessed | tf_op | source)
XLA Modules:
  0.0 76.6 jit_solution(6262579843547257008)
XLA Ops:
  1.3 11.7 %main_scores.1 = (bf16[8,2048,256]{2,1,0:T(8,128)(2,1)S(1)}, f32[8,16,256]{2,1,0:T(8,128)S(1)}, f32[8,256]{1,0:T(8,128)S(1)}) custom-call(s32[1,128]{1,0:T(1,128)S(1)} %bitcast.5, bf16[16,576,128]{2,1,0:T(8,128)(2,1)} %bitcast.6, bf16[576,2048]{1,0:T(8,128)(2,1)} %bitcast.7), custom_call_target="tpu_custom_call" | custom-call | tf_op jit(solution)/shard_map/main_scores/pallas_call | solution.py:155
  13.0 5.1 %collective-permute-start = (f32[8,256]{1,0:T(8,128)S(1)}, f32[8,256]{1,0:T(8,128)S(1)}, u32[]{:S(2)}, u32[]{:S(2)}) collective-permute-start(f32[8,256]{1,0:T(8,128)S(1)} %get-tuple-element.32._.refs_0_), channel_id=1, source_target_pairs={{0,3},{1,2},{2,1},{3,0},{4,7},{5,6},{6,5},{7,4},{8,11},{9,10},{10,... | collective-permute-start | bytes 24584 | tf_op jit(solution)/shard_map/ppermute | solution.py:401
  18.8 1.0 %collective-permute-done.refs_1_ = f32[8,256]{1,0:T(8,128)S(1)} collective-permute-done((f32[8,256]{1,0:T(8,128)S(1)}, f32[8,256]{1,0:T(8,128)S(1)}, u32[]{:S(2)}, u32[]{:S(2)}) %collective-permute-start) | collective-permute-done | bytes 8224 | tf_op jit(solution)/shard_map/ppermute | solution.py:401
  19.8 2.9 %collective-permute-done.1.refs_2_ = f32[8,256]{1,0:T(8,128)S(1)} collective-permute-done((f32[8,256]{1,0:T(8,128)S(1)}, f32[8,256]{1,0:T(8,128)S(1)}, u32[]{:S(2)}, u32[]{:S(2)}) %collective-permute-start.1) | collective-permute-done | bytes 8224 | tf_op jit(solution)/shard_map/ppermute | solution.py:401
  22.7 1.8 %head_sum.1 = (f32[4,16,2048]{2,1,0:T(8,128)S(1)}, f32[4,16,2048]{2,1,0:T(8,128)S(1)}) custom-call(bf16[8,2048,256]{2,1,0:T(8,128)(2,1)S(1)} %get-tuple-element.35.prob_ref, f32[8,16,256]{2,1,0:T(8,128)S(1)} %get-tuple-element.36.top_ref, f32[8,256]{1,0:T(8,128)S(1)} %get-tuple-element.32._.refs_0_, f32[8,256]{1,0:T(8,128)S(1)} %collective-permute-done.refs_1_, ...), custom_call_target="tpu_custom_call" | custom-call | flops 1000000000 | tf_op jit(solution)/shard_map/head_sum/pallas_call | solution.py:36
  24.6 1.9 %collective-permute-done.3.right_ref = f32[4,16,2048]{2,1,0:T(8,128)S(1)} collective-permute-done((f32[4,16,2048]{2,1,0:T(8,128)S(1)}, f32[4,16,2048]{2,1,0:T(8,128)S(1)}, u32[]{:S(2)}, u32[]{:S(2)}) %collective-permute-start.3) | collective-permute-done | bytes 524320 | tf_op jit(solution)/shard_map/ppermute | solution.py:404
  26.6 2.5 %collective-permute-start.7 = (f32[16,2048]{1,0:T(8,128)S(1)}, f32[16,2048]{1,0:T(8,128)S(1)}, u32[]{:S(2)}, u32[]{:S(2)}) collective-permute-start(f32[16,2048]{1,0:T(8,128)S(1)} %get-tuple-element.41), channel_id=1, source_target_pairs={{0,24},{4,28},{8,16},{12,20},{16,8},{20,12},{24,0},{28,4},{1,25},{... | collective-permute-start | bytes 393224 | tf_op jit(solution)/shard_map/ppermute | solution.py:404
  30.1 2.7 %index_forward.1 = (f32[16,2048]{1,0:T(8,128)S(1)}, f32[16,128]{1,0:T(8,128)S(1)}, bf16[4,128,256]{2,1,0:T(8,128)(2,1)S(1)}) custom-call(s32[128]{0:T(128)S(1)} %copy-done.3, bf16[16,64,128]{2,1,0:T(8,128)(2,1)S(1)} %copy-done, bf16[2048,128]{1,0:T(8,128)(2,1)S(1)} %copy-done.4, f32[16,64]{1,0:T(8,128)S(1)} %copy-done.1, ...), custom_call_target="tpu_custom_call" | custom-call | flops 1000000000 | tf_op jit(solution)/shard_map/index_forward/pallas_call | solution.py:90
  32.9 1.5 %collective-permute-start.4 = (f32[16,128]{1,0:T(8,128)S(1)}, f32[16,128]{1,0:T(8,128)S(1)}, u32[]{:S(2)}, u32[]{:S(2)}) collective-permute-start(f32[16,128]{1,0:T(8,128)S(1)} %get-tuple-element.40.refs_0_), channel_id=1, source_target_pairs={{0,3},{1,2},{2,1},{3,0},{4,7},{5,6},{6,5},{7,4},{8,11},{9,10},{10,... | collective-permute-start | bytes 24584 | tf_op jit(solution)/shard_map/ppermute | solution.py:401
  35.0 3.4 %collective-permute-done.4.refs_1_ = f32[16,128]{1,0:T(8,128)S(1)} collective-permute-done((f32[16,128]{1,0:T(8,128)S(1)}, f32[16,128]{1,0:T(8,128)S(1)}, u32[]{:S(2)}, u32[]{:S(2)}) %collective-permute-start.4) | collective-permute-done | bytes 8224 | tf_op jit(solution)/shard_map/ppermute | solution.py:401
  38.9 3.1 %collective-permute-done.6.refs_3_ = f32[16,128]{1,0:T(8,128)S(1)} collective-permute-done((f32[16,128]{1,0:T(8,128)S(1)}, f32[16,128]{1,0:T(8,128)S(1)}, u32[]{:S(2)}, u32[]{:S(2)}) %collective-permute-start.6) | collective-permute-done | bytes 8224 | tf_op jit(solution)/shard_map/ppermute | solution.py:401
  42.2 0.7 query_part.7
  42.9 0.7 query_part.6
  43.6 0.7 query_part.5
  44.3 0.7 query_part.4
  45.0 0.9 %key_part.1 = (f32[4,256,128]{2,1,0:T(8,128)S(1)}, f32[4,256,128]{2,1,0:T(8,128)S(1)}) custom-call(bf16[4,128,256]{2,1,0:T(8,128)(2,1)S(1)} %get-tuple-element.49.wiq_ref, bf16[256,2048]{1,0:T(8,128)(2,1)S(1)} %get-tuple-element.50.refs_0_, bf16[256,2048]{1,0:T(8,128)(2,1)S(1)} %get-tuple-element.51.refs_1_, ...), custom_call_target="tpu_custom_call" | custom-call | flops 1000000000 | tf_op jit(solution)/shard_map/key_part/pallas_call | solution.py:36
  46.0 1.5 %collective-permute-start.10 = (f32[256,128]{1,0:T(8,128)S(1)}, f32[256,128]{1,0:T(8,128)S(1)}, u32[]{:S(2)}, u32[]{:S(2)}) collective-permute-start(f32[256,128]{1,0:T(8,128)S(1)} %get-tuple-element.44), channel_id=1, source_target_pairs={{0,3},{1,2},{2,1},{3,0},{4,7},{5,6},{6,5},{7,4},{8,11},{9,10},{10,... | collective-permute-start | bytes 393224 | tf_op jit(solution)/shard_map/ppermute | solution.py:401
  47.5 2.9 %collective-permute-start.12 = (f32[256,128]{1,0:T(8,128)S(1)}, f32[256,128]{1,0:T(8,128)S(1)}, u32[]{:S(2)}, u32[]{:S(2)}) collective-permute-start(f32[256,128]{1,0:T(8,128)S(1)} %get-tuple-element.46), channel_id=1, source_target_pairs={{0,1},{1,0},{2,3},{3,2},{4,5},{5,4},{6,7},{7,6},{8,9},{9,8},{10,11... | collective-permute-start | bytes 393224 | tf_op jit(solution)/shard_map/ppermute | solution.py:401
  50.5 2.5 %collective-permute-start.17 = (f32[256,128]{1,0:T(8,128)S(1)}, f32[256,128]{1,0:T(8,128)S(1)}, u32[]{:S(2)}, u32[]{:S(2)}) collective-permute-start(f32[256,128]{1,0:T(8,128)S(1)} %get-tuple-element.57), channel_id=1, source_target_pairs={{0,24},{4,28},{8,16},{12,20},{16,8},{20,12},{24,0},{28,4},{1,25},{... | collective-permute-start | bytes 393224 | tf_op jit(solution)/shard_map/ppermute | solution.py:404
  53.5 0.8 collective-permute-done.10.refs_0_
  54.3 1.5 %collective-permute-start.19 = (f32[256,128]{1,0:T(8,128)S(1)}, f32[256,128]{1,0:T(8,128)S(1)}, u32[]{:S(2)}, u32[]{:S(2)}) collective-permute-start(f32[256,128]{1,0:T(8,128)S(1)} %get-tuple-element.59), channel_id=1, source_target_pairs={{0,8},{4,12},{8,0},{12,4},{16,24},{20,28},{24,16},{28,20},{1,9},{5... | collective-permute-start | bytes 393224 | tf_op jit(solution)/shard_map/ppermute | solution.py:404
  55.8 4.0 %collective-permute-done.11.refs_1_ = f32[256,128]{1,0:T(8,128)S(1)} collective-permute-done((f32[256,128]{1,0:T(8,128)S(1)}, f32[256,128]{1,0:T(8,128)S(1)}, u32[]{:S(2)}, u32[]{:S(2)}) %collective-permute-start.11) | collective-permute-done | bytes 131104 | tf_op jit(solution)/shard_map/ppermute | solution.py:401
  60.2 2.2 %collective-permute-start.14 = (f32[264,128]{1,0:T(8,128)S(1)}, f32[264,128]{1,0:T(8,128)S(1)}, u32[]{:S(2)}, u32[]{:S(2)}) collective-permute-start(f32[264,128]{1,0:T(8,128)S(1)} %own_rows.1.refs_0_), channel_id=1, source_target_pairs={{0,2},{1,3},{2,0},{3,1},{4,6},{5,7},{6,4},{7,5},{8,10},{9,11},{10,... | collective-permute-start | bytes 405512 | tf_op jit(solution)/shard_map/ppermute | solution.py:401
  62.5 1.6 %collective-permute-start.20 = (f32[256,128]{1,0:T(8,128)S(1)}, f32[256,128]{1,0:T(8,128)S(1)}, u32[]{:S(2)}, u32[]{:S(2)}) collective-permute-start(f32[256,128]{1,0:T(8,128)S(1)} %add_all.1.refs_0_), channel_id=1, source_target_pairs={{0,8},{4,12},{8,0},{12,4},{16,24},{20,28},{24,16},{28,20},{1,9},{5... | collective-permute-start | bytes 393224 | tf_op jit(solution)/shard_map/ppermute | solution.py:404
  64.0 1.5 %collective-permute-start.21 = (f32[256,128]{1,0:T(8,128)S(1)}, f32[256,128]{1,0:T(8,128)S(1)}, u32[]{:S(2)}, u32[]{:S(2)}) collective-permute-start(f32[256,128]{1,0:T(8,128)S(1)} %add_all.1.refs_0_), channel_id=1, source_target_pairs={{0,16},{4,20},{8,24},{12,28},{16,0},{20,4},{24,8},{28,12},{1,17},{... | collective-permute-start | bytes 393224 | tf_op jit(solution)/shard_map/ppermute | solution.py:404
  66.0 1.2 %collective-permute-done.13.refs_1_ = f32[264,128]{1,0:T(8,128)S(1)} collective-permute-done((f32[264,128]{1,0:T(8,128)S(1)}, f32[264,128]{1,0:T(8,128)S(1)}, u32[]{:S(2)}, u32[]{:S(2)}) %collective-permute-start.13) | collective-permute-done | bytes 135200 | tf_op jit(solution)/shard_map/ppermute | solution.py:401
  67.2 2.3 %collective-permute-start.15 = (f32[264,128]{1,0:T(8,128)S(1)}, f32[264,128]{1,0:T(8,128)S(1)}, u32[]{:S(2)}, u32[]{:S(2)}) collective-permute-start(f32[264,128]{1,0:T(8,128)S(1)} %own_rows.1.refs_0_), channel_id=1, source_target_pairs={{0,3},{1,2},{2,1},{3,0},{4,7},{5,6},{6,5},{7,4},{8,11},{9,10},{10,... | collective-permute-start | bytes 405512 | tf_op jit(solution)/shard_map/ppermute | solution.py:401
  69.5 1.0 %collective-permute-done.14.refs_2_ = f32[264,128]{1,0:T(8,128)S(1)} collective-permute-done((f32[264,128]{1,0:T(8,128)S(1)}, f32[264,128]{1,0:T(8,128)S(1)}, u32[]{:S(2)}, u32[]{:S(2)}) %collective-permute-start.14) | collective-permute-done | bytes 135200 | tf_op jit(solution)/shard_map/ppermute | solution.py:401
  71.0 0.8 collective-permute-done.21.refs_2_
  72.3 1.8 %collective-permute-done.15.refs_3_ = f32[264,128]{1,0:T(8,128)S(1)} collective-permute-done((f32[264,128]{1,0:T(8,128)S(1)}, f32[264,128]{1,0:T(8,128)S(1)}, u32[]{:S(2)}, u32[]{:S(2)}) %collective-permute-start.15) | collective-permute-done | bytes 135200 | tf_op jit(solution)/shard_map/ppermute | solution.py:401
  74.1 1.4 %place_query.1 = (f32[1024,128]{1,0:T(8,128)}, f32[16,64]{1,0:T(8,128)}) custom-call(f32[264,128]{1,0:T(8,128)S(1)} %own_rows.1.refs_0_, f32[264,128]{1,0:T(8,128)S(1)} %collective-permute-done.13.refs_1_, f32[264,128]{1,0:T(8,128)S(1)} %collective-permute-done.14.refs_2_, f32[264,128]{1,0:T(8,128)S(1)} %collective-permute-done.15.refs_3_), custom_call_target="tpu_custom_call" | custom-call | tf_op jit(solution)/shard_map/place_query/pallas_call | solution.py:36
  75.6 1.0 %place_keys.1 = f32[2048,128]{1,0:T(8,128)} custom-call(f32[256,128]{1,0:T(8,128)S(1)} %add_all.1.refs_0_, f32[256,128]{1,0:T(8,128)S(1)} %collective-permute-done.20.refs_1_, f32[256,128]{1,0:T(8,128)S(1)} %collective-permute-done.21.refs_2_, f32[256,128]{1,0:T(8,128)S(1)} %collective-permute-done.22.refs_3_, ...), custom_call_target="tpu_custom_call" | custom-call | tf_op jit(solution)/shard_map/place_keys/pallas_call | solution.py:36
  (50 shorter events, 6.4 us)
Async XLA Ops:
  13.0 6.7 %collective-permute-start = (f32[8,256]{1,0:T(8,128)S(1)}, f32[8,256]{1,0:T(8,128)S(1)}, u32[]{:S(2)}, u32[]{:S(2)}) collective-permute-start(f32[8,256]{1,0:T(8,128)S(1)} %get-tuple-element.32._.refs_0_), channel_id=1, source_target_pairs={{0,3},{1,2},{2,1},{3,0},{4,7},{5,6},{6,5},{7,4},{8,11},{9,10},{10,... | collective-permute-start | bytes 24584 | tf_op jit(solution)/shard_map/ppermute | solution.py:401
  18.1 4.5 %collective-permute-start.1 = (f32[8,256]{1,0:T(8,128)S(1)}, f32[8,256]{1,0:T(8,128)S(1)}, u32[]{:S(2)}, u32[]{:S(2)}) collective-permute-start(f32[8,256]{1,0:T(8,128)S(1)} %get-tuple-element.32._.refs_0_), channel_id=1, source_target_pairs={{0,2},{1,3},{2,0},{3,1},{4,6},{5,7},{6,4},{7,5},{8,10},{9,11},{10,... | collective-permute-start | bytes 24584 | tf_op jit(solution)/shard_map/ppermute | solution.py:401
  18.1 4.5 %collective-permute-start.2 = (f32[8,256]{1,0:T(8,128)S(1)}, f32[8,256]{1,0:T(8,128)S(1)}, u32[]{:S(2)}, u32[]{:S(2)}) collective-permute-start(f32[8,256]{1,0:T(8,128)S(1)} %get-tuple-element.32._.refs_0_), channel_id=1, source_target_pairs={{0,1},{1,0},{2,3},{3,2},{4,5},{5,4},{6,7},{7,6},{8,9},{9,8},{10,11... | collective-permute-start | bytes 24584 | tf_op jit(solution)/shard_map/ppermute | solution.py:401
  22.7 7.5 %copy-start = (bf16[16,64,128]{2,1,0:T(8,128)(2,1)S(1)}, bf16[16,64,128]{2,1,0:T(8,128)(2,1)}, u32[]{:S(2)}) copy-start(bf16[16,64,128]{2,1,0:T(8,128)(2,1)} %query_ref.11) | copy-start | bytes 786436
  22.7 7.5 %copy-start.1 = (f32[16,64]{1,0:T(8,128)S(1)}, f32[16,64]{1,0:T(8,128)}, u32[]{:S(2)}) copy-start(f32[16,64]{1,0:T(8,128)} %weight_ref.3) | copy-start | bytes 12292
  22.7 7.5 %copy-start.3 = (s32[128]{0:T(128)S(1)}, s32[128]{0:T(128)}, u32[]{:S(2)}) copy-start(s32[128]{0:T(128)} %pos_ref.1) | copy-start | bytes 1540
  22.7 7.5 %copy-start.4 = (bf16[2048,128]{1,0:T(8,128)(2,1)S(1)}, bf16[2048,128]{1,0:T(8,128)(2,1)}, u32[]{:S(2)}) copy-start(bf16[2048,128]{1,0:T(8,128)(2,1)} %keys_ref.9) | copy-start | bytes 1572868
  24.5 2.0 %collective-permute-start.3 = (f32[4,16,2048]{2,1,0:T(8,128)S(1)}, f32[4,16,2048]{2,1,0:T(8,128)S(1)}, u32[]{:S(2)}, u32[]{:S(2)}) collective-permute-start(f32[4,16,2048]{2,1,0:T(8,128)S(1)} %get-tuple-element.38), channel_id=1, source_target_pairs={{0,4},{4,0},{8,12},{12,8},{16,20},{20,16},{24,28},{28,24},{1,5},{5... | collective-permute-start | bytes 1572872 | tf_op jit(solution)/shard_map/ppermute | solution.py:404
  26.5 11.9 %copy-start.5 = (f32[16]{0:T(128)S(1)}, f32[16]{0:T(128)}, u32[]{:S(2)}) copy-start(f32[16]{0:T(128)} %param.13) | copy-start | bytes 196
  26.6 15.4 %collective-permute-start.7 = (f32[16,2048]{1,0:T(8,128)S(1)}, f32[16,2048]{1,0:T(8,128)S(1)}, u32[]{:S(2)}, u32[]{:S(2)}) collective-permute-start(f32[16,2048]{1,0:T(8,128)S(1)} %get-tuple-element.41), channel_id=1, source_target_pairs={{0,24},{4,28},{8,16},{12,20},{16,8},{20,12},{24,0},{28,4},{1,25},{... | collective-permute-start | bytes 393224 | tf_op jit(solution)/shard_map/ppermute | solution.py:404
  29.1 12.9 %collective-permute-start.8 = (f32[16,2048]{1,0:T(8,128)S(1)}, f32[16,2048]{1,0:T(8,128)S(1)}, u32[]{:S(2)}, u32[]{:S(2)}) collective-permute-start(f32[16,2048]{1,0:T(8,128)S(1)} %get-tuple-element.42), channel_id=1, source_target_pairs={{0,16},{4,20},{8,24},{12,28},{16,0},{20,4},{24,8},{28,12},{1,17},{... | collective-permute-start | bytes 393224 | tf_op jit(solution)/shard_map/ppermute | solution.py:404
  29.6 12.4 %collective-permute-start.9 = (f32[16,2048]{1,0:T(8,128)S(1)}, f32[16,2048]{1,0:T(8,128)S(1)}, u32[]{:S(2)}, u32[]{:S(2)}) collective-permute-start(f32[16,2048]{1,0:T(8,128)S(1)} %get-tuple-element.43), channel_id=1, source_target_pairs={{0,8},{4,12},{8,0},{12,4},{16,24},{20,28},{24,16},{28,20},{1,9},{5... | collective-permute-start | bytes 393224 | tf_op jit(solution)/shard_map/ppermute | solution.py:404
  32.9 5.5 %collective-permute-start.4 = (f32[16,128]{1,0:T(8,128)S(1)}, f32[16,128]{1,0:T(8,128)S(1)}, u32[]{:S(2)}, u32[]{:S(2)}) collective-permute-start(f32[16,128]{1,0:T(8,128)S(1)} %get-tuple-element.40.refs_0_), channel_id=1, source_target_pairs={{0,3},{1,2},{2,1},{3,0},{4,7},{5,6},{6,5},{7,4},{8,11},{9,10},{10,... | collective-permute-start | bytes 24584 | tf_op jit(solution)/shard_map/ppermute | solution.py:401
  34.4 4.5 %collective-permute-start.5 = (f32[16,128]{1,0:T(8,128)S(1)}, f32[16,128]{1,0:T(8,128)S(1)}, u32[]{:S(2)}, u32[]{:S(2)}) collective-permute-start(f32[16,128]{1,0:T(8,128)S(1)} %get-tuple-element.40.refs_0_), channel_id=1, source_target_pairs={{0,2},{1,3},{2,0},{3,1},{4,6},{5,7},{6,4},{7,5},{8,10},{9,11},{10,... | collective-permute-start | bytes 24584 | tf_op jit(solution)/shard_map/ppermute | solution.py:401
  38.4 3.7 %collective-permute-start.6 = (f32[16,128]{1,0:T(8,128)S(1)}, f32[16,128]{1,0:T(8,128)S(1)}, u32[]{:S(2)}, u32[]{:S(2)}) collective-permute-start(f32[16,128]{1,0:T(8,128)S(1)} %get-tuple-element.40.refs_0_), channel_id=1, source_target_pairs={{0,1},{1,0},{2,3},{3,2},{4,5},{5,4},{6,7},{7,6},{8,9},{9,8},{10,11... | collective-permute-start | bytes 24584 | tf_op jit(solution)/shard_map/ppermute | solution.py:401
  45.9 4.5 %collective-permute-start.16 = (f32[4,256,128]{2,1,0:T(8,128)S(1)}, f32[4,256,128]{2,1,0:T(8,128)S(1)}, u32[]{:S(2)}, u32[]{:S(2)}) collective-permute-start(f32[4,256,128]{2,1,0:T(8,128)S(1)} %get-tuple-element.55), channel_id=1, source_target_pairs={{0,4},{4,0},{8,12},{12,8},{16,20},{20,16},{24,28},{28,24},{1,5},{5... | collective-permute-start | bytes 1572872 | tf_op jit(solution)/shard_map/ppermute | solution.py:404
  46.0 8.3 %collective-permute-start.10 = (f32[256,128]{1,0:T(8,128)S(1)}, f32[256,128]{1,0:T(8,128)S(1)}, u32[]{:S(2)}, u32[]{:S(2)}) collective-permute-start(f32[256,128]{1,0:T(8,128)S(1)} %get-tuple-element.44), channel_id=1, source_target_pairs={{0,3},{1,2},{2,1},{3,0},{4,7},{5,6},{6,5},{7,4},{8,11},{9,10},{10,... | collective-permute-start | bytes 393224 | tf_op jit(solution)/shard_map/ppermute | solution.py:401
  47.5 12.3 %collective-permute-start.11 = (f32[256,128]{1,0:T(8,128)S(1)}, f32[256,128]{1,0:T(8,128)S(1)}, u32[]{:S(2)}, u32[]{:S(2)}) collective-permute-start(f32[256,128]{1,0:T(8,128)S(1)} %get-tuple-element.45), channel_id=1, source_target_pairs={{0,2},{1,3},{2,0},{3,1},{4,6},{5,7},{6,4},{7,5},{8,10},{9,11},{10,... | collective-permute-start | bytes 393224 | tf_op jit(solution)/shard_map/ppermute | solution.py:401
  47.5 12.3 %collective-permute-start.12 = (f32[256,128]{1,0:T(8,128)S(1)}, f32[256,128]{1,0:T(8,128)S(1)}, u32[]{:S(2)}, u32[]{:S(2)}) collective-permute-start(f32[256,128]{1,0:T(8,128)S(1)} %get-tuple-element.46), channel_id=1, source_target_pairs={{0,1},{1,0},{2,3},{3,2},{4,5},{5,4},{6,7},{7,6},{8,9},{9,8},{10,11... | collective-permute-start | bytes 393224 | tf_op jit(solution)/shard_map/ppermute | solution.py:401
  50.5 11.9 %collective-permute-start.17 = (f32[256,128]{1,0:T(8,128)S(1)}, f32[256,128]{1,0:T(8,128)S(1)}, u32[]{:S(2)}, u32[]{:S(2)}) collective-permute-start(f32[256,128]{1,0:T(8,128)S(1)} %get-tuple-element.57), channel_id=1, source_target_pairs={{0,24},{4,28},{8,16},{12,20},{16,8},{20,12},{24,0},{28,4},{1,25},{... | collective-permute-start | bytes 393224 | tf_op jit(solution)/shard_map/ppermute | solution.py:404
  53.0 9.4 %collective-permute-start.18 = (f32[256,128]{1,0:T(8,128)S(1)}, f32[256,128]{1,0:T(8,128)S(1)}, u32[]{:S(2)}, u32[]{:S(2)}) collective-permute-start(f32[256,128]{1,0:T(8,128)S(1)} %get-tuple-element.58), channel_id=1, source_target_pairs={{0,16},{4,20},{8,24},{12,28},{16,0},{20,4},{24,8},{28,12},{1,17},{... | collective-permute-start | bytes 393224 | tf_op jit(solution)/shard_map/ppermute | solution.py:404
  54.3 8.1 %collective-permute-start.19 = (f32[256,128]{1,0:T(8,128)S(1)}, f32[256,128]{1,0:T(8,128)S(1)}, u32[]{:S(2)}, u32[]{:S(2)}) collective-permute-start(f32[256,128]{1,0:T(8,128)S(1)} %get-tuple-element.59), channel_id=1, source_target_pairs={{0,8},{4,12},{8,0},{12,4},{16,24},{20,28},{24,16},{28,20},{1,9},{5... | collective-permute-start | bytes 393224 | tf_op jit(solution)/shard_map/ppermute | solution.py:404
  60.1 7.1 %collective-permute-start.13 = (f32[264,128]{1,0:T(8,128)S(1)}, f32[264,128]{1,0:T(8,128)S(1)}, u32[]{:S(2)}, u32[]{:S(2)}) collective-permute-start(f32[264,128]{1,0:T(8,128)S(1)} %own_rows.1.refs_0_), channel_id=1, source_target_pairs={{0,1},{1,0},{2,3},{3,2},{4,5},{5,4},{6,7},{7,6},{8,9},{9,8},{10,11... | collective-permute-start | bytes 405512 | tf_op jit(solution)/shard_map/ppermute | solution.py:401
  60.2 10.3 %collective-permute-start.14 = (f32[264,128]{1,0:T(8,128)S(1)}, f32[264,128]{1,0:T(8,128)S(1)}, u32[]{:S(2)}, u32[]{:S(2)}) collective-permute-start(f32[264,128]{1,0:T(8,128)S(1)} %own_rows.1.refs_0_), channel_id=1, source_target_pairs={{0,2},{1,3},{2,0},{3,1},{4,6},{5,7},{6,4},{7,5},{8,10},{9,11},{10,... | collective-permute-start | bytes 405512 | tf_op jit(solution)/shard_map/ppermute | solution.py:401
  62.5 8.1 %collective-permute-start.20 = (f32[256,128]{1,0:T(8,128)S(1)}, f32[256,128]{1,0:T(8,128)S(1)}, u32[]{:S(2)}, u32[]{:S(2)}) collective-permute-start(f32[256,128]{1,0:T(8,128)S(1)} %add_all.1.refs_0_), channel_id=1, source_target_pairs={{0,8},{4,12},{8,0},{12,4},{16,24},{20,28},{24,16},{28,20},{1,9},{5... | collective-permute-start | bytes 393224 | tf_op jit(solution)/shard_map/ppermute | solution.py:404
  64.0 7.8 %collective-permute-start.21 = (f32[256,128]{1,0:T(8,128)S(1)}, f32[256,128]{1,0:T(8,128)S(1)}, u32[]{:S(2)}, u32[]{:S(2)}) collective-permute-start(f32[256,128]{1,0:T(8,128)S(1)} %add_all.1.refs_0_), channel_id=1, source_target_pairs={{0,16},{4,20},{8,24},{12,28},{16,0},{20,4},{24,8},{28,12},{1,17},{... | collective-permute-start | bytes 393224 | tf_op jit(solution)/shard_map/ppermute | solution.py:404
  65.5 6.3 %collective-permute-start.22 = (f32[256,128]{1,0:T(8,128)S(1)}, f32[256,128]{1,0:T(8,128)S(1)}, u32[]{:S(2)}, u32[]{:S(2)}) collective-permute-start(f32[256,128]{1,0:T(8,128)S(1)} %add_all.1.refs_0_), channel_id=1, source_target_pairs={{0,24},{4,28},{8,16},{12,20},{16,8},{20,12},{24,0},{28,4},{1,25},{... | collective-permute-start | bytes 393224 | tf_op jit(solution)/shard_map/ppermute | solution.py:404
  67.2 6.9 %collective-permute-start.15 = (f32[264,128]{1,0:T(8,128)S(1)}, f32[264,128]{1,0:T(8,128)S(1)}, u32[]{:S(2)}, u32[]{:S(2)}) collective-permute-start(f32[264,128]{1,0:T(8,128)S(1)} %own_rows.1.refs_0_), channel_id=1, source_target_pairs={{0,3},{1,2},{2,1},{3,0},{4,7},{5,6},{6,5},{7,4},{8,11},{9,10},{10,... | collective-permute-start | bytes 405512 | tf_op jit(solution)/shard_map/ppermute | solution.py:401
  70.5 5.0 %collective-permute-start.23 = (f32[256,128]{1,0:T(8,128)S(1)}, f32[256,128]{1,0:T(8,128)S(1)}, u32[]{:S(2)}, u32[]{:S(2)}) collective-permute-start(f32[256,128]{1,0:T(8,128)S(1)} %add_all.1.refs_0_), channel_id=1, source_target_pairs={{0,4},{4,0},{8,12},{12,8},{16,20},{20,16},{24,28},{28,24},{1,5},{5... | collective-permute-start | bytes 393224 | tf_op jit(solution)/shard_map/ppermute | solution.py:404
  70.5 5.0 %collective-permute-start.24 = (f32[256,128]{1,0:T(8,128)S(1)}, f32[256,128]{1,0:T(8,128)S(1)}, u32[]{:S(2)}, u32[]{:S(2)}) collective-permute-start(f32[256,128]{1,0:T(8,128)S(1)} %collective-permute-done.20.refs_1_), channel_id=1, source_target_pairs={{0,4},{4,0},{8,12},{12,8},{16,20},{20,16},{24,28},{28,24},{1,5},{5... | collective-permute-start | bytes 393224 | tf_op jit(solution)/shard_map/ppermute | solution.py:404
  71.8 3.7 %collective-permute-start.25 = (f32[256,128]{1,0:T(8,128)S(1)}, f32[256,128]{1,0:T(8,128)S(1)}, u32[]{:S(2)}, u32[]{:S(2)}) collective-permute-start(f32[256,128]{1,0:T(8,128)S(1)} %collective-permute-done.21.refs_2_), channel_id=1, source_target_pairs={{0,4},{4,0},{8,12},{12,8},{16,20},{20,16},{24,28},{28,24},{1,5},{5... | collective-permute-start | bytes 393224 | tf_op jit(solution)/shard_map/ppermute | solution.py:404
  71.8 3.8 %collective-permute-start.26 = (f32[256,128]{1,0:T(8,128)S(1)}, f32[256,128]{1,0:T(8,128)S(1)}, u32[]{:S(2)}, u32[]{:S(2)}) collective-permute-start(f32[256,128]{1,0:T(8,128)S(1)} %collective-permute-done.22.refs_3_), channel_id=1, source_target_pairs={{0,4},{4,0},{8,12},{12,8},{16,20},{20,16},{24,28},{28,24},{1,5},{5... | collective-permute-start | bytes 393224 | tf_op jit(solution)/shard_map/ppermute | solution.py:404
  (1 other events, 0.7 us)

commit v3 on v2

--- a/solution.py
+++ b/solution.py
@@ -16,8 +16,11 @@
 F32 = jnp.float32
 BF16 = jnp.bfloat16
 MIB = 1024 * 1024
+SHORT = 0
+LONG = 4 * 10**10
 
 vmem_spec = pl.BlockSpec(memory_space=pltpu.VMEM)
+smem_spec = pl.BlockSpec(memory_space=pltpu.SMEM)
 any_spec = pl.BlockSpec(memory_space=pl.ANY)
 
 
@@ -29,20 +32,22 @@
     return pltpu.with_memory_space_constraint(array, pltpu.HBM)
 
 
-def vmem_call(body, name, outs, operands, scratch=(), out_specs=None, limit=32 * MIB, cost=0):
+def vmem_call(
+    body, name, outs, operands, scratch=(), out_specs=None, scalars=(), limit=12 * MIB, cost=0
+):
     several = isinstance(outs, (tuple, list))
     if out_specs is None:
         out_specs = tuple(vmem_spec for _ in outs) if several else vmem_spec
     return pl.pallas_call(
         body,
         out_shape=outs,
-        in_specs=[vmem_spec] * len(operands),
+        in_specs=[smem_spec] * len(scalars) + [vmem_spec] * len(operands),
         out_specs=out_specs,
         scratch_shapes=list(scratch),
         compiler_params=pltpu.CompilerParams(vmem_limit_bytes=limit),
         cost_estimate=pl.CostEstimate(flops=cost, bytes_accessed=0, transcendentals=0),
         name=name,
-    )(*[in_vmem(a) for a in operands])
+    )(*scalars, *[in_vmem(a) for a in operands])
 
 
 def tile_of(extent, wanted):
@@ -58,16 +63,17 @@
     return at // 2, at % 2
 
 
-def index_forward(query_pos, index_query, index_keys, index_weight, groups, after):
+def index_forward(query_pos, kl, index_query, index_keys, index_weight, groups, after):
     rows, heads, width = index_query.shape
     keys = index_keys.shape[0]
     tile = tile_of(keys, 256)
     own = rows // groups
 
-    def body(pos_ref, query_ref, keys_ref, weight_ref, _, score_ref, lse_ref, wiq_ref):
+    def body(pos_ref, kl_ref, query_ref, keys_ref, weight_ref, _, score_ref, lse_ref, kl_out, wiq_ref, gate_ref):
         columns = weight_ref[...].T
         flat = query_ref[...].reshape(rows * heads, width)
         for row in range(rows):
+            kl_out[row : row + 1, :] = jnp.full((1, 128), kl_ref[row], F32)
             piece = query_ref[row].astype(F32) * columns[:, row : row + 1]
             wiq_ref[row // own, :, (row % own) * heads : (row % own + 1) * heads] = piece.T.astype(BF16)
         first_key = lax.axis_index("keys") * keys
@@ -76,6 +82,8 @@
             logits = lax.dot_general(
                 flat, keys_ref[at : at + tile, :], (((1,), (1,)), ((), ())), preferred_element_type=F32
             )
+            for g in range(groups):
+                gate_ref[g, :, at : at + tile] = logits[g * own * heads : (g + 1) * own * heads, :].astype(BF16)
             index = first_key + at + lax.broadcasted_iota(jnp.int32, (1, tile), 1)
             for row in range(rows):
                 active = jnp.maximum(logits[row * heads : (row + 1) * heads, :], 0.0)
@@ -92,14 +100,16 @@
         out_shape=(
             pltpu.VMEM((rows, keys), F32),
             pltpu.VMEM((rows, 128), F32),
+            pltpu.VMEM((rows, 128), F32),
             pltpu.VMEM((groups, width, own * heads), BF16),
+            pltpu.VMEM((groups, own * heads, keys), BF16),
         ),
-        in_specs=[pl.BlockSpec(memory_space=pltpu.SMEM)] + [vmem_spec] * 4,
-        out_specs=(vmem_spec,) * 3,
-        compiler_params=pltpu.CompilerParams(vmem_limit_bytes=32 * MIB),
-        cost_estimate=pl.CostEstimate(flops=10**9, bytes_accessed=0, transcendentals=0),
+        in_specs=[smem_spec] * 2 + [vmem_spec] * 4,
+        out_specs=(vmem_spec,) * 5,
+        compiler_params=pltpu.CompilerParams(vmem_limit_bytes=16 * MIB),
+        cost_estimate=pl.CostEstimate(flops=0, bytes_accessed=0, transcendentals=0),
         name="index_forward",
-    )(query_pos, *[in_vmem(a) for a in (index_query, index_keys, index_weight, after)])
+    )(query_pos, kl, *[in_vmem(a) for a in (index_query, index_keys, index_weight, after)])
 
 
 def main_scores(pos, query_t, keys_t):
@@ -167,9 +177,9 @@
         ],
         out_specs=(vmem_spec,) * 3,
         scratch_shapes=[pltpu.VMEM((keys, depth), BF16), pltpu.VMEM((depth, lanes), BF16)],
-        compiler_params=pltpu.CompilerParams(vmem_limit_bytes=28 * MIB),
+        compiler_params=pltpu.CompilerParams(vmem_limit_bytes=16 * MIB),
         name="main_scores",
-    )(pos, in_hbm(query_t), in_hbm(keys_t))
+    )(in_hbm(pos), in_hbm(query_t), in_hbm(keys_t))
 
 
 def joined(stats):
@@ -179,16 +189,15 @@
     return best + jnp.log2(sum(jnp.exp2(stat - best) for stat in stats))
 
 
-def head_sum(probs, tops, stats, queries, row_local):
+def head_sum(probs, tops, stat, queries, row_local):
     blocks, keys, lanes = probs.shape
     tiles = tops.shape[1]
     tile = keys // tiles
     per = lanes // queries
     chips = queries // row_local // 2
 
-    def body(prob_ref, top_ref, *refs):
-        stat_refs, (keep_ref, send_ref, summed) = refs[:-3], refs[-3:]
-        whole = joined([ref[...] for ref in stat_refs])
+    def body(prob_ref, top_ref, stat_ref, keep_ref, send_ref, summed):
+        whole = stat_ref[...]
         factors = [jnp.exp2(top_ref[b] - whole[b : b + 1, :]) * (1.0 / H) for b in range(blocks)]
         for t in range(tiles):
             span = slice(t * tile, (t + 1) * tile)
@@ -207,7 +216,7 @@
 
     half = pltpu.VMEM((chips, row_local, keys), F32)
     return vmem_call(
-        body, "head_sum", (half, half), (probs, tops, *stats), [pltpu.VMEM((queries, keys), F32)], cost=10**9
+        body, "head_sum", (half, half), (probs, tops, stat), [pltpu.VMEM((queries, keys), F32)], cost=10**9
     )
 
 
@@ -233,74 +242,101 @@
     return vmem_call(body, "add_all", pltpu.VMEM(parts[0].shape, F32), parts)
 
 
-def deltas(scores, stats, targets, kl, groups):
+def stack_all(parts):
+    def body(*refs):
+        for r, ref in enumerate(refs[:-1]):
+            refs[-1][r] = ref[...]
+
+    return vmem_call(body, "stack_all", pltpu.VMEM((len(parts), *parts[0].shape), F32), parts)
+
+
+def join_first(left, right, below):
+    blocks, lanes = left.shape
+    rows = below.shape[0]
+
+    def body(left_ref, right_ref, below_ref, out_ref):
+        out_ref[:blocks, :] = joined([left_ref[...], right_ref[...]])
+        out_ref[blocks:, :] = jnp.concatenate([below_ref[...]] * (lanes // 128), axis=1)
+
+    return vmem_call(body, "join_first", pltpu.VMEM((blocks + rows, lanes), F32), (left, right, below))
+
+
+def join_more(left, right, blocks):
+    count, lanes = left.shape
+
+    def body(left_ref, right_ref, main_ref, index_ref):
+        both = joined([left_ref[...], right_ref[...]])
+        main_ref[...] = both[:blocks, :]
+        index_ref[...] = both[blocks:, :128]
+
+    outs = (pltpu.VMEM((blocks, lanes), F32), pltpu.VMEM((count - blocks, 128), F32))
+    return vmem_call(body, "join_more", outs, (left, right))
+
+
+def join_pair(left, right):
+    def body(left_ref, right_ref, out_ref):
+        out_ref[...] = joined([left_ref[...], right_ref[...]])
+
+    return vmem_call(body, "join_pair", pltpu.VMEM(left.shape, F32), (left, right))
+
+
+def deltas(scores, index_stats, targets, kl, groups):
     rows, keys = scores.shape
     own = rows // groups
 
-    def body(score_ref, kl_ref, *refs):
-        stat_refs, target_refs, out_ref = refs[: len(stats)], refs[len(stats) : -1], refs[-1]
-        whole = joined([ref[:, :1] for ref in stat_refs])
+    def body(score_ref, kl_ref, lse_ref, other_ref, *refs):
+        target_refs, out_ref = refs[:-1], refs[-1]
+        whole = joined([lse_ref[:, :1], other_ref[:, :1]])
         target = target_refs[0][...]
         for ref in target_refs[1:]:
             target = target + ref[...]
-        delta = kl_ref[...] * (jnp.exp2(score_ref[...] - whole) - target)
+        delta = kl_ref[:, :1] * (jnp.exp2(score_ref[...] - whole) - target)
         for g in range(groups):
             out_ref[g] = delta[g * own : (g + 1) * own, :]
 
-    return vmem_call(body, "deltas", pltpu.VMEM((groups, own, keys), F32), (scores, kl, *stats, *targets))
-
-
-def query_part(r, delta, index_query, index_keys):
+    return vmem_call(body, "deltas", pltpu.VMEM((groups, own, keys), F32), (scores, kl, *index_stats, *targets))
+
+
+def query_part(r, delta, gate, index_keys):
     groups, own, keys = delta.shape
-    heads, width = index_query.shape[1:]
-    tile = tile_of(keys, 512)
-
-    def body(delta_ref, query_ref, keys_ref, slope_ref, out_ref):
+    size = gate.shape[1]
+    heads = size // own
+    width = index_keys.shape[1]
+
+    def body(delta_ref, gate_ref, keys_ref, slope_ref, out_ref):
         group = lax.axis_index("keys") ^ r
-        flat = query_ref[pl.ds(group * own, own)].reshape(own * heads, width)
-        for at in range(0, keys, tile):
-            span = slice(at, at + tile)
-            logits = lax.dot_general(
-                flat, keys_ref[span, :], (((1,), (1,)), ((), ())), preferred_element_type=F32
-            ).astype(BF16)
-            delta_rows = delta_ref[group, :, span]
-            for row in range(own):
-                line = jnp.broadcast_to(delta_rows[row : row + 1, :], (heads, tile)).astype(BF16)
-                part = slice(row * heads, (row + 1) * heads)
-                slope_ref[part, span] = jnp.where(logits[part, :] > 0, line, jnp.zeros((), BF16))
+        delta_rows = delta_ref[group]
+        for row in range(own):
+            line = jnp.broadcast_to(delta_rows[row : row + 1, :], (heads, keys)).astype(BF16)
+            part = slice(row * heads, (row + 1) * heads)
+            slope_ref[part, :] = jnp.where(gate_ref[group, part, :] > 0, line, jnp.zeros((), BF16))
         out_ref[...] = jnp.dot(slope_ref[...], keys_ref[...], preferred_element_type=F32)
 
-    outs = (pltpu.VMEM((own * heads, keys), BF16), pltpu.VMEM((own * heads, width), F32))
-    return vmem_call(body, "query_part", outs, (delta, index_query, index_keys), cost=3 * 10**8)
+    outs = (pltpu.VMEM((size, keys), BF16), pltpu.VMEM((size, width), F32))
+    return vmem_call(body, "query_part", outs, (delta, gate, index_keys), cost=SHORT)
 
 
 def key_part(slopes, wiq, head_devices):
     groups, width = wiq.shape[:2]
     keys = slopes[0].shape[1]
-    tile = tile_of(keys, 512)
     chips = head_devices // 2
     chunk = keys // head_devices
 
     def body(wiq_ref, *refs):
-        slope_refs, (keep_ref, send_ref, total) = refs[:groups], refs[groups:]
+        slope_refs, (keep_ref, send_ref) = refs[:groups], refs[groups:]
         z = lax.axis_index("keys")
-        for at in range(0, keys, tile):
-            span = slice(at, at + tile)
-            summed = None
-            for r in range(groups):
-                part = jnp.dot(wiq_ref[z ^ r], slope_refs[r][:, span], preferred_element_type=F32)
-                summed = part if summed is None else summed + part
-            total[span, :] = summed.T
         chip, core = head_place()
-        for r in range(chips):
-            first = (chip ^ r) * 2
-            keep_ref[r] = rows_of(total, (first + core) * chunk, chunk)
-            send_ref[r] = rows_of(total, (first + 1 - core) * chunk, chunk)
+        for out_ref, side in ((send_ref, 1 - core), (keep_ref, core)):
+            for n in range(chips):
+                span = pl.ds(pl.multiple_of(((chip ^ n) * 2 + side) * chunk, chunk), chunk)
+                summed = None
+                for r in range(groups):
+                    part = jnp.dot(wiq_ref[z ^ r], slope_refs[r][:, span], preferred_element_type=F32)
+                    summed = part if summed is None else summed + part
+                out_ref[n] = summed.T
 
     half = pltpu.VMEM((chips, chunk, width), F32)
-    return vmem_call(
-        body, "key_part", (half, half), (wiq, *slopes), [pltpu.VMEM((keys, width), F32)], cost=10**9
-    )
+    return vmem_call(body, "key_part", (half, half), (wiq, *slopes), cost=SHORT)
 
 
 def own_rows(parts, index_query, index_weight):
@@ -330,7 +366,7 @@
             out_ref[size + own :, :] = jnp.zeros((extra - own, width), F32)
 
     return vmem_call(
-        body, "own_rows", pltpu.VMEM((size + extra, width), F32), (index_query, index_weight, *parts)
+        body, "own_rows", pltpu.VMEM((size + extra, width), F32), (index_query, index_weight, *parts), cost=LONG
     )
 
 
@@ -359,23 +395,21 @@
         pieces,
         [pltpu.SemaphoreType.DMA((len(pieces),))],
         out_specs=(any_spec, vmem_spec),
+        cost=LONG,
     )
     return query.reshape(rows, heads, width), weight
 
 
-def place_keys(mine, others):
-    chips = len(mine)
-    chunk, width = mine[0].shape
-
-    def body(*refs):
-        out_ref, sems = refs[-2:]
+def place_keys(mine, other):
+    chips, chunk, width = mine.shape
+
+    def body(mine_ref, other_ref, out_ref, sems):
         chip, core = head_place()
         copies = []
-        for r in range(chips):
-            for side in range(2):
-                at = pl.multiple_of(((chip ^ r) * 2 + (core ^ side)) * chunk, chunk)
-                n = side * chips + r
-                copies.append(pltpu.make_async_copy(refs[n], out_ref.at[pl.ds(at, chunk)], sems.at[n]))
+        for n, (ref, side) in enumerate(((mine_ref, core), (other_ref, 1 - core))):
+            for r in range(chips):
+                at = pl.multiple_of(((chip ^ r) * 2 + side) * chunk, chunk)
+                copies.append(pltpu.make_async_copy(ref.at[r], out_ref.at[pl.ds(at, chunk)], sems.at[n, r]))
                 copies[-1].start()
         for copy in copies:
             copy.wait()
@@ -384,8 +418,8 @@
         body,
         "place_keys",
         jax.ShapeDtypeStruct((2 * chips * chunk, width), F32),
-        (*mine, *others),
-        [pltpu.SemaphoreType.DMA((2 * chips,))],
+        (mine, other),
+        [pltpu.SemaphoreType.DMA((2, chips))],
         out_specs=any_spec,
     )
 
@@ -407,29 +441,39 @@
     chips_far_first = list(reversed(range(1, chips)))
 
     probs, tops, stat = main_scores(query_pos[None, :], main_query.transpose(1, 2, 0), latent_keys.T)
-    stats = [stat] + [to_keys(stat, bits) for bits in far_first]
-    scores, index_lse, wiq = index_forward(
-        query_pos, index_query, index_keys, index_weight, key_devices, stat
-    )
-    keep, send = head_sum(probs, tops, stats, queries, row_local)
+    scores, index_lse, kl, wiq, gate = index_forward(
+        query_pos, kl_weight, index_query, index_keys, index_weight, key_devices, stat
+    )
+    blocks = stat.shape[0]
+    both = join_first(stat, to_keys(stat, 1), index_lse)
+    bits = 2
+    while bits < key_devices // 2:
+        both = join_pair(both, to_keys(both, bits))
+        bits *= 2
+    stat, index_lse = join_more(both, to_keys(both, bits), blocks)
+    keep, send = head_sum(probs, tops, stat, queries, row_local)
+    index_lse, send = lax.optimization_barrier((index_lse, send))
     sums = add_stacks(keep, to_heads(send, 1))
     targets = [sums[0]] + [to_heads(sums[r], 2 * r) for r in chips_far_first]
-    index_lse, _ = lax.optimization_barrier((index_lse, sums[0]))
-    index_stats = [index_lse] + [to_keys(index_lse, bits) for bits in far_first]
-    delta = deltas(scores, index_stats, targets, kl_weight[:, None], key_devices)
+    delta = deltas(scores, (index_lse, to_keys(index_lse, 1)), targets, kl, key_devices)
 
     slopes, arrived = {}, []
     for r in far_first + [0]:
-        slopes[r], part = query_part(r, delta, index_query, index_keys)
+        slopes[r], part = query_part(r, delta, gate, index_keys)
         arrived.append(to_keys(part, r) if r else part)
     keep, send = key_part([slopes[r] for r in range(key_devices)], wiq, head_devices)
     sums = add_stacks(keep, to_heads(send, 1))
-    key_own = add_all([sums[0]] + [to_heads(sums[r], 2 * r) for r in chips_far_first])
     query_own = own_rows(arrived, index_query, index_weight)
+    key_parts = [sums[0]] + [to_heads(sums[r], 2 * r) for r in chips_far_first]
+    query_own, key_parts[0] = lax.optimization_barrier((query_own, key_parts[0]))
+    key_own = add_all(key_parts)
     pieces = [query_own] + [to_keys(query_own, r) for r in range(1, key_devices)]
-    mine = [key_own] + [to_heads(key_own, 2 * r) for r in range(1, chips)]
-    others = [to_heads(piece, 1) for piece in mine]
-    key_grad = place_keys(mine, others)
+    mine, bits = [key_own], 2
+    while bits < head_devices:
+        mine = mine + [to_heads(piece, bits) for piece in mine]
+        bits *= 2
+    mine = stack_all(mine)
+    key_grad = place_keys(mine, to_heads(mine, 1))
     query_grad, weight_grad = place_query(pieces, row_local, index_heads)
     return query_grad, key_grad, weight_grad
 

time: 76.8 us -> 73 us (0.951)
  starting transfers between devices: 29.7 us -> 27.8 us
  Pallas kernels: 23.1 us -> 22.2 us
    ppermute x12 -> x9, waiting for transfers between devices: 19.5 us -> 12.9 us  [to_keys(): lax.ppermute(value, 'keys', [(i, i ^ bits) for i in range(key_devices)])]
    ppermute x15 -> x12, waiting for transfers between devices: 2.69 us -> 9.05 us  [to_heads(): lax.ppermute(value, 'heads', [(i, i ^ bits) for i in range(head_devices)])]
    pallas_call x13 -> x16, Pallas kernels: 8.66 us -> 7.62 us  [vmem_call(): pl.pallas_call(body, out_shape=outs, in_specs=[smem_spec] * len(scalars)...]
    ppermute x12 -> x9, starting transfers between devices: 16.9 us -> 15.9 us  [to_keys(): lax.ppermute(value, 'keys', [(i, i ^ bits) for i in range(key_devices)])]
    ppermute x15 -> x12, starting transfers between devices: 12.8 us -> 11.9 us  [to_heads(): lax.ppermute(value, 'heads', [(i, i ^ bits) for i in range(head_devices)])]
  transfers between devices with their start and end apart: 27 -> 21, of which waited for: 12 -> 10; matrix products, arithmetic and copies ran while one was open for 0% -> 0% of each run, Pallas kernels for 6% -> 6%
where the time goes in v3:
time: 73 us; the launch traced here: 72.9 us
  starting transfers between devices  27.8 us (38%)
  Pallas kernels  22.2 us (30%)
  waiting for transfers between devices  21.9 us (30%)
  between operations  0.83 us (1%)
    ppermute x9, starting transfers between devices, to_keys(): lax.ppermute(value, 'keys', [(i, i ^ bits) for i in range(key_devices)])  15.9 us
    ppermute x9, waiting for transfers between devices, to_keys(): lax.ppermute(value, 'keys', [(i, i ^ bits) for i in range(key_devices)])  12.9 us
    ppermute x12, starting transfers between devices, to_heads(): lax.ppermute(value, 'heads', [(i, i ^ bits) for i in range(head_devices)])  11.9 us
    pallas_call x1, Pallas kernels, main_scores(): pl.pallas_call(body, grid=(blocks,), out_shape=(pltpu.VMEM((blocks, keys,...  11.8 us
    ppermute x12, waiting for transfers between devices, to_heads(): lax.ppermute(value, 'heads', [(i, i ^ bits) for i in range(head_devices)])  9.05 us
    pallas_call x16, Pallas kernels, vmem_call(): pl.pallas_call(body, out_shape=outs, in_specs=[smem_spec] * len(scalars)...  7.62 us
    pallas_call x1, Pallas kernels, index_forward(): pl.pallas_call(body, out_shape=(pltpu.VMEM((rows, keys), F32), pltpu.VMEM...  2.83 us
  transfers between devices with their start and end apart: 21, of which 10 were waited for; matrix products, arithmetic and copies ran while one was open for 0% of the time, Pallas kernels for 6%

profile of v3, /device:TPU:0, one launch (start us, length us, event | category | flops | bytes accessed | tf_op | source)
XLA Modules:
  0.0 72.9 jit_solution(9691948988824255644)
XLA Ops:
  0.7 11.8 %main_scores.1 = (bf16[8,2048,256]{2,1,0:T(8,128)(2,1)S(1)}, f32[8,16,256]{2,1,0:T(8,128)S(1)}, f32[8,256]{1,0:T(8,128)S(1)}) custom-call(s32[1,128]{1,0:T(1,128)} %bitcast.4, bf16[16,576,128]{2,1,0:T(8,128)(2,1)} %bitcast.5, bf16[576,2048]{1,0:T(8,128)(2,1)} %bitcast.6), custom_call_target="tpu_custom_call" | custom-call | tf_op jit(solution)/shard_map/main_scores/pallas_call | solution.py:165
  12.5 3.1 %collective-permute-start = (f32[8,256]{1,0:T(8,128)S(1)}, f32[8,256]{1,0:T(8,128)S(1)}, u32[]{:S(2)}, u32[]{:S(2)}) collective-permute-start(f32[8,256]{1,0:T(8,128)S(1)} %get-tuple-element.39._.left_ref), channel_id=1, source_target_pairs={{0,1},{1,0},{2,3},{3,2},{4,5},{5,4},{6,7},{7,6},{8,9},{9,8},{10,11... | collective-permute-start | bytes 24584 | tf_op jit(solution)/shard_map/ppermute | solution.py:435
  15.6 2.8 %index_forward.1 = (f32[16,2048]{1,0:T(8,128)S(1)}, f32[16,128]{1,0:T(8,128)S(1)}, f32[16,128]{1,0:T(8,128)S(1)}, bf16[4,128,256]{2,1,0:T(8,128)(2,1)S(1)}, bf16[4,256,2048]{2,1,0:T(8,128)(2,1)S(1)}) custom-call(s32[128]{0:T(128)S(1)} %copy-done.3, f32[16]{0:T(128)S(1)} %copy-done.4, bf16[16,64,128]{2,1,0:T(8,128)(2,1)S(1)} %copy-done.1, ...), custom_call_target="tpu_custom_call" | custom-call | tf_op jit(solution)/shard_map/index_forward/pallas_call | solution.py:98
  18.5 2.7 %collective-permute-start.1 = (f32[24,256]{1,0:T(8,128)S(1)}, f32[24,256]{1,0:T(8,128)S(1)}, u32[]{:S(2)}, u32[]{:S(2)}) collective-permute-start(f32[24,256]{1,0:T(8,128)S(1)} %join_first.1.left_ref), channel_id=1, source_target_pairs={{0,2},{1,3},{2,0},{3,1},{4,6},{5,7},{6,4},{7,5},{8,10},{9,11},{10,... | collective-permute-start | bytes 73736 | tf_op jit(solution)/shard_map/ppermute | solution.py:435
  21.1 2.1 %collective-permute-done.1.right_ref = f32[24,256]{1,0:T(8,128)S(1)} collective-permute-done((f32[24,256]{1,0:T(8,128)S(1)}, f32[24,256]{1,0:T(8,128)S(1)}, u32[]{:S(2)}, u32[]{:S(2)}) %collective-permute-start.1) | collective-permute-done | bytes 24608 | tf_op jit(solution)/shard_map/ppermute | solution.py:435
  23.3 1.9 %head_sum.1 = (f32[4,16,2048]{2,1,0:T(8,128)S(1)}, f32[4,16,2048]{2,1,0:T(8,128)S(1)}) custom-call(bf16[8,2048,256]{2,1,0:T(8,128)(2,1)S(1)} %get-tuple-element.44.prob_ref, f32[8,16,256]{2,1,0:T(8,128)S(1)} %get-tuple-element.45.top_ref, f32[8,256]{1,0:T(8,128)S(1)} %get-tuple-element.46.stat_ref), custom_call_target="tpu_custom_call" | custom-call | flops 1000000000 | tf_op jit(solution)/shard_map/head_sum/pallas_call | solution.py:41
  25.2 1.9 %collective-permute-done.3.right_ref = f32[4,16,2048]{2,1,0:T(8,128)S(1)} collective-permute-done((f32[4,16,2048]{2,1,0:T(8,128)S(1)}, f32[4,16,2048]{2,1,0:T(8,128)S(1)}, u32[]{:S(2)}, u32[]{:S(2)}) %collective-permute-start.3) | collective-permute-done | bytes 524320 | tf_op jit(solution)/shard_map/ppermute | solution.py:438
  27.2 2.5 %collective-permute-start.4 = (f32[16,2048]{1,0:T(8,128)S(1)}, f32[16,2048]{1,0:T(8,128)S(1)}, u32[]{:S(2)}, u32[]{:S(2)}) collective-permute-start(f32[16,2048]{1,0:T(8,128)S(1)} %get-tuple-element.52), channel_id=1, source_target_pairs={{0,24},{4,28},{8,16},{12,20},{16,8},{20,12},{24,0},{28,4},{1,25},{... | collective-permute-start | bytes 393224 | tf_op jit(solution)/shard_map/ppermute | solution.py:438
  30.2 0.5 collective-permute-start.6
  30.7 0.8 %collective-permute-start.2 = (f32[16,128]{1,0:T(8,128)S(1)}, f32[16,128]{1,0:T(8,128)S(1)}, u32[]{:S(2)}, u32[]{:S(2)}) collective-permute-start(f32[16,128]{1,0:T(8,128)S(1)} %get-tuple-element.48.lse_ref), channel_id=1, source_target_pairs={{0,1},{1,0},{2,3},{3,2},{4,5},{5,4},{6,7},{7,6},{8,9},{9,8},{10,11... | collective-permute-start | bytes 24584 | tf_op jit(solution)/shard_map/ppermute | solution.py:435
  31.6 2.8 %collective-permute-done.2.other_ref = f32[16,128]{1,0:T(8,128)S(1)} collective-permute-done((f32[16,128]{1,0:T(8,128)S(1)}, f32[16,128]{1,0:T(8,128)S(1)}, u32[]{:S(2)}, u32[]{:S(2)}) %collective-permute-start.2) | collective-permute-done | bytes 8224 | tf_op jit(solution)/shard_map/ppermute | solution.py:435
  34.4 2.1 %collective-permute-done.5.refs_2_ = f32[16,2048]{1,0:T(8,128)S(1)} collective-permute-done((f32[16,2048]{1,0:T(8,128)S(1)}, f32[16,2048]{1,0:T(8,128)S(1)}, u32[]{:S(2)}, u32[]{:S(2)}) %collective-permute-start.5) | collective-permute-done | bytes 131104 | tf_op jit(solution)/shard_map/ppermute | solution.py:438
  38.4 0.9 %key_part.1 = (f32[4,256,128]{2,1,0:T(8,128)S(1)}, f32[4,256,128]{2,1,0:T(8,128)S(1)}) custom-call(bf16[4,128,256]{2,1,0:T(8,128)(2,1)S(1)} %get-tuple-element.60.wiq_ref, bf16[256,2048]{1,0:T(8,128)(2,1)S(1)} %get-tuple-element.61.refs_0_, bf16[256,2048]{1,0:T(8,128)(2,1)S(1)} %get-tuple-element.62.refs_1_, ...), custom_call_target="tpu_custom_call" | custom-call | tf_op jit(solution)/shard_map/key_part/pallas_call | solution.py:41
  39.4 0.9 %collective-permute-start.9 = (f32[256,128]{1,0:T(8,128)S(1)}, f32[256,128]{1,0:T(8,128)S(1)}, u32[]{:S(2)}, u32[]{:S(2)}) collective-permute-start(f32[256,128]{1,0:T(8,128)S(1)} %get-tuple-element.58), channel_id=1, source_target_pairs={{0,1},{1,0},{2,3},{3,2},{4,5},{5,4},{6,7},{7,6},{8,9},{9,8},{10,11... | collective-permute-start | bytes 393224 | tf_op jit(solution)/shard_map/ppermute | solution.py:435
  40.3 2.5 %collective-permute-start.8 = (f32[256,128]{1,0:T(8,128)S(1)}, f32[256,128]{1,0:T(8,128)S(1)}, u32[]{:S(2)}, u32[]{:S(2)}) collective-permute-start(f32[256,128]{1,0:T(8,128)S(1)} %get-tuple-element.57), channel_id=1, source_target_pairs={{0,2},{1,3},{2,0},{3,1},{4,6},{5,7},{6,4},{7,5},{8,10},{9,11},{10,... | collective-permute-start | bytes 393224 | tf_op jit(solution)/shard_map/ppermute | solution.py:435
  42.9 1.0 %collective-permute-start.7 = (f32[256,128]{1,0:T(8,128)S(1)}, f32[256,128]{1,0:T(8,128)S(1)}, u32[]{:S(2)}, u32[]{:S(2)}) collective-permute-start(f32[256,128]{1,0:T(8,128)S(1)} %get-tuple-element.56), channel_id=1, source_target_pairs={{0,3},{1,2},{2,1},{3,0},{4,7},{5,6},{6,5},{7,4},{8,11},{9,10},{10,... | collective-permute-start | bytes 393224 | tf_op jit(solution)/shard_map/ppermute | solution.py:435
  43.9 1.7 %collective-permute-start.14 = (f32[256,128]{1,0:T(8,128)S(1)}, f32[256,128]{1,0:T(8,128)S(1)}, u32[]{:S(2)}, u32[]{:S(2)}) collective-permute-start(f32[256,128]{1,0:T(8,128)S(1)} %get-tuple-element.71), channel_id=1, source_target_pairs={{0,24},{4,28},{8,16},{12,20},{16,8},{20,12},{24,0},{28,4},{1,25},{... | collective-permute-start | bytes 393224 | tf_op jit(solution)/shard_map/ppermute | solution.py:438
  45.7 1.3 %collective-permute-start.15 = (f32[256,128]{1,0:T(8,128)S(1)}, f32[256,128]{1,0:T(8,128)S(1)}, u32[]{:S(2)}, u32[]{:S(2)}) collective-permute-start(f32[256,128]{1,0:T(8,128)S(1)} %get-tuple-element.72), channel_id=1, source_target_pairs={{0,16},{4,20},{8,24},{12,28},{16,0},{20,4},{24,8},{28,12},{1,17},{... | collective-permute-start | bytes 393224 | tf_op jit(solution)/shard_map/ppermute | solution.py:438
  47.0 1.1 %collective-permute-done.9.refs_2_ = f32[256,128]{1,0:T(8,128)S(1)} collective-permute-done((f32[256,128]{1,0:T(8,128)S(1)}, f32[256,128]{1,0:T(8,128)S(1)}, u32[]{:S(2)}, u32[]{:S(2)}) %collective-permute-start.9) | collective-permute-done | bytes 131104 | tf_op jit(solution)/shard_map/ppermute | solution.py:435
  48.1 1.5 %collective-permute-start.16 = (f32[256,128]{1,0:T(8,128)S(1)}, f32[256,128]{1,0:T(8,128)S(1)}, u32[]{:S(2)}, u32[]{:S(2)}) collective-permute-start(f32[256,128]{1,0:T(8,128)S(1)} %get-tuple-element.73), channel_id=1, source_target_pairs={{0,8},{4,12},{8,0},{12,4},{16,24},{20,28},{24,16},{28,20},{1,9},{5... | collective-permute-start | bytes 393224 | tf_op jit(solution)/shard_map/ppermute | solution.py:438
  49.6 3.6 %collective-permute-done.8.refs_1_ = f32[256,128]{1,0:T(8,128)S(1)} collective-permute-done((f32[256,128]{1,0:T(8,128)S(1)}, f32[256,128]{1,0:T(8,128)S(1)}, u32[]{:S(2)}, u32[]{:S(2)}) %collective-permute-start.8) | collective-permute-done | bytes 131104 | tf_op jit(solution)/shard_map/ppermute | solution.py:435
  53.7 1.6 %collective-permute-start.17 = (f32[256,128]{1,0:T(8,128)S(1)}, f32[256,128]{1,0:T(8,128)S(1)}, u32[]{:S(2)}, u32[]{:S(2)}) collective-permute-start(f32[256,128]{1,0:T(8,128)S(1)} %add_all.1.refs_0_), channel_id=1, source_target_pairs={{0,8},{4,12},{8,0},{12,4},{16,24},{20,28},{24,16},{28,20},{1,9},{5... | collective-permute-start | bytes 393224 | tf_op jit(solution)/shard_map/ppermute | solution.py:438
  55.2 2.9 %collective-permute-start.13 = (f32[264,128]{1,0:T(8,128)S(1)}, f32[264,128]{1,0:T(8,128)S(1)}, u32[]{:S(2)}, u32[]{:S(2)}) collective-permute-start(f32[264,128]{1,0:T(8,128)S(1)} %own_rows.1.refs_0_), channel_id=1, source_target_pairs={{0,3},{1,2},{2,1},{3,0},{4,7},{5,6},{6,5},{7,4},{8,11},{9,10},{10,... | collective-permute-start | bytes 405512 | tf_op jit(solution)/shard_map/ppermute | solution.py:435
  58.1 1.4 %collective-permute-start.12 = (f32[264,128]{1,0:T(8,128)S(1)}, f32[264,128]{1,0:T(8,128)S(1)}, u32[]{:S(2)}, u32[]{:S(2)}) collective-permute-start(f32[264,128]{1,0:T(8,128)S(1)} %own_rows.1.refs_0_), channel_id=1, source_target_pairs={{0,2},{1,3},{2,0},{3,1},{4,6},{5,7},{6,4},{7,5},{8,10},{9,11},{10,... | collective-permute-start | bytes 405512 | tf_op jit(solution)/shard_map/ppermute | solution.py:435
  59.5 0.6 collective-permute-start.11
  60.1 0.7 collective-permute-start.18
  60.8 1.3 %collective-permute-start.19 = (f32[256,128]{1,0:T(8,128)S(1)}, f32[256,128]{1,0:T(8,128)S(1)}, u32[]{:S(2)}, u32[]{:S(2)}) collective-permute-start(f32[256,128]{1,0:T(8,128)S(1)} %collective-permute-done.17.refs_1_), channel_id=1, source_target_pairs={{0,16},{4,20},{8,24},{12,28},{16,0},{20,4},{24,8},{28,12},{1,17},{... | collective-permute-start | bytes 393224 | tf_op jit(solution)/shard_map/ppermute | solution.py:438
  62.1 3.5 %collective-permute-done.18.refs_2_ = f32[256,128]{1,0:T(8,128)S(1)} collective-permute-done((f32[256,128]{1,0:T(8,128)S(1)}, f32[256,128]{1,0:T(8,128)S(1)}, u32[]{:S(2)}, u32[]{:S(2)}) %collective-permute-start.18) | collective-permute-done | bytes 131104 | tf_op jit(solution)/shard_map/ppermute | solution.py:438
  65.7 1.4 %collective-permute-done.19.refs_3_ = f32[256,128]{1,0:T(8,128)S(1)} collective-permute-done((f32[256,128]{1,0:T(8,128)S(1)}, f32[256,128]{1,0:T(8,128)S(1)}, u32[]{:S(2)}, u32[]{:S(2)}) %collective-permute-start.19) | collective-permute-done | bytes 131104 | tf_op jit(solution)/shard_map/ppermute | solution.py:438
  67.2 3.2 %collective-permute-done.12.refs_2_ = f32[264,128]{1,0:T(8,128)S(1)} collective-permute-done((f32[264,128]{1,0:T(8,128)S(1)}, f32[264,128]{1,0:T(8,128)S(1)}, u32[]{:S(2)}, u32[]{:S(2)}) %collective-permute-start.12) | collective-permute-done | bytes 135200 | tf_op jit(solution)/shard_map/ppermute | solution.py:435
  70.4 1.4 %place_query.1 = (f32[1024,128]{1,0:T(8,128)}, f32[16,64]{1,0:T(8,128)}) custom-call(f32[264,128]{1,0:T(8,128)S(1)} %own_rows.1.refs_0_, f32[264,128]{1,0:T(8,128)S(1)} %collective-permute-done.11.refs_1_, f32[264,128]{1,0:T(8,128)S(1)} %collective-permute-done.12.refs_2_, f32[264,128]{1,0:T(8,128)S(1)} %collective-permute-done.13.refs_3_), custom_call_target="tpu_custom_call" | custom-call | flops 40000000000 | tf_op jit(solution)/shard_map/place_query/pallas_call | solution.py:41
  71.8 1.0 %place_keys.1 = f32[2048,128]{1,0:T(8,128)} custom-call(f32[4,256,128]{2,1,0:T(8,128)S(1)} %stack_all.1.mine_ref, f32[4,256,128]{2,1,0:T(8,128)S(1)} %collective-permute-done.20.other_ref), custom_call_target="tpu_custom_call" | custom-call | tf_op jit(solution)/shard_map/place_keys/pallas_call | solution.py:41
  (38 shorter events, 3.3 us)
Async XLA Ops:
  0.6 14.9 %copy-start.3 = (s32[128]{0:T(128)S(1)}, s32[128]{0:T(128)}, u32[]{:S(2)}) copy-start(s32[128]{0:T(128)} %pos_ref.1) | copy-start | bytes 1540
  0.6 14.9 %copy-start = (bf16[2048,128]{1,0:T(8,128)(2,1)S(1)}, bf16[2048,128]{1,0:T(8,128)(2,1)}, u32[]{:S(2)}) copy-start(bf16[2048,128]{1,0:T(8,128)(2,1)} %keys_ref.9) | copy-start | bytes 1572868
  0.7 14.9 %copy-start.2 = (f32[16,64]{1,0:T(8,128)S(1)}, f32[16,64]{1,0:T(8,128)}, u32[]{:S(2)}) copy-start(f32[16,64]{1,0:T(8,128)} %weight_ref.3) | copy-start | bytes 12292
  0.7 14.9 %copy-start.1 = (bf16[16,64,128]{2,1,0:T(8,128)(2,1)S(1)}, bf16[16,64,128]{2,1,0:T(8,128)(2,1)}, u32[]{:S(2)}) copy-start(bf16[16,64,128]{2,1,0:T(8,128)(2,1)} %query_ref.3) | copy-start | bytes 786436
  0.7 14.9 %copy-start.4 = (f32[16]{0:T(128)S(1)}, f32[16]{0:T(128)}, u32[]{:S(2)}) copy-start(f32[16]{0:T(128)} %kl_ref.1) | copy-start | bytes 196
  12.5 5.9 %collective-permute-start = (f32[8,256]{1,0:T(8,128)S(1)}, f32[8,256]{1,0:T(8,128)S(1)}, u32[]{:S(2)}, u32[]{:S(2)}) collective-permute-start(f32[8,256]{1,0:T(8,128)S(1)} %get-tuple-element.39._.left_ref), channel_id=1, source_target_pairs={{0,1},{1,0},{2,3},{3,2},{4,5},{5,4},{6,7},{7,6},{8,9},{9,8},{10,11... | collective-permute-start | bytes 24584 | tf_op jit(solution)/shard_map/ppermute | solution.py:435
  18.5 4.8 %collective-permute-start.1 = (f32[24,256]{1,0:T(8,128)S(1)}, f32[24,256]{1,0:T(8,128)S(1)}, u32[]{:S(2)}, u32[]{:S(2)}) collective-permute-start(f32[24,256]{1,0:T(8,128)S(1)} %join_first.1.left_ref), channel_id=1, source_target_pairs={{0,2},{1,3},{2,0},{3,1},{4,6},{5,7},{6,4},{7,5},{8,10},{9,11},{10,... | collective-permute-start | bytes 73736 | tf_op jit(solution)/shard_map/ppermute | solution.py:435
  25.1 2.0 %collective-permute-start.3 = (f32[4,16,2048]{2,1,0:T(8,128)S(1)}, f32[4,16,2048]{2,1,0:T(8,128)S(1)}, u32[]{:S(2)}, u32[]{:S(2)}) collective-permute-start(f32[4,16,2048]{2,1,0:T(8,128)S(1)} %get-tuple-element.50), channel_id=1, source_target_pairs={{0,4},{4,0},{8,12},{12,8},{16,20},{20,16},{24,28},{28,24},{1,5},{5... | collective-permute-start | bytes 1572872 | tf_op jit(solution)/shard_map/ppermute | solution.py:438
  27.2 7.2 %collective-permute-start.4 = (f32[16,2048]{1,0:T(8,128)S(1)}, f32[16,2048]{1,0:T(8,128)S(1)}, u32[]{:S(2)}, u32[]{:S(2)}) collective-permute-start(f32[16,2048]{1,0:T(8,128)S(1)} %get-tuple-element.52), channel_id=1, source_target_pairs={{0,24},{4,28},{8,16},{12,20},{16,8},{20,12},{24,0},{28,4},{1,25},{... | collective-permute-start | bytes 393224 | tf_op jit(solution)/shard_map/ppermute | solution.py:438
  29.7 6.8 %collective-permute-start.5 = (f32[16,2048]{1,0:T(8,128)S(1)}, f32[16,2048]{1,0:T(8,128)S(1)}, u32[]{:S(2)}, u32[]{:S(2)}) collective-permute-start(f32[16,2048]{1,0:T(8,128)S(1)} %get-tuple-element.53), channel_id=1, source_target_pairs={{0,16},{4,20},{8,24},{12,28},{16,0},{20,4},{24,8},{28,12},{1,17},{... | collective-permute-start | bytes 393224 | tf_op jit(solution)/shard_map/ppermute | solution.py:438
  30.2 6.4 %collective-permute-start.6 = (f32[16,2048]{1,0:T(8,128)S(1)}, f32[16,2048]{1,0:T(8,128)S(1)}, u32[]{:S(2)}, u32[]{:S(2)}) collective-permute-start(f32[16,2048]{1,0:T(8,128)S(1)} %get-tuple-element.54), channel_id=1, source_target_pairs={{0,8},{4,12},{8,0},{12,4},{16,24},{20,28},{24,16},{28,20},{1,9},{5... | collective-permute-start | bytes 393224 | tf_op jit(solution)/shard_map/ppermute | solution.py:438
  30.7 3.7 %collective-permute-start.2 = (f32[16,128]{1,0:T(8,128)S(1)}, f32[16,128]{1,0:T(8,128)S(1)}, u32[]{:S(2)}, u32[]{:S(2)}) collective-permute-start(f32[16,128]{1,0:T(8,128)S(1)} %get-tuple-element.48.lse_ref), channel_id=1, source_target_pairs={{0,1},{1,0},{2,3},{3,2},{4,5},{5,4},{6,7},{7,6},{8,9},{9,8},{10,11... | collective-permute-start | bytes 24584 | tf_op jit(solution)/shard_map/ppermute | solution.py:435
  39.3 4.5 %collective-permute-start.10 = (f32[4,256,128]{2,1,0:T(8,128)S(1)}, f32[4,256,128]{2,1,0:T(8,128)S(1)}, u32[]{:S(2)}, u32[]{:S(2)}) collective-permute-start(f32[4,256,128]{2,1,0:T(8,128)S(1)} %get-tuple-element.66), channel_id=1, source_target_pairs={{0,4},{4,0},{8,12},{12,8},{16,20},{20,16},{24,28},{28,24},{1,5},{5... | collective-permute-start | bytes 1572872 | tf_op jit(solution)/shard_map/ppermute | solution.py:438
  39.4 8.6 %collective-permute-start.9 = (f32[256,128]{1,0:T(8,128)S(1)}, f32[256,128]{1,0:T(8,128)S(1)}, u32[]{:S(2)}, u32[]{:S(2)}) collective-permute-start(f32[256,128]{1,0:T(8,128)S(1)} %get-tuple-element.58), channel_id=1, source_target_pairs={{0,1},{1,0},{2,3},{3,2},{4,5},{5,4},{6,7},{7,6},{8,9},{9,8},{10,11... | collective-permute-start | bytes 393224 | tf_op jit(solution)/shard_map/ppermute | solution.py:435
  40.3 12.9 %collective-permute-start.8 = (f32[256,128]{1,0:T(8,128)S(1)}, f32[256,128]{1,0:T(8,128)S(1)}, u32[]{:S(2)}, u32[]{:S(2)}) collective-permute-start(f32[256,128]{1,0:T(8,128)S(1)} %get-tuple-element.57), channel_id=1, source_target_pairs={{0,2},{1,3},{2,0},{3,1},{4,6},{5,7},{6,4},{7,5},{8,10},{9,11},{10,... | collective-permute-start | bytes 393224 | tf_op jit(solution)/shard_map/ppermute | solution.py:435
  42.9 10.4 %collective-permute-start.7 = (f32[256,128]{1,0:T(8,128)S(1)}, f32[256,128]{1,0:T(8,128)S(1)}, u32[]{:S(2)}, u32[]{:S(2)}) collective-permute-start(f32[256,128]{1,0:T(8,128)S(1)} %get-tuple-element.56), channel_id=1, source_target_pairs={{0,3},{1,2},{2,1},{3,0},{4,7},{5,6},{6,5},{7,4},{8,11},{9,10},{10,... | collective-permute-start | bytes 393224 | tf_op jit(solution)/shard_map/ppermute | solution.py:435
  43.9 9.6 %collective-permute-start.14 = (f32[256,128]{1,0:T(8,128)S(1)}, f32[256,128]{1,0:T(8,128)S(1)}, u32[]{:S(2)}, u32[]{:S(2)}) collective-permute-start(f32[256,128]{1,0:T(8,128)S(1)} %get-tuple-element.71), channel_id=1, source_target_pairs={{0,24},{4,28},{8,16},{12,20},{16,8},{20,12},{24,0},{28,4},{1,25},{... | collective-permute-start | bytes 393224 | tf_op jit(solution)/shard_map/ppermute | solution.py:438
  45.7 7.9 %collective-permute-start.15 = (f32[256,128]{1,0:T(8,128)S(1)}, f32[256,128]{1,0:T(8,128)S(1)}, u32[]{:S(2)}, u32[]{:S(2)}) collective-permute-start(f32[256,128]{1,0:T(8,128)S(1)} %get-tuple-element.72), channel_id=1, source_target_pairs={{0,16},{4,20},{8,24},{12,28},{16,0},{20,4},{24,8},{28,12},{1,17},{... | collective-permute-start | bytes 393224 | tf_op jit(solution)/shard_map/ppermute | solution.py:438
  48.1 5.5 %collective-permute-start.16 = (f32[256,128]{1,0:T(8,128)S(1)}, f32[256,128]{1,0:T(8,128)S(1)}, u32[]{:S(2)}, u32[]{:S(2)}) collective-permute-start(f32[256,128]{1,0:T(8,128)S(1)} %get-tuple-element.73), channel_id=1, source_target_pairs={{0,8},{4,12},{8,0},{12,4},{16,24},{20,28},{24,16},{28,20},{1,9},{5... | collective-permute-start | bytes 393224 | tf_op jit(solution)/shard_map/ppermute | solution.py:438
  53.7 7.2 %collective-permute-start.17 = (f32[256,128]{1,0:T(8,128)S(1)}, f32[256,128]{1,0:T(8,128)S(1)}, u32[]{:S(2)}, u32[]{:S(2)}) collective-permute-start(f32[256,128]{1,0:T(8,128)S(1)} %add_all.1.refs_0_), channel_id=1, source_target_pairs={{0,8},{4,12},{8,0},{12,4},{16,24},{20,28},{24,16},{28,20},{1,9},{5... | collective-permute-start | bytes 393224 | tf_op jit(solution)/shard_map/ppermute | solution.py:438
  55.2 12.0 %collective-permute-start.13 = (f32[264,128]{1,0:T(8,128)S(1)}, f32[264,128]{1,0:T(8,128)S(1)}, u32[]{:S(2)}, u32[]{:S(2)}) collective-permute-start(f32[264,128]{1,0:T(8,128)S(1)} %own_rows.1.refs_0_), channel_id=1, source_target_pairs={{0,3},{1,2},{2,1},{3,0},{4,7},{5,6},{6,5},{7,4},{8,11},{9,10},{10,... | collective-permute-start | bytes 405512 | tf_op jit(solution)/shard_map/ppermute | solution.py:435
  58.1 12.2 %collective-permute-start.12 = (f32[264,128]{1,0:T(8,128)S(1)}, f32[264,128]{1,0:T(8,128)S(1)}, u32[]{:S(2)}, u32[]{:S(2)}) collective-permute-start(f32[264,128]{1,0:T(8,128)S(1)} %own_rows.1.refs_0_), channel_id=1, source_target_pairs={{0,2},{1,3},{2,0},{3,1},{4,6},{5,7},{6,4},{7,5},{8,10},{9,11},{10,... | collective-permute-start | bytes 405512 | tf_op jit(solution)/shard_map/ppermute | solution.py:435
  59.5 10.8 %collective-permute-start.11 = (f32[264,128]{1,0:T(8,128)S(1)}, f32[264,128]{1,0:T(8,128)S(1)}, u32[]{:S(2)}, u32[]{:S(2)}) collective-permute-start(f32[264,128]{1,0:T(8,128)S(1)} %own_rows.1.refs_0_), channel_id=1, source_target_pairs={{0,1},{1,0},{2,3},{3,2},{4,5},{5,4},{6,7},{7,6},{8,9},{9,8},{10,11... | collective-permute-start | bytes 405512 | tf_op jit(solution)/shard_map/ppermute | solution.py:435
  60.1 5.6 %collective-permute-start.18 = (f32[256,128]{1,0:T(8,128)S(1)}, f32[256,128]{1,0:T(8,128)S(1)}, u32[]{:S(2)}, u32[]{:S(2)}) collective-permute-start(f32[256,128]{1,0:T(8,128)S(1)} %add_all.1.refs_0_), channel_id=1, source_target_pairs={{0,16},{4,20},{8,24},{12,28},{16,0},{20,4},{24,8},{28,12},{1,17},{... | collective-permute-start | bytes 393224 | tf_op jit(solution)/shard_map/ppermute | solution.py:438
  60.8 6.3 %collective-permute-start.19 = (f32[256,128]{1,0:T(8,128)S(1)}, f32[256,128]{1,0:T(8,128)S(1)}, u32[]{:S(2)}, u32[]{:S(2)}) collective-permute-start(f32[256,128]{1,0:T(8,128)S(1)} %collective-permute-done.17.refs_1_), channel_id=1, source_target_pairs={{0,16},{4,20},{8,24},{12,28},{16,0},{20,4},{24,8},{28,12},{1,17},{... | collective-permute-start | bytes 393224 | tf_op jit(solution)/shard_map/ppermute | solution.py:438
  67.1 4.7 %collective-permute-start.20 = (f32[4,256,128]{2,1,0:T(8,128)S(1)}, f32[4,256,128]{2,1,0:T(8,128)S(1)}, u32[]{:S(2)}, u32[]{:S(2)}) collective-permute-start(f32[4,256,128]{2,1,0:T(8,128)S(1)} %stack_all.1.mine_ref), channel_id=1, source_target_pairs={{0,4},{4,0},{8,12},{12,8},{16,20},{20,16},{24,28},{28,24},{1,5},{5... | collective-permute-start | bytes 1572872 | tf_op jit(solution)/shard_map/ppermute | solution.py:438

commit v4 on v3

--- a/solution.py
+++ b/solution.py
@@ -118,6 +118,7 @@
     per = 256 // queries if queries < 256 and head_local % (256 // queries) == 0 else 1
     lanes = per * queries
     blocks = head_local // per
+    many = 2 if blocks % 2 == 0 else 1
     tile = tile_of(keys, 128)
     tiles = keys // tile
     mask_at = -(-feature // 128) * 128
@@ -133,50 +134,54 @@
                 key_rows[at : at + chunk, :feature] = keys_ref[:, at : at + chunk].T
             if mask_at > feature:
                 key_rows[:, feature:mask_at] = jnp.zeros((keys, mask_at - feature), BF16)
-                weights[feature:mask_at, :] = jnp.zeros((mask_at - feature, lanes), BF16)
+                weights[:, feature:mask_at, :] = jnp.zeros((many, mask_at - feature, lanes), BF16)
             index = lax.axis_index("keys") * keys + lax.broadcasted_iota(jnp.int32, (keys, queries), 0)
             hidden = jnp.where(index <= pos_ref[...], 0.0, masked_fill).astype(BF16)
             key_rows[:, mask_at : mask_at + queries] = hidden
             at_row = lax.broadcasted_iota(jnp.int32, (depth - mask_at, lanes), 0)
             at_lane = lax.broadcasted_iota(jnp.int32, (depth - mask_at, lanes), 1)
-            weights[mask_at:, :] = jnp.where(at_row == at_lane % queries, 1.0, 0.0).astype(BF16)
+            for k in range(many):
+                weights[k, mask_at:, :] = jnp.where(at_row == at_lane % queries, 1.0, 0.0).astype(BF16)
             if depth > mask_at + queries:
                 key_rows[:, mask_at + queries :] = jnp.zeros((keys, depth - mask_at - queries), BF16)
 
-        for i in range(per):
-            weights[:feature, i * queries : (i + 1) * queries] = query_ref[i]
-        tops, totals = [], []
-        for t in range(tiles):
-            span = slice(t * tile, (t + 1) * tile)
-            scores = jnp.dot(key_rows[span, :], weights[...], preferred_element_type=F32)
-            top = jnp.max(scores, axis=0, keepdims=True)
-            prob = jnp.exp2((scores - top) * score_scale)
-            top = top * score_scale
-            tops.append(top)
-            totals.append(jnp.sum(prob, axis=0, keepdims=True))
-            prob_ref[step, span, :] = prob.astype(prob_ref.dtype)
-            top_ref[step, t : t + 1, :] = top
-        best = tops[0]
-        for top in tops[1:]:
-            best = jnp.maximum(best, top)
-        total = sum(s * jnp.exp2(top - best) for s, top in zip(totals, tops))
-        stat_ref[pl.ds(step, 1), :] = best + jnp.log2(total)
+        for k in range(many):
+            for i in range(per):
+                weights[k, :feature, i * queries : (i + 1) * queries] = query_ref[k * per + i]
+        for k in range(many):
+            block = step * many + k
+            tops, totals = [], []
+            for t in range(tiles):
+                span = slice(t * tile, (t + 1) * tile)
+                scores = jnp.dot(key_rows[span, :], weights[k], preferred_element_type=F32)
+                top = jnp.max(scores, axis=0, keepdims=True)
+                prob = jnp.exp2((scores - top) * score_scale)
+                top = top * score_scale
+                tops.append(top)
+                totals.append(jnp.sum(prob, axis=0, keepdims=True))
+                prob_ref[block, span, :] = prob.astype(prob_ref.dtype)
+                top_ref[block, t : t + 1, :] = top
+            best = tops[0]
+            for top in tops[1:]:
+                best = jnp.maximum(best, top)
+            total = sum(s * jnp.exp2(top - best) for s, top in zip(totals, tops))
+            stat_ref[pl.ds(block, 1), :] = best + jnp.log2(total)
 
     return pl.pallas_call(
         body,
-        grid=(blocks,),
+        grid=(blocks // many,),
         out_shape=(
-            pltpu.VMEM((blocks, keys, lanes), BF16),
+            pltpu.VMEM((blocks, keys, lanes), F32),
             pltpu.VMEM((blocks, tiles, lanes), F32),
             pltpu.VMEM((blocks, lanes), F32),
         ),
         in_specs=[
             pl.BlockSpec((1, queries), lambda i: (0, 0)),
-            pl.BlockSpec((per, feature, queries), lambda i: (i, 0, 0)),
+            pl.BlockSpec((many * per, feature, queries), lambda i: (i, 0, 0)),
             pl.BlockSpec((feature, keys), lambda i: (0, 0)),
         ],
         out_specs=(vmem_spec,) * 3,
-        scratch_shapes=[pltpu.VMEM((keys, depth), BF16), pltpu.VMEM((depth, lanes), BF16)],
+        scratch_shapes=[pltpu.VMEM((keys, depth), BF16), pltpu.VMEM((many, depth, lanes), BF16)],
         compiler_params=pltpu.CompilerParams(vmem_limit_bytes=16 * MIB),
         name="main_scores",
     )(in_hbm(pos), in_hbm(query_t), in_hbm(keys_t))
@@ -280,68 +285,58 @@
     return vmem_call(body, "join_pair", pltpu.VMEM(left.shape, F32), (left, right))
 
 
-def deltas(scores, index_stats, targets, kl, groups):
+def gradients(scores, index_stats, targets, kl, gate, index_keys, wiq, head_devices):
     rows, keys = scores.shape
+    groups, size = gate.shape[:2]
     own = rows // groups
-
-    def body(score_ref, kl_ref, lse_ref, other_ref, *refs):
-        target_refs, out_ref = refs[:-1], refs[-1]
+    heads = size // own
+    width = index_keys.shape[1]
+    chips = head_devices // 2
+    chunk = keys // head_devices
+
+    def body(score_ref, kl_ref, lse_ref, other_ref, gate_ref, keys_ref, wiq_ref, *refs):
+        target_refs, refs = refs[: len(targets)], refs[len(targets) :]
+        query_outs, (keep_ref, send_ref, delta_ref, slope_ref, wiq_rows) = refs[:groups], refs[groups:]
         whole = joined([lse_ref[:, :1], other_ref[:, :1]])
         target = target_refs[0][...]
         for ref in target_refs[1:]:
             target = target + ref[...]
         delta = kl_ref[:, :1] * (jnp.exp2(score_ref[...] - whole) - target)
         for g in range(groups):
-            out_ref[g] = delta[g * own : (g + 1) * own, :]
-
-    return vmem_call(body, "deltas", pltpu.VMEM((groups, own, keys), F32), (scores, kl, *index_stats, *targets))
-
-
-def query_part(r, delta, gate, index_keys):
-    groups, own, keys = delta.shape
-    size = gate.shape[1]
-    heads = size // own
-    width = index_keys.shape[1]
-
-    def body(delta_ref, gate_ref, keys_ref, slope_ref, out_ref):
-        group = lax.axis_index("keys") ^ r
-        delta_rows = delta_ref[group]
-        for row in range(own):
-            line = jnp.broadcast_to(delta_rows[row : row + 1, :], (heads, keys)).astype(BF16)
-            part = slice(row * heads, (row + 1) * heads)
-            slope_ref[part, :] = jnp.where(gate_ref[group, part, :] > 0, line, jnp.zeros((), BF16))
-        out_ref[...] = jnp.dot(slope_ref[...], keys_ref[...], preferred_element_type=F32)
-
-    outs = (pltpu.VMEM((size, keys), BF16), pltpu.VMEM((size, width), F32))
-    return vmem_call(body, "query_part", outs, (delta, gate, index_keys), cost=SHORT)
-
-
-def key_part(slopes, wiq, head_devices):
-    groups, width = wiq.shape[:2]
-    keys = slopes[0].shape[1]
-    chips = head_devices // 2
-    chunk = keys // head_devices
-
-    def body(wiq_ref, *refs):
-        slope_refs, (keep_ref, send_ref) = refs[:groups], refs[groups:]
+            delta_ref[g] = delta[g * own : (g + 1) * own, :]
         z = lax.axis_index("keys")
         chip, core = head_place()
+        for r in range(groups):
+            lines = delta_ref[z ^ r]
+            for i in range(own):
+                line = jnp.broadcast_to(lines[i : i + 1, :], (heads, keys)).astype(BF16)
+                signs = gate_ref[z ^ r, i * heads : (i + 1) * heads, :]
+                at = r * size + i * heads
+                slope_ref[at : at + heads, :] = jnp.where(signs > 0, line, jnp.zeros((), BF16))
+            wiq_rows[:, r * size : (r + 1) * size] = wiq_ref[z ^ r]
+        part = jnp.dot(slope_ref[...], keys_ref[...], preferred_element_type=F32)
+        for r in range(groups):
+            query_outs[r][:size, :] = part[r * size : (r + 1) * size, :]
+            query_outs[r][size:, :] = jnp.zeros((8, width), F32)
         for out_ref, side in ((send_ref, 1 - core), (keep_ref, core)):
             for n in range(chips):
                 span = pl.ds(pl.multiple_of(((chip ^ n) * 2 + side) * chunk, chunk), chunk)
-                summed = None
-                for r in range(groups):
-                    part = jnp.dot(wiq_ref[z ^ r], slope_refs[r][:, span], preferred_element_type=F32)
-                    summed = part if summed is None else summed + part
-                out_ref[n] = summed.T
+                out_ref[n] = jnp.dot(wiq_rows[...], slope_ref[:, span], preferred_element_type=F32).T
 
     half = pltpu.VMEM((chips, chunk, width), F32)
-    return vmem_call(body, "key_part", (half, half), (wiq, *slopes), cost=SHORT)
+    outs = tuple(pltpu.VMEM((size + 8, width), F32) for _ in range(groups)) + (half, half)
+    scratch = [
+        pltpu.VMEM((groups, own, keys), F32),
+        pltpu.VMEM((rows * heads, keys), BF16),
+        pltpu.VMEM((width, rows * heads), BF16),
+    ]
+    operands = (scores, kl, *index_stats, gate, index_keys, wiq, *targets)
+    return vmem_call(body, "gradients", outs, operands, scratch, limit=16 * MIB, cost=SHORT)
 
 
 def own_rows(parts, index_query, index_weight):
     rows, heads, width = index_query.shape
-    size = parts[0].shape[0]
+    size = parts[0].shape[0] - 8
     own = size // heads
     extra = -(-own // 8) * 8
 
@@ -376,7 +371,7 @@
     width = pieces[0].shape[1]
 
     def body(*refs):
-        piece_refs, (query_out, weight_out, sems) = refs[: len(pieces)], refs[len(pieces) :]
+        piece_refs, (query_out, weight_out, weights, sems) = refs[: len(pieces)], refs[len(pieces) :]
         z = lax.axis_index("keys")
         copies = []
         for r, ref in enumerate(piece_refs):
@@ -384,7 +379,9 @@
             copies.append(pltpu.make_async_copy(ref.at[:size], query_out.at[pl.ds(at, size)], sems.at[r]))
             copies[-1].start()
         for r, ref in enumerate(piece_refs):
-            weight_out[pl.ds((z ^ r) * own, own), :] = ref[size : size + own, :heads]
+            weights[pl.ds((z ^ r) * own, own), :] = ref[size : size + own, :heads]
+        copies.append(pltpu.make_async_copy(weights, weight_out, sems.at[len(pieces)]))
+        copies[-1].start()
         for copy in copies:
             copy.wait()
 
@@ -393,8 +390,8 @@
         "place_query",
         (jax.ShapeDtypeStruct((rows * heads, width), F32), jax.ShapeDtypeStruct((rows, heads), F32)),
         pieces,
-        [pltpu.SemaphoreType.DMA((len(pieces),))],
-        out_specs=(any_spec, vmem_spec),
+        [pltpu.VMEM((rows, heads), F32), pltpu.SemaphoreType.DMA((len(pieces) + 1,))],
+        out_specs=(any_spec, any_spec),
         cost=LONG,
     )
     return query.reshape(rows, heads, width), weight
@@ -455,15 +452,13 @@
     index_lse, send = lax.optimization_barrier((index_lse, send))
     sums = add_stacks(keep, to_heads(send, 1))
     targets = [sums[0]] + [to_heads(sums[r], 2 * r) for r in chips_far_first]
-    delta = deltas(scores, (index_lse, to_keys(index_lse, 1)), targets, kl, key_devices)
-
-    slopes, arrived = {}, []
-    for r in far_first + [0]:
-        slopes[r], part = query_part(r, delta, gate, index_keys)
-        arrived.append(to_keys(part, r) if r else part)
-    keep, send = key_part([slopes[r] for r in range(key_devices)], wiq, head_devices)
+    index_stats = (index_lse, to_keys(index_lse, 1))
+    *parts, keep, send = gradients(
+        scores, index_stats, targets, kl, gate, index_keys, wiq, head_devices
+    )
+    arrived = [to_keys(parts[r], r) for r in far_first] + [parts[0]]
+    query_own = own_rows(arrived, index_query, index_weight)
     sums = add_stacks(keep, to_heads(send, 1))
-    query_own = own_rows(arrived, index_query, index_weight)
     key_parts = [sums[0]] + [to_heads(sums[r], 2 * r) for r in chips_far_first]
     query_own, key_parts[0] = lax.optimization_barrier((query_own, key_parts[0]))
     key_own = add_all(key_parts)

time: 73 us -> 71.5 us (0.979)
  Pallas kernels: 22.2 us -> 19.9 us
  waiting for transfers between devices: 21.9 us -> 23.2 us
    ppermute x9, waiting for transfers between devices: 12.9 us -> 14.2 us  [to_keys(): lax.ppermute(value, 'keys', [(i, i ^ bits) for i in range(key_devices)])]
    pallas_call x16 -> x11, Pallas kernels: 7.62 us -> 6.32 us  [vmem_call(): pl.pallas_call(body, out_shape=outs, in_specs=[smem_spec] * len(scalars)...]
    pallas_call x1, Pallas kernels: 11.8 us -> 10.8 us  [main_scores(): pl.pallas_call(body, grid=(blocks // many,), out_shape=(pltpu.VMEM((block...]
where the time goes in v4:
time: 71.5 us; the launch traced here: 71.4 us
  starting transfers between devices  27.4 us (38%)
  waiting for transfers between devices  23.2 us (32%)
  Pallas kernels  19.9 us (28%)
  between operations  0.8 us (1%)
    ppermute x9, starting transfers between devices, to_keys(): lax.ppermute(value, 'keys', [(i, i ^ bits) for i in range(key_devices)])  15.5 us
    ppermute x9, waiting for transfers between devices, to_keys(): lax.ppermute(value, 'keys', [(i, i ^ bits) for i in range(key_devices)])  14.2 us
    ppermute x12, starting transfers between devices, to_heads(): lax.ppermute(value, 'heads', [(i, i ^ bits) for i in range(head_devices)])  12 us
    pallas_call x1, Pallas kernels, main_scores(): pl.pallas_call(body, grid=(blocks // many,), out_shape=(pltpu.VMEM((block...  10.8 us
    ppermute x12, waiting for transfers between devices, to_heads(): lax.ppermute(value, 'heads', [(i, i ^ bits) for i in range(head_devices)])  8.94 us
    pallas_call x11, Pallas kernels, vmem_call(): pl.pallas_call(body, out_shape=outs, in_specs=[smem_spec] * len(scalars)...  6.32 us
    pallas_call x1, Pallas kernels, index_forward(): pl.pallas_call(body, out_shape=(pltpu.VMEM((rows, keys), F32), pltpu.VMEM...  2.83 us
  transfers between devices with their start and end apart: 21, of which 10 were waited for; matrix products, arithmetic and copies ran while one was open for 0% of the time, Pallas kernels for 6%

profile of v4, /device:TPU:0, one launch (start us, length us, event | category | flops | bytes accessed | tf_op | source)
XLA Modules:
  0.0 71.4 jit_solution(3942871954537766520)
XLA Ops:
  0.7 10.8 %main_scores.1 = (f32[8,2048,256]{2,1,0:T(8,128)S(1)}, f32[8,16,256]{2,1,0:T(8,128)S(1)}, f32[8,256]{1,0:T(8,128)S(1)}) custom-call(s32[1,128]{1,0:T(1,128)} %bitcast.4, bf16[16,576,128]{2,1,0:T(8,128)(2,1)} %bitcast.5, bf16[576,2048]{1,0:T(8,128)(2,1)} %bitcast.6), custom_call_target="tpu_custom_call" | custom-call | tf_op jit(solution)/shard_map/main_scores/pallas_call | solution.py:170
  11.5 3.1 %collective-permute-start = (f32[8,256]{1,0:T(8,128)S(1)}, f32[8,256]{1,0:T(8,128)S(1)}, u32[]{:S(2)}, u32[]{:S(2)}) collective-permute-start(f32[8,256]{1,0:T(8,128)S(1)} %get-tuple-element.35._.left_ref), channel_id=1, source_target_pairs={{0,1},{1,0},{2,3},{3,2},{4,5},{5,4},{6,7},{7,6},{8,9},{9,8},{10,11... | collective-permute-start | bytes 24584 | tf_op jit(solution)/shard_map/ppermute | solution.py:432
  14.6 2.8 %index_forward.1 = (f32[16,2048]{1,0:T(8,128)S(1)}, f32[16,128]{1,0:T(8,128)S(1)}, f32[16,128]{1,0:T(8,128)S(1)}, bf16[4,128,256]{2,1,0:T(8,128)(2,1)S(1)}, bf16[4,256,2048]{2,1,0:T(8,128)(2,1)S(1)}) custom-call(s32[128]{0:T(128)S(1)} %copy-done.3, f32[16]{0:T(128)S(1)} %copy-done.4, bf16[16,64,128]{2,1,0:T(8,128)(2,1)S(1)} %copy-done.1, ...), custom_call_target="tpu_custom_call" | custom-call | tf_op jit(solution)/shard_map/index_forward/pallas_call | solution.py:98
  17.5 2.7 %collective-permute-start.1 = (f32[24,256]{1,0:T(8,128)S(1)}, f32[24,256]{1,0:T(8,128)S(1)}, u32[]{:S(2)}, u32[]{:S(2)}) collective-permute-start(f32[24,256]{1,0:T(8,128)S(1)} %join_first.1.left_ref), channel_id=1, source_target_pairs={{0,2},{1,3},{2,0},{3,1},{4,6},{5,7},{6,4},{7,5},{8,10},{9,11},{10,... | collective-permute-start | bytes 73736 | tf_op jit(solution)/shard_map/ppermute | solution.py:432
  20.1 2.1 %collective-permute-done.1.right_ref = f32[24,256]{1,0:T(8,128)S(1)} collective-permute-done((f32[24,256]{1,0:T(8,128)S(1)}, f32[24,256]{1,0:T(8,128)S(1)}, u32[]{:S(2)}, u32[]{:S(2)}) %collective-permute-start.1) | collective-permute-done | bytes 24608 | tf_op jit(solution)/shard_map/ppermute | solution.py:432
  22.3 1.4 %head_sum.1 = (f32[4,16,2048]{2,1,0:T(8,128)S(1)}, f32[4,16,2048]{2,1,0:T(8,128)S(1)}) custom-call(f32[8,2048,256]{2,1,0:T(8,128)S(1)} %get-tuple-element.40.prob_ref, f32[8,16,256]{2,1,0:T(8,128)S(1)} %get-tuple-element.41.top_ref, f32[8,256]{1,0:T(8,128)S(1)} %get-tuple-element.42.stat_ref), custom_call_target="tpu_custom_call" | custom-call | flops 1000000000 | tf_op jit(solution)/shard_map/head_sum/pallas_call | solution.py:41
  23.8 1.9 %collective-permute-done.3.right_ref = f32[4,16,2048]{2,1,0:T(8,128)S(1)} collective-permute-done((f32[4,16,2048]{2,1,0:T(8,128)S(1)}, f32[4,16,2048]{2,1,0:T(8,128)S(1)}, u32[]{:S(2)}, u32[]{:S(2)}) %collective-permute-start.3) | collective-permute-done | bytes 524320 | tf_op jit(solution)/shard_map/ppermute | solution.py:435
  25.7 2.5 %collective-permute-start.4 = (f32[16,2048]{1,0:T(8,128)S(1)}, f32[16,2048]{1,0:T(8,128)S(1)}, u32[]{:S(2)}, u32[]{:S(2)}) collective-permute-start(f32[16,2048]{1,0:T(8,128)S(1)} %get-tuple-element.50), channel_id=1, source_target_pairs={{0,24},{4,28},{8,16},{12,20},{16,8},{20,12},{24,0},{28,4},{1,25},{... | collective-permute-start | bytes 393224 | tf_op jit(solution)/shard_map/ppermute | solution.py:435
  28.2 0.5 collective-permute-start.5
  28.7 0.5 collective-permute-start.6
  29.3 0.8 %collective-permute-start.2 = (f32[16,128]{1,0:T(8,128)S(1)}, f32[16,128]{1,0:T(8,128)S(1)}, u32[]{:S(2)}, u32[]{:S(2)}) collective-permute-start(f32[16,128]{1,0:T(8,128)S(1)} %get-tuple-element.44.lse_ref), channel_id=1, source_target_pairs={{0,1},{1,0},{2,3},{3,2},{4,5},{5,4},{6,7},{7,6},{8,9},{9,8},{10,11... | collective-permute-start | bytes 24584 | tf_op jit(solution)/shard_map/ppermute | solution.py:432
  30.1 2.8 %collective-permute-done.2.other_ref = f32[16,128]{1,0:T(8,128)S(1)} collective-permute-done((f32[16,128]{1,0:T(8,128)S(1)}, f32[16,128]{1,0:T(8,128)S(1)}, u32[]{:S(2)}, u32[]{:S(2)}) %collective-permute-start.2) | collective-permute-done | bytes 8224 | tf_op jit(solution)/shard_map/ppermute | solution.py:432
  32.9 2.1 %collective-permute-done.5.refs_2_ = f32[16,2048]{1,0:T(8,128)S(1)} collective-permute-done((f32[16,2048]{1,0:T(8,128)S(1)}, f32[16,2048]{1,0:T(8,128)S(1)}, u32[]{:S(2)}, u32[]{:S(2)}) %collective-permute-start.5) | collective-permute-done | bytes 131104 | tf_op jit(solution)/shard_map/ppermute | solution.py:435
  35.1 2.5 %gradients.1 = (f32[264,128]{1,0:T(8,128)S(1)}, f32[264,128]{1,0:T(8,128)S(1)}, f32[264,128]{1,0:T(8,128)S(1)}, f32[264,128]{1,0:T(8,128)S(1)}, f32[4,256,128]{2,1,0:T(8,128)S(1)}, /*index=5*/f32[4,256,128]{2,1,0:T(8,128)S(1)}) custom-call(f32[16,2048]{1,0:T(8,128)S(1)} %get-tuple-element.36.score_ref, f32[16,128]{1,0:T(8,128)S(1)} %get-tuple-element.37.kl_ref, ...), custom_call_target="tpu_custom_call" | custom-call | tf_op jit(solution)/shard_map/gradients/pallas_call | solution.py:41
  37.7 2.9 %collective-permute-start.7 = (f32[264,128]{1,0:T(8,128)S(1)}, f32[264,128]{1,0:T(8,128)S(1)}, u32[]{:S(2)}, u32[]{:S(2)}) collective-permute-start(f32[264,128]{1,0:T(8,128)S(1)} %get-tuple-element.53), channel_id=1, source_target_pairs={{0,3},{1,2},{2,1},{3,0},{4,7},{5,6},{6,5},{7,4},{8,11},{9,10},{10,... | collective-permute-start | bytes 405512 | tf_op jit(solution)/shard_map/ppermute | solution.py:432
  40.5 1.6 %collective-permute-start.9 = (f32[264,128]{1,0:T(8,128)S(1)}, f32[264,128]{1,0:T(8,128)S(1)}, u32[]{:S(2)}, u32[]{:S(2)}) collective-permute-start(f32[264,128]{1,0:T(8,128)S(1)} %get-tuple-element.55), channel_id=1, source_target_pairs={{0,1},{1,0},{2,3},{3,2},{4,5},{5,4},{6,7},{7,6},{8,9},{9,8},{10,11... | collective-permute-start | bytes 405512 | tf_op jit(solution)/shard_map/ppermute | solution.py:432
  42.2 1.7 %collective-permute-start.14 = (f32[256,128]{1,0:T(8,128)S(1)}, f32[256,128]{1,0:T(8,128)S(1)}, u32[]{:S(2)}, u32[]{:S(2)}) collective-permute-start(f32[256,128]{1,0:T(8,128)S(1)} %get-tuple-element.63), channel_id=1, source_target_pairs={{0,24},{4,28},{8,16},{12,20},{16,8},{20,12},{24,0},{28,4},{1,25},{... | collective-permute-start | bytes 393224 | tf_op jit(solution)/shard_map/ppermute | solution.py:435
  43.9 1.3 %collective-permute-start.15 = (f32[256,128]{1,0:T(8,128)S(1)}, f32[256,128]{1,0:T(8,128)S(1)}, u32[]{:S(2)}, u32[]{:S(2)}) collective-permute-start(f32[256,128]{1,0:T(8,128)S(1)} %get-tuple-element.64), channel_id=1, source_target_pairs={{0,16},{4,20},{8,24},{12,28},{16,0},{20,4},{24,8},{28,12},{1,17},{... | collective-permute-start | bytes 393224 | tf_op jit(solution)/shard_map/ppermute | solution.py:435
  45.2 0.8 %collective-permute-done.7.refs_0_ = f32[264,128]{1,0:T(8,128)S(1)} collective-permute-done((f32[264,128]{1,0:T(8,128)S(1)}, f32[264,128]{1,0:T(8,128)S(1)}, u32[]{:S(2)}, u32[]{:S(2)}) %collective-permute-start.7) | collective-permute-done | bytes 135200 | tf_op jit(solution)/shard_map/ppermute | solution.py:432
  46.0 1.5 %collective-permute-start.16 = (f32[256,128]{1,0:T(8,128)S(1)}, f32[256,128]{1,0:T(8,128)S(1)}, u32[]{:S(2)}, u32[]{:S(2)}) collective-permute-start(f32[256,128]{1,0:T(8,128)S(1)} %get-tuple-element.65), channel_id=1, source_target_pairs={{0,8},{4,12},{8,0},{12,4},{16,24},{20,28},{24,16},{28,20},{1,9},{5... | collective-permute-start | bytes 393224 | tf_op jit(solution)/shard_map/ppermute | solution.py:435
  47.6 5.6 %collective-permute-done.8.refs_1_ = f32[264,128]{1,0:T(8,128)S(1)} collective-permute-done((f32[264,128]{1,0:T(8,128)S(1)}, f32[264,128]{1,0:T(8,128)S(1)}, u32[]{:S(2)}, u32[]{:S(2)}) %collective-permute-start.8) | collective-permute-done | bytes 135200 | tf_op jit(solution)/shard_map/ppermute | solution.py:432
  53.6 1.6 %collective-permute-start.17 = (f32[256,128]{1,0:T(8,128)S(1)}, f32[256,128]{1,0:T(8,128)S(1)}, u32[]{:S(2)}, u32[]{:S(2)}) collective-permute-start(f32[256,128]{1,0:T(8,128)S(1)} %add_all.1.refs_0_), channel_id=1, source_target_pairs={{0,8},{4,12},{8,0},{12,4},{16,24},{20,28},{24,16},{28,20},{1,9},{5... | collective-permute-start | bytes 393224 | tf_op jit(solution)/shard_map/ppermute | solution.py:435
  55.2 2.7 %collective-permute-start.13 = (f32[264,128]{1,0:T(8,128)S(1)}, f32[264,128]{1,0:T(8,128)S(1)}, u32[]{:S(2)}, u32[]{:S(2)}) collective-permute-start(f32[264,128]{1,0:T(8,128)S(1)} %own_rows.1.refs_0_), channel_id=1, source_target_pairs={{0,3},{1,2},{2,1},{3,0},{4,7},{5,6},{6,5},{7,4},{8,11},{9,10},{10,... | collective-permute-start | bytes 405512 | tf_op jit(solution)/shard_map/ppermute | solution.py:432
  57.8 1.3 %collective-permute-start.12 = (f32[264,128]{1,0:T(8,128)S(1)}, f32[264,128]{1,0:T(8,128)S(1)}, u32[]{:S(2)}, u32[]{:S(2)}) collective-permute-start(f32[264,128]{1,0:T(8,128)S(1)} %own_rows.1.refs_0_), channel_id=1, source_target_pairs={{0,2},{1,3},{2,0},{3,1},{4,6},{5,7},{6,4},{7,5},{8,10},{9,11},{10,... | collective-permute-start | bytes 405512 | tf_op jit(solution)/shard_map/ppermute | solution.py:432
  59.2 0.5 collective-permute-start.11
  59.6 0.7 %collective-permute-start.18 = (f32[256,128]{1,0:T(8,128)S(1)}, f32[256,128]{1,0:T(8,128)S(1)}, u32[]{:S(2)}, u32[]{:S(2)}) collective-permute-start(f32[256,128]{1,0:T(8,128)S(1)} %add_all.1.refs_0_), channel_id=1, source_target_pairs={{0,16},{4,20},{8,24},{12,28},{16,0},{20,4},{24,8},{28,12},{1,17},{... | collective-permute-start | bytes 393224 | tf_op jit(solution)/shard_map/ppermute | solution.py:435
  60.4 1.3 %collective-permute-start.19 = (f32[256,128]{1,0:T(8,128)S(1)}, f32[256,128]{1,0:T(8,128)S(1)}, u32[]{:S(2)}, u32[]{:S(2)}) collective-permute-start(f32[256,128]{1,0:T(8,128)S(1)} %collective-permute-done.17.refs_1_), channel_id=1, source_target_pairs={{0,16},{4,20},{8,24},{12,28},{16,0},{20,4},{24,8},{28,12},{1,17},{... | collective-permute-start | bytes 393224 | tf_op jit(solution)/shard_map/ppermute | solution.py:435
  61.7 3.4 %collective-permute-done.18.refs_2_ = f32[256,128]{1,0:T(8,128)S(1)} collective-permute-done((f32[256,128]{1,0:T(8,128)S(1)}, f32[256,128]{1,0:T(8,128)S(1)}, u32[]{:S(2)}, u32[]{:S(2)}) %collective-permute-start.18) | collective-permute-done | bytes 131104 | tf_op jit(solution)/shard_map/ppermute | solution.py:435
  65.1 1.4 %collective-permute-done.19.refs_3_ = f32[256,128]{1,0:T(8,128)S(1)} collective-permute-done((f32[256,128]{1,0:T(8,128)S(1)}, f32[256,128]{1,0:T(8,128)S(1)}, u32[]{:S(2)}, u32[]{:S(2)}) %collective-permute-start.19) | collective-permute-done | bytes 131104 | tf_op jit(solution)/shard_map/ppermute | solution.py:435
  66.6 2.8 %collective-permute-done.12.refs_2_ = f32[264,128]{1,0:T(8,128)S(1)} collective-permute-done((f32[264,128]{1,0:T(8,128)S(1)}, f32[264,128]{1,0:T(8,128)S(1)}, u32[]{:S(2)}, u32[]{:S(2)}) %collective-permute-start.12) | collective-permute-done | bytes 135200 | tf_op jit(solution)/shard_map/ppermute | solution.py:432
  69.5 0.8 %place_query.1 = (f32[1024,128]{1,0:T(8,128)}, f32[16,64]{1,0:T(8,128)}) custom-call(f32[264,128]{1,0:T(8,128)S(1)} %own_rows.1.refs_0_, f32[264,128]{1,0:T(8,128)S(1)} %collective-permute-done.11.refs_1_, f32[264,128]{1,0:T(8,128)S(1)} %collective-permute-done.12.refs_2_, f32[264,128]{1,0:T(8,128)S(1)} %collective-permute-done.13.refs_3_), custom_call_target="tpu_custom_call" | custom-call | flops 40000000000 | tf_op jit(solution)/shard_map/place_query/pallas_call | solution.py:41
  70.3 1.0 %place_keys.1 = f32[2048,128]{1,0:T(8,128)} custom-call(f32[4,256,128]{2,1,0:T(8,128)S(1)} %stack_all.1.mine_ref, f32[4,256,128]{2,1,0:T(8,128)S(1)} %collective-permute-done.20.other_ref), custom_call_target="tpu_custom_call" | custom-call | tf_op jit(solution)/shard_map/place_keys/pallas_call | solution.py:41
  (33 shorter events, 0.9 us)
Async XLA Ops:
  0.6 13.9 %copy-start.3 = (s32[128]{0:T(128)S(1)}, s32[128]{0:T(128)}, u32[]{:S(2)}) copy-start(s32[128]{0:T(128)} %pos_ref.1) | copy-start | bytes 1540
  0.6 13.9 %copy-start.2 = (f32[16,64]{1,0:T(8,128)S(1)}, f32[16,64]{1,0:T(8,128)}, u32[]{:S(2)}) copy-start(f32[16,64]{1,0:T(8,128)} %weight_ref.3) | copy-start | bytes 12292
  0.7 13.9 %copy-start = (bf16[2048,128]{1,0:T(8,128)(2,1)S(1)}, bf16[2048,128]{1,0:T(8,128)(2,1)}, u32[]{:S(2)}) copy-start(bf16[2048,128]{1,0:T(8,128)(2,1)} %keys_ref.3) | copy-start | bytes 1572868
  0.7 13.9 %copy-start.1 = (bf16[16,64,128]{2,1,0:T(8,128)(2,1)S(1)}, bf16[16,64,128]{2,1,0:T(8,128)(2,1)}, u32[]{:S(2)}) copy-start(bf16[16,64,128]{2,1,0:T(8,128)(2,1)} %query_ref.3) | copy-start | bytes 786436
  0.7 13.9 %copy-start.4 = (f32[16]{0:T(128)S(1)}, f32[16]{0:T(128)}, u32[]{:S(2)}) copy-start(f32[16]{0:T(128)} %kl_ref.1) | copy-start | bytes 196
  11.5 5.9 %collective-permute-start = (f32[8,256]{1,0:T(8,128)S(1)}, f32[8,256]{1,0:T(8,128)S(1)}, u32[]{:S(2)}, u32[]{:S(2)}) collective-permute-start(f32[8,256]{1,0:T(8,128)S(1)} %get-tuple-element.35._.left_ref), channel_id=1, source_target_pairs={{0,1},{1,0},{2,3},{3,2},{4,5},{5,4},{6,7},{7,6},{8,9},{9,8},{10,11... | collective-permute-start | bytes 24584 | tf_op jit(solution)/shard_map/ppermute | solution.py:432
  17.5 4.8 %collective-permute-start.1 = (f32[24,256]{1,0:T(8,128)S(1)}, f32[24,256]{1,0:T(8,128)S(1)}, u32[]{:S(2)}, u32[]{:S(2)}) collective-permute-start(f32[24,256]{1,0:T(8,128)S(1)} %join_first.1.left_ref), channel_id=1, source_target_pairs={{0,2},{1,3},{2,0},{3,1},{4,6},{5,7},{6,4},{7,5},{8,10},{9,11},{10,... | collective-permute-start | bytes 73736 | tf_op jit(solution)/shard_map/ppermute | solution.py:432
  23.7 2.0 %collective-permute-start.3 = (f32[4,16,2048]{2,1,0:T(8,128)S(1)}, f32[4,16,2048]{2,1,0:T(8,128)S(1)}, u32[]{:S(2)}, u32[]{:S(2)}) collective-permute-start(f32[4,16,2048]{2,1,0:T(8,128)S(1)} %get-tuple-element.48), channel_id=1, source_target_pairs={{0,4},{4,0},{8,12},{12,8},{16,20},{20,16},{24,28},{28,24},{1,5},{5... | collective-permute-start | bytes 1572872 | tf_op jit(solution)/shard_map/ppermute | solution.py:435
  25.7 7.2 %collective-permute-start.4 = (f32[16,2048]{1,0:T(8,128)S(1)}, f32[16,2048]{1,0:T(8,128)S(1)}, u32[]{:S(2)}, u32[]{:S(2)}) collective-permute-start(f32[16,2048]{1,0:T(8,128)S(1)} %get-tuple-element.50), channel_id=1, source_target_pairs={{0,24},{4,28},{8,16},{12,20},{16,8},{20,12},{24,0},{28,4},{1,25},{... | collective-permute-start | bytes 393224 | tf_op jit(solution)/shard_map/ppermute | solution.py:435
  28.2 6.8 %collective-permute-start.5 = (f32[16,2048]{1,0:T(8,128)S(1)}, f32[16,2048]{1,0:T(8,128)S(1)}, u32[]{:S(2)}, u32[]{:S(2)}) collective-permute-start(f32[16,2048]{1,0:T(8,128)S(1)} %get-tuple-element.51), channel_id=1, source_target_pairs={{0,16},{4,20},{8,24},{12,28},{16,0},{20,4},{24,8},{28,12},{1,17},{... | collective-permute-start | bytes 393224 | tf_op jit(solution)/shard_map/ppermute | solution.py:435
  28.7 6.4 %collective-permute-start.6 = (f32[16,2048]{1,0:T(8,128)S(1)}, f32[16,2048]{1,0:T(8,128)S(1)}, u32[]{:S(2)}, u32[]{:S(2)}) collective-permute-start(f32[16,2048]{1,0:T(8,128)S(1)} %get-tuple-element.52), channel_id=1, source_target_pairs={{0,8},{4,12},{8,0},{12,4},{16,24},{20,28},{24,16},{28,20},{1,9},{5... | collective-permute-start | bytes 393224 | tf_op jit(solution)/shard_map/ppermute | solution.py:435
  29.3 3.7 %collective-permute-start.2 = (f32[16,128]{1,0:T(8,128)S(1)}, f32[16,128]{1,0:T(8,128)S(1)}, u32[]{:S(2)}, u32[]{:S(2)}) collective-permute-start(f32[16,128]{1,0:T(8,128)S(1)} %get-tuple-element.44.lse_ref), channel_id=1, source_target_pairs={{0,1},{1,0},{2,3},{3,2},{4,5},{5,4},{6,7},{7,6},{8,9},{9,8},{10,11... | collective-permute-start | bytes 24584 | tf_op jit(solution)/shard_map/ppermute | solution.py:432
  37.6 4.5 %collective-permute-start.10 = (f32[4,256,128]{2,1,0:T(8,128)S(1)}, f32[4,256,128]{2,1,0:T(8,128)S(1)}, u32[]{:S(2)}, u32[]{:S(2)}) collective-permute-start(f32[4,256,128]{2,1,0:T(8,128)S(1)} %get-tuple-element.58), channel_id=1, source_target_pairs={{0,4},{4,0},{8,12},{12,8},{16,20},{20,16},{24,28},{28,24},{1,5},{5... | collective-permute-start | bytes 1572872 | tf_op jit(solution)/shard_map/ppermute | solution.py:435
  37.7 8.4 %collective-permute-start.7 = (f32[264,128]{1,0:T(8,128)S(1)}, f32[264,128]{1,0:T(8,128)S(1)}, u32[]{:S(2)}, u32[]{:S(2)}) collective-permute-start(f32[264,128]{1,0:T(8,128)S(1)} %get-tuple-element.53), channel_id=1, source_target_pairs={{0,3},{1,2},{2,1},{3,0},{4,7},{5,6},{6,5},{7,4},{8,11},{9,10},{10,... | collective-permute-start | bytes 405512 | tf_op jit(solution)/shard_map/ppermute | solution.py:432
  40.5 12.7 %collective-permute-start.8 = (f32[264,128]{1,0:T(8,128)S(1)}, f32[264,128]{1,0:T(8,128)S(1)}, u32[]{:S(2)}, u32[]{:S(2)}) collective-permute-start(f32[264,128]{1,0:T(8,128)S(1)} %get-tuple-element.54), channel_id=1, source_target_pairs={{0,2},{1,3},{2,0},{3,1},{4,6},{5,7},{6,4},{7,5},{8,10},{9,11},{10,... | collective-permute-start | bytes 405512 | tf_op jit(solution)/shard_map/ppermute | solution.py:432
  40.5 12.7 %collective-permute-start.9 = (f32[264,128]{1,0:T(8,128)S(1)}, f32[264,128]{1,0:T(8,128)S(1)}, u32[]{:S(2)}, u32[]{:S(2)}) collective-permute-start(f32[264,128]{1,0:T(8,128)S(1)} %get-tuple-element.55), channel_id=1, source_target_pairs={{0,1},{1,0},{2,3},{3,2},{4,5},{5,4},{6,7},{7,6},{8,9},{9,8},{10,11... | collective-permute-start | bytes 405512 | tf_op jit(solution)/shard_map/ppermute | solution.py:432
  42.2 11.4 %collective-permute-start.14 = (f32[256,128]{1,0:T(8,128)S(1)}, f32[256,128]{1,0:T(8,128)S(1)}, u32[]{:S(2)}, u32[]{:S(2)}) collective-permute-start(f32[256,128]{1,0:T(8,128)S(1)} %get-tuple-element.63), channel_id=1, source_target_pairs={{0,24},{4,28},{8,16},{12,20},{16,8},{20,12},{24,0},{28,4},{1,25},{... | collective-permute-start | bytes 393224 | tf_op jit(solution)/shard_map/ppermute | solution.py:435
  43.9 9.6 %collective-permute-start.15 = (f32[256,128]{1,0:T(8,128)S(1)}, f32[256,128]{1,0:T(8,128)S(1)}, u32[]{:S(2)}, u32[]{:S(2)}) collective-permute-start(f32[256,128]{1,0:T(8,128)S(1)} %get-tuple-element.64), channel_id=1, source_target_pairs={{0,16},{4,20},{8,24},{12,28},{16,0},{20,4},{24,8},{28,12},{1,17},{... | collective-permute-start | bytes 393224 | tf_op jit(solution)/shard_map/ppermute | solution.py:435
  46.0 7.5 %collective-permute-start.16 = (f32[256,128]{1,0:T(8,128)S(1)}, f32[256,128]{1,0:T(8,128)S(1)}, u32[]{:S(2)}, u32[]{:S(2)}) collective-permute-start(f32[256,128]{1,0:T(8,128)S(1)} %get-tuple-element.65), channel_id=1, source_target_pairs={{0,8},{4,12},{8,0},{12,4},{16,24},{20,28},{24,16},{28,20},{1,9},{5... | collective-permute-start | bytes 393224 | tf_op jit(solution)/shard_map/ppermute | solution.py:435
  53.6 6.8 %collective-permute-start.17 = (f32[256,128]{1,0:T(8,128)S(1)}, f32[256,128]{1,0:T(8,128)S(1)}, u32[]{:S(2)}, u32[]{:S(2)}) collective-permute-start(f32[256,128]{1,0:T(8,128)S(1)} %add_all.1.refs_0_), channel_id=1, source_target_pairs={{0,8},{4,12},{8,0},{12,4},{16,24},{20,28},{24,16},{28,20},{1,9},{5... | collective-permute-start | bytes 393224 | tf_op jit(solution)/shard_map/ppermute | solution.py:435
  55.2 11.5 %collective-permute-start.13 = (f32[264,128]{1,0:T(8,128)S(1)}, f32[264,128]{1,0:T(8,128)S(1)}, u32[]{:S(2)}, u32[]{:S(2)}) collective-permute-start(f32[264,128]{1,0:T(8,128)S(1)} %own_rows.1.refs_0_), channel_id=1, source_target_pairs={{0,3},{1,2},{2,1},{3,0},{4,7},{5,6},{6,5},{7,4},{8,11},{9,10},{10,... | collective-permute-start | bytes 405512 | tf_op jit(solution)/shard_map/ppermute | solution.py:432
  57.8 11.6 %collective-permute-start.12 = (f32[264,128]{1,0:T(8,128)S(1)}, f32[264,128]{1,0:T(8,128)S(1)}, u32[]{:S(2)}, u32[]{:S(2)}) collective-permute-start(f32[264,128]{1,0:T(8,128)S(1)} %own_rows.1.refs_0_), channel_id=1, source_target_pairs={{0,2},{1,3},{2,0},{3,1},{4,6},{5,7},{6,4},{7,5},{8,10},{9,11},{10,... | collective-permute-start | bytes 405512 | tf_op jit(solution)/shard_map/ppermute | solution.py:432
  59.2 10.3 %collective-permute-start.11 = (f32[264,128]{1,0:T(8,128)S(1)}, f32[264,128]{1,0:T(8,128)S(1)}, u32[]{:S(2)}, u32[]{:S(2)}) collective-permute-start(f32[264,128]{1,0:T(8,128)S(1)} %own_rows.1.refs_0_), channel_id=1, source_target_pairs={{0,1},{1,0},{2,3},{3,2},{4,5},{5,4},{6,7},{7,6},{8,9},{9,8},{10,11... | collective-permute-start | bytes 405512 | tf_op jit(solution)/shard_map/ppermute | solution.py:432
  59.6 5.5 %collective-permute-start.18 = (f32[256,128]{1,0:T(8,128)S(1)}, f32[256,128]{1,0:T(8,128)S(1)}, u32[]{:S(2)}, u32[]{:S(2)}) collective-permute-start(f32[256,128]{1,0:T(8,128)S(1)} %add_all.1.refs_0_), channel_id=1, source_target_pairs={{0,16},{4,20},{8,24},{12,28},{16,0},{20,4},{24,8},{28,12},{1,17},{... | collective-permute-start | bytes 393224 | tf_op jit(solution)/shard_map/ppermute | solution.py:435
  60.4 6.1 %collective-permute-start.19 = (f32[256,128]{1,0:T(8,128)S(1)}, f32[256,128]{1,0:T(8,128)S(1)}, u32[]{:S(2)}, u32[]{:S(2)}) collective-permute-start(f32[256,128]{1,0:T(8,128)S(1)} %collective-permute-done.17.refs_1_), channel_id=1, source_target_pairs={{0,16},{4,20},{8,24},{12,28},{16,0},{20,4},{24,8},{28,12},{1,17},{... | collective-permute-start | bytes 393224 | tf_op jit(solution)/shard_map/ppermute | solution.py:435
  66.6 3.8 %collective-permute-start.20 = (f32[4,256,128]{2,1,0:T(8,128)S(1)}, f32[4,256,128]{2,1,0:T(8,128)S(1)}, u32[]{:S(2)}, u32[]{:S(2)}) collective-permute-start(f32[4,256,128]{2,1,0:T(8,128)S(1)} %stack_all.1.mine_ref), channel_id=1, source_target_pairs={{0,4},{4,0},{8,12},{12,8},{16,20},{20,16},{24,28},{28,24},{1,5},{5... | collective-permute-start | bytes 1572872 | tf_op jit(solution)/shard_map/ppermute | solution.py:435

commit v5 on v4

--- a/solution.py
+++ b/solution.py
@@ -63,27 +63,30 @@
     return at // 2, at % 2
 
 
-def index_forward(query_pos, kl, index_query, index_keys, index_weight, groups, after):
+def weighted_columns(query_ref, columns, rows, heads):
+    for row in range(rows):
+        piece = query_ref[row * heads : (row + 1) * heads, :].astype(F32) * columns[:, row : row + 1]
+        yield row, piece.T.astype(BF16)
+
+
+def index_forward(query_pos, index_query, index_keys, index_weight, after):
     rows, heads, width = index_query.shape
     keys = index_keys.shape[0]
     tile = tile_of(keys, 256)
-    own = rows // groups
-
-    def body(pos_ref, kl_ref, query_ref, keys_ref, weight_ref, _, score_ref, lse_ref, kl_out, wiq_ref, gate_ref):
+
+    def body(pos_ref, query_ref, keys_ref, weight_ref, _, score_ref, lse_ref, pack_ref):
         columns = weight_ref[...].T
         flat = query_ref[...].reshape(rows * heads, width)
-        for row in range(rows):
-            kl_out[row : row + 1, :] = jnp.full((1, 128), kl_ref[row], F32)
-            piece = query_ref[row].astype(F32) * columns[:, row : row + 1]
-            wiq_ref[row // own, :, (row % own) * heads : (row % own + 1) * heads] = piece.T.astype(BF16)
+        pack_ref[: rows * heads, :] = flat.astype(F32)
+        pack_ref[rows * heads :, :] = jnp.concatenate(
+            [weight_ref[...], jnp.zeros((rows, width - heads), F32)], axis=1
+        )
         first_key = lax.axis_index("keys") * keys
         first_row = lax.axis_index("heads") * rows
         for at in range(0, keys, tile):
             logits = lax.dot_general(
                 flat, keys_ref[at : at + tile, :], (((1,), (1,)), ((), ())), preferred_element_type=F32
             )
-            for g in range(groups):
-                gate_ref[g, :, at : at + tile] = logits[g * own * heads : (g + 1) * own * heads, :].astype(BF16)
             index = first_key + at + lax.broadcasted_iota(jnp.int32, (1, tile), 1)
             for row in range(rows):
                 active = jnp.maximum(logits[row * heads : (row + 1) * heads, :], 0.0)
@@ -95,21 +98,64 @@
         total = jnp.sum(jnp.exp2(scores - top), axis=1, keepdims=True)
         lse_ref[...] = jnp.broadcast_to(top + jnp.log2(total), lse_ref.shape)
 
-    return pl.pallas_call(
-        body,
-        out_shape=(
-            pltpu.VMEM((rows, keys), F32),
-            pltpu.VMEM((rows, 128), F32),
-            pltpu.VMEM((rows, 128), F32),
-            pltpu.VMEM((groups, width, own * heads), BF16),
-            pltpu.VMEM((groups, own * heads, keys), BF16),
-        ),
-        in_specs=[smem_spec] * 2 + [vmem_spec] * 4,
-        out_specs=(vmem_spec,) * 5,
-        compiler_params=pltpu.CompilerParams(vmem_limit_bytes=16 * MIB),
-        cost_estimate=pl.CostEstimate(flops=0, bytes_accessed=0, transcendentals=0),
-        name="index_forward",
-    )(query_pos, kl, *[in_vmem(a) for a in (index_query, index_keys, index_weight, after)])
+    outs = (
+        pltpu.VMEM((rows, keys), F32),
+        pltpu.VMEM((rows, 128), F32),
+        pltpu.VMEM((rows * heads + rows, width), F32),
+    )
+    operands = (index_query, index_keys, index_weight, after)
+    return vmem_call(body, "index_forward", outs, operands, scalars=(query_pos,), limit=16 * MIB)
+
+
+def index_signs(kl, index_query, index_keys, index_weight, groups):
+    rows, heads, width = index_query.shape
+    keys = index_keys.shape[0]
+    tile = tile_of(keys, 256)
+    own = rows // groups
+    size = own * heads
+
+    def body(kl_ref, query_ref, keys_ref, weight_ref, gate_ref, wiq_ref, kl_out):
+        for row in range(rows):
+            kl_out[row : row + 1, :] = jnp.full((1, 128), kl_ref[row], F32)
+        flat = query_ref[...].reshape(rows * heads, width)
+        for row, piece in weighted_columns(flat, weight_ref[...].T, rows, heads):
+            wiq_ref[row // own, :, (row % own) * heads : (row % own + 1) * heads] = piece
+        for at in range(0, keys, tile):
+            logits = lax.dot_general(
+                flat, keys_ref[at : at + tile, :], (((1,), (1,)), ((), ())), preferred_element_type=F32
+            )
+            for g in range(groups):
+                gate_ref[g, :, at : at + tile] = logits[g * size : (g + 1) * size, :].astype(BF16)
+
+    outs = (
+        pltpu.VMEM((groups, size, keys), BF16),
+        pltpu.VMEM((groups, width, size), BF16),
+        pltpu.VMEM((rows, 128), F32),
+    )
+    operands = (index_query, index_keys, index_weight)
+    return vmem_call(body, "index_signs", outs, operands, scalars=(kl,), limit=16 * MIB)
+
+
+def other_signs(pack, index_keys, rows):
+    keys, width = index_keys.shape
+    heads = pack.shape[0] // rows - 1
+    half = keys // 2
+    tile = tile_of(half, 256)
+
+    def body(pack_ref, keys_ref, gate_ref, wiq_ref):
+        flat = pack_ref[: rows * heads, :].astype(BF16)
+        columns = pack_ref[rows * heads :, :].T[:heads, :]
+        for row, piece in weighted_columns(flat, columns, rows, heads):
+            wiq_ref[:, row * heads : (row + 1) * heads] = piece
+        _, core = head_place()
+        for at in range(0, half, tile):
+            span = pl.ds(pl.multiple_of(core * half + at, tile), tile)
+            gate_ref[:, at : at + tile] = lax.dot_general(
+                flat, keys_ref[span, :], (((1,), (1,)), ((), ())), preferred_element_type=F32
+            ).astype(BF16)
+
+    outs = (pltpu.VMEM((rows * heads, half), BF16), pltpu.VMEM((width, rows * heads), BF16))
+    return vmem_call(body, "other_signs", outs, (pack, index_keys), limit=16 * MIB)
 
 
 def main_scores(pos, query_t, keys_t):
@@ -285,18 +331,17 @@
     return vmem_call(body, "join_pair", pltpu.VMEM(left.shape, F32), (left, right))
 
 
-def gradients(scores, index_stats, targets, kl, gate, index_keys, wiq, head_devices):
+def query_part(scores, index_stats, targets, kl, gate, index_keys):
     rows, keys = scores.shape
     groups, size = gate.shape[:2]
     own = rows // groups
     heads = size // own
     width = index_keys.shape[1]
-    chips = head_devices // 2
-    chunk = keys // head_devices
-
-    def body(score_ref, kl_ref, lse_ref, other_ref, gate_ref, keys_ref, wiq_ref, *refs):
+    half = keys // 2
+
+    def body(score_ref, kl_ref, lse_ref, other_ref, gate_ref, keys_ref, *refs):
         target_refs, refs = refs[: len(targets)], refs[len(targets) :]
-        query_outs, (keep_ref, send_ref, delta_ref, slope_ref, wiq_rows) = refs[:groups], refs[groups:]
+        keep_ref, send_ref, slope_ref, across_ref, delta_ref = refs
         whole = joined([lse_ref[:, :1], other_ref[:, :1]])
         target = target_refs[0][...]
         for ref in target_refs[1:]:
@@ -305,7 +350,8 @@
         for g in range(groups):
             delta_ref[g] = delta[g * own : (g + 1) * own, :]
         z = lax.axis_index("keys")
-        chip, core = head_place()
+        _, core = head_place()
+        across_ref[...] = jnp.where(core == 0, delta[:, half:], delta[:, :half])
         for r in range(groups):
             lines = delta_ref[z ^ r]
             for i in range(own):
@@ -313,72 +359,100 @@
                 signs = gate_ref[z ^ r, i * heads : (i + 1) * heads, :]
                 at = r * size + i * heads
                 slope_ref[at : at + heads, :] = jnp.where(signs > 0, line, jnp.zeros((), BF16))
-            wiq_rows[:, r * size : (r + 1) * size] = wiq_ref[z ^ r]
         part = jnp.dot(slope_ref[...], keys_ref[...], preferred_element_type=F32)
         for r in range(groups):
-            query_outs[r][:size, :] = part[r * size : (r + 1) * size, :]
-            query_outs[r][size:, :] = jnp.zeros((8, width), F32)
-        for out_ref, side in ((send_ref, 1 - core), (keep_ref, core)):
-            for n in range(chips):
-                span = pl.ds(pl.multiple_of(((chip ^ n) * 2 + side) * chunk, chunk), chunk)
-                out_ref[n] = jnp.dot(wiq_rows[...], slope_ref[:, span], preferred_element_type=F32).T
-
-    half = pltpu.VMEM((chips, chunk, width), F32)
-    outs = tuple(pltpu.VMEM((size + 8, width), F32) for _ in range(groups)) + (half, half)
-    scratch = [
-        pltpu.VMEM((groups, own, keys), F32),
-        pltpu.VMEM((rows * heads, keys), BF16),
-        pltpu.VMEM((width, rows * heads), BF16),
-    ]
-    operands = (scores, kl, *index_stats, gate, index_keys, wiq, *targets)
-    return vmem_call(body, "gradients", outs, operands, scratch, limit=16 * MIB, cost=SHORT)
-
-
-def own_rows(parts, index_query, index_weight):
+            out_ref = send_ref if r % 2 else keep_ref
+            out_ref[r // 2] = part[r * size : (r + 1) * size, :]
+
+    side = pltpu.VMEM((groups // 2, size, width), F32)
+    outs = (side, side, pltpu.VMEM((rows * heads, keys), BF16), pltpu.VMEM((rows, half), F32))
+    scratch = [pltpu.VMEM((groups, own, keys), F32)]
+    operands = (scores, kl, *index_stats, gate, index_keys, *targets)
+    return vmem_call(body, "query_part", outs, operands, scratch, limit=16 * MIB)
+
+
+def key_part(slopes, wiq, other_delta, other_gate, other_wiq, chips):
+    groups, width, size = wiq.shape
+    rows, half = other_delta.shape
+    count = other_gate.shape[0]
+    heads = count // rows
+    chunk = half // chips
+
+    def body(slope_ref, wiq_ref, delta_ref, gate_ref, other_ref, *refs):
+        outs, (wiq_rows, other_slopes) = refs[:chips], refs[chips:]
+        z = lax.axis_index("keys")
+        for r in range(groups):
+            wiq_rows[:, r * size : (r + 1) * size] = wiq_ref[z ^ r]
+        for row in range(rows):
+            span = slice(row * heads, (row + 1) * heads)
+            line = jnp.broadcast_to(delta_ref[row : row + 1, :], (heads, half)).astype(BF16)
+            other_slopes[span, :] = jnp.where(gate_ref[span, :] > 0, line, jnp.zeros((), BF16))
+        chip, core = head_place()
+        for n, out_ref in enumerate(outs):
+            at = pl.multiple_of((chip ^ n) * chunk, chunk)
+            here = pl.ds(pl.multiple_of(core * half + at, chunk), chunk)
+            total = jnp.dot(wiq_rows[...], slope_ref[:, here], preferred_element_type=F32)
+            total += jnp.dot(other_ref[...], other_slopes[:, pl.ds(at, chunk)], preferred_element_type=F32)
+            out_ref[...] = total.T
+
+    outs = tuple(pltpu.VMEM((chunk, width), F32) for _ in range(chips))
+    scratch = [pltpu.VMEM((width, count), BF16), pltpu.VMEM((count, half), BF16)]
+    operands = (slopes, wiq, other_delta, other_gate, other_wiq)
+    return vmem_call(body, "key_part", outs, operands, scratch, limit=16 * MIB)
+
+
+def add_halve(left, right):
+    count = left.shape[0]
+
+    def body(left_ref, right_ref, even_ref, odd_ref):
+        for n in range(count):
+            (odd_ref if n % 2 else even_ref)[n // 2] = left_ref[n] + right_ref[n]
+
+    side = pltpu.VMEM((count // 2, *left.shape[1:]), F32)
+    return vmem_call(body, "add_halve", (side, side), (left, right))
+
+
+def own_rows(left, right, index_query, index_weight):
     rows, heads, width = index_query.shape
-    size = parts[0].shape[0] - 8
+    size = left.shape[1]
     own = size // heads
     extra = -(-own // 8) * 8
 
-    def body(query_ref, weight_ref, *refs):
+    def body(query_ref, weight_ref, left_ref, right_ref, out_ref):
         first = lax.axis_index("keys") * own
-        part_refs, out_ref = refs[:-1], refs[-1]
         columns = weight_ref[...].T
         lane = lax.broadcasted_iota(jnp.int32, (heads, rows), 1)
         for i in range(own):
             span = slice(i * heads, (i + 1) * heads)
-            total = part_refs[0][span, :]
-            for ref in part_refs[1:]:
-                total = total + ref[span, :]
+            total = left_ref[0, span, :] + right_ref[0, span, :]
             column = jnp.sum(jnp.where(lane == first + i, columns, 0.0), axis=1, keepdims=True)
             out_ref[span, :] = total * column
             summed = jnp.sum(total * query_ref[first + i].astype(F32), axis=1, keepdims=True)
-            line = summed.T
             out_ref[size + i : size + i + 1, :] = jnp.concatenate(
-                [line, jnp.zeros((1, width - heads), F32)], axis=1
+                [summed.T, jnp.zeros((1, width - heads), F32)], axis=1
             )
         if extra > own:
             out_ref[size + own :, :] = jnp.zeros((extra - own, width), F32)
 
-    return vmem_call(
-        body, "own_rows", pltpu.VMEM((size + extra, width), F32), (index_query, index_weight, *parts), cost=LONG
-    )
+    out = pltpu.VMEM((size + extra, width), F32)
+    return vmem_call(body, "own_rows", out, (index_query, index_weight, left, right), cost=LONG)
 
 
 def place_query(pieces, rows, heads):
     own = rows // len(pieces)
     size = own * heads
     width = pieces[0].shape[1]
+    order = list(pieces)
 
     def body(*refs):
         piece_refs, (query_out, weight_out, weights, sems) = refs[: len(pieces)], refs[len(pieces) :]
         z = lax.axis_index("keys")
         copies = []
-        for r, ref in enumerate(piece_refs):
+        for r, ref in zip(order, piece_refs):
             at = pl.multiple_of((z ^ r) * size, size)
             copies.append(pltpu.make_async_copy(ref.at[:size], query_out.at[pl.ds(at, size)], sems.at[r]))
             copies[-1].start()
-        for r, ref in enumerate(piece_refs):
+        for r, ref in zip(order, piece_refs):
             weights[pl.ds((z ^ r) * own, own), :] = ref[size : size + own, :heads]
         copies.append(pltpu.make_async_copy(weights, weight_out, sems.at[len(pieces)]))
         copies[-1].start()
@@ -389,7 +463,7 @@
         body,
         "place_query",
         (jax.ShapeDtypeStruct((rows * heads, width), F32), jax.ShapeDtypeStruct((rows, heads), F32)),
-        pieces,
+        list(pieces.values()),
         [pltpu.VMEM((rows, heads), F32), pltpu.SemaphoreType.DMA((len(pieces) + 1,))],
         out_specs=(any_spec, any_spec),
         cost=LONG,
@@ -405,7 +479,7 @@
         copies = []
         for n, (ref, side) in enumerate(((mine_ref, core), (other_ref, 1 - core))):
             for r in range(chips):
-                at = pl.multiple_of(((chip ^ r) * 2 + side) * chunk, chunk)
+                at = pl.multiple_of(side * (chips * chunk) + (chip ^ r) * chunk, chunk)
                 copies.append(pltpu.make_async_copy(ref.at[r], out_ref.at[pl.ds(at, chunk)], sems.at[n, r]))
                 copies[-1].start()
         for copy in copies:
@@ -434,13 +508,11 @@
     def to_heads(value, bits):
         return lax.ppermute(value, "heads", [(i, i ^ bits) for i in range(head_devices)])
 
-    far_first = list(reversed(range(1, key_devices)))
-    chips_far_first = list(reversed(range(1, chips)))
+    chip_order = list(reversed(range(1, chips)))
+    key_order = [key_devices - 1] + list(range(1, key_devices - 1))
 
     probs, tops, stat = main_scores(query_pos[None, :], main_query.transpose(1, 2, 0), latent_keys.T)
-    scores, index_lse, kl, wiq, gate = index_forward(
-        query_pos, kl_weight, index_query, index_keys, index_weight, key_devices, stat
-    )
+    scores, index_lse, pack = index_forward(query_pos, index_query, index_keys, index_weight, stat)
     blocks = stat.shape[0]
     both = join_first(stat, to_keys(stat, 1), index_lse)
     bits = 2
@@ -449,20 +521,25 @@
         bits *= 2
     stat, index_lse = join_more(both, to_keys(both, bits), blocks)
     keep, send = head_sum(probs, tops, stat, queries, row_local)
-    index_lse, send = lax.optimization_barrier((index_lse, send))
+    index_lse, send, index_query, pack = lax.optimization_barrier((index_lse, send, index_query, pack))
     sums = add_stacks(keep, to_heads(send, 1))
-    targets = [sums[0]] + [to_heads(sums[r], 2 * r) for r in chips_far_first]
+    targets = [sums[0]] + [to_heads(sums[r], 2 * r) for r in chip_order]
+    gate, wiq, kl = index_signs(kl_weight, index_query, index_keys, index_weight, key_devices)
+    other_gate, other_wiq = other_signs(to_heads(pack, 1), index_keys, row_local)
     index_stats = (index_lse, to_keys(index_lse, 1))
-    *parts, keep, send = gradients(
-        scores, index_stats, targets, kl, gate, index_keys, wiq, head_devices
-    )
-    arrived = [to_keys(parts[r], r) for r in far_first] + [parts[0]]
-    query_own = own_rows(arrived, index_query, index_weight)
-    sums = add_stacks(keep, to_heads(send, 1))
-    key_parts = [sums[0]] + [to_heads(sums[r], 2 * r) for r in chips_far_first]
-    query_own, key_parts[0] = lax.optimization_barrier((query_own, key_parts[0]))
-    key_own = add_all(key_parts)
-    pieces = [query_own] + [to_keys(query_own, r) for r in range(1, key_devices)]
+    other_gate, gate = lax.optimization_barrier((other_gate, gate))
+    even, odd, slopes, across = query_part(scores, index_stats, targets, kl, gate, index_keys)
+
+    bits, other_odd = 1, to_keys(odd, 1)
+    parts = key_part(slopes, wiq, to_heads(across, 1), other_gate, other_wiq, chips)
+    key_own = add_all([parts[0]] + [to_heads(parts[r], 2 * r) for r in chip_order])
+    while bits < key_devices // 2:
+        even, odd = add_halve(even, other_odd)
+        bits *= 2
+        other_odd = to_keys(odd, bits)
+    even, key_own = lax.optimization_barrier((even, key_own))
+    query_own = own_rows(even, other_odd, index_query, index_weight)
+    pieces = {0: query_own, **{r: to_keys(query_own, r) for r in key_order}}
     mine, bits = [key_own], 2
     while bits < head_devices:
         mine = mine + [to_heads(piece, bits) for piece in mine]

time: 71.5 us -> 68.2 us (0.954)
  waiting for transfers between devices: 23.2 us -> 15.9 us
  Pallas kernels: 19.9 us -> 23.9 us
    ppermute x9 -> x8, waiting for transfers between devices: 14.2 us -> 5.8 us  [to_keys(): lax.ppermute(value, 'keys', [(i, i ^ bits) for i in range(key_devices)])]
    pallas_call x11 -> x15, Pallas kernels: 6.32 us -> 12.9 us  [vmem_call(): pl.pallas_call(body, out_shape=outs, in_specs=[smem_spec] * len(scalars)...]
    pallas_call x1 -> x0, Pallas kernels: 2.83 us -> none  [index_forward(): pl.pallas_call(body, out_shape=(pltpu.VMEM((rows, keys), F32), pltpu.VMEM...]
    ppermute x12 -> x13, waiting for transfers between devices: 8.94 us -> 10.1 us  [to_heads(): lax.ppermute(value, 'heads', [(i, i ^ bits) for i in range(head_devices)])]
    ppermute x12 -> x13, starting transfers between devices: 12 us -> 11.4 us  [to_heads(): lax.ppermute(value, 'heads', [(i, i ^ bits) for i in range(head_devices)])]
    ppermute x9 -> x8, starting transfers between devices: 15.5 us -> 15.9 us  [to_keys(): lax.ppermute(value, 'keys', [(i, i ^ bits) for i in range(key_devices)])]
  transfers between devices with their start and end apart: 21 -> 21, of which waited for: 10 -> 12; matrix products, arithmetic and copies ran while one was open for 0% -> 0% of each run, Pallas kernels for 6% -> 13%
where the time goes in v5:
time: 68.2 us; the launch traced here: 68.1 us
  starting transfers between devices  27.2 us (40%)
  Pallas kernels  23.9 us (35%)
  waiting for transfers between devices  15.9 us (23%)
  between operations  0.98 us (1%)
    ppermute x8, starting transfers between devices, to_keys(): lax.ppermute(value, 'keys', [(i, i ^ bits) for i in range(key_devices)])  15.9 us
    pallas_call x15, Pallas kernels, vmem_call(): pl.pallas_call(body, out_shape=outs, in_specs=[smem_spec] * len(scalars)...  12.9 us
    ppermute x13, starting transfers between devices, to_heads(): lax.ppermute(value, 'heads', [(i, i ^ bits) for i in range(head_devices)])  11.4 us
    pallas_call x1, Pallas kernels, main_scores(): pl.pallas_call(body, grid=(blocks // many,), out_shape=(pltpu.VMEM((block...  11 us
    ppermute x13, waiting for transfers between devices, to_heads(): lax.ppermute(value, 'heads', [(i, i ^ bits) for i in range(head_devices)])  10.1 us
    ppermute x8, waiting for transfers between devices, to_keys(): lax.ppermute(value, 'keys', [(i, i ^ bits) for i in range(key_devices)])  5.8 us
  transfers between devices with their start and end apart: 21, of which 12 were waited for; matrix products, arithmetic and copies ran while one was open for 0% of the time, Pallas kernels for 13%

profile of v5, /device:TPU:0, one launch (start us, length us, event | category | flops | bytes accessed | tf_op | source)
XLA Modules:
  0.0 68.1 jit_solution(16378153764758058619)
XLA Ops:
  0.7 11.0 %main_scores.1 = (f32[8,2048,256]{2,1,0:T(8,128)S(1)}, f32[8,16,256]{2,1,0:T(8,128)S(1)}, f32[8,256]{1,0:T(8,128)S(1)}) custom-call(s32[1,128]{1,0:T(1,128)} %bitcast.4, bf16[16,576,128]{2,1,0:T(8,128)(2,1)} %bitcast.5, bf16[576,2048]{1,0:T(8,128)(2,1)} %bitcast.6), custom_call_target="tpu_custom_call" | custom-call | tf_op jit(solution)/shard_map/main_scores/pallas_call | solution.py:216
  11.7 3.1 %collective-permute-start = (f32[8,256]{1,0:T(8,128)S(1)}, f32[8,256]{1,0:T(8,128)S(1)}, u32[]{:S(2)}, u32[]{:S(2)}) collective-permute-start(f32[8,256]{1,0:T(8,128)S(1)} %get-tuple-element.42._.left_ref), channel_id=1, source_target_pairs={{0,1},{1,0},{2,3},{3,2},{4,5},{5,4},{6,7},{7,6},{8,9},{9,8},{10,11... | collective-permute-start | bytes 24584 | tf_op jit(solution)/shard_map/ppermute | solution.py:506
  14.8 2.1 %index_forward.1 = (f32[16,2048]{1,0:T(8,128)S(1)}, f32[16,128]{1,0:T(8,128)S(1)}, f32[1040,128]{1,0:T(8,128)S(1)}) custom-call(s32[128]{0:T(128)S(1)} %copy-done.3, bf16[16,64,128]{2,1,0:T(8,128)(2,1)S(1)} %copy-done.1, bf16[2048,128]{1,0:T(8,128)(2,1)S(1)} %copy-done, f32[16,64]{1,0:T(8,128)S(1)} %copy-done.2, f32[8,256]{1,0:T(8,128)S(1)} %get-tuple-element.42._.left_ref), custom_call_target="tpu_custom_call" | custom-call | tf_op jit(solution)/shard_map/index_forward/pallas_call | solution.py:41
  16.9 2.7 %collective-permute-start.1 = (f32[24,256]{1,0:T(8,128)S(1)}, f32[24,256]{1,0:T(8,128)S(1)}, u32[]{:S(2)}, u32[]{:S(2)}) collective-permute-start(f32[24,256]{1,0:T(8,128)S(1)} %join_first.1.left_ref), channel_id=1, source_target_pairs={{0,2},{1,3},{2,0},{3,1},{4,6},{5,7},{6,4},{7,5},{8,10},{9,11},{10,... | collective-permute-start | bytes 73736 | tf_op jit(solution)/shard_map/ppermute | solution.py:506
  19.6 2.1 %collective-permute-done.1.right_ref = f32[24,256]{1,0:T(8,128)S(1)} collective-permute-done((f32[24,256]{1,0:T(8,128)S(1)}, f32[24,256]{1,0:T(8,128)S(1)}, u32[]{:S(2)}, u32[]{:S(2)}) %collective-permute-start.1) | collective-permute-done | bytes 24608 | tf_op jit(solution)/shard_map/ppermute | solution.py:506
  21.7 1.4 %head_sum.1 = (f32[4,16,2048]{2,1,0:T(8,128)S(1)}, f32[4,16,2048]{2,1,0:T(8,128)S(1)}) custom-call(f32[8,2048,256]{2,1,0:T(8,128)S(1)} %get-tuple-element.45.prob_ref, f32[8,16,256]{2,1,0:T(8,128)S(1)} %get-tuple-element.46.top_ref, f32[8,256]{1,0:T(8,128)S(1)} %get-tuple-element.47.stat_ref), custom_call_target="tpu_custom_call" | custom-call | flops 1000000000 | tf_op jit(solution)/shard_map/head_sum/pallas_call | solution.py:41
  23.7 1.4 %collective-permute-done.4.right_ref = f32[4,16,2048]{2,1,0:T(8,128)S(1)} collective-permute-done((f32[4,16,2048]{2,1,0:T(8,128)S(1)}, f32[4,16,2048]{2,1,0:T(8,128)S(1)}, u32[]{:S(2)}, u32[]{:S(2)}) %collective-permute-start.4) | collective-permute-done | bytes 524320 | tf_op jit(solution)/shard_map/ppermute | solution.py:509
  25.2 2.5 %collective-permute-start.5 = (f32[16,2048]{1,0:T(8,128)S(1)}, f32[16,2048]{1,0:T(8,128)S(1)}, u32[]{:S(2)}, u32[]{:S(2)}) collective-permute-start(f32[16,2048]{1,0:T(8,128)S(1)} %get-tuple-element.61), channel_id=1, source_target_pairs={{0,24},{4,28},{8,16},{12,20},{16,8},{20,12},{24,0},{28,4},{1,25},{... | collective-permute-start | bytes 393224 | tf_op jit(solution)/shard_map/ppermute | solution.py:509
  28.2 0.5 collective-permute-start.7
  28.7 1.5 %collective-permute-start.2 = (f32[16,128]{1,0:T(8,128)S(1)}, f32[16,128]{1,0:T(8,128)S(1)}, u32[]{:S(2)}, u32[]{:S(2)}) collective-permute-start(f32[16,128]{1,0:T(8,128)S(1)} %get-tuple-element.53.lse_ref), channel_id=1, source_target_pairs={{0,1},{1,0},{2,3},{3,2},{4,5},{5,4},{6,7},{7,6},{8,9},{9,8},{10,11... | collective-permute-start | bytes 24584 | tf_op jit(solution)/shard_map/ppermute | solution.py:506
  30.2 2.4 %index_signs.1 = (bf16[4,256,2048]{2,1,0:T(8,128)(2,1)S(1)}, bf16[4,128,256]{2,1,0:T(8,128)(2,1)S(1)}, f32[16,128]{1,0:T(8,128)S(1)}) custom-call(f32[16]{0:T(128)S(1)} %copy-done.4, bf16[16,64,128]{2,1,0:T(8,128)(2,1)S(1)} %copy-done.1, bf16[2048,128]{1,0:T(8,128)(2,1)S(1)} %copy-done, f32[16,64]{1,0:T(8,128)S(1)} %copy-done.2), custom_call_target="tpu_custom_call" | custom-call | tf_op jit(solution)/shard_map/index_signs/pallas_call | solution.py:41
  32.6 1.7 %other_signs.1 = (bf16[1024,1024]{1,0:T(8,128)(2,1)S(1)}, bf16[128,1024]{1,0:T(8,128)(2,1)S(1)}) custom-call(f32[1040,128]{1,0:T(8,128)S(1)} %collective-permute-done.3.pack_ref, bf16[2048,128]{1,0:T(8,128)(2,1)S(1)} %copy-done), custom_call_target="tpu_custom_call" | custom-call | tf_op jit(solution)/shard_map/other_signs/pallas_call | solution.py:41
  34.6 1.8 %query_part.1 = (f32[2,256,128]{2,1,0:T(8,128)S(1)}, f32[2,256,128]{2,1,0:T(8,128)S(1)}, bf16[1024,2048]{1,0:T(8,128)(2,1)S(1)}, f32[16,1024]{1,0:T(8,128)S(1)}) custom-call(f32[16,2048]{1,0:T(8,128)S(1)} %get-tuple-element.51.score_ref, f32[16,128]{1,0:T(8,128)S(1)} %get-tuple-element.52.kl_ref, f32[16,128]{1,0:T(8,128)S(1)} %get-tuple-element.53.lse_ref, ...), custom_call_target="tpu_custom_call" | custom-call | tf_op jit(solution)/shard_map/query_part/pallas_call | solution.py:41
  36.4 1.5 %collective-permute-start.8 = (f32[2,256,128]{2,1,0:T(8,128)S(1)}, f32[2,256,128]{2,1,0:T(8,128)S(1)}, u32[]{:S(2)}, u32[]{:S(2)}) collective-permute-start(f32[2,256,128]{2,1,0:T(8,128)S(1)} %get-tuple-element.65), channel_id=1, source_target_pairs={{0,1},{1,0},{2,3},{3,2},{4,5},{5,4},{6,7},{7,6},{8,9},{9,8},{10,11... | collective-permute-start | bytes 786440 | tf_op jit(solution)/shard_map/ppermute | solution.py:506
  38.0 1.3 %collective-permute-done.9.delta_ref = f32[16,1024]{1,0:T(8,128)S(1)} collective-permute-done((f32[16,1024]{1,0:T(8,128)S(1)}, f32[16,1024]{1,0:T(8,128)S(1)}, u32[]{:S(2)}, u32[]{:S(2)}) %collective-permute-start.9) | collective-permute-done | bytes 65568 | tf_op jit(solution)/shard_map/ppermute | solution.py:509
  39.2 1.1 %key_part.1 = (f32[256,128]{1,0:T(8,128)S(1)}, f32[256,128]{1,0:T(8,128)S(1)}, f32[256,128]{1,0:T(8,128)S(1)}, f32[256,128]{1,0:T(8,128)S(1)}) custom-call(bf16[1024,2048]{1,0:T(8,128)(2,1)S(1)} %get-tuple-element.67.slope_ref, bf16[4,128,256]{2,1,0:T(8,128)(2,1)S(1)} %get-tuple-element.68.wiq_ref, f32[16,1024]{1,0:T(8,128)S(1)} %collective-permute-done.9.delta_ref, ...), custom_call_target="tpu_custom_call" | custom-call | tf_op jit(solution)/shard_map/key_part/pallas_call | solution.py:41
  40.3 1.7 %collective-permute-start.10 = (f32[256,128]{1,0:T(8,128)S(1)}, f32[256,128]{1,0:T(8,128)S(1)}, u32[]{:S(2)}, u32[]{:S(2)}) collective-permute-start(f32[256,128]{1,0:T(8,128)S(1)} %get-tuple-element.73), channel_id=1, source_target_pairs={{0,24},{4,28},{8,16},{12,20},{16,8},{20,12},{24,0},{28,4},{1,25},{... | collective-permute-start | bytes 393224 | tf_op jit(solution)/shard_map/ppermute | solution.py:509
  42.0 1.3 %collective-permute-start.11 = (f32[256,128]{1,0:T(8,128)S(1)}, f32[256,128]{1,0:T(8,128)S(1)}, u32[]{:S(2)}, u32[]{:S(2)}) collective-permute-start(f32[256,128]{1,0:T(8,128)S(1)} %get-tuple-element.74), channel_id=1, source_target_pairs={{0,16},{4,20},{8,24},{12,28},{16,0},{20,4},{24,8},{28,12},{1,17},{... | collective-permute-start | bytes 393224 | tf_op jit(solution)/shard_map/ppermute | solution.py:509
  43.4 0.5 collective-permute-start.12
  43.9 0.7 %collective-permute-done.8.right_ref = f32[2,256,128]{2,1,0:T(8,128)S(1)} collective-permute-done((f32[2,256,128]{2,1,0:T(8,128)S(1)}, f32[2,256,128]{2,1,0:T(8,128)S(1)}, u32[]{:S(2)}, u32[]{:S(2)}) %collective-permute-start.8) | collective-permute-done | bytes 262176 | tf_op jit(solution)/shard_map/ppermute | solution.py:506
  44.7 2.7 %collective-permute-start.13 = (f32[1,256,128]{2,1,0:T(8,128)S(1)}, f32[1,256,128]{2,1,0:T(8,128)S(1)}, u32[]{:S(2)}, u32[]{:S(2)}) collective-permute-start(f32[1,256,128]{2,1,0:T(8,128)S(1)} %get-tuple-element.77), channel_id=1, source_target_pairs={{0,2},{1,3},{2,0},{3,1},{4,6},{5,7},{6,4},{7,5},{8,10},{9,11},{10,... | collective-permute-start | bytes 393224 | tf_op jit(solution)/shard_map/ppermute | solution.py:506
  47.6 2.0 %collective-permute-done.11.refs_2_ = f32[256,128]{1,0:T(8,128)S(1)} collective-permute-done((f32[256,128]{1,0:T(8,128)S(1)}, f32[256,128]{1,0:T(8,128)S(1)}, u32[]{:S(2)}, u32[]{:S(2)}) %collective-permute-start.11) | collective-permute-done | bytes 131104 | tf_op jit(solution)/shard_map/ppermute | solution.py:509
  49.7 1.6 %collective-permute-start.17 = (f32[256,128]{1,0:T(8,128)S(1)}, f32[256,128]{1,0:T(8,128)S(1)}, u32[]{:S(2)}, u32[]{:S(2)}) collective-permute-start(f32[256,128]{1,0:T(8,128)S(1)} %add_all.1.refs_0_), channel_id=1, source_target_pairs={{0,8},{4,12},{8,0},{12,4},{16,24},{20,28},{24,16},{28,20},{1,9},{5... | collective-permute-start | bytes 393224 | tf_op jit(solution)/shard_map/ppermute | solution.py:509
  51.3 1.6 %collective-permute-done.13.right_ref = f32[1,256,128]{2,1,0:T(8,128)S(1)} collective-permute-done((f32[1,256,128]{2,1,0:T(8,128)S(1)}, f32[1,256,128]{2,1,0:T(8,128)S(1)}, u32[]{:S(2)}, u32[]{:S(2)}) %collective-permute-start.13) | collective-permute-done | bytes 131104 | tf_op jit(solution)/shard_map/ppermute | solution.py:506
  53.2 1.2 %collective-permute-start.16 = (f32[264,128]{1,0:T(8,128)S(1)}, f32[264,128]{1,0:T(8,128)S(1)}, u32[]{:S(2)}, u32[]{:S(2)}) collective-permute-start(f32[264,128]{1,0:T(8,128)S(1)} %own_rows.1.refs_0_), channel_id=1, source_target_pairs={{0,2},{1,3},{2,0},{3,1},{4,6},{5,7},{6,4},{7,5},{8,10},{9,11},{10,... | collective-permute-start | bytes 405512 | tf_op jit(solution)/shard_map/ppermute | solution.py:506
  54.5 2.9 %collective-permute-start.15 = (f32[264,128]{1,0:T(8,128)S(1)}, f32[264,128]{1,0:T(8,128)S(1)}, u32[]{:S(2)}, u32[]{:S(2)}) collective-permute-start(f32[264,128]{1,0:T(8,128)S(1)} %own_rows.1.refs_0_), channel_id=1, source_target_pairs={{0,1},{1,0},{2,3},{3,2},{4,5},{5,4},{6,7},{7,6},{8,9},{9,8},{10,11... | collective-permute-start | bytes 405512 | tf_op jit(solution)/shard_map/ppermute | solution.py:506
  57.7 1.6 %collective-permute-start.18 = (f32[256,128]{1,0:T(8,128)S(1)}, f32[256,128]{1,0:T(8,128)S(1)}, u32[]{:S(2)}, u32[]{:S(2)}) collective-permute-start(f32[256,128]{1,0:T(8,128)S(1)} %add_all.1.refs_0_), channel_id=1, source_target_pairs={{0,16},{4,20},{8,24},{12,28},{16,0},{20,4},{24,8},{28,12},{1,17},{... | collective-permute-start | bytes 393224 | tf_op jit(solution)/shard_map/ppermute | solution.py:509
  59.7 3.5 %collective-permute-done.18.refs_2_ = f32[256,128]{1,0:T(8,128)S(1)} collective-permute-done((f32[256,128]{1,0:T(8,128)S(1)}, f32[256,128]{1,0:T(8,128)S(1)}, u32[]{:S(2)}, u32[]{:S(2)}) %collective-permute-start.18) | collective-permute-done | bytes 131104 | tf_op jit(solution)/shard_map/ppermute | solution.py:509
  63.2 1.4 %collective-permute-done.19.refs_3_ = f32[256,128]{1,0:T(8,128)S(1)} collective-permute-done((f32[256,128]{1,0:T(8,128)S(1)}, f32[256,128]{1,0:T(8,128)S(1)}, u32[]{:S(2)}, u32[]{:S(2)}) %collective-permute-start.19) | collective-permute-done | bytes 131104 | tf_op jit(solution)/shard_map/ppermute | solution.py:509
  64.7 1.3 %collective-permute-done.14.refs_1_ = f32[264,128]{1,0:T(8,128)S(1)} collective-permute-done((f32[264,128]{1,0:T(8,128)S(1)}, f32[264,128]{1,0:T(8,128)S(1)}, u32[]{:S(2)}, u32[]{:S(2)}) %collective-permute-start.14) | collective-permute-done | bytes 135200 | tf_op jit(solution)/shard_map/ppermute | solution.py:506
  66.0 0.8 %place_query.1 = (f32[1024,128]{1,0:T(8,128)}, f32[16,64]{1,0:T(8,128)}) custom-call(f32[264,128]{1,0:T(8,128)S(1)} %own_rows.1.refs_0_, f32[264,128]{1,0:T(8,128)S(1)} %collective-permute-done.14.refs_1_, f32[264,128]{1,0:T(8,128)S(1)} %collective-permute-done.15.refs_2_, f32[264,128]{1,0:T(8,128)S(1)} %collective-permute-done.16.refs_3_), custom_call_target="tpu_custom_call" | custom-call | flops 40000000000 | tf_op jit(solution)/shard_map/place_query/pallas_call | solution.py:41
  66.9 1.0 %place_keys.1 = f32[2048,128]{1,0:T(8,128)} custom-call(f32[4,256,128]{2,1,0:T(8,128)S(1)} %stack_all.1.mine_ref, f32[4,256,128]{2,1,0:T(8,128)S(1)} %collective-permute-done.20.other_ref), custom_call_target="tpu_custom_call" | custom-call | tf_op jit(solution)/shard_map/place_keys/pallas_call | solution.py:41
  (36 shorter events, 3.0 us)
Async XLA Ops:
  0.6 14.1 %copy-start.3 = (s32[128]{0:T(128)S(1)}, s32[128]{0:T(128)}, u32[]{:S(2)}) copy-start(s32[128]{0:T(128)} %pos_ref.1) | copy-start | bytes 1540
  0.6 14.1 %copy-start = (bf16[2048,128]{1,0:T(8,128)(2,1)S(1)}, bf16[2048,128]{1,0:T(8,128)(2,1)}, u32[]{:S(2)}) copy-start(bf16[2048,128]{1,0:T(8,128)(2,1)} %keys_ref.7) | copy-start | bytes 1572868
  0.7 14.1 %copy-start.2 = (f32[16,64]{1,0:T(8,128)S(1)}, f32[16,64]{1,0:T(8,128)}, u32[]{:S(2)}) copy-start(f32[16,64]{1,0:T(8,128)} %weight_ref.5) | copy-start | bytes 12292
  0.7 14.1 %copy-start.1 = (bf16[16,64,128]{2,1,0:T(8,128)(2,1)S(1)}, bf16[16,64,128]{2,1,0:T(8,128)(2,1)}, u32[]{:S(2)}) copy-start(bf16[16,64,128]{2,1,0:T(8,128)(2,1)} %query_ref.3) | copy-start | bytes 786436
  11.7 5.2 %collective-permute-start = (f32[8,256]{1,0:T(8,128)S(1)}, f32[8,256]{1,0:T(8,128)S(1)}, u32[]{:S(2)}, u32[]{:S(2)}) collective-permute-start(f32[8,256]{1,0:T(8,128)S(1)} %get-tuple-element.42._.left_ref), channel_id=1, source_target_pairs={{0,1},{1,0},{2,3},{3,2},{4,5},{5,4},{6,7},{7,6},{8,9},{9,8},{10,11... | collective-permute-start | bytes 24584 | tf_op jit(solution)/shard_map/ppermute | solution.py:506
  16.9 4.8 %collective-permute-start.1 = (f32[24,256]{1,0:T(8,128)S(1)}, f32[24,256]{1,0:T(8,128)S(1)}, u32[]{:S(2)}, u32[]{:S(2)}) collective-permute-start(f32[24,256]{1,0:T(8,128)S(1)} %join_first.1.left_ref), channel_id=1, source_target_pairs={{0,2},{1,3},{2,0},{3,1},{4,6},{5,7},{6,4},{7,5},{8,10},{9,11},{10,... | collective-permute-start | bytes 73736 | tf_op jit(solution)/shard_map/ppermute | solution.py:506
  21.7 8.5 %copy-start.4 = (f32[16]{0:T(128)S(1)}, f32[16]{0:T(128)}, u32[]{:S(2)}) copy-start(f32[16]{0:T(128)} %kl_ref.1) | copy-start | bytes 196
  23.2 2.0 %collective-permute-start.4 = (f32[4,16,2048]{2,1,0:T(8,128)S(1)}, f32[4,16,2048]{2,1,0:T(8,128)S(1)}, u32[]{:S(2)}, u32[]{:S(2)}) collective-permute-start(f32[4,16,2048]{2,1,0:T(8,128)S(1)} %get-tuple-element.59), channel_id=1, source_target_pairs={{0,4},{4,0},{8,12},{12,8},{16,20},{20,16},{24,28},{28,24},{1,5},{5... | collective-permute-start | bytes 1572872 | tf_op jit(solution)/shard_map/ppermute | solution.py:509
  23.2 9.4 %collective-permute-start.3 = (f32[1040,128]{1,0:T(8,128)S(1)}, f32[1040,128]{1,0:T(8,128)S(1)}, u32[]{:S(2)}, u32[]{:S(2)}) collective-permute-start(f32[1040,128]{1,0:T(8,128)S(1)} %get-tuple-element.54), channel_id=1, source_target_pairs={{0,4},{4,0},{8,12},{12,8},{16,20},{20,16},{24,28},{28,24},{1,5},{5... | collective-permute-start | bytes 1597448 | tf_op jit(solution)/shard_map/ppermute | solution.py:509
  25.2 9.1 %collective-permute-start.5 = (f32[16,2048]{1,0:T(8,128)S(1)}, f32[16,2048]{1,0:T(8,128)S(1)}, u32[]{:S(2)}, u32[]{:S(2)}) collective-permute-start(f32[16,2048]{1,0:T(8,128)S(1)} %get-tuple-element.61), channel_id=1, source_target_pairs={{0,24},{4,28},{8,16},{12,20},{16,8},{20,12},{24,0},{28,4},{1,25},{... | collective-permute-start | bytes 393224 | tf_op jit(solution)/shard_map/ppermute | solution.py:509
  27.7 6.8 %collective-permute-start.6 = (f32[16,2048]{1,0:T(8,128)S(1)}, f32[16,2048]{1,0:T(8,128)S(1)}, u32[]{:S(2)}, u32[]{:S(2)}) collective-permute-start(f32[16,2048]{1,0:T(8,128)S(1)} %get-tuple-element.62), channel_id=1, source_target_pairs={{0,16},{4,20},{8,24},{12,28},{16,0},{20,4},{24,8},{28,12},{1,17},{... | collective-permute-start | bytes 393224 | tf_op jit(solution)/shard_map/ppermute | solution.py:509
  28.2 6.4 %collective-permute-start.7 = (f32[16,2048]{1,0:T(8,128)S(1)}, f32[16,2048]{1,0:T(8,128)S(1)}, u32[]{:S(2)}, u32[]{:S(2)}) collective-permute-start(f32[16,2048]{1,0:T(8,128)S(1)} %get-tuple-element.63), channel_id=1, source_target_pairs={{0,8},{4,12},{8,0},{12,4},{16,24},{20,28},{24,16},{28,20},{1,9},{5... | collective-permute-start | bytes 393224 | tf_op jit(solution)/shard_map/ppermute | solution.py:509
  28.7 5.6 %collective-permute-start.2 = (f32[16,128]{1,0:T(8,128)S(1)}, f32[16,128]{1,0:T(8,128)S(1)}, u32[]{:S(2)}, u32[]{:S(2)}) collective-permute-start(f32[16,128]{1,0:T(8,128)S(1)} %get-tuple-element.53.lse_ref), channel_id=1, source_target_pairs={{0,1},{1,0},{2,3},{3,2},{4,5},{5,4},{6,7},{7,6},{8,9},{9,8},{10,11... | collective-permute-start | bytes 24584 | tf_op jit(solution)/shard_map/ppermute | solution.py:506
  36.4 8.2 %collective-permute-start.8 = (f32[2,256,128]{2,1,0:T(8,128)S(1)}, f32[2,256,128]{2,1,0:T(8,128)S(1)}, u32[]{:S(2)}, u32[]{:S(2)}) collective-permute-start(f32[2,256,128]{2,1,0:T(8,128)S(1)} %get-tuple-element.65), channel_id=1, source_target_pairs={{0,1},{1,0},{2,3},{3,2},{4,5},{5,4},{6,7},{7,6},{8,9},{9,8},{10,11... | collective-permute-start | bytes 786440 | tf_op jit(solution)/shard_map/ppermute | solution.py:506
  38.0 1.3 %collective-permute-start.9 = (f32[16,1024]{1,0:T(8,128)S(1)}, f32[16,1024]{1,0:T(8,128)S(1)}, u32[]{:S(2)}, u32[]{:S(2)}) collective-permute-start(f32[16,1024]{1,0:T(8,128)S(1)} %get-tuple-element.69), channel_id=1, source_target_pairs={{0,4},{4,0},{8,12},{12,8},{16,20},{20,16},{24,28},{28,24},{1,5},{5... | collective-permute-start | bytes 196616 | tf_op jit(solution)/shard_map/ppermute | solution.py:509
  40.3 7.3 %collective-permute-start.10 = (f32[256,128]{1,0:T(8,128)S(1)}, f32[256,128]{1,0:T(8,128)S(1)}, u32[]{:S(2)}, u32[]{:S(2)}) collective-permute-start(f32[256,128]{1,0:T(8,128)S(1)} %get-tuple-element.73), channel_id=1, source_target_pairs={{0,24},{4,28},{8,16},{12,20},{16,8},{20,12},{24,0},{28,4},{1,25},{... | collective-permute-start | bytes 393224 | tf_op jit(solution)/shard_map/ppermute | solution.py:509
  42.0 7.6 %collective-permute-start.11 = (f32[256,128]{1,0:T(8,128)S(1)}, f32[256,128]{1,0:T(8,128)S(1)}, u32[]{:S(2)}, u32[]{:S(2)}) collective-permute-start(f32[256,128]{1,0:T(8,128)S(1)} %get-tuple-element.74), channel_id=1, source_target_pairs={{0,16},{4,20},{8,24},{12,28},{16,0},{20,4},{24,8},{28,12},{1,17},{... | collective-permute-start | bytes 393224 | tf_op jit(solution)/shard_map/ppermute | solution.py:509
  43.4 6.3 %collective-permute-start.12 = (f32[256,128]{1,0:T(8,128)S(1)}, f32[256,128]{1,0:T(8,128)S(1)}, u32[]{:S(2)}, u32[]{:S(2)}) collective-permute-start(f32[256,128]{1,0:T(8,128)S(1)} %get-tuple-element.75), channel_id=1, source_target_pairs={{0,8},{4,12},{8,0},{12,4},{16,24},{20,28},{24,16},{28,20},{1,9},{5... | collective-permute-start | bytes 393224 | tf_op jit(solution)/shard_map/ppermute | solution.py:509
  44.7 8.2 %collective-permute-start.13 = (f32[1,256,128]{2,1,0:T(8,128)S(1)}, f32[1,256,128]{2,1,0:T(8,128)S(1)}, u32[]{:S(2)}, u32[]{:S(2)}) collective-permute-start(f32[1,256,128]{2,1,0:T(8,128)S(1)} %get-tuple-element.77), channel_id=1, source_target_pairs={{0,2},{1,3},{2,0},{3,1},{4,6},{5,7},{6,4},{7,5},{8,10},{9,11},{10,... | collective-permute-start | bytes 393224 | tf_op jit(solution)/shard_map/ppermute | solution.py:506
  49.7 9.6 %collective-permute-start.17 = (f32[256,128]{1,0:T(8,128)S(1)}, f32[256,128]{1,0:T(8,128)S(1)}, u32[]{:S(2)}, u32[]{:S(2)}) collective-permute-start(f32[256,128]{1,0:T(8,128)S(1)} %add_all.1.refs_0_), channel_id=1, source_target_pairs={{0,8},{4,12},{8,0},{12,4},{16,24},{20,28},{24,16},{28,20},{1,9},{5... | collective-permute-start | bytes 393224 | tf_op jit(solution)/shard_map/ppermute | solution.py:509
  53.2 11.5 %collective-permute-start.16 = (f32[264,128]{1,0:T(8,128)S(1)}, f32[264,128]{1,0:T(8,128)S(1)}, u32[]{:S(2)}, u32[]{:S(2)}) collective-permute-start(f32[264,128]{1,0:T(8,128)S(1)} %own_rows.1.refs_0_), channel_id=1, source_target_pairs={{0,2},{1,3},{2,0},{3,1},{4,6},{5,7},{6,4},{7,5},{8,10},{9,11},{10,... | collective-permute-start | bytes 405512 | tf_op jit(solution)/shard_map/ppermute | solution.py:506
  54.5 10.2 %collective-permute-start.15 = (f32[264,128]{1,0:T(8,128)S(1)}, f32[264,128]{1,0:T(8,128)S(1)}, u32[]{:S(2)}, u32[]{:S(2)}) collective-permute-start(f32[264,128]{1,0:T(8,128)S(1)} %own_rows.1.refs_0_), channel_id=1, source_target_pairs={{0,1},{1,0},{2,3},{3,2},{4,5},{5,4},{6,7},{7,6},{8,9},{9,8},{10,11... | collective-permute-start | bytes 405512 | tf_op jit(solution)/shard_map/ppermute | solution.py:506
  57.4 8.6 %collective-permute-start.14 = (f32[264,128]{1,0:T(8,128)S(1)}, f32[264,128]{1,0:T(8,128)S(1)}, u32[]{:S(2)}, u32[]{:S(2)}) collective-permute-start(f32[264,128]{1,0:T(8,128)S(1)} %own_rows.1.refs_0_), channel_id=1, source_target_pairs={{0,3},{1,2},{2,1},{3,0},{4,7},{5,6},{6,5},{7,4},{8,11},{9,10},{10,... | collective-permute-start | bytes 405512 | tf_op jit(solution)/shard_map/ppermute | solution.py:506
  57.7 5.5 %collective-permute-start.18 = (f32[256,128]{1,0:T(8,128)S(1)}, f32[256,128]{1,0:T(8,128)S(1)}, u32[]{:S(2)}, u32[]{:S(2)}) collective-permute-start(f32[256,128]{1,0:T(8,128)S(1)} %add_all.1.refs_0_), channel_id=1, source_target_pairs={{0,16},{4,20},{8,24},{12,28},{16,0},{20,4},{24,8},{28,12},{1,17},{... | collective-permute-start | bytes 393224 | tf_op jit(solution)/shard_map/ppermute | solution.py:509
  59.3 5.3 %collective-permute-start.19 = (f32[256,128]{1,0:T(8,128)S(1)}, f32[256,128]{1,0:T(8,128)S(1)}, u32[]{:S(2)}, u32[]{:S(2)}) collective-permute-start(f32[256,128]{1,0:T(8,128)S(1)} %collective-permute-done.17.refs_1_), channel_id=1, source_target_pairs={{0,16},{4,20},{8,24},{12,28},{16,0},{20,4},{24,8},{28,12},{1,17},{... | collective-permute-start | bytes 393224 | tf_op jit(solution)/shard_map/ppermute | solution.py:509
  64.6 2.2 %collective-permute-start.20 = (f32[4,256,128]{2,1,0:T(8,128)S(1)}, f32[4,256,128]{2,1,0:T(8,128)S(1)}, u32[]{:S(2)}, u32[]{:S(2)}) collective-permute-start(f32[4,256,128]{2,1,0:T(8,128)S(1)} %stack_all.1.mine_ref), channel_id=1, source_target_pairs={{0,4},{4,0},{8,12},{12,8},{16,20},{20,16},{24,28},{28,24},{1,5},{5... | collective-permute-start | bytes 1572872 | tf_op jit(solution)/shard_map/ppermute | solution.py:509

commit v6 on v5

--- a/solution.py
+++ b/solution.py
@@ -331,17 +331,34 @@
     return vmem_call(body, "join_pair", pltpu.VMEM(left.shape, F32), (left, right))
 
 
+def group_order(groups):
+    return [*range(1, groups, 2), *range(0, groups, 2)]
+
+
+def fill_slopes(delta_ref, gate_ref, slope_ref, order, z):
+    own, keys = delta_ref.shape[1:]
+    size = gate_ref.shape[1]
+    heads = size // own
+    for n, r in enumerate(order):
+        lines = delta_ref[z ^ r]
+        for i in range(own):
+            line = jnp.broadcast_to(lines[i : i + 1, :], (heads, keys)).astype(BF16)
+            signs = gate_ref[z ^ r, i * heads : (i + 1) * heads, :]
+            at = n * size + i * heads
+            slope_ref[at : at + heads, :] = jnp.where(signs > 0, line, jnp.zeros((), BF16))
+
+
 def query_part(scores, index_stats, targets, kl, gate, index_keys):
     rows, keys = scores.shape
     groups, size = gate.shape[:2]
     own = rows // groups
-    heads = size // own
     width = index_keys.shape[1]
     half = keys // 2
+    order = group_order(groups)[: groups // 2]
+    many = len(order)
 
     def body(score_ref, kl_ref, lse_ref, other_ref, gate_ref, keys_ref, *refs):
-        target_refs, refs = refs[: len(targets)], refs[len(targets) :]
-        keep_ref, send_ref, slope_ref, across_ref, delta_ref = refs
+        target_refs, (send_ref, slope_ref, delta_ref, across_ref) = refs[: len(targets)], refs[len(targets) :]
         whole = joined([lse_ref[:, :1], other_ref[:, :1]])
         target = target_refs[0][...]
         for ref in target_refs[1:]:
@@ -349,26 +366,35 @@
         delta = kl_ref[:, :1] * (jnp.exp2(score_ref[...] - whole) - target)
         for g in range(groups):
             delta_ref[g] = delta[g * own : (g + 1) * own, :]
-        z = lax.axis_index("keys")
         _, core = head_place()
         across_ref[...] = jnp.where(core == 0, delta[:, half:], delta[:, :half])
-        for r in range(groups):
-            lines = delta_ref[z ^ r]
-            for i in range(own):
-                line = jnp.broadcast_to(lines[i : i + 1, :], (heads, keys)).astype(BF16)
-                signs = gate_ref[z ^ r, i * heads : (i + 1) * heads, :]
-                at = r * size + i * heads
-                slope_ref[at : at + heads, :] = jnp.where(signs > 0, line, jnp.zeros((), BF16))
+        fill_slopes(delta_ref, gate_ref, slope_ref, order, lax.axis_index("keys"))
         part = jnp.dot(slope_ref[...], keys_ref[...], preferred_element_type=F32)
-        for r in range(groups):
-            out_ref = send_ref if r % 2 else keep_ref
-            out_ref[r // 2] = part[r * size : (r + 1) * size, :]
-
-    side = pltpu.VMEM((groups // 2, size, width), F32)
-    outs = (side, side, pltpu.VMEM((rows * heads, keys), BF16), pltpu.VMEM((rows, half), F32))
-    scratch = [pltpu.VMEM((groups, own, keys), F32)]
+        send_ref[...] = part.reshape(many, size, width)
+
+    outs = (
+        pltpu.VMEM((many, size, width), F32),
+        pltpu.VMEM((many * size, keys), BF16),
+        pltpu.VMEM((groups, own, keys), F32),
+        pltpu.VMEM((rows, half), F32),
+    )
     operands = (scores, kl, *index_stats, gate, index_keys, *targets)
-    return vmem_call(body, "query_part", outs, operands, scratch, limit=16 * MIB)
+    return vmem_call(body, "query_part", outs, operands, limit=16 * MIB)
+
+
+def query_rest(delta, gate, index_keys):
+    groups, size, keys = gate.shape
+    width = index_keys.shape[1]
+    order = group_order(groups)[groups // 2 :]
+    many = len(order)
+
+    def body(delta_ref, gate_ref, keys_ref, keep_ref, slope_ref):
+        fill_slopes(delta_ref, gate_ref, slope_ref, order, lax.axis_index("keys"))
+        part = jnp.dot(slope_ref[...], keys_ref[...], preferred_element_type=F32)
+        keep_ref[...] = part.reshape(many, size, width)
+
+    outs = (pltpu.VMEM((many, size, width), F32), pltpu.VMEM((many * size, keys), BF16))
+    return vmem_call(body, "query_rest", outs, (delta, gate, index_keys), limit=16 * MIB)
 
 
 def key_part(slopes, wiq, other_delta, other_gate, other_wiq, chips):
@@ -377,12 +403,13 @@
     count = other_gate.shape[0]
     heads = count // rows
     chunk = half // chips
-
-    def body(slope_ref, wiq_ref, delta_ref, gate_ref, other_ref, *refs):
+    first = slopes[0].shape[0]
+
+    def body(odd_ref, even_ref, wiq_ref, delta_ref, gate_ref, other_ref, *refs):
         outs, (wiq_rows, other_slopes) = refs[:chips], refs[chips:]
         z = lax.axis_index("keys")
-        for r in range(groups):
-            wiq_rows[:, r * size : (r + 1) * size] = wiq_ref[z ^ r]
+        for n, r in enumerate(group_order(groups)):
+            wiq_rows[:, n * size : (n + 1) * size] = wiq_ref[z ^ r]
         for row in range(rows):
             span = slice(row * heads, (row + 1) * heads)
             line = jnp.broadcast_to(delta_ref[row : row + 1, :], (heads, half)).astype(BF16)
@@ -391,13 +418,14 @@
         for n, out_ref in enumerate(outs):
             at = pl.multiple_of((chip ^ n) * chunk, chunk)
             here = pl.ds(pl.multiple_of(core * half + at, chunk), chunk)
-            total = jnp.dot(wiq_rows[...], slope_ref[:, here], preferred_element_type=F32)
+            total = jnp.dot(wiq_rows[:, :first], odd_ref[:, here], preferred_element_type=F32)
+            total += jnp.dot(wiq_rows[:, first:], even_ref[:, here], preferred_element_type=F32)
             total += jnp.dot(other_ref[...], other_slopes[:, pl.ds(at, chunk)], preferred_element_type=F32)
             out_ref[...] = total.T
 
     outs = tuple(pltpu.VMEM((chunk, width), F32) for _ in range(chips))
     scratch = [pltpu.VMEM((width, count), BF16), pltpu.VMEM((count, half), BF16)]
-    operands = (slopes, wiq, other_delta, other_gate, other_wiq)
+    operands = (*slopes, wiq, other_delta, other_gate, other_wiq)
     return vmem_call(body, "key_part", outs, operands, scratch, limit=16 * MIB)
 
 
@@ -438,61 +466,59 @@
     return vmem_call(body, "own_rows", out, (index_query, index_weight, left, right), cost=LONG)
 
 
-def place_query(pieces, rows, heads):
+def gather_weights(pieces, rows, heads):
     own = rows // len(pieces)
     size = own * heads
-    width = pieces[0].shape[1]
     order = list(pieces)
 
     def body(*refs):
-        piece_refs, (query_out, weight_out, weights, sems) = refs[: len(pieces)], refs[len(pieces) :]
         z = lax.axis_index("keys")
-        copies = []
+        for r, ref in zip(order, refs):
+            refs[-1][pl.ds((z ^ r) * own, own), :] = ref[size : size + own, :heads]
+
+    out = pltpu.VMEM((rows, heads), F32)
+    return vmem_call(body, "gather_weights", out, list(pieces.values()), cost=LONG)
+
+
+def place_all(pieces, weights, mine, other):
+    rows, heads = weights.shape
+    own = rows // len(pieces)
+    size = own * heads
+    order = list(pieces)
+    count = len(order)
+    chips, chunk, width = mine.shape
+
+    def body(weight_ref, mine_ref, other_ref, *refs):
+        piece_refs, (query_out, key_out, weight_out, sems) = refs[:count], refs[count:]
+        z = lax.axis_index("keys")
+        chip, core = head_place()
+        pairs = [(weight_ref, weight_out)]
         for r, ref in zip(order, piece_refs):
             at = pl.multiple_of((z ^ r) * size, size)
-            copies.append(pltpu.make_async_copy(ref.at[:size], query_out.at[pl.ds(at, size)], sems.at[r]))
-            copies[-1].start()
-        for r, ref in zip(order, piece_refs):
-            weights[pl.ds((z ^ r) * own, own), :] = ref[size : size + own, :heads]
-        copies.append(pltpu.make_async_copy(weights, weight_out, sems.at[len(pieces)]))
-        copies[-1].start()
+            pairs.append((ref.at[:size], query_out.at[pl.ds(at, size)]))
+        for ref, side in ((mine_ref, core), (other_ref, 1 - core)):
+            for r in range(chips):
+                at = pl.multiple_of(side * (chips * chunk) + (chip ^ r) * chunk, chunk)
+                pairs.append((ref.at[r], key_out.at[pl.ds(at, chunk)]))
+        copies = [pltpu.make_async_copy(*pair, sems.at[n]) for n, pair in enumerate(pairs)]
+        for copy in copies:
+            copy.start()
         for copy in copies:
             copy.wait()
 
-    query, weight = vmem_call(
+    query, key, weight = vmem_call(
         body,
-        "place_query",
-        (jax.ShapeDtypeStruct((rows * heads, width), F32), jax.ShapeDtypeStruct((rows, heads), F32)),
-        list(pieces.values()),
-        [pltpu.VMEM((rows, heads), F32), pltpu.SemaphoreType.DMA((len(pieces) + 1,))],
-        out_specs=(any_spec, any_spec),
-        cost=LONG,
-    )
-    return query.reshape(rows, heads, width), weight
-
-
-def place_keys(mine, other):
-    chips, chunk, width = mine.shape
-
-    def body(mine_ref, other_ref, out_ref, sems):
-        chip, core = head_place()
-        copies = []
-        for n, (ref, side) in enumerate(((mine_ref, core), (other_ref, 1 - core))):
-            for r in range(chips):
-                at = pl.multiple_of(side * (chips * chunk) + (chip ^ r) * chunk, chunk)
-                copies.append(pltpu.make_async_copy(ref.at[r], out_ref.at[pl.ds(at, chunk)], sems.at[n, r]))
-                copies[-1].start()
-        for copy in copies:
-            copy.wait()
-
-    return vmem_call(
-        body,
-        "place_keys",
-        jax.ShapeDtypeStruct((2 * chips * chunk, width), F32),
-        (mine, other),
-        [pltpu.SemaphoreType.DMA((2, chips))],
-        out_specs=any_spec,
-    )
+        "place_all",
+        (
+            jax.ShapeDtypeStruct((rows * heads, width), F32),
+            jax.ShapeDtypeStruct((2 * chips * chunk, width), F32),
+            jax.ShapeDtypeStruct((rows, heads), F32),
+        ),
+        (weights, mine, other, *pieces.values()),
+        [pltpu.SemaphoreType.DMA((1 + count + 2 * chips,))],
+        out_specs=(any_spec,) * 3,
+    )
+    return query.reshape(rows, heads, width), key, weight
 
 
 def shards(main_query, latent_keys, index_query, index_keys, index_weight, query_pos, kl_weight):
@@ -528,7 +554,9 @@
     other_gate, other_wiq = other_signs(to_heads(pack, 1), index_keys, row_local)
     index_stats = (index_lse, to_keys(index_lse, 1))
     other_gate, gate = lax.optimization_barrier((other_gate, gate))
-    even, odd, slopes, across = query_part(scores, index_stats, targets, kl, gate, index_keys)
+    odd, odd_slopes, delta, across = query_part(scores, index_stats, targets, kl, gate, index_keys)
+    even, even_slopes = query_rest(delta, gate, index_keys)
+    slopes = (odd_slopes, even_slopes)
 
     bits, other_odd = 1, to_keys(odd, 1)
     parts = key_part(slopes, wiq, to_heads(across, 1), other_gate, other_wiq, chips)
@@ -540,14 +568,11 @@
     even, key_own = lax.optimization_barrier((even, key_own))
     query_own = own_rows(even, other_odd, index_query, index_weight)
     pieces = {0: query_own, **{r: to_keys(query_own, r) for r in key_order}}
-    mine, bits = [key_own], 2
-    while bits < head_devices:
-        mine = mine + [to_heads(piece, bits) for piece in mine]
-        bits *= 2
+    mine = {r: to_heads(key_own, 2 * r) for r in range(1, chips)}
+    mine = [key_own] + [mine[r] for r in range(1, chips)]
     mine = stack_all(mine)
-    key_grad = place_keys(mine, to_heads(mine, 1))
-    query_grad, weight_grad = place_query(pieces, row_local, index_heads)
-    return query_grad, key_grad, weight_grad
+    weights = gather_weights(pieces, row_local, index_heads)
+    return place_all(pieces, weights, mine, to_heads(mine, 1))
 
 
 def solution(mesh):

time: 68.2 us -> 67.1 us (0.984)
    pallas_call x15 -> x16, Pallas kernels: 12.9 us -> 12.3 us  [vmem_call(): pl.pallas_call(body, out_shape=outs, in_specs=[smem_spec] * len(scalars)...]
  transfers between devices with their start and end apart: 21 -> 21, of which waited for: 12 -> 13; matrix products, arithmetic and copies ran while one was open for 0% -> 0% of each run, Pallas kernels for 13% -> 13%
where the time goes in v6:
time: 67.1 us; the launch traced here: 66.9 us
  starting transfers between devices  27.3 us (41%)
  Pallas kernels  23.3 us (35%)
  waiting for transfers between devices  15.4 us (23%)
  between operations  0.97 us (1%)
    ppermute x8, starting transfers between devices, to_keys(): lax.ppermute(value, 'keys', [(i, i ^ bits) for i in range(key_devices)])  15.8 us
    pallas_call x16, Pallas kernels, vmem_call(): pl.pallas_call(body, out_shape=outs, in_specs=[smem_spec] * len(scalars)...  12.3 us
    ppermute x13, starting transfers between devices, to_heads(): lax.ppermute(value, 'heads', [(i, i ^ bits) for i in range(head_devices)])  11.4 us
    pallas_call x1, Pallas kernels, main_scores(): pl.pallas_call(body, grid=(blocks // many,), out_shape=(pltpu.VMEM((block...  11 us
    ppermute x13, waiting for transfers between devices, to_heads(): lax.ppermute(value, 'heads', [(i, i ^ bits) for i in range(head_devices)])  9.47 us
    ppermute x8, waiting for transfers between devices, to_keys(): lax.ppermute(value, 'keys', [(i, i ^ bits) for i in range(key_devices)])  5.89 us
  transfers between devices with their start and end apart: 21, of which 13 were waited for; matrix products, arithmetic and copies ran while one was open for 0% of the time, Pallas kernels for 13%

profile of v6, /device:TPU:0, one launch (start us, length us, event | category | flops | bytes accessed | tf_op | source)
XLA Modules:
  0.0 66.9 jit_solution(3752113715919014800)
XLA Ops:
  0.7 11.0 %main_scores.1 = (f32[8,2048,256]{2,1,0:T(8,128)S(1)}, f32[8,16,256]{2,1,0:T(8,128)S(1)}, f32[8,256]{1,0:T(8,128)S(1)}) custom-call(s32[1,128]{1,0:T(1,128)} %bitcast.4, bf16[16,576,128]{2,1,0:T(8,128)(2,1)} %bitcast.5, bf16[576,2048]{1,0:T(8,128)(2,1)} %bitcast.6), custom_call_target="tpu_custom_call" | custom-call | tf_op jit(solution)/shard_map/main_scores/pallas_call | solution.py:216
  11.7 3.1 %collective-permute-start = (f32[8,256]{1,0:T(8,128)S(1)}, f32[8,256]{1,0:T(8,128)S(1)}, u32[]{:S(2)}, u32[]{:S(2)}) collective-permute-start(f32[8,256]{1,0:T(8,128)S(1)} %get-tuple-element.45._.left_ref), channel_id=1, source_target_pairs={{0,1},{1,0},{2,3},{3,2},{4,5},{5,4},{6,7},{7,6},{8,9},{9,8},{10,11... | collective-permute-start | bytes 24584 | tf_op jit(solution)/shard_map/ppermute | solution.py:532
  14.8 2.1 %index_forward.1 = (f32[16,2048]{1,0:T(8,128)S(1)}, f32[16,128]{1,0:T(8,128)S(1)}, f32[1040,128]{1,0:T(8,128)S(1)}) custom-call(s32[128]{0:T(128)S(1)} %copy-done.3, bf16[16,64,128]{2,1,0:T(8,128)(2,1)S(1)} %copy-done.1, bf16[2048,128]{1,0:T(8,128)(2,1)S(1)} %copy-done, f32[16,64]{1,0:T(8,128)S(1)} %copy-done.2, f32[8,256]{1,0:T(8,128)S(1)} %get-tuple-element.45._.left_ref), custom_call_target="tpu_custom_call" | custom-call | tf_op jit(solution)/shard_map/index_forward/pallas_call | solution.py:41
  16.9 2.6 %collective-permute-start.1 = (f32[24,256]{1,0:T(8,128)S(1)}, f32[24,256]{1,0:T(8,128)S(1)}, u32[]{:S(2)}, u32[]{:S(2)}) collective-permute-start(f32[24,256]{1,0:T(8,128)S(1)} %join_first.1.left_ref), channel_id=1, source_target_pairs={{0,2},{1,3},{2,0},{3,1},{4,6},{5,7},{6,4},{7,5},{8,10},{9,11},{10,... | collective-permute-start | bytes 73736 | tf_op jit(solution)/shard_map/ppermute | solution.py:532
  19.6 2.1 %collective-permute-done.1.right_ref = f32[24,256]{1,0:T(8,128)S(1)} collective-permute-done((f32[24,256]{1,0:T(8,128)S(1)}, f32[24,256]{1,0:T(8,128)S(1)}, u32[]{:S(2)}, u32[]{:S(2)}) %collective-permute-start.1) | collective-permute-done | bytes 24608 | tf_op jit(solution)/shard_map/ppermute | solution.py:532
  21.8 1.4 %head_sum.1 = (f32[4,16,2048]{2,1,0:T(8,128)S(1)}, f32[4,16,2048]{2,1,0:T(8,128)S(1)}) custom-call(f32[8,2048,256]{2,1,0:T(8,128)S(1)} %get-tuple-element.48.prob_ref, f32[8,16,256]{2,1,0:T(8,128)S(1)} %get-tuple-element.49.top_ref, f32[8,256]{1,0:T(8,128)S(1)} %get-tuple-element.50.stat_ref), custom_call_target="tpu_custom_call" | custom-call | flops 1000000000 | tf_op jit(solution)/shard_map/head_sum/pallas_call | solution.py:41
  23.7 1.4 %collective-permute-done.4.right_ref = f32[4,16,2048]{2,1,0:T(8,128)S(1)} collective-permute-done((f32[4,16,2048]{2,1,0:T(8,128)S(1)}, f32[4,16,2048]{2,1,0:T(8,128)S(1)}, u32[]{:S(2)}, u32[]{:S(2)}) %collective-permute-start.4) | collective-permute-done | bytes 524320 | tf_op jit(solution)/shard_map/ppermute | solution.py:535
  25.2 2.5 %collective-permute-start.5 = (f32[16,2048]{1,0:T(8,128)S(1)}, f32[16,2048]{1,0:T(8,128)S(1)}, u32[]{:S(2)}, u32[]{:S(2)}) collective-permute-start(f32[16,2048]{1,0:T(8,128)S(1)} %get-tuple-element.64), channel_id=1, source_target_pairs={{0,24},{4,28},{8,16},{12,20},{16,8},{20,12},{24,0},{28,4},{1,25},{... | collective-permute-start | bytes 393224 | tf_op jit(solution)/shard_map/ppermute | solution.py:535
  27.7 0.5 collective-permute-start.6
  28.2 0.5 collective-permute-start.7
  28.8 1.5 %collective-permute-start.2 = (f32[16,128]{1,0:T(8,128)S(1)}, f32[16,128]{1,0:T(8,128)S(1)}, u32[]{:S(2)}, u32[]{:S(2)}) collective-permute-start(f32[16,128]{1,0:T(8,128)S(1)} %get-tuple-element.56.lse_ref), channel_id=1, source_target_pairs={{0,1},{1,0},{2,3},{3,2},{4,5},{5,4},{6,7},{7,6},{8,9},{9,8},{10,11... | collective-permute-start | bytes 24584 | tf_op jit(solution)/shard_map/ppermute | solution.py:532
  30.2 2.4 %index_signs.1 = (bf16[4,256,2048]{2,1,0:T(8,128)(2,1)S(1)}, bf16[4,128,256]{2,1,0:T(8,128)(2,1)S(1)}, f32[16,128]{1,0:T(8,128)S(1)}) custom-call(f32[16]{0:T(128)S(1)} %copy-done.4, bf16[16,64,128]{2,1,0:T(8,128)(2,1)S(1)} %copy-done.1, bf16[2048,128]{1,0:T(8,128)(2,1)S(1)} %copy-done, f32[16,64]{1,0:T(8,128)S(1)} %copy-done.2), custom_call_target="tpu_custom_call" | custom-call | tf_op jit(solution)/shard_map/index_signs/pallas_call | solution.py:41
  32.6 1.7 %other_signs.1 = (bf16[1024,1024]{1,0:T(8,128)(2,1)S(1)}, bf16[128,1024]{1,0:T(8,128)(2,1)S(1)}) custom-call(f32[1040,128]{1,0:T(8,128)S(1)} %collective-permute-done.3.pack_ref, bf16[2048,128]{1,0:T(8,128)(2,1)S(1)} %copy-done), custom_call_target="tpu_custom_call" | custom-call | tf_op jit(solution)/shard_map/other_signs/pallas_call | solution.py:41
  34.6 1.0 %query_part.1 = (f32[2,256,128]{2,1,0:T(8,128)S(1)}, bf16[512,2048]{1,0:T(8,128)(2,1)S(1)}, f32[4,4,2048]{2,1,0:T(4,128)S(1)}, f32[16,1024]{1,0:T(8,128)S(1)}) custom-call(f32[16,2048]{1,0:T(8,128)S(1)} %get-tuple-element.54.score_ref, f32[16,128]{1,0:T(8,128)S(1)} %get-tuple-element.55.kl_ref, f32[16,128]{1,0:T(8,128)S(1)} %get-tuple-element.56.lse_ref, ...), custom_call_target="tpu_custom_call" | custom-call | tf_op jit(solution)/shard_map/query_part/pallas_call | solution.py:41
  35.6 1.5 %collective-permute-start.8 = (f32[2,256,128]{2,1,0:T(8,128)S(1)}, f32[2,256,128]{2,1,0:T(8,128)S(1)}, u32[]{:S(2)}, u32[]{:S(2)}) collective-permute-start(f32[2,256,128]{2,1,0:T(8,128)S(1)} %get-tuple-element.69), channel_id=1, source_target_pairs={{0,1},{1,0},{2,3},{3,2},{4,5},{5,4},{6,7},{7,6},{8,9},{9,8},{10,11... | collective-permute-start | bytes 786440 | tf_op jit(solution)/shard_map/ppermute | solution.py:532
  37.2 0.7 %query_rest.1 = (f32[2,256,128]{2,1,0:T(8,128)S(1)}, bf16[512,2048]{1,0:T(8,128)(2,1)S(1)}) custom-call(f32[4,4,2048]{2,1,0:T(4,128)S(1)} %get-tuple-element.67.delta_ref, bf16[4,256,2048]{2,1,0:T(8,128)(2,1)S(1)} %get-tuple-element.60.gate_ref, bf16[2048,128]{1,0:T(8,128)(2,1)S(1)} %copy-done), custom_call_target="tpu_custom_call" | custom-call | tf_op jit(solution)/shard_map/query_rest/pallas_call | solution.py:41
  38.4 1.2 %key_part.1 = (f32[256,128]{1,0:T(8,128)S(1)}, f32[256,128]{1,0:T(8,128)S(1)}, f32[256,128]{1,0:T(8,128)S(1)}, f32[256,128]{1,0:T(8,128)S(1)}) custom-call(bf16[512,2048]{1,0:T(8,128)(2,1)S(1)} %get-tuple-element.71.odd_ref, bf16[512,2048]{1,0:T(8,128)(2,1)S(1)} %get-tuple-element.72.even_ref, bf16[4,128,256]{2,1,0:T(8,128)(2,1)S(1)} %get-tuple-element.73.wiq_ref, ...), custom_call_target="tpu_custom_call" | custom-call | tf_op jit(solution)/shard_map/key_part/pallas_call | solution.py:41
  39.6 1.7 %collective-permute-start.10 = (f32[256,128]{1,0:T(8,128)S(1)}, f32[256,128]{1,0:T(8,128)S(1)}, u32[]{:S(2)}, u32[]{:S(2)}) collective-permute-start(f32[256,128]{1,0:T(8,128)S(1)} %get-tuple-element.78), channel_id=1, source_target_pairs={{0,24},{4,28},{8,16},{12,20},{16,8},{20,12},{24,0},{28,4},{1,25},{... | collective-permute-start | bytes 393224 | tf_op jit(solution)/shard_map/ppermute | solution.py:535
  41.3 1.3 %collective-permute-start.11 = (f32[256,128]{1,0:T(8,128)S(1)}, f32[256,128]{1,0:T(8,128)S(1)}, u32[]{:S(2)}, u32[]{:S(2)}) collective-permute-start(f32[256,128]{1,0:T(8,128)S(1)} %get-tuple-element.79), channel_id=1, source_target_pairs={{0,16},{4,20},{8,24},{12,28},{16,0},{20,4},{24,8},{28,12},{1,17},{... | collective-permute-start | bytes 393224 | tf_op jit(solution)/shard_map/ppermute | solution.py:535
  42.6 0.5 collective-permute-start.12
  43.2 0.7 %collective-permute-done.8.right_ref = f32[2,256,128]{2,1,0:T(8,128)S(1)} collective-permute-done((f32[2,256,128]{2,1,0:T(8,128)S(1)}, f32[2,256,128]{2,1,0:T(8,128)S(1)}, u32[]{:S(2)}, u32[]{:S(2)}) %collective-permute-start.8) | collective-permute-done | bytes 262176 | tf_op jit(solution)/shard_map/ppermute | solution.py:532
  43.9 2.7 %collective-permute-start.13 = (f32[1,256,128]{2,1,0:T(8,128)S(1)}, f32[1,256,128]{2,1,0:T(8,128)S(1)}, u32[]{:S(2)}, u32[]{:S(2)}) collective-permute-start(f32[1,256,128]{2,1,0:T(8,128)S(1)} %get-tuple-element.82), channel_id=1, source_target_pairs={{0,2},{1,3},{2,0},{3,1},{4,6},{5,7},{6,4},{7,5},{8,10},{9,11},{10,... | collective-permute-start | bytes 393224 | tf_op jit(solution)/shard_map/ppermute | solution.py:532
  46.9 2.0 %collective-permute-done.11.refs_2_ = f32[256,128]{1,0:T(8,128)S(1)} collective-permute-done((f32[256,128]{1,0:T(8,128)S(1)}, f32[256,128]{1,0:T(8,128)S(1)}, u32[]{:S(2)}, u32[]{:S(2)}) %collective-permute-start.11) | collective-permute-done | bytes 131104 | tf_op jit(solution)/shard_map/ppermute | solution.py:535
  49.0 1.7 %collective-permute-start.19 = (f32[256,128]{1,0:T(8,128)S(1)}, f32[256,128]{1,0:T(8,128)S(1)}, u32[]{:S(2)}, u32[]{:S(2)}) collective-permute-start(f32[256,128]{1,0:T(8,128)S(1)} %add_all.1.refs_0_), channel_id=1, source_target_pairs={{0,24},{4,28},{8,16},{12,20},{16,8},{20,12},{24,0},{28,4},{1,25},{... | collective-permute-start | bytes 393224 | tf_op jit(solution)/shard_map/ppermute | solution.py:535
  50.7 1.4 %collective-permute-done.13.right_ref = f32[1,256,128]{2,1,0:T(8,128)S(1)} collective-permute-done((f32[1,256,128]{2,1,0:T(8,128)S(1)}, f32[1,256,128]{2,1,0:T(8,128)S(1)}, u32[]{:S(2)}, u32[]{:S(2)}) %collective-permute-start.13) | collective-permute-done | bytes 131104 | tf_op jit(solution)/shard_map/ppermute | solution.py:532
  52.5 1.4 %collective-permute-start.16 = (f32[264,128]{1,0:T(8,128)S(1)}, f32[264,128]{1,0:T(8,128)S(1)}, u32[]{:S(2)}, u32[]{:S(2)}) collective-permute-start(f32[264,128]{1,0:T(8,128)S(1)} %own_rows.1.refs_0_), channel_id=1, source_target_pairs={{0,2},{1,3},{2,0},{3,1},{4,6},{5,7},{6,4},{7,5},{8,10},{9,11},{10,... | collective-permute-start | bytes 405512 | tf_op jit(solution)/shard_map/ppermute | solution.py:532
  53.9 2.7 %collective-permute-start.15 = (f32[264,128]{1,0:T(8,128)S(1)}, f32[264,128]{1,0:T(8,128)S(1)}, u32[]{:S(2)}, u32[]{:S(2)}) collective-permute-start(f32[264,128]{1,0:T(8,128)S(1)} %own_rows.1.refs_0_), channel_id=1, source_target_pairs={{0,1},{1,0},{2,3},{3,2},{4,5},{5,4},{6,7},{7,6},{8,9},{9,8},{10,11... | collective-permute-start | bytes 405512 | tf_op jit(solution)/shard_map/ppermute | solution.py:532
  56.9 1.6 %collective-permute-start.18 = (f32[256,128]{1,0:T(8,128)S(1)}, f32[256,128]{1,0:T(8,128)S(1)}, u32[]{:S(2)}, u32[]{:S(2)}) collective-permute-start(f32[256,128]{1,0:T(8,128)S(1)} %add_all.1.refs_0_), channel_id=1, source_target_pairs={{0,16},{4,20},{8,24},{12,28},{16,0},{20,4},{24,8},{28,12},{1,17},{... | collective-permute-start | bytes 393224 | tf_op jit(solution)/shard_map/ppermute | solution.py:535
  58.9 3.0 %collective-permute-done.18.refs_2_ = f32[256,128]{1,0:T(8,128)S(1)} collective-permute-done((f32[256,128]{1,0:T(8,128)S(1)}, f32[256,128]{1,0:T(8,128)S(1)}, u32[]{:S(2)}, u32[]{:S(2)}) %collective-permute-start.18) | collective-permute-done | bytes 131104 | tf_op jit(solution)/shard_map/ppermute | solution.py:535
  61.9 1.6 %collective-permute-done.17.refs_1_ = f32[256,128]{1,0:T(8,128)S(1)} collective-permute-done((f32[256,128]{1,0:T(8,128)S(1)}, f32[256,128]{1,0:T(8,128)S(1)}, u32[]{:S(2)}, u32[]{:S(2)}) %collective-permute-start.17) | collective-permute-done | bytes 131104 | tf_op jit(solution)/shard_map/ppermute | solution.py:535
  63.6 1.6 %collective-permute-done.14.refs_1_ = f32[264,128]{1,0:T(8,128)S(1)} collective-permute-done((f32[264,128]{1,0:T(8,128)S(1)}, f32[264,128]{1,0:T(8,128)S(1)}, u32[]{:S(2)}, u32[]{:S(2)}) %collective-permute-start.14) | collective-permute-done | bytes 135200 | tf_op jit(solution)/shard_map/ppermute | solution.py:532
  65.5 1.2 %place_all.1 = (f32[1024,128]{1,0:T(8,128)}, f32[2048,128]{1,0:T(8,128)}, f32[16,64]{1,0:T(8,128)}) custom-call(f32[16,64]{1,0:T(8,128)S(1)} %gather_weights.1.weight_ref, f32[4,256,128]{2,1,0:T(8,128)S(1)} %stack_all.1.mine_ref, f32[4,256,128]{2,1,0:T(8,128)S(1)} %collective-permute-done.20.other_ref, f32[264,128]{1,0:T(8,128)S(1)} %own_rows.1.refs_0_, ...), custom_call_target="tpu_custom_call" | custom-call | tf_op jit(solution)/shard_map/place_all/pallas_call | solution.py:41
  (37 shorter events, 3.3 us)
Async XLA Ops:
  0.6 14.1 %copy-start = (bf16[2048,128]{1,0:T(8,128)(2,1)S(1)}, bf16[2048,128]{1,0:T(8,128)(2,1)}, u32[]{:S(2)}) copy-start(bf16[2048,128]{1,0:T(8,128)(2,1)} %keys_ref.9) | copy-start | bytes 1572868
  0.6 14.1 %copy-start.1 = (bf16[16,64,128]{2,1,0:T(8,128)(2,1)S(1)}, bf16[16,64,128]{2,1,0:T(8,128)(2,1)}, u32[]{:S(2)}) copy-start(bf16[16,64,128]{2,1,0:T(8,128)(2,1)} %query_ref.3) | copy-start | bytes 786436
  0.7 14.1 %copy-start.2 = (f32[16,64]{1,0:T(8,128)S(1)}, f32[16,64]{1,0:T(8,128)}, u32[]{:S(2)}) copy-start(f32[16,64]{1,0:T(8,128)} %weight_ref.5) | copy-start | bytes 12292
  0.7 14.1 %copy-start.3 = (s32[128]{0:T(128)S(1)}, s32[128]{0:T(128)}, u32[]{:S(2)}) copy-start(s32[128]{0:T(128)} %pos_ref.1) | copy-start | bytes 1540
  11.7 5.3 %collective-permute-start = (f32[8,256]{1,0:T(8,128)S(1)}, f32[8,256]{1,0:T(8,128)S(1)}, u32[]{:S(2)}, u32[]{:S(2)}) collective-permute-start(f32[8,256]{1,0:T(8,128)S(1)} %get-tuple-element.45._.left_ref), channel_id=1, source_target_pairs={{0,1},{1,0},{2,3},{3,2},{4,5},{5,4},{6,7},{7,6},{8,9},{9,8},{10,11... | collective-permute-start | bytes 24584 | tf_op jit(solution)/shard_map/ppermute | solution.py:532
  16.9 4.8 %collective-permute-start.1 = (f32[24,256]{1,0:T(8,128)S(1)}, f32[24,256]{1,0:T(8,128)S(1)}, u32[]{:S(2)}, u32[]{:S(2)}) collective-permute-start(f32[24,256]{1,0:T(8,128)S(1)} %join_first.1.left_ref), channel_id=1, source_target_pairs={{0,2},{1,3},{2,0},{3,1},{4,6},{5,7},{6,4},{7,5},{8,10},{9,11},{10,... | collective-permute-start | bytes 73736 | tf_op jit(solution)/shard_map/ppermute | solution.py:532
  21.8 8.5 %copy-start.4 = (f32[16]{0:T(128)S(1)}, f32[16]{0:T(128)}, u32[]{:S(2)}) copy-start(f32[16]{0:T(128)} %kl_ref.1) | copy-start | bytes 196
  23.2 2.0 %collective-permute-start.4 = (f32[4,16,2048]{2,1,0:T(8,128)S(1)}, f32[4,16,2048]{2,1,0:T(8,128)S(1)}, u32[]{:S(2)}, u32[]{:S(2)}) collective-permute-start(f32[4,16,2048]{2,1,0:T(8,128)S(1)} %get-tuple-element.62), channel_id=1, source_target_pairs={{0,4},{4,0},{8,12},{12,8},{16,20},{20,16},{24,28},{28,24},{1,5},{5... | collective-permute-start | bytes 1572872 | tf_op jit(solution)/shard_map/ppermute | solution.py:535
  23.2 9.4 %collective-permute-start.3 = (f32[1040,128]{1,0:T(8,128)S(1)}, f32[1040,128]{1,0:T(8,128)S(1)}, u32[]{:S(2)}, u32[]{:S(2)}) collective-permute-start(f32[1040,128]{1,0:T(8,128)S(1)} %get-tuple-element.57), channel_id=1, source_target_pairs={{0,4},{4,0},{8,12},{12,8},{16,20},{20,16},{24,28},{28,24},{1,5},{5... | collective-permute-start | bytes 1597448 | tf_op jit(solution)/shard_map/ppermute | solution.py:535
  25.2 9.1 %collective-permute-start.5 = (f32[16,2048]{1,0:T(8,128)S(1)}, f32[16,2048]{1,0:T(8,128)S(1)}, u32[]{:S(2)}, u32[]{:S(2)}) collective-permute-start(f32[16,2048]{1,0:T(8,128)S(1)} %get-tuple-element.64), channel_id=1, source_target_pairs={{0,24},{4,28},{8,16},{12,20},{16,8},{20,12},{24,0},{28,4},{1,25},{... | collective-permute-start | bytes 393224 | tf_op jit(solution)/shard_map/ppermute | solution.py:535
  27.7 6.8 %collective-permute-start.6 = (f32[16,2048]{1,0:T(8,128)S(1)}, f32[16,2048]{1,0:T(8,128)S(1)}, u32[]{:S(2)}, u32[]{:S(2)}) collective-permute-start(f32[16,2048]{1,0:T(8,128)S(1)} %get-tuple-element.65), channel_id=1, source_target_pairs={{0,16},{4,20},{8,24},{12,28},{16,0},{20,4},{24,8},{28,12},{1,17},{... | collective-permute-start | bytes 393224 | tf_op jit(solution)/shard_map/ppermute | solution.py:535
  28.2 6.4 %collective-permute-start.7 = (f32[16,2048]{1,0:T(8,128)S(1)}, f32[16,2048]{1,0:T(8,128)S(1)}, u32[]{:S(2)}, u32[]{:S(2)}) collective-permute-start(f32[16,2048]{1,0:T(8,128)S(1)} %get-tuple-element.66), channel_id=1, source_target_pairs={{0,8},{4,12},{8,0},{12,4},{16,24},{20,28},{24,16},{28,20},{1,9},{5... | collective-permute-start | bytes 393224 | tf_op jit(solution)/shard_map/ppermute | solution.py:535
  28.8 5.6 %collective-permute-start.2 = (f32[16,128]{1,0:T(8,128)S(1)}, f32[16,128]{1,0:T(8,128)S(1)}, u32[]{:S(2)}, u32[]{:S(2)}) collective-permute-start(f32[16,128]{1,0:T(8,128)S(1)} %get-tuple-element.56.lse_ref), channel_id=1, source_target_pairs={{0,1},{1,0},{2,3},{3,2},{4,5},{5,4},{6,7},{7,6},{8,9},{9,8},{10,11... | collective-permute-start | bytes 24584 | tf_op jit(solution)/shard_map/ppermute | solution.py:532
  35.6 8.2 %collective-permute-start.8 = (f32[2,256,128]{2,1,0:T(8,128)S(1)}, f32[2,256,128]{2,1,0:T(8,128)S(1)}, u32[]{:S(2)}, u32[]{:S(2)}) collective-permute-start(f32[2,256,128]{2,1,0:T(8,128)S(1)} %get-tuple-element.69), channel_id=1, source_target_pairs={{0,1},{1,0},{2,3},{3,2},{4,5},{5,4},{6,7},{7,6},{8,9},{9,8},{10,11... | collective-permute-start | bytes 786440 | tf_op jit(solution)/shard_map/ppermute | solution.py:532
  37.2 1.3 %collective-permute-start.9 = (f32[16,1024]{1,0:T(8,128)S(1)}, f32[16,1024]{1,0:T(8,128)S(1)}, u32[]{:S(2)}, u32[]{:S(2)}) collective-permute-start(f32[16,1024]{1,0:T(8,128)S(1)} %get-tuple-element.74), channel_id=1, source_target_pairs={{0,4},{4,0},{8,12},{12,8},{16,20},{20,16},{24,28},{28,24},{1,5},{5... | collective-permute-start | bytes 196616 | tf_op jit(solution)/shard_map/ppermute | solution.py:535
  39.6 7.3 %collective-permute-start.10 = (f32[256,128]{1,0:T(8,128)S(1)}, f32[256,128]{1,0:T(8,128)S(1)}, u32[]{:S(2)}, u32[]{:S(2)}) collective-permute-start(f32[256,128]{1,0:T(8,128)S(1)} %get-tuple-element.78), channel_id=1, source_target_pairs={{0,24},{4,28},{8,16},{12,20},{16,8},{20,12},{24,0},{28,4},{1,25},{... | collective-permute-start | bytes 393224 | tf_op jit(solution)/shard_map/ppermute | solution.py:535
  41.3 7.6 %collective-permute-start.11 = (f32[256,128]{1,0:T(8,128)S(1)}, f32[256,128]{1,0:T(8,128)S(1)}, u32[]{:S(2)}, u32[]{:S(2)}) collective-permute-start(f32[256,128]{1,0:T(8,128)S(1)} %get-tuple-element.79), channel_id=1, source_target_pairs={{0,16},{4,20},{8,24},{12,28},{16,0},{20,4},{24,8},{28,12},{1,17},{... | collective-permute-start | bytes 393224 | tf_op jit(solution)/shard_map/ppermute | solution.py:535
  42.6 6.3 %collective-permute-start.12 = (f32[256,128]{1,0:T(8,128)S(1)}, f32[256,128]{1,0:T(8,128)S(1)}, u32[]{:S(2)}, u32[]{:S(2)}) collective-permute-start(f32[256,128]{1,0:T(8,128)S(1)} %get-tuple-element.80), channel_id=1, source_target_pairs={{0,8},{4,12},{8,0},{12,4},{16,24},{20,28},{24,16},{28,20},{1,9},{5... | collective-permute-start | bytes 393224 | tf_op jit(solution)/shard_map/ppermute | solution.py:535
  43.9 8.2 %collective-permute-start.13 = (f32[1,256,128]{2,1,0:T(8,128)S(1)}, f32[1,256,128]{2,1,0:T(8,128)S(1)}, u32[]{:S(2)}, u32[]{:S(2)}) collective-permute-start(f32[1,256,128]{2,1,0:T(8,128)S(1)} %get-tuple-element.82), channel_id=1, source_target_pairs={{0,2},{1,3},{2,0},{3,1},{4,6},{5,7},{6,4},{7,5},{8,10},{9,11},{10,... | collective-permute-start | bytes 393224 | tf_op jit(solution)/shard_map/ppermute | solution.py:532
  49.0 9.6 %collective-permute-start.19 = (f32[256,128]{1,0:T(8,128)S(1)}, f32[256,128]{1,0:T(8,128)S(1)}, u32[]{:S(2)}, u32[]{:S(2)}) collective-permute-start(f32[256,128]{1,0:T(8,128)S(1)} %add_all.1.refs_0_), channel_id=1, source_target_pairs={{0,24},{4,28},{8,16},{12,20},{16,8},{20,12},{24,0},{28,4},{1,25},{... | collective-permute-start | bytes 393224 | tf_op jit(solution)/shard_map/ppermute | solution.py:535
  52.5 11.1 %collective-permute-start.16 = (f32[264,128]{1,0:T(8,128)S(1)}, f32[264,128]{1,0:T(8,128)S(1)}, u32[]{:S(2)}, u32[]{:S(2)}) collective-permute-start(f32[264,128]{1,0:T(8,128)S(1)} %own_rows.1.refs_0_), channel_id=1, source_target_pairs={{0,2},{1,3},{2,0},{3,1},{4,6},{5,7},{6,4},{7,5},{8,10},{9,11},{10,... | collective-permute-start | bytes 405512 | tf_op jit(solution)/shard_map/ppermute | solution.py:532
  53.9 9.7 %collective-permute-start.15 = (f32[264,128]{1,0:T(8,128)S(1)}, f32[264,128]{1,0:T(8,128)S(1)}, u32[]{:S(2)}, u32[]{:S(2)}) collective-permute-start(f32[264,128]{1,0:T(8,128)S(1)} %own_rows.1.refs_0_), channel_id=1, source_target_pairs={{0,1},{1,0},{2,3},{3,2},{4,5},{5,4},{6,7},{7,6},{8,9},{9,8},{10,11... | collective-permute-start | bytes 405512 | tf_op jit(solution)/shard_map/ppermute | solution.py:532
  56.6 8.6 %collective-permute-start.14 = (f32[264,128]{1,0:T(8,128)S(1)}, f32[264,128]{1,0:T(8,128)S(1)}, u32[]{:S(2)}, u32[]{:S(2)}) collective-permute-start(f32[264,128]{1,0:T(8,128)S(1)} %own_rows.1.refs_0_), channel_id=1, source_target_pairs={{0,3},{1,2},{2,1},{3,0},{4,7},{5,6},{6,5},{7,4},{8,11},{9,10},{10,... | collective-permute-start | bytes 405512 | tf_op jit(solution)/shard_map/ppermute | solution.py:532
  56.9 5.0 %collective-permute-start.18 = (f32[256,128]{1,0:T(8,128)S(1)}, f32[256,128]{1,0:T(8,128)S(1)}, u32[]{:S(2)}, u32[]{:S(2)}) collective-permute-start(f32[256,128]{1,0:T(8,128)S(1)} %add_all.1.refs_0_), channel_id=1, source_target_pairs={{0,16},{4,20},{8,24},{12,28},{16,0},{20,4},{24,8},{28,12},{1,17},{... | collective-permute-start | bytes 393224 | tf_op jit(solution)/shard_map/ppermute | solution.py:535
  58.5 5.0 %collective-permute-start.17 = (f32[256,128]{1,0:T(8,128)S(1)}, f32[256,128]{1,0:T(8,128)S(1)}, u32[]{:S(2)}, u32[]{:S(2)}) collective-permute-start(f32[256,128]{1,0:T(8,128)S(1)} %add_all.1.refs_0_), channel_id=1, source_target_pairs={{0,8},{4,12},{8,0},{12,4},{16,24},{20,28},{24,16},{28,20},{1,9},{5... | collective-permute-start | bytes 393224 | tf_op jit(solution)/shard_map/ppermute | solution.py:535
  63.5 2.0 %collective-permute-start.20 = (f32[4,256,128]{2,1,0:T(8,128)S(1)}, f32[4,256,128]{2,1,0:T(8,128)S(1)}, u32[]{:S(2)}, u32[]{:S(2)}) collective-permute-start(f32[4,256,128]{2,1,0:T(8,128)S(1)} %stack_all.1.mine_ref), channel_id=1, source_target_pairs={{0,4},{4,0},{8,12},{12,8},{16,20},{20,16},{24,28},{28,24},{1,5},{5... | collective-permute-start | bytes 1572872 | tf_op jit(solution)/shard_map/ppermute | solution.py:535

commit v7 on v6

--- a/solution.py
+++ b/solution.py
@@ -16,7 +16,6 @@
 F32 = jnp.float32
 BF16 = jnp.bfloat16
 MIB = 1024 * 1024
-SHORT = 0
 LONG = 4 * 10**10
 
 vmem_spec = pl.BlockSpec(memory_space=pltpu.VMEM)
@@ -164,7 +163,7 @@
     per = 256 // queries if queries < 256 and head_local % (256 // queries) == 0 else 1
     lanes = per * queries
     blocks = head_local // per
-    many = 2 if blocks % 2 == 0 else 1
+    many = 4 if blocks % 4 == 0 else 1
     tile = tile_of(keys, 128)
     tiles = keys // tile
     mask_at = -(-feature // 128) * 128
@@ -284,21 +283,29 @@
 
 
 def add_all(parts):
+    count, width = parts[0].shape
+
     def body(*refs):
         total = refs[0][...]
-        for ref in refs[1:-1]:
+        for ref in refs[1:-2]:
             total = total + ref[...]
-        refs[-1][...] = total
-
-    return vmem_call(body, "add_all", pltpu.VMEM(parts[0].shape, F32), parts)
-
-
-def stack_all(parts):
+        refs[-2][...] = total
+        refs[-1][:count, :] = total
+        refs[-1][count:, :] = jnp.zeros((16, width), F32)
+
+    outs = (pltpu.VMEM((count, width), F32), pltpu.VMEM((count + 16, width), F32))
+    return vmem_call(body, "add_all", outs, parts)
+
+
+def stack_chips(parts):
+    chunk, width = parts[0].shape
+
     def body(*refs):
+        chip, _ = head_place()
         for r, ref in enumerate(refs[:-1]):
-            refs[-1][r] = ref[...]
-
-    return vmem_call(body, "stack_all", pltpu.VMEM((len(parts), *parts[0].shape), F32), parts)
+            refs[-1][pl.ds(pl.multiple_of((chip ^ r) * chunk, chunk), chunk), :] = ref[:chunk, :]
+
+    return vmem_call(body, "stack_chips", pltpu.VMEM((len(parts) * chunk, width), F32), parts)
 
 
 def join_first(left, right, below):
@@ -482,24 +489,21 @@
 
 def place_all(pieces, weights, mine, other):
     rows, heads = weights.shape
-    own = rows // len(pieces)
-    size = own * heads
+    size = rows // len(pieces) * heads
     order = list(pieces)
     count = len(order)
-    chips, chunk, width = mine.shape
+    half, width = mine.shape
 
     def body(weight_ref, mine_ref, other_ref, *refs):
         piece_refs, (query_out, key_out, weight_out, sems) = refs[:count], refs[count:]
         z = lax.axis_index("keys")
-        chip, core = head_place()
+        _, core = head_place()
         pairs = [(weight_ref, weight_out)]
         for r, ref in zip(order, piece_refs):
             at = pl.multiple_of((z ^ r) * size, size)
             pairs.append((ref.at[:size], query_out.at[pl.ds(at, size)]))
         for ref, side in ((mine_ref, core), (other_ref, 1 - core)):
-            for r in range(chips):
-                at = pl.multiple_of(side * (chips * chunk) + (chip ^ r) * chunk, chunk)
-                pairs.append((ref.at[r], key_out.at[pl.ds(at, chunk)]))
+            pairs.append((ref, key_out.at[pl.ds(pl.multiple_of(side * half, half), half)]))
         copies = [pltpu.make_async_copy(*pair, sems.at[n]) for n, pair in enumerate(pairs)]
         for copy in copies:
             copy.start()
@@ -511,11 +515,11 @@
         "place_all",
         (
             jax.ShapeDtypeStruct((rows * heads, width), F32),
-            jax.ShapeDtypeStruct((2 * chips * chunk, width), F32),
+            jax.ShapeDtypeStruct((2 * half, width), F32),
             jax.ShapeDtypeStruct((rows, heads), F32),
         ),
         (weights, mine, other, *pieces.values()),
-        [pltpu.SemaphoreType.DMA((1 + count + 2 * chips,))],
+        [pltpu.SemaphoreType.DMA((3 + count,))],
         out_specs=(any_spec,) * 3,
     )
     return query.reshape(rows, heads, width), key, weight
@@ -560,7 +564,7 @@
 
     bits, other_odd = 1, to_keys(odd, 1)
     parts = key_part(slopes, wiq, to_heads(across, 1), other_gate, other_wiq, chips)
-    key_own = add_all([parts[0]] + [to_heads(parts[r], 2 * r) for r in chip_order])
+    key_own, key_wide = add_all([parts[0]] + [to_heads(parts[r], 2 * r) for r in chip_order])
     while bits < key_devices // 2:
         even, odd = add_halve(even, other_odd)
         bits *= 2
@@ -568,9 +572,9 @@
     even, key_own = lax.optimization_barrier((even, key_own))
     query_own = own_rows(even, other_odd, index_query, index_weight)
     pieces = {0: query_own, **{r: to_keys(query_own, r) for r in key_order}}
-    mine = {r: to_heads(key_own, 2 * r) for r in range(1, chips)}
+    mine = {r: to_heads(key_own if r == chips - 1 else key_wide, 2 * r) for r in range(1, chips)}
     mine = [key_own] + [mine[r] for r in range(1, chips)]
-    mine = stack_all(mine)
+    mine = stack_chips(mine)
     weights = gather_weights(pieces, row_local, index_heads)
     return place_all(pieces, weights, mine, to_heads(mine, 1))
 

time: 67.1 us -> 66.4 us (0.990)
  transfers between devices with their start and end apart: 21 -> 21, of which waited for: 13 -> 12; matrix products, arithmetic and copies ran while one was open for 0% -> 0% of each run, Pallas kernels for 13% -> 13%
where the time goes in v7:
time: 66.4 us; the launch traced here: 66.2 us
  starting transfers between devices  27.3 us (41%)
  Pallas kernels  22.9 us (34%)
  waiting for transfers between devices  15 us (23%)
  between operations  0.96 us (1%)
    ppermute x8, starting transfers between devices, to_keys(): lax.ppermute(value, 'keys', [(i, i ^ bits) for i in range(key_devices)])  15.9 us
    pallas_call x16, Pallas kernels, vmem_call(): pl.pallas_call(body, out_shape=outs, in_specs=[smem_spec] * len(scalars)...  12.3 us
    ppermute x13, starting transfers between devices, to_heads(): lax.ppermute(value, 'heads', [(i, i ^ bits) for i in range(head_devices)])  11.5 us
    pallas_call x1, Pallas kernels, main_scores(): pl.pallas_call(body, grid=(blocks // many,), out_shape=(pltpu.VMEM((block...  10.6 us
    ppermute x13, waiting for transfers between devices, to_heads(): lax.ppermute(value, 'heads', [(i, i ^ bits) for i in range(head_devices)])  9.02 us
    ppermute x8, waiting for transfers between devices, to_keys(): lax.ppermute(value, 'keys', [(i, i ^ bits) for i in range(key_devices)])  5.97 us
  transfers between devices with their start and end apart: 21, of which 12 were waited for; matrix products, arithmetic and copies ran while one was open for 0% of the time, Pallas kernels for 13%

profile of v7, /device:TPU:0, one launch (start us, length us, event | category | flops | bytes accessed | tf_op | source)
XLA Modules:
  0.0 66.2 jit_solution(7591909735833239765)
XLA Ops:
  0.7 10.6 %main_scores.1 = (f32[8,2048,256]{2,1,0:T(8,128)S(1)}, f32[8,16,256]{2,1,0:T(8,128)S(1)}, f32[8,256]{1,0:T(8,128)S(1)}) custom-call(s32[1,128]{1,0:T(1,128)} %bitcast.4, bf16[16,576,128]{2,1,0:T(8,128)(2,1)} %bitcast.5, bf16[576,2048]{1,0:T(8,128)(2,1)} %bitcast.6), custom_call_target="tpu_custom_call" | custom-call | tf_op jit(solution)/shard_map/main_scores/pallas_call | solution.py:215
  11.3 3.1 %collective-permute-start = (f32[8,256]{1,0:T(8,128)S(1)}, f32[8,256]{1,0:T(8,128)S(1)}, u32[]{:S(2)}, u32[]{:S(2)}) collective-permute-start(f32[8,256]{1,0:T(8,128)S(1)} %get-tuple-element.47._.left_ref), channel_id=1, source_target_pairs={{0,1},{1,0},{2,3},{3,2},{4,5},{5,4},{6,7},{7,6},{8,9},{9,8},{10,11... | collective-permute-start | bytes 24584 | tf_op jit(solution)/shard_map/ppermute | solution.py:536
  14.4 2.1 %index_forward.1 = (f32[16,2048]{1,0:T(8,128)S(1)}, f32[16,128]{1,0:T(8,128)S(1)}, f32[1040,128]{1,0:T(8,128)S(1)}) custom-call(s32[128]{0:T(128)S(1)} %copy-done.3, bf16[16,64,128]{2,1,0:T(8,128)(2,1)S(1)} %copy-done.1, bf16[2048,128]{1,0:T(8,128)(2,1)S(1)} %copy-done, f32[16,64]{1,0:T(8,128)S(1)} %copy-done.2, f32[8,256]{1,0:T(8,128)S(1)} %get-tuple-element.47._.left_ref), custom_call_target="tpu_custom_call" | custom-call | tf_op jit(solution)/shard_map/index_forward/pallas_call | solution.py:40
  16.6 2.7 %collective-permute-start.1 = (f32[24,256]{1,0:T(8,128)S(1)}, f32[24,256]{1,0:T(8,128)S(1)}, u32[]{:S(2)}, u32[]{:S(2)}) collective-permute-start(f32[24,256]{1,0:T(8,128)S(1)} %join_first.1.left_ref), channel_id=1, source_target_pairs={{0,2},{1,3},{2,0},{3,1},{4,6},{5,7},{6,4},{7,5},{8,10},{9,11},{10,... | collective-permute-start | bytes 73736 | tf_op jit(solution)/shard_map/ppermute | solution.py:536
  19.2 2.1 %collective-permute-done.1.right_ref = f32[24,256]{1,0:T(8,128)S(1)} collective-permute-done((f32[24,256]{1,0:T(8,128)S(1)}, f32[24,256]{1,0:T(8,128)S(1)}, u32[]{:S(2)}, u32[]{:S(2)}) %collective-permute-start.1) | collective-permute-done | bytes 24608 | tf_op jit(solution)/shard_map/ppermute | solution.py:536
  21.4 1.4 %head_sum.1 = (f32[4,16,2048]{2,1,0:T(8,128)S(1)}, f32[4,16,2048]{2,1,0:T(8,128)S(1)}) custom-call(f32[8,2048,256]{2,1,0:T(8,128)S(1)} %get-tuple-element.50.prob_ref, f32[8,16,256]{2,1,0:T(8,128)S(1)} %get-tuple-element.51.top_ref, f32[8,256]{1,0:T(8,128)S(1)} %get-tuple-element.52.stat_ref), custom_call_target="tpu_custom_call" | custom-call | flops 1000000000 | tf_op jit(solution)/shard_map/head_sum/pallas_call | solution.py:40
  23.4 1.4 %collective-permute-done.4.right_ref = f32[4,16,2048]{2,1,0:T(8,128)S(1)} collective-permute-done((f32[4,16,2048]{2,1,0:T(8,128)S(1)}, f32[4,16,2048]{2,1,0:T(8,128)S(1)}, u32[]{:S(2)}, u32[]{:S(2)}) %collective-permute-start.4) | collective-permute-done | bytes 524320 | tf_op jit(solution)/shard_map/ppermute | solution.py:539
  24.8 2.5 %collective-permute-start.5 = (f32[16,2048]{1,0:T(8,128)S(1)}, f32[16,2048]{1,0:T(8,128)S(1)}, u32[]{:S(2)}, u32[]{:S(2)}) collective-permute-start(f32[16,2048]{1,0:T(8,128)S(1)} %get-tuple-element.66), channel_id=1, source_target_pairs={{0,24},{4,28},{8,16},{12,20},{16,8},{20,12},{24,0},{28,4},{1,25},{... | collective-permute-start | bytes 393224 | tf_op jit(solution)/shard_map/ppermute | solution.py:539
  27.8 0.5 collective-permute-start.7
  28.4 1.5 %collective-permute-start.2 = (f32[16,128]{1,0:T(8,128)S(1)}, f32[16,128]{1,0:T(8,128)S(1)}, u32[]{:S(2)}, u32[]{:S(2)}) collective-permute-start(f32[16,128]{1,0:T(8,128)S(1)} %get-tuple-element.58.lse_ref), channel_id=1, source_target_pairs={{0,1},{1,0},{2,3},{3,2},{4,5},{5,4},{6,7},{7,6},{8,9},{9,8},{10,11... | collective-permute-start | bytes 24584 | tf_op jit(solution)/shard_map/ppermute | solution.py:536
  29.9 2.4 %index_signs.1 = (bf16[4,256,2048]{2,1,0:T(8,128)(2,1)S(1)}, bf16[4,128,256]{2,1,0:T(8,128)(2,1)S(1)}, f32[16,128]{1,0:T(8,128)S(1)}) custom-call(f32[16]{0:T(128)S(1)} %copy-done.4, bf16[16,64,128]{2,1,0:T(8,128)(2,1)S(1)} %copy-done.1, bf16[2048,128]{1,0:T(8,128)(2,1)S(1)} %copy-done, f32[16,64]{1,0:T(8,128)S(1)} %copy-done.2), custom_call_target="tpu_custom_call" | custom-call | tf_op jit(solution)/shard_map/index_signs/pallas_call | solution.py:40
  32.2 1.7 %other_signs.1 = (bf16[1024,1024]{1,0:T(8,128)(2,1)S(1)}, bf16[128,1024]{1,0:T(8,128)(2,1)S(1)}) custom-call(f32[1040,128]{1,0:T(8,128)S(1)} %collective-permute-done.3.pack_ref, bf16[2048,128]{1,0:T(8,128)(2,1)S(1)} %copy-done), custom_call_target="tpu_custom_call" | custom-call | tf_op jit(solution)/shard_map/other_signs/pallas_call | solution.py:40
  34.2 1.0 %query_part.1 = (f32[2,256,128]{2,1,0:T(8,128)S(1)}, bf16[512,2048]{1,0:T(8,128)(2,1)S(1)}, f32[4,4,2048]{2,1,0:T(4,128)S(1)}, f32[16,1024]{1,0:T(8,128)S(1)}) custom-call(f32[16,2048]{1,0:T(8,128)S(1)} %get-tuple-element.56.score_ref, f32[16,128]{1,0:T(8,128)S(1)} %get-tuple-element.57.kl_ref, f32[16,128]{1,0:T(8,128)S(1)} %get-tuple-element.58.lse_ref, ...), custom_call_target="tpu_custom_call" | custom-call | tf_op jit(solution)/shard_map/query_part/pallas_call | solution.py:40
  35.3 1.6 %collective-permute-start.8 = (f32[2,256,128]{2,1,0:T(8,128)S(1)}, f32[2,256,128]{2,1,0:T(8,128)S(1)}, u32[]{:S(2)}, u32[]{:S(2)}) collective-permute-start(f32[2,256,128]{2,1,0:T(8,128)S(1)} %get-tuple-element.71), channel_id=1, source_target_pairs={{0,1},{1,0},{2,3},{3,2},{4,5},{5,4},{6,7},{7,6},{8,9},{9,8},{10,11... | collective-permute-start | bytes 786440 | tf_op jit(solution)/shard_map/ppermute | solution.py:536
  36.8 0.7 %query_rest.1 = (f32[2,256,128]{2,1,0:T(8,128)S(1)}, bf16[512,2048]{1,0:T(8,128)(2,1)S(1)}) custom-call(f32[4,4,2048]{2,1,0:T(4,128)S(1)} %get-tuple-element.69.delta_ref, bf16[4,256,2048]{2,1,0:T(8,128)(2,1)S(1)} %get-tuple-element.62.gate_ref, bf16[2048,128]{1,0:T(8,128)(2,1)S(1)} %copy-done), custom_call_target="tpu_custom_call" | custom-call | tf_op jit(solution)/shard_map/query_rest/pallas_call | solution.py:40
  37.5 0.5 collective-permute-done.9.delta_ref
  38.1 1.2 %key_part.1 = (f32[256,128]{1,0:T(8,128)S(1)}, f32[256,128]{1,0:T(8,128)S(1)}, f32[256,128]{1,0:T(8,128)S(1)}, f32[256,128]{1,0:T(8,128)S(1)}) custom-call(bf16[512,2048]{1,0:T(8,128)(2,1)S(1)} %get-tuple-element.73.odd_ref, bf16[512,2048]{1,0:T(8,128)(2,1)S(1)} %get-tuple-element.74.even_ref, bf16[4,128,256]{2,1,0:T(8,128)(2,1)S(1)} %get-tuple-element.75.wiq_ref, ...), custom_call_target="tpu_custom_call" | custom-call | tf_op jit(solution)/shard_map/key_part/pallas_call | solution.py:40
  39.2 1.7 %collective-permute-start.10 = (f32[256,128]{1,0:T(8,128)S(1)}, f32[256,128]{1,0:T(8,128)S(1)}, u32[]{:S(2)}, u32[]{:S(2)}) collective-permute-start(f32[256,128]{1,0:T(8,128)S(1)} %get-tuple-element.80), channel_id=1, source_target_pairs={{0,24},{4,28},{8,16},{12,20},{16,8},{20,12},{24,0},{28,4},{1,25},{... | collective-permute-start | bytes 393224 | tf_op jit(solution)/shard_map/ppermute | solution.py:539
  41.0 1.3 %collective-permute-start.11 = (f32[256,128]{1,0:T(8,128)S(1)}, f32[256,128]{1,0:T(8,128)S(1)}, u32[]{:S(2)}, u32[]{:S(2)}) collective-permute-start(f32[256,128]{1,0:T(8,128)S(1)} %get-tuple-element.81), channel_id=1, source_target_pairs={{0,16},{4,20},{8,24},{12,28},{16,0},{20,4},{24,8},{28,12},{1,17},{... | collective-permute-start | bytes 393224 | tf_op jit(solution)/shard_map/ppermute | solution.py:539
  42.3 0.5 collective-permute-start.12
  42.8 0.7 %collective-permute-done.8.right_ref = f32[2,256,128]{2,1,0:T(8,128)S(1)} collective-permute-done((f32[2,256,128]{2,1,0:T(8,128)S(1)}, f32[2,256,128]{2,1,0:T(8,128)S(1)}, u32[]{:S(2)}, u32[]{:S(2)}) %collective-permute-start.8) | collective-permute-done | bytes 262176 | tf_op jit(solution)/shard_map/ppermute | solution.py:536
  43.5 2.7 %collective-permute-start.13 = (f32[1,256,128]{2,1,0:T(8,128)S(1)}, f32[1,256,128]{2,1,0:T(8,128)S(1)}, u32[]{:S(2)}, u32[]{:S(2)}) collective-permute-start(f32[1,256,128]{2,1,0:T(8,128)S(1)} %get-tuple-element.85), channel_id=1, source_target_pairs={{0,2},{1,3},{2,0},{3,1},{4,6},{5,7},{6,4},{7,5},{8,10},{9,11},{10,... | collective-permute-start | bytes 393224 | tf_op jit(solution)/shard_map/ppermute | solution.py:536
  46.6 2.0 %collective-permute-done.11.refs_2_ = f32[256,128]{1,0:T(8,128)S(1)} collective-permute-done((f32[256,128]{1,0:T(8,128)S(1)}, f32[256,128]{1,0:T(8,128)S(1)}, u32[]{:S(2)}, u32[]{:S(2)}) %collective-permute-start.11) | collective-permute-done | bytes 131104 | tf_op jit(solution)/shard_map/ppermute | solution.py:539
  48.6 1.5 %collective-permute-start.18 = (f32[272,128]{1,0:T(8,128)S(1)}, f32[272,128]{1,0:T(8,128)S(1)}, u32[]{:S(2)}, u32[]{:S(2)}) collective-permute-start(f32[272,128]{1,0:T(8,128)S(1)} %get-tuple-element.87), channel_id=1, source_target_pairs={{0,16},{4,20},{8,24},{12,28},{16,0},{20,4},{24,8},{28,12},{1,17},{... | collective-permute-start | bytes 417800 | tf_op jit(solution)/shard_map/ppermute | solution.py:539
  50.1 0.8 %collective-permute-start.17 = (f32[272,128]{1,0:T(8,128)S(1)}, f32[272,128]{1,0:T(8,128)S(1)}, u32[]{:S(2)}, u32[]{:S(2)}) collective-permute-start(f32[272,128]{1,0:T(8,128)S(1)} %get-tuple-element.87), channel_id=1, source_target_pairs={{0,8},{4,12},{8,0},{12,4},{16,24},{20,28},{24,16},{28,20},{1,9},{5... | collective-permute-start | bytes 417800 | tf_op jit(solution)/shard_map/ppermute | solution.py:539
  50.9 0.9 %collective-permute-done.13.right_ref = f32[1,256,128]{2,1,0:T(8,128)S(1)} collective-permute-done((f32[1,256,128]{2,1,0:T(8,128)S(1)}, f32[1,256,128]{2,1,0:T(8,128)S(1)}, u32[]{:S(2)}, u32[]{:S(2)}) %collective-permute-start.13) | collective-permute-done | bytes 131104 | tf_op jit(solution)/shard_map/ppermute | solution.py:536
  52.1 2.0 %collective-permute-start.16 = (f32[264,128]{1,0:T(8,128)S(1)}, f32[264,128]{1,0:T(8,128)S(1)}, u32[]{:S(2)}, u32[]{:S(2)}) collective-permute-start(f32[264,128]{1,0:T(8,128)S(1)} %own_rows.1.refs_0_), channel_id=1, source_target_pairs={{0,2},{1,3},{2,0},{3,1},{4,6},{5,7},{6,4},{7,5},{8,10},{9,11},{10,... | collective-permute-start | bytes 405512 | tf_op jit(solution)/shard_map/ppermute | solution.py:536
  54.1 2.1 %collective-permute-start.15 = (f32[264,128]{1,0:T(8,128)S(1)}, f32[264,128]{1,0:T(8,128)S(1)}, u32[]{:S(2)}, u32[]{:S(2)}) collective-permute-start(f32[264,128]{1,0:T(8,128)S(1)} %own_rows.1.refs_0_), channel_id=1, source_target_pairs={{0,1},{1,0},{2,3},{3,2},{4,5},{5,4},{6,7},{7,6},{8,9},{9,8},{10,11... | collective-permute-start | bytes 405512 | tf_op jit(solution)/shard_map/ppermute | solution.py:536
  56.5 1.4 %collective-permute-start.19 = (f32[256,128]{1,0:T(8,128)S(1)}, f32[256,128]{1,0:T(8,128)S(1)}, u32[]{:S(2)}, u32[]{:S(2)}) collective-permute-start(f32[256,128]{1,0:T(8,128)S(1)} %get-tuple-element.86.refs_0_), channel_id=1, source_target_pairs={{0,24},{4,28},{8,16},{12,20},{16,8},{20,12},{24,0},{28,4},{1,25},{... | collective-permute-start | bytes 393224 | tf_op jit(solution)/shard_map/ppermute | solution.py:539
  57.9 4.4 %collective-permute-done.19.refs_3_ = f32[256,128]{1,0:T(8,128)S(1)} collective-permute-done((f32[256,128]{1,0:T(8,128)S(1)}, f32[256,128]{1,0:T(8,128)S(1)}, u32[]{:S(2)}, u32[]{:S(2)}) %collective-permute-start.19) | collective-permute-done | bytes 131104 | tf_op jit(solution)/shard_map/ppermute | solution.py:539
  62.8 2.0 %collective-permute-done.14.refs_1_ = f32[264,128]{1,0:T(8,128)S(1)} collective-permute-done((f32[264,128]{1,0:T(8,128)S(1)}, f32[264,128]{1,0:T(8,128)S(1)}, u32[]{:S(2)}, u32[]{:S(2)}) %collective-permute-start.14) | collective-permute-done | bytes 135200 | tf_op jit(solution)/shard_map/ppermute | solution.py:536
  64.8 1.2 %place_all.1 = (f32[1024,128]{1,0:T(8,128)}, f32[2048,128]{1,0:T(8,128)}, f32[16,64]{1,0:T(8,128)}) custom-call(f32[16,64]{1,0:T(8,128)S(1)} %gather_weights.1.weight_ref, f32[1024,128]{1,0:T(8,128)S(1)} %stack_chips.1.mine_ref, f32[1024,128]{1,0:T(8,128)S(1)} %collective-permute-done.20.other_ref, f32[264,128]{1,0:T(8,128)S(1)} %own_rows.1.refs_0_, ...), custom_call_target="tpu_custom_call" | custom-call | tf_op jit(solution)/shard_map/place_all/pallas_call | solution.py:40
  (37 shorter events, 3.0 us)
Async XLA Ops:
  0.6 13.8 %copy-start = (bf16[2048,128]{1,0:T(8,128)(2,1)S(1)}, bf16[2048,128]{1,0:T(8,128)(2,1)}, u32[]{:S(2)}) copy-start(bf16[2048,128]{1,0:T(8,128)(2,1)} %keys_ref.9) | copy-start | bytes 1572868
  0.6 13.7 %copy-start.1 = (bf16[16,64,128]{2,1,0:T(8,128)(2,1)S(1)}, bf16[16,64,128]{2,1,0:T(8,128)(2,1)}, u32[]{:S(2)}) copy-start(bf16[16,64,128]{2,1,0:T(8,128)(2,1)} %query_ref.3) | copy-start | bytes 786436
  0.7 13.7 %copy-start.2 = (f32[16,64]{1,0:T(8,128)S(1)}, f32[16,64]{1,0:T(8,128)}, u32[]{:S(2)}) copy-start(f32[16,64]{1,0:T(8,128)} %weight_ref.5) | copy-start | bytes 12292
  0.7 13.7 %copy-start.3 = (s32[128]{0:T(128)S(1)}, s32[128]{0:T(128)}, u32[]{:S(2)}) copy-start(s32[128]{0:T(128)} %pos_ref.1) | copy-start | bytes 1540
  11.3 5.2 %collective-permute-start = (f32[8,256]{1,0:T(8,128)S(1)}, f32[8,256]{1,0:T(8,128)S(1)}, u32[]{:S(2)}, u32[]{:S(2)}) collective-permute-start(f32[8,256]{1,0:T(8,128)S(1)} %get-tuple-element.47._.left_ref), channel_id=1, source_target_pairs={{0,1},{1,0},{2,3},{3,2},{4,5},{5,4},{6,7},{7,6},{8,9},{9,8},{10,11... | collective-permute-start | bytes 24584 | tf_op jit(solution)/shard_map/ppermute | solution.py:536
  16.6 4.8 %collective-permute-start.1 = (f32[24,256]{1,0:T(8,128)S(1)}, f32[24,256]{1,0:T(8,128)S(1)}, u32[]{:S(2)}, u32[]{:S(2)}) collective-permute-start(f32[24,256]{1,0:T(8,128)S(1)} %join_first.1.left_ref), channel_id=1, source_target_pairs={{0,2},{1,3},{2,0},{3,1},{4,6},{5,7},{6,4},{7,5},{8,10},{9,11},{10,... | collective-permute-start | bytes 73736 | tf_op jit(solution)/shard_map/ppermute | solution.py:536
  21.4 8.5 %copy-start.4 = (f32[16]{0:T(128)S(1)}, f32[16]{0:T(128)}, u32[]{:S(2)}) copy-start(f32[16]{0:T(128)} %kl_ref.1) | copy-start | bytes 196
  22.8 2.0 %collective-permute-start.4 = (f32[4,16,2048]{2,1,0:T(8,128)S(1)}, f32[4,16,2048]{2,1,0:T(8,128)S(1)}, u32[]{:S(2)}, u32[]{:S(2)}) collective-permute-start(f32[4,16,2048]{2,1,0:T(8,128)S(1)} %get-tuple-element.64), channel_id=1, source_target_pairs={{0,4},{4,0},{8,12},{12,8},{16,20},{20,16},{24,28},{28,24},{1,5},{5... | collective-permute-start | bytes 1572872 | tf_op jit(solution)/shard_map/ppermute | solution.py:539
  22.9 9.4 %collective-permute-start.3 = (f32[1040,128]{1,0:T(8,128)S(1)}, f32[1040,128]{1,0:T(8,128)S(1)}, u32[]{:S(2)}, u32[]{:S(2)}) collective-permute-start(f32[1040,128]{1,0:T(8,128)S(1)} %get-tuple-element.59), channel_id=1, source_target_pairs={{0,4},{4,0},{8,12},{12,8},{16,20},{20,16},{24,28},{28,24},{1,5},{5... | collective-permute-start | bytes 1597448 | tf_op jit(solution)/shard_map/ppermute | solution.py:539
  24.8 9.1 %collective-permute-start.5 = (f32[16,2048]{1,0:T(8,128)S(1)}, f32[16,2048]{1,0:T(8,128)S(1)}, u32[]{:S(2)}, u32[]{:S(2)}) collective-permute-start(f32[16,2048]{1,0:T(8,128)S(1)} %get-tuple-element.66), channel_id=1, source_target_pairs={{0,24},{4,28},{8,16},{12,20},{16,8},{20,12},{24,0},{28,4},{1,25},{... | collective-permute-start | bytes 393224 | tf_op jit(solution)/shard_map/ppermute | solution.py:539
  27.3 6.8 %collective-permute-start.6 = (f32[16,2048]{1,0:T(8,128)S(1)}, f32[16,2048]{1,0:T(8,128)S(1)}, u32[]{:S(2)}, u32[]{:S(2)}) collective-permute-start(f32[16,2048]{1,0:T(8,128)S(1)} %get-tuple-element.67), channel_id=1, source_target_pairs={{0,16},{4,20},{8,24},{12,28},{16,0},{20,4},{24,8},{28,12},{1,17},{... | collective-permute-start | bytes 393224 | tf_op jit(solution)/shard_map/ppermute | solution.py:539
  27.8 6.4 %collective-permute-start.7 = (f32[16,2048]{1,0:T(8,128)S(1)}, f32[16,2048]{1,0:T(8,128)S(1)}, u32[]{:S(2)}, u32[]{:S(2)}) collective-permute-start(f32[16,2048]{1,0:T(8,128)S(1)} %get-tuple-element.68), channel_id=1, source_target_pairs={{0,8},{4,12},{8,0},{12,4},{16,24},{20,28},{24,16},{28,20},{1,9},{5... | collective-permute-start | bytes 393224 | tf_op jit(solution)/shard_map/ppermute | solution.py:539
  28.4 5.6 %collective-permute-start.2 = (f32[16,128]{1,0:T(8,128)S(1)}, f32[16,128]{1,0:T(8,128)S(1)}, u32[]{:S(2)}, u32[]{:S(2)}) collective-permute-start(f32[16,128]{1,0:T(8,128)S(1)} %get-tuple-element.58.lse_ref), channel_id=1, source_target_pairs={{0,1},{1,0},{2,3},{3,2},{4,5},{5,4},{6,7},{7,6},{8,9},{9,8},{10,11... | collective-permute-start | bytes 24584 | tf_op jit(solution)/shard_map/ppermute | solution.py:536
  35.3 8.2 %collective-permute-start.8 = (f32[2,256,128]{2,1,0:T(8,128)S(1)}, f32[2,256,128]{2,1,0:T(8,128)S(1)}, u32[]{:S(2)}, u32[]{:S(2)}) collective-permute-start(f32[2,256,128]{2,1,0:T(8,128)S(1)} %get-tuple-element.71), channel_id=1, source_target_pairs={{0,1},{1,0},{2,3},{3,2},{4,5},{5,4},{6,7},{7,6},{8,9},{9,8},{10,11... | collective-permute-start | bytes 786440 | tf_op jit(solution)/shard_map/ppermute | solution.py:536
  36.8 1.3 %collective-permute-start.9 = (f32[16,1024]{1,0:T(8,128)S(1)}, f32[16,1024]{1,0:T(8,128)S(1)}, u32[]{:S(2)}, u32[]{:S(2)}) collective-permute-start(f32[16,1024]{1,0:T(8,128)S(1)} %get-tuple-element.76), channel_id=1, source_target_pairs={{0,4},{4,0},{8,12},{12,8},{16,20},{20,16},{24,28},{28,24},{1,5},{5... | collective-permute-start | bytes 196616 | tf_op jit(solution)/shard_map/ppermute | solution.py:539
  39.2 7.3 %collective-permute-start.10 = (f32[256,128]{1,0:T(8,128)S(1)}, f32[256,128]{1,0:T(8,128)S(1)}, u32[]{:S(2)}, u32[]{:S(2)}) collective-permute-start(f32[256,128]{1,0:T(8,128)S(1)} %get-tuple-element.80), channel_id=1, source_target_pairs={{0,24},{4,28},{8,16},{12,20},{16,8},{20,12},{24,0},{28,4},{1,25},{... | collective-permute-start | bytes 393224 | tf_op jit(solution)/shard_map/ppermute | solution.py:539
  41.0 7.6 %collective-permute-start.11 = (f32[256,128]{1,0:T(8,128)S(1)}, f32[256,128]{1,0:T(8,128)S(1)}, u32[]{:S(2)}, u32[]{:S(2)}) collective-permute-start(f32[256,128]{1,0:T(8,128)S(1)} %get-tuple-element.81), channel_id=1, source_target_pairs={{0,16},{4,20},{8,24},{12,28},{16,0},{20,4},{24,8},{28,12},{1,17},{... | collective-permute-start | bytes 393224 | tf_op jit(solution)/shard_map/ppermute | solution.py:539
  42.3 6.3 %collective-permute-start.12 = (f32[256,128]{1,0:T(8,128)S(1)}, f32[256,128]{1,0:T(8,128)S(1)}, u32[]{:S(2)}, u32[]{:S(2)}) collective-permute-start(f32[256,128]{1,0:T(8,128)S(1)} %get-tuple-element.82), channel_id=1, source_target_pairs={{0,8},{4,12},{8,0},{12,4},{16,24},{20,28},{24,16},{28,20},{1,9},{5... | collective-permute-start | bytes 393224 | tf_op jit(solution)/shard_map/ppermute | solution.py:539
  43.5 8.2 %collective-permute-start.13 = (f32[1,256,128]{2,1,0:T(8,128)S(1)}, f32[1,256,128]{2,1,0:T(8,128)S(1)}, u32[]{:S(2)}, u32[]{:S(2)}) collective-permute-start(f32[1,256,128]{2,1,0:T(8,128)S(1)} %get-tuple-element.85), channel_id=1, source_target_pairs={{0,2},{1,3},{2,0},{3,1},{4,6},{5,7},{6,4},{7,5},{8,10},{9,11},{10,... | collective-permute-start | bytes 393224 | tf_op jit(solution)/shard_map/ppermute | solution.py:536
  48.6 7.9 %collective-permute-start.18 = (f32[272,128]{1,0:T(8,128)S(1)}, f32[272,128]{1,0:T(8,128)S(1)}, u32[]{:S(2)}, u32[]{:S(2)}) collective-permute-start(f32[272,128]{1,0:T(8,128)S(1)} %get-tuple-element.87), channel_id=1, source_target_pairs={{0,16},{4,20},{8,24},{12,28},{16,0},{20,4},{24,8},{28,12},{1,17},{... | collective-permute-start | bytes 417800 | tf_op jit(solution)/shard_map/ppermute | solution.py:539
  50.1 7.8 %collective-permute-start.17 = (f32[272,128]{1,0:T(8,128)S(1)}, f32[272,128]{1,0:T(8,128)S(1)}, u32[]{:S(2)}, u32[]{:S(2)}) collective-permute-start(f32[272,128]{1,0:T(8,128)S(1)} %get-tuple-element.87), channel_id=1, source_target_pairs={{0,8},{4,12},{8,0},{12,4},{16,24},{20,28},{24,16},{28,20},{1,9},{5... | collective-permute-start | bytes 417800 | tf_op jit(solution)/shard_map/ppermute | solution.py:539
  52.1 10.7 %collective-permute-start.16 = (f32[264,128]{1,0:T(8,128)S(1)}, f32[264,128]{1,0:T(8,128)S(1)}, u32[]{:S(2)}, u32[]{:S(2)}) collective-permute-start(f32[264,128]{1,0:T(8,128)S(1)} %own_rows.1.refs_0_), channel_id=1, source_target_pairs={{0,2},{1,3},{2,0},{3,1},{4,6},{5,7},{6,4},{7,5},{8,10},{9,11},{10,... | collective-permute-start | bytes 405512 | tf_op jit(solution)/shard_map/ppermute | solution.py:536
  54.1 8.7 %collective-permute-start.15 = (f32[264,128]{1,0:T(8,128)S(1)}, f32[264,128]{1,0:T(8,128)S(1)}, u32[]{:S(2)}, u32[]{:S(2)}) collective-permute-start(f32[264,128]{1,0:T(8,128)S(1)} %own_rows.1.refs_0_), channel_id=1, source_target_pairs={{0,1},{1,0},{2,3},{3,2},{4,5},{5,4},{6,7},{7,6},{8,9},{9,8},{10,11... | collective-permute-start | bytes 405512 | tf_op jit(solution)/shard_map/ppermute | solution.py:536
  56.2 8.6 %collective-permute-start.14 = (f32[264,128]{1,0:T(8,128)S(1)}, f32[264,128]{1,0:T(8,128)S(1)}, u32[]{:S(2)}, u32[]{:S(2)}) collective-permute-start(f32[264,128]{1,0:T(8,128)S(1)} %own_rows.1.refs_0_), channel_id=1, source_target_pairs={{0,3},{1,2},{2,1},{3,0},{4,7},{5,6},{6,5},{7,4},{8,11},{9,10},{10,... | collective-permute-start | bytes 405512 | tf_op jit(solution)/shard_map/ppermute | solution.py:536
  56.5 5.9 %collective-permute-start.19 = (f32[256,128]{1,0:T(8,128)S(1)}, f32[256,128]{1,0:T(8,128)S(1)}, u32[]{:S(2)}, u32[]{:S(2)}) collective-permute-start(f32[256,128]{1,0:T(8,128)S(1)} %get-tuple-element.86.refs_0_), channel_id=1, source_target_pairs={{0,24},{4,28},{8,16},{12,20},{16,8},{20,12},{24,0},{28,4},{1,25},{... | collective-permute-start | bytes 393224 | tf_op jit(solution)/shard_map/ppermute | solution.py:539
  62.4 2.4 %collective-permute-start.20 = (f32[1024,128]{1,0:T(8,128)S(1)}, f32[1024,128]{1,0:T(8,128)S(1)}, u32[]{:S(2)}, u32[]{:S(2)}) collective-permute-start(f32[1024,128]{1,0:T(8,128)S(1)} %stack_chips.1.mine_ref), channel_id=1, source_target_pairs={{0,4},{4,0},{8,12},{12,8},{16,20},{20,16},{24,28},{28,24},{1,5},{5... | collective-permute-start | bytes 1572872 | tf_op jit(solution)/shard_map/ppermute | solution.py:539

commit v8 on v7

--- a/solution.py
+++ b/solution.py
@@ -355,8 +355,29 @@
             slope_ref[at : at + heads, :] = jnp.where(signs > 0, line, jnp.zeros((), BF16))
 
 
-def query_part(scores, index_stats, targets, kl, gate, index_keys):
-    rows, keys = scores.shape
+def prepare(scores, index_stats, kl, index_query, index_weight, groups):
+    rows, heads, width = index_query.shape
+    own = rows // groups
+
+    def body(score_ref, lse_ref, other_ref, kl_ref, query_ref, weight_ref, base_ref, column_ref, row_ref):
+        whole = joined([lse_ref[:, :1], other_ref[:, :1]])
+        base_ref[...] = kl_ref[:, :1] * jnp.exp2(score_ref[...] - whole)
+        first = lax.axis_index("keys") * own
+        columns = weight_ref[...].T
+        lane = lax.broadcasted_iota(jnp.int32, (heads, rows), 1)
+        for i in range(own):
+            span = slice(i * heads, (i + 1) * heads)
+            column = jnp.sum(jnp.where(lane == first + i, columns, 0.0), axis=1, keepdims=True)
+            column_ref[span, :] = jnp.broadcast_to(column, (heads, width))
+            row_ref[span, :] = query_ref[first + i].astype(F32)
+
+    side = pltpu.VMEM((own * heads, width), F32)
+    operands = (scores, *index_stats, kl, index_query, index_weight)
+    return vmem_call(body, "prepare", (pltpu.VMEM(scores.shape, F32), side, side), operands)
+
+
+def query_part(base, targets, kl, gate, index_keys):
+    rows, keys = base.shape
     groups, size = gate.shape[:2]
     own = rows // groups
     width = index_keys.shape[1]
@@ -364,13 +385,12 @@
     order = group_order(groups)[: groups // 2]
     many = len(order)
 
-    def body(score_ref, kl_ref, lse_ref, other_ref, gate_ref, keys_ref, *refs):
+    def body(base_ref, kl_ref, gate_ref, keys_ref, *refs):
         target_refs, (send_ref, slope_ref, delta_ref, across_ref) = refs[: len(targets)], refs[len(targets) :]
-        whole = joined([lse_ref[:, :1], other_ref[:, :1]])
         target = target_refs[0][...]
         for ref in target_refs[1:]:
             target = target + ref[...]
-        delta = kl_ref[:, :1] * (jnp.exp2(score_ref[...] - whole) - target)
+        delta = base_ref[...] - kl_ref[:, :1] * target
         for g in range(groups):
             delta_ref[g] = delta[g * own : (g + 1) * own, :]
         _, core = head_place()
@@ -385,7 +405,7 @@
         pltpu.VMEM((groups, own, keys), F32),
         pltpu.VMEM((rows, half), F32),
     )
-    operands = (scores, kl, *index_stats, gate, index_keys, *targets)
+    operands = (base, kl, gate, index_keys, *targets)
     return vmem_call(body, "query_part", outs, operands, limit=16 * MIB)
 
 
@@ -447,30 +467,24 @@
     return vmem_call(body, "add_halve", (side, side), (left, right))
 
 
-def own_rows(left, right, index_query, index_weight):
-    rows, heads, width = index_query.shape
-    size = left.shape[1]
+def own_rows(left, right, column, row, heads):
+    size, width = column.shape
     own = size // heads
     extra = -(-own // 8) * 8
 
-    def body(query_ref, weight_ref, left_ref, right_ref, out_ref):
-        first = lax.axis_index("keys") * own
-        columns = weight_ref[...].T
-        lane = lax.broadcasted_iota(jnp.int32, (heads, rows), 1)
+    def body(left_ref, right_ref, column_ref, row_ref, out_ref):
+        total = left_ref[0] + right_ref[0]
+        out_ref[:size, :] = total * column_ref[...]
+        summed = jnp.sum(total * row_ref[...], axis=1, keepdims=True)
         for i in range(own):
-            span = slice(i * heads, (i + 1) * heads)
-            total = left_ref[0, span, :] + right_ref[0, span, :]
-            column = jnp.sum(jnp.where(lane == first + i, columns, 0.0), axis=1, keepdims=True)
-            out_ref[span, :] = total * column
-            summed = jnp.sum(total * query_ref[first + i].astype(F32), axis=1, keepdims=True)
             out_ref[size + i : size + i + 1, :] = jnp.concatenate(
-                [summed.T, jnp.zeros((1, width - heads), F32)], axis=1
+                [summed[i * heads : (i + 1) * heads, :].T, jnp.zeros((1, width - heads), F32)], axis=1
             )
         if extra > own:
             out_ref[size + own :, :] = jnp.zeros((extra - own, width), F32)
 
     out = pltpu.VMEM((size + extra, width), F32)
-    return vmem_call(body, "own_rows", out, (index_query, index_weight, left, right), cost=LONG)
+    return vmem_call(body, "own_rows", out, (left, right, column, row), cost=LONG)
 
 
 def gather_weights(pieces, rows, heads):
@@ -545,32 +559,35 @@
     scores, index_lse, pack = index_forward(query_pos, index_query, index_keys, index_weight, stat)
     blocks = stat.shape[0]
     both = join_first(stat, to_keys(stat, 1), index_lse)
+    both, signs_query = lax.optimization_barrier((both, index_query))
     bits = 2
     while bits < key_devices // 2:
         both = join_pair(both, to_keys(both, bits))
         bits *= 2
+    gate, wiq, kl = index_signs(kl_weight, signs_query, index_keys, index_weight, key_devices)
     stat, index_lse = join_more(both, to_keys(both, bits), blocks)
+    stat, gate = lax.optimization_barrier((stat, gate))
     keep, send = head_sum(probs, tops, stat, queries, row_local)
     index_lse, send, index_query, pack = lax.optimization_barrier((index_lse, send, index_query, pack))
     sums = add_stacks(keep, to_heads(send, 1))
     targets = [sums[0]] + [to_heads(sums[r], 2 * r) for r in chip_order]
-    gate, wiq, kl = index_signs(kl_weight, index_query, index_keys, index_weight, key_devices)
     other_gate, other_wiq = other_signs(to_heads(pack, 1), index_keys, row_local)
     index_stats = (index_lse, to_keys(index_lse, 1))
     other_gate, gate = lax.optimization_barrier((other_gate, gate))
-    odd, odd_slopes, delta, across = query_part(scores, index_stats, targets, kl, gate, index_keys)
+    base, own_column, own_query = prepare(scores, index_stats, kl, index_query, index_weight, key_devices)
+    odd, odd_slopes, delta, across = query_part(base, targets, kl, gate, index_keys)
     even, even_slopes = query_rest(delta, gate, index_keys)
     slopes = (odd_slopes, even_slopes)
 
     bits, other_odd = 1, to_keys(odd, 1)
     parts = key_part(slopes, wiq, to_heads(across, 1), other_gate, other_wiq, chips)
-    key_own, key_wide = add_all([parts[0]] + [to_heads(parts[r], 2 * r) for r in chip_order])
+    key_own, key_wide = add_all([parts[0]] + [to_heads(parts[r], 2 * r) for r in [*range(2, chips), 1]])
     while bits < key_devices // 2:
         even, odd = add_halve(even, other_odd)
         bits *= 2
         other_odd = to_keys(odd, bits)
     even, key_own = lax.optimization_barrier((even, key_own))
-    query_own = own_rows(even, other_odd, index_query, index_weight)
+    query_own = own_rows(even, other_odd, own_column, own_query, index_heads)
     pieces = {0: query_own, **{r: to_keys(query_own, r) for r in key_order}}
     mine = {r: to_heads(key_own if r == chips - 1 else key_wide, 2 * r) for r in range(1, chips)}
     mine = [key_own] + [mine[r] for r in range(1, chips)]

time: 66.4 us -> 66.2 us (level)
  starting transfers between devices: 27.3 us -> 28 us
  waiting for transfers between devices: 15 us -> 14.3 us
    ppermute x8, waiting for transfers between devices: 5.97 us -> 4.96 us  [to_keys(): lax.ppermute(value, 'keys', [(i, i ^ bits) for i in range(key_devices)])]
    ppermute x13, starting transfers between devices: 11.5 us -> 12.3 us  [to_heads(): lax.ppermute(value, 'heads', [(i, i ^ bits) for i in range(head_devices)])]
    pallas_call x16 -> x17, Pallas kernels: 12.3 us -> 12.2 us  [vmem_call(): pl.pallas_call(body, out_shape=outs, in_specs=[smem_spec] * len(scalars)...]
  transfers between devices with their start and end apart: 21 -> 21, of which waited for: 12 -> 11; matrix products, arithmetic and copies ran while one was open for 0% -> 0% of each run, Pallas kernels for 13% -> 13%
where the time goes in v8:
time: 66.2 us; the launch traced here: 66 us
  starting transfers between devices  28 us (42%)
  Pallas kernels  22.8 us (34%)
  waiting for transfers between devices  14.3 us (22%)
  between operations  0.98 us (1%)
    ppermute x8, starting transfers between devices, to_keys(): lax.ppermute(value, 'keys', [(i, i ^ bits) for i in range(key_devices)])  15.6 us
    ppermute x13, starting transfers between devices, to_heads(): lax.ppermute(value, 'heads', [(i, i ^ bits) for i in range(head_devices)])  12.3 us
    pallas_call x17, Pallas kernels, vmem_call(): pl.pallas_call(body, out_shape=outs, in_specs=[smem_spec] * len(scalars)...  12.2 us
    pallas_call x1, Pallas kernels, main_scores(): pl.pallas_call(body, grid=(blocks // many,), out_shape=(pltpu.VMEM((block...  10.6 us
    ppermute x13, waiting for transfers between devices, to_heads(): lax.ppermute(value, 'heads', [(i, i ^ bits) for i in range(head_devices)])  9.29 us
    ppermute x8, waiting for transfers between devices, to_keys(): lax.ppermute(value, 'keys', [(i, i ^ bits) for i in range(key_devices)])  4.96 us
  transfers between devices with their start and end apart: 21, of which 11 were waited for; matrix products, arithmetic and copies ran while one was open for 0% of the time, Pallas kernels for 13%

profile of v8, /device:TPU:0, one launch (start us, length us, event | category | flops | bytes accessed | tf_op | source)
XLA Modules:
  0.0 66.0 jit_solution(766504728968093632)
XLA Ops:
  0.7 10.6 %main_scores.1 = (f32[8,2048,256]{2,1,0:T(8,128)S(1)}, f32[8,16,256]{2,1,0:T(8,128)S(1)}, f32[8,256]{1,0:T(8,128)S(1)}) custom-call(s32[1,128]{1,0:T(1,128)} %bitcast.4, bf16[16,576,128]{2,1,0:T(8,128)(2,1)} %bitcast.5, bf16[576,2048]{1,0:T(8,128)(2,1)} %bitcast.6), custom_call_target="tpu_custom_call" | custom-call | tf_op jit(solution)/shard_map/main_scores/pallas_call | solution.py:215
  11.3 3.1 %collective-permute-start = (f32[8,256]{1,0:T(8,128)S(1)}, f32[8,256]{1,0:T(8,128)S(1)}, u32[]{:S(2)}, u32[]{:S(2)}) collective-permute-start(f32[8,256]{1,0:T(8,128)S(1)} %get-tuple-element.54._.left_ref), channel_id=1, source_target_pairs={{0,1},{1,0},{2,3},{3,2},{4,5},{5,4},{6,7},{7,6},{8,9},{9,8},{10,11... | collective-permute-start | bytes 24584 | tf_op jit(solution)/shard_map/ppermute | solution.py:550
  14.4 2.1 %index_forward.1 = (f32[16,2048]{1,0:T(8,128)S(1)}, f32[16,128]{1,0:T(8,128)S(1)}, f32[1040,128]{1,0:T(8,128)S(1)}) custom-call(s32[128]{0:T(128)S(1)} %copy-done.3, bf16[16,64,128]{2,1,0:T(8,128)(2,1)S(1)} %copy-done.1, bf16[2048,128]{1,0:T(8,128)(2,1)S(1)} %copy-done, f32[16,64]{1,0:T(8,128)S(1)} %copy-done.2, f32[8,256]{1,0:T(8,128)S(1)} %get-tuple-element.54._.left_ref), custom_call_target="tpu_custom_call" | custom-call | tf_op jit(solution)/shard_map/index_forward/pallas_call | solution.py:40
  16.6 2.6 %collective-permute-start.1 = (f32[24,256]{1,0:T(8,128)S(1)}, f32[24,256]{1,0:T(8,128)S(1)}, u32[]{:S(2)}, u32[]{:S(2)}) collective-permute-start(f32[24,256]{1,0:T(8,128)S(1)} %join_first.1.left_ref), channel_id=1, source_target_pairs={{0,2},{1,3},{2,0},{3,1},{4,6},{5,7},{6,4},{7,5},{8,10},{9,11},{10,... | collective-permute-start | bytes 73736 | tf_op jit(solution)/shard_map/ppermute | solution.py:550
  19.2 2.4 %index_signs.1 = (bf16[4,256,2048]{2,1,0:T(8,128)(2,1)S(1)}, bf16[4,128,256]{2,1,0:T(8,128)(2,1)S(1)}, f32[16,128]{1,0:T(8,128)S(1)}) custom-call(f32[16]{0:T(128)S(1)} %copy-done.4, bf16[16,64,128]{2,1,0:T(8,128)(2,1)S(1)} %copy-done.1, bf16[2048,128]{1,0:T(8,128)(2,1)S(1)} %copy-done, f32[16,64]{1,0:T(8,128)S(1)} %copy-done.2), custom_call_target="tpu_custom_call" | custom-call | tf_op jit(solution)/shard_map/index_signs/pallas_call | solution.py:40
  21.6 1.4 %head_sum.1 = (f32[4,16,2048]{2,1,0:T(8,128)S(1)}, f32[4,16,2048]{2,1,0:T(8,128)S(1)}) custom-call(f32[8,2048,256]{2,1,0:T(8,128)S(1)} %get-tuple-element.59.prob_ref, f32[8,16,256]{2,1,0:T(8,128)S(1)} %get-tuple-element.60.top_ref, f32[8,256]{1,0:T(8,128)S(1)} %get-tuple-element.64.stat_ref), custom_call_target="tpu_custom_call" | custom-call | flops 1000000000 | tf_op jit(solution)/shard_map/head_sum/pallas_call | solution.py:40
  23.6 1.4 %collective-permute-done.4.right_ref = f32[4,16,2048]{2,1,0:T(8,128)S(1)} collective-permute-done((f32[4,16,2048]{2,1,0:T(8,128)S(1)}, f32[4,16,2048]{2,1,0:T(8,128)S(1)}, u32[]{:S(2)}, u32[]{:S(2)}) %collective-permute-start.4) | collective-permute-done | bytes 524320 | tf_op jit(solution)/shard_map/ppermute | solution.py:553
  25.1 2.5 %collective-permute-start.5 = (f32[16,2048]{1,0:T(8,128)S(1)}, f32[16,2048]{1,0:T(8,128)S(1)}, u32[]{:S(2)}, u32[]{:S(2)}) collective-permute-start(f32[16,2048]{1,0:T(8,128)S(1)} %get-tuple-element.78), channel_id=1, source_target_pairs={{0,24},{4,28},{8,16},{12,20},{16,8},{20,12},{24,0},{28,4},{1,25},{... | collective-permute-start | bytes 393224 | tf_op jit(solution)/shard_map/ppermute | solution.py:553
  28.1 0.5 collective-permute-start.7
  28.6 1.5 %collective-permute-start.2 = (f32[16,128]{1,0:T(8,128)S(1)}, f32[16,128]{1,0:T(8,128)S(1)}, u32[]{:S(2)}, u32[]{:S(2)}) collective-permute-start(f32[16,128]{1,0:T(8,128)S(1)} %get-tuple-element.67.lse_ref), channel_id=1, source_target_pairs={{0,1},{1,0},{2,3},{3,2},{4,5},{5,4},{6,7},{7,6},{8,9},{9,8},{10,11... | collective-permute-start | bytes 24584 | tf_op jit(solution)/shard_map/ppermute | solution.py:550
  30.1 2.2 %collective-permute-done.2.other_ref = f32[16,128]{1,0:T(8,128)S(1)} collective-permute-done((f32[16,128]{1,0:T(8,128)S(1)}, f32[16,128]{1,0:T(8,128)S(1)}, u32[]{:S(2)}, u32[]{:S(2)}) %collective-permute-start.2) | collective-permute-done | bytes 8224 | tf_op jit(solution)/shard_map/ppermute | solution.py:550
  32.5 1.7 %other_signs.1 = (bf16[1024,1024]{1,0:T(8,128)(2,1)S(1)}, bf16[128,1024]{1,0:T(8,128)(2,1)S(1)}) custom-call(f32[1040,128]{1,0:T(8,128)S(1)} %collective-permute-done.3.pack_ref, bf16[2048,128]{1,0:T(8,128)(2,1)S(1)} %copy-done), custom_call_target="tpu_custom_call" | custom-call | tf_op jit(solution)/shard_map/other_signs/pallas_call | solution.py:40
  34.5 0.9 %query_part.1 = (f32[2,256,128]{2,1,0:T(8,128)S(1)}, bf16[512,2048]{1,0:T(8,128)(2,1)S(1)}, f32[4,4,2048]{2,1,0:T(4,128)S(1)}, f32[16,1024]{1,0:T(8,128)S(1)}) custom-call(f32[16,2048]{1,0:T(8,128)S(1)} %get-tuple-element.70.base_ref, f32[16,128]{1,0:T(8,128)S(1)} %get-tuple-element.68.kl_ref, bf16[4,256,2048]{2,1,0:T(8,128)(2,1)S(1)} %get-tuple-element.74.gate_ref, ...), custom_call_target="tpu_custom_call" | custom-call | tf_op jit(solution)/shard_map/query_part/pallas_call | solution.py:40
  35.4 1.6 %collective-permute-start.8 = (f32[2,256,128]{2,1,0:T(8,128)S(1)}, f32[2,256,128]{2,1,0:T(8,128)S(1)}, u32[]{:S(2)}, u32[]{:S(2)}) collective-permute-start(f32[2,256,128]{2,1,0:T(8,128)S(1)} %get-tuple-element.83), channel_id=1, source_target_pairs={{0,1},{1,0},{2,3},{3,2},{4,5},{5,4},{6,7},{7,6},{8,9},{9,8},{10,11... | collective-permute-start | bytes 786440 | tf_op jit(solution)/shard_map/ppermute | solution.py:550
  37.0 0.7 %query_rest.1 = (f32[2,256,128]{2,1,0:T(8,128)S(1)}, bf16[512,2048]{1,0:T(8,128)(2,1)S(1)}) custom-call(f32[4,4,2048]{2,1,0:T(4,128)S(1)} %get-tuple-element.81.delta_ref, bf16[4,256,2048]{2,1,0:T(8,128)(2,1)S(1)} %get-tuple-element.74.gate_ref, bf16[2048,128]{1,0:T(8,128)(2,1)S(1)} %copy-done), custom_call_target="tpu_custom_call" | custom-call | tf_op jit(solution)/shard_map/query_rest/pallas_call | solution.py:40
  38.2 1.2 %key_part.1 = (f32[256,128]{1,0:T(8,128)S(1)}, f32[256,128]{1,0:T(8,128)S(1)}, f32[256,128]{1,0:T(8,128)S(1)}, f32[256,128]{1,0:T(8,128)S(1)}) custom-call(bf16[512,2048]{1,0:T(8,128)(2,1)S(1)} %get-tuple-element.85.odd_ref, bf16[512,2048]{1,0:T(8,128)(2,1)S(1)} %get-tuple-element.86.even_ref, bf16[4,128,256]{2,1,0:T(8,128)(2,1)S(1)} %get-tuple-element.87.wiq_ref, ...), custom_call_target="tpu_custom_call" | custom-call | tf_op jit(solution)/shard_map/key_part/pallas_call | solution.py:40
  39.4 1.5 %collective-permute-start.10 = (f32[256,128]{1,0:T(8,128)S(1)}, f32[256,128]{1,0:T(8,128)S(1)}, u32[]{:S(2)}, u32[]{:S(2)}) collective-permute-start(f32[256,128]{1,0:T(8,128)S(1)} %get-tuple-element.92), channel_id=1, source_target_pairs={{0,16},{4,20},{8,24},{12,28},{16,0},{20,4},{24,8},{28,12},{1,17},{... | collective-permute-start | bytes 393224 | tf_op jit(solution)/shard_map/ppermute | solution.py:553
  40.9 1.5 %collective-permute-start.11 = (f32[256,128]{1,0:T(8,128)S(1)}, f32[256,128]{1,0:T(8,128)S(1)}, u32[]{:S(2)}, u32[]{:S(2)}) collective-permute-start(f32[256,128]{1,0:T(8,128)S(1)} %get-tuple-element.93), channel_id=1, source_target_pairs={{0,24},{4,28},{8,16},{12,20},{16,8},{20,12},{24,0},{28,4},{1,25},{... | collective-permute-start | bytes 393224 | tf_op jit(solution)/shard_map/ppermute | solution.py:553
  43.0 0.7 %collective-permute-done.8.right_ref = f32[2,256,128]{2,1,0:T(8,128)S(1)} collective-permute-done((f32[2,256,128]{2,1,0:T(8,128)S(1)}, f32[2,256,128]{2,1,0:T(8,128)S(1)}, u32[]{:S(2)}, u32[]{:S(2)}) %collective-permute-start.8) | collective-permute-done | bytes 262176 | tf_op jit(solution)/shard_map/ppermute | solution.py:550
  43.7 2.4 %collective-permute-start.13 = (f32[1,256,128]{2,1,0:T(8,128)S(1)}, f32[1,256,128]{2,1,0:T(8,128)S(1)}, u32[]{:S(2)}, u32[]{:S(2)}) collective-permute-start(f32[1,256,128]{2,1,0:T(8,128)S(1)} %get-tuple-element.97), channel_id=1, source_target_pairs={{0,2},{1,3},{2,0},{3,1},{4,6},{5,7},{6,4},{7,5},{8,10},{9,11},{10,... | collective-permute-start | bytes 393224 | tf_op jit(solution)/shard_map/ppermute | solution.py:550
  46.1 1.4 %collective-permute-done.10.refs_1_ = f32[256,128]{1,0:T(8,128)S(1)} collective-permute-done((f32[256,128]{1,0:T(8,128)S(1)}, f32[256,128]{1,0:T(8,128)S(1)}, u32[]{:S(2)}, u32[]{:S(2)}) %collective-permute-start.10) | collective-permute-done | bytes 131104 | tf_op jit(solution)/shard_map/ppermute | solution.py:553
  47.5 0.7 %collective-permute-done.11.refs_2_ = f32[256,128]{1,0:T(8,128)S(1)} collective-permute-done((f32[256,128]{1,0:T(8,128)S(1)}, f32[256,128]{1,0:T(8,128)S(1)}, u32[]{:S(2)}, u32[]{:S(2)}) %collective-permute-start.11) | collective-permute-done | bytes 131104 | tf_op jit(solution)/shard_map/ppermute | solution.py:553
  48.2 0.9 %collective-permute-done.12.refs_3_ = f32[256,128]{1,0:T(8,128)S(1)} collective-permute-done((f32[256,128]{1,0:T(8,128)S(1)}, f32[256,128]{1,0:T(8,128)S(1)}, u32[]{:S(2)}, u32[]{:S(2)}) %collective-permute-start.12) | collective-permute-done | bytes 131104 | tf_op jit(solution)/shard_map/ppermute | solution.py:553
  49.1 1.5 %collective-permute-start.18 = (f32[272,128]{1,0:T(8,128)S(1)}, f32[272,128]{1,0:T(8,128)S(1)}, u32[]{:S(2)}, u32[]{:S(2)}) collective-permute-start(f32[272,128]{1,0:T(8,128)S(1)} %get-tuple-element.101), channel_id=1, source_target_pairs={{0,16},{4,20},{8,24},{12,28},{16,0},{20,4},{24,8},{28,12},{1,17},{... | collective-permute-start | bytes 417800 | tf_op jit(solution)/shard_map/ppermute | solution.py:553
  50.6 1.3 %collective-permute-start.17 = (f32[272,128]{1,0:T(8,128)S(1)}, f32[272,128]{1,0:T(8,128)S(1)}, u32[]{:S(2)}, u32[]{:S(2)}) collective-permute-start(f32[272,128]{1,0:T(8,128)S(1)} %get-tuple-element.101), channel_id=1, source_target_pairs={{0,8},{4,12},{8,0},{12,4},{16,24},{20,28},{24,16},{28,20},{1,9},{5... | collective-permute-start | bytes 417800 | tf_op jit(solution)/shard_map/ppermute | solution.py:553
  52.1 2.6 %collective-permute-start.16 = (f32[264,128]{1,0:T(8,128)S(1)}, f32[264,128]{1,0:T(8,128)S(1)}, u32[]{:S(2)}, u32[]{:S(2)}) collective-permute-start(f32[264,128]{1,0:T(8,128)S(1)} %own_rows.1.refs_0_), channel_id=1, source_target_pairs={{0,2},{1,3},{2,0},{3,1},{4,6},{5,7},{6,4},{7,5},{8,10},{9,11},{10,... | collective-permute-start | bytes 405512 | tf_op jit(solution)/shard_map/ppermute | solution.py:550
  54.7 1.2 %collective-permute-start.15 = (f32[264,128]{1,0:T(8,128)S(1)}, f32[264,128]{1,0:T(8,128)S(1)}, u32[]{:S(2)}, u32[]{:S(2)}) collective-permute-start(f32[264,128]{1,0:T(8,128)S(1)} %own_rows.1.refs_0_), channel_id=1, source_target_pairs={{0,1},{1,0},{2,3},{3,2},{4,5},{5,4},{6,7},{7,6},{8,9},{9,8},{10,11... | collective-permute-start | bytes 405512 | tf_op jit(solution)/shard_map/ppermute | solution.py:550
  55.9 0.6 collective-permute-start.14
  56.5 1.7 %collective-permute-start.19 = (f32[256,128]{1,0:T(8,128)S(1)}, f32[256,128]{1,0:T(8,128)S(1)}, u32[]{:S(2)}, u32[]{:S(2)}) collective-permute-start(f32[256,128]{1,0:T(8,128)S(1)} %get-tuple-element.100.refs_0_), channel_id=1, source_target_pairs={{0,24},{4,28},{8,16},{12,20},{16,8},{20,12},{24,0},{28,4},{1,25},{... | collective-permute-start | bytes 393224 | tf_op jit(solution)/shard_map/ppermute | solution.py:553
  58.3 4.1 %collective-permute-done.19.refs_3_ = f32[256,128]{1,0:T(8,128)S(1)} collective-permute-done((f32[256,128]{1,0:T(8,128)S(1)}, f32[256,128]{1,0:T(8,128)S(1)}, u32[]{:S(2)}, u32[]{:S(2)}) %collective-permute-start.19) | collective-permute-done | bytes 131104 | tf_op jit(solution)/shard_map/ppermute | solution.py:553
  62.5 2.1 %collective-permute-done.16.refs_3_ = f32[264,128]{1,0:T(8,128)S(1)} collective-permute-done((f32[264,128]{1,0:T(8,128)S(1)}, f32[264,128]{1,0:T(8,128)S(1)}, u32[]{:S(2)}, u32[]{:S(2)}) %collective-permute-start.16) | collective-permute-done | bytes 135200 | tf_op jit(solution)/shard_map/ppermute | solution.py:550
  64.7 1.2 %place_all.1 = (f32[1024,128]{1,0:T(8,128)}, f32[2048,128]{1,0:T(8,128)}, f32[16,64]{1,0:T(8,128)}) custom-call(f32[16,64]{1,0:T(8,128)S(1)} %gather_weights.1.weight_ref, f32[1024,128]{1,0:T(8,128)S(1)} %stack_chips.1.mine_ref, f32[1024,128]{1,0:T(8,128)S(1)} %collective-permute-done.20.other_ref, f32[264,128]{1,0:T(8,128)S(1)} %own_rows.1.refs_0_, ...), custom_call_target="tpu_custom_call" | custom-call | tf_op jit(solution)/shard_map/place_all/pallas_call | solution.py:40
  (38 shorter events, 3.1 us)
Async XLA Ops:
  0.6 13.8 %copy-start = (bf16[2048,128]{1,0:T(8,128)(2,1)S(1)}, bf16[2048,128]{1,0:T(8,128)(2,1)}, u32[]{:S(2)}) copy-start(bf16[2048,128]{1,0:T(8,128)(2,1)} %keys_ref.9) | copy-start | bytes 1572868
  0.6 13.8 %copy-start.1 = (bf16[16,64,128]{2,1,0:T(8,128)(2,1)S(1)}, bf16[16,64,128]{2,1,0:T(8,128)(2,1)}, u32[]{:S(2)}) copy-start(bf16[16,64,128]{2,1,0:T(8,128)(2,1)} %query_ref.3) | copy-start | bytes 786436
  0.7 13.8 %copy-start.2 = (f32[16,64]{1,0:T(8,128)S(1)}, f32[16,64]{1,0:T(8,128)}, u32[]{:S(2)}) copy-start(f32[16,64]{1,0:T(8,128)} %weight_ref.5) | copy-start | bytes 12292
  0.7 13.7 %copy-start.3 = (s32[128]{0:T(128)S(1)}, s32[128]{0:T(128)}, u32[]{:S(2)}) copy-start(s32[128]{0:T(128)} %pos_ref.1) | copy-start | bytes 1540
  0.7 18.6 %copy-start.4 = (f32[16]{0:T(128)S(1)}, f32[16]{0:T(128)}, u32[]{:S(2)}) copy-start(f32[16]{0:T(128)} %kl_ref.1) | copy-start | bytes 196
  11.3 5.3 %collective-permute-start = (f32[8,256]{1,0:T(8,128)S(1)}, f32[8,256]{1,0:T(8,128)S(1)}, u32[]{:S(2)}, u32[]{:S(2)}) collective-permute-start(f32[8,256]{1,0:T(8,128)S(1)} %get-tuple-element.54._.left_ref), channel_id=1, source_target_pairs={{0,1},{1,0},{2,3},{3,2},{4,5},{5,4},{6,7},{7,6},{8,9},{9,8},{10,11... | collective-permute-start | bytes 24584 | tf_op jit(solution)/shard_map/ppermute | solution.py:550
  16.6 5.0 %collective-permute-start.1 = (f32[24,256]{1,0:T(8,128)S(1)}, f32[24,256]{1,0:T(8,128)S(1)}, u32[]{:S(2)}, u32[]{:S(2)}) collective-permute-start(f32[24,256]{1,0:T(8,128)S(1)} %join_first.1.left_ref), channel_id=1, source_target_pairs={{0,2},{1,3},{2,0},{3,1},{4,6},{5,7},{6,4},{7,5},{8,10},{9,11},{10,... | collective-permute-start | bytes 73736 | tf_op jit(solution)/shard_map/ppermute | solution.py:550
  23.0 2.0 %collective-permute-start.4 = (f32[4,16,2048]{2,1,0:T(8,128)S(1)}, f32[4,16,2048]{2,1,0:T(8,128)S(1)}, u32[]{:S(2)}, u32[]{:S(2)}) collective-permute-start(f32[4,16,2048]{2,1,0:T(8,128)S(1)} %get-tuple-element.76), channel_id=1, source_target_pairs={{0,4},{4,0},{8,12},{12,8},{16,20},{20,16},{24,28},{28,24},{1,5},{5... | collective-permute-start | bytes 1572872 | tf_op jit(solution)/shard_map/ppermute | solution.py:553
  23.1 9.4 %collective-permute-start.3 = (f32[1040,128]{1,0:T(8,128)S(1)}, f32[1040,128]{1,0:T(8,128)S(1)}, u32[]{:S(2)}, u32[]{:S(2)}) collective-permute-start(f32[1040,128]{1,0:T(8,128)S(1)} %get-tuple-element.71), channel_id=1, source_target_pairs={{0,4},{4,0},{8,12},{12,8},{16,20},{20,16},{24,28},{28,24},{1,5},{5... | collective-permute-start | bytes 1597448 | tf_op jit(solution)/shard_map/ppermute | solution.py:553
  25.1 9.1 %collective-permute-start.5 = (f32[16,2048]{1,0:T(8,128)S(1)}, f32[16,2048]{1,0:T(8,128)S(1)}, u32[]{:S(2)}, u32[]{:S(2)}) collective-permute-start(f32[16,2048]{1,0:T(8,128)S(1)} %get-tuple-element.78), channel_id=1, source_target_pairs={{0,24},{4,28},{8,16},{12,20},{16,8},{20,12},{24,0},{28,4},{1,25},{... | collective-permute-start | bytes 393224 | tf_op jit(solution)/shard_map/ppermute | solution.py:553
  27.6 6.8 %collective-permute-start.6 = (f32[16,2048]{1,0:T(8,128)S(1)}, f32[16,2048]{1,0:T(8,128)S(1)}, u32[]{:S(2)}, u32[]{:S(2)}) collective-permute-start(f32[16,2048]{1,0:T(8,128)S(1)} %get-tuple-element.79), channel_id=1, source_target_pairs={{0,16},{4,20},{8,24},{12,28},{16,0},{20,4},{24,8},{28,12},{1,17},{... | collective-permute-start | bytes 393224 | tf_op jit(solution)/shard_map/ppermute | solution.py:553
  28.1 6.4 %collective-permute-start.7 = (f32[16,2048]{1,0:T(8,128)S(1)}, f32[16,2048]{1,0:T(8,128)S(1)}, u32[]{:S(2)}, u32[]{:S(2)}) collective-permute-start(f32[16,2048]{1,0:T(8,128)S(1)} %get-tuple-element.80), channel_id=1, source_target_pairs={{0,8},{4,12},{8,0},{12,4},{16,24},{20,28},{24,16},{28,20},{1,9},{5... | collective-permute-start | bytes 393224 | tf_op jit(solution)/shard_map/ppermute | solution.py:553
  28.6 3.7 %collective-permute-start.2 = (f32[16,128]{1,0:T(8,128)S(1)}, f32[16,128]{1,0:T(8,128)S(1)}, u32[]{:S(2)}, u32[]{:S(2)}) collective-permute-start(f32[16,128]{1,0:T(8,128)S(1)} %get-tuple-element.67.lse_ref), channel_id=1, source_target_pairs={{0,1},{1,0},{2,3},{3,2},{4,5},{5,4},{6,7},{7,6},{8,9},{9,8},{10,11... | collective-permute-start | bytes 24584 | tf_op jit(solution)/shard_map/ppermute | solution.py:550
  35.4 8.2 %collective-permute-start.8 = (f32[2,256,128]{2,1,0:T(8,128)S(1)}, f32[2,256,128]{2,1,0:T(8,128)S(1)}, u32[]{:S(2)}, u32[]{:S(2)}) collective-permute-start(f32[2,256,128]{2,1,0:T(8,128)S(1)} %get-tuple-element.83), channel_id=1, source_target_pairs={{0,1},{1,0},{2,3},{3,2},{4,5},{5,4},{6,7},{7,6},{8,9},{9,8},{10,11... | collective-permute-start | bytes 786440 | tf_op jit(solution)/shard_map/ppermute | solution.py:550
  37.0 1.3 %collective-permute-start.9 = (f32[16,1024]{1,0:T(8,128)S(1)}, f32[16,1024]{1,0:T(8,128)S(1)}, u32[]{:S(2)}, u32[]{:S(2)}) collective-permute-start(f32[16,1024]{1,0:T(8,128)S(1)} %get-tuple-element.88), channel_id=1, source_target_pairs={{0,4},{4,0},{8,12},{12,8},{16,20},{20,16},{24,28},{28,24},{1,5},{5... | collective-permute-start | bytes 196616 | tf_op jit(solution)/shard_map/ppermute | solution.py:553
  39.4 8.1 %collective-permute-start.10 = (f32[256,128]{1,0:T(8,128)S(1)}, f32[256,128]{1,0:T(8,128)S(1)}, u32[]{:S(2)}, u32[]{:S(2)}) collective-permute-start(f32[256,128]{1,0:T(8,128)S(1)} %get-tuple-element.92), channel_id=1, source_target_pairs={{0,16},{4,20},{8,24},{12,28},{16,0},{20,4},{24,8},{28,12},{1,17},{... | collective-permute-start | bytes 393224 | tf_op jit(solution)/shard_map/ppermute | solution.py:553
  40.9 7.3 %collective-permute-start.11 = (f32[256,128]{1,0:T(8,128)S(1)}, f32[256,128]{1,0:T(8,128)S(1)}, u32[]{:S(2)}, u32[]{:S(2)}) collective-permute-start(f32[256,128]{1,0:T(8,128)S(1)} %get-tuple-element.93), channel_id=1, source_target_pairs={{0,24},{4,28},{8,16},{12,20},{16,8},{20,12},{24,0},{28,4},{1,25},{... | collective-permute-start | bytes 393224 | tf_op jit(solution)/shard_map/ppermute | solution.py:553
  42.4 6.6 %collective-permute-start.12 = (f32[256,128]{1,0:T(8,128)S(1)}, f32[256,128]{1,0:T(8,128)S(1)}, u32[]{:S(2)}, u32[]{:S(2)}) collective-permute-start(f32[256,128]{1,0:T(8,128)S(1)} %get-tuple-element.94), channel_id=1, source_target_pairs={{0,8},{4,12},{8,0},{12,4},{16,24},{20,28},{24,16},{28,20},{1,9},{5... | collective-permute-start | bytes 393224 | tf_op jit(solution)/shard_map/ppermute | solution.py:553
  43.7 8.3 %collective-permute-start.13 = (f32[1,256,128]{2,1,0:T(8,128)S(1)}, f32[1,256,128]{2,1,0:T(8,128)S(1)}, u32[]{:S(2)}, u32[]{:S(2)}) collective-permute-start(f32[1,256,128]{2,1,0:T(8,128)S(1)} %get-tuple-element.97), channel_id=1, source_target_pairs={{0,2},{1,3},{2,0},{3,1},{4,6},{5,7},{6,4},{7,5},{8,10},{9,11},{10,... | collective-permute-start | bytes 393224 | tf_op jit(solution)/shard_map/ppermute | solution.py:550
  49.1 7.4 %collective-permute-start.18 = (f32[272,128]{1,0:T(8,128)S(1)}, f32[272,128]{1,0:T(8,128)S(1)}, u32[]{:S(2)}, u32[]{:S(2)}) collective-permute-start(f32[272,128]{1,0:T(8,128)S(1)} %get-tuple-element.101), channel_id=1, source_target_pairs={{0,16},{4,20},{8,24},{12,28},{16,0},{20,4},{24,8},{28,12},{1,17},{... | collective-permute-start | bytes 417800 | tf_op jit(solution)/shard_map/ppermute | solution.py:553
  50.6 7.7 %collective-permute-start.17 = (f32[272,128]{1,0:T(8,128)S(1)}, f32[272,128]{1,0:T(8,128)S(1)}, u32[]{:S(2)}, u32[]{:S(2)}) collective-permute-start(f32[272,128]{1,0:T(8,128)S(1)} %get-tuple-element.101), channel_id=1, source_target_pairs={{0,8},{4,12},{8,0},{12,4},{16,24},{20,28},{24,16},{28,20},{1,9},{5... | collective-permute-start | bytes 417800 | tf_op jit(solution)/shard_map/ppermute | solution.py:553
  52.1 12.5 %collective-permute-start.16 = (f32[264,128]{1,0:T(8,128)S(1)}, f32[264,128]{1,0:T(8,128)S(1)}, u32[]{:S(2)}, u32[]{:S(2)}) collective-permute-start(f32[264,128]{1,0:T(8,128)S(1)} %own_rows.1.refs_0_), channel_id=1, source_target_pairs={{0,2},{1,3},{2,0},{3,1},{4,6},{5,7},{6,4},{7,5},{8,10},{9,11},{10,... | collective-permute-start | bytes 405512 | tf_op jit(solution)/shard_map/ppermute | solution.py:550
  54.7 9.9 %collective-permute-start.15 = (f32[264,128]{1,0:T(8,128)S(1)}, f32[264,128]{1,0:T(8,128)S(1)}, u32[]{:S(2)}, u32[]{:S(2)}) collective-permute-start(f32[264,128]{1,0:T(8,128)S(1)} %own_rows.1.refs_0_), channel_id=1, source_target_pairs={{0,1},{1,0},{2,3},{3,2},{4,5},{5,4},{6,7},{7,6},{8,9},{9,8},{10,11... | collective-permute-start | bytes 405512 | tf_op jit(solution)/shard_map/ppermute | solution.py:550
  55.9 8.7 %collective-permute-start.14 = (f32[264,128]{1,0:T(8,128)S(1)}, f32[264,128]{1,0:T(8,128)S(1)}, u32[]{:S(2)}, u32[]{:S(2)}) collective-permute-start(f32[264,128]{1,0:T(8,128)S(1)} %own_rows.1.refs_0_), channel_id=1, source_target_pairs={{0,3},{1,2},{2,1},{3,0},{4,7},{5,6},{6,5},{7,4},{8,11},{9,10},{10,... | collective-permute-start | bytes 405512 | tf_op jit(solution)/shard_map/ppermute | solution.py:550
  56.5 5.9 %collective-permute-start.19 = (f32[256,128]{1,0:T(8,128)S(1)}, f32[256,128]{1,0:T(8,128)S(1)}, u32[]{:S(2)}, u32[]{:S(2)}) collective-permute-start(f32[256,128]{1,0:T(8,128)S(1)} %get-tuple-element.100.refs_0_), channel_id=1, source_target_pairs={{0,24},{4,28},{8,16},{12,20},{16,8},{20,12},{24,0},{28,4},{1,25},{... | collective-permute-start | bytes 393224 | tf_op jit(solution)/shard_map/ppermute | solution.py:553
  62.4 2.2 %collective-permute-start.20 = (f32[1024,128]{1,0:T(8,128)S(1)}, f32[1024,128]{1,0:T(8,128)S(1)}, u32[]{:S(2)}, u32[]{:S(2)}) collective-permute-start(f32[1024,128]{1,0:T(8,128)S(1)} %stack_chips.1.mine_ref), channel_id=1, source_target_pairs={{0,4},{4,0},{8,12},{12,8},{16,20},{20,16},{24,28},{28,24},{1,5},{5... | collective-permute-start | bytes 1572872 | tf_op jit(solution)/shard_map/ppermute | solution.py:553

commit v9 on v8

--- a/solution.py
+++ b/solution.py
@@ -559,18 +559,16 @@
     scores, index_lse, pack = index_forward(query_pos, index_query, index_keys, index_weight, stat)
     blocks = stat.shape[0]
     both = join_first(stat, to_keys(stat, 1), index_lse)
-    both, signs_query = lax.optimization_barrier((both, index_query))
     bits = 2
     while bits < key_devices // 2:
         both = join_pair(both, to_keys(both, bits))
         bits *= 2
-    gate, wiq, kl = index_signs(kl_weight, signs_query, index_keys, index_weight, key_devices)
     stat, index_lse = join_more(both, to_keys(both, bits), blocks)
-    stat, gate = lax.optimization_barrier((stat, gate))
     keep, send = head_sum(probs, tops, stat, queries, row_local)
     index_lse, send, index_query, pack = lax.optimization_barrier((index_lse, send, index_query, pack))
     sums = add_stacks(keep, to_heads(send, 1))
     targets = [sums[0]] + [to_heads(sums[r], 2 * r) for r in chip_order]
+    gate, wiq, kl = index_signs(kl_weight, index_query, index_keys, index_weight, key_devices)
     other_gate, other_wiq = other_signs(to_heads(pack, 1), index_keys, row_local)
     index_stats = (index_lse, to_keys(index_lse, 1))
     other_gate, gate = lax.optimization_barrier((other_gate, gate))

time: 66.2 us -> 65.8 us (level)
  waiting for transfers between devices: 14.3 us -> 13.3 us
    ppermute x13, waiting for transfers between devices: 9.29 us -> 8.6 us  [to_heads(): lax.ppermute(value, 'heads', [(i, i ^ bits) for i in range(head_devices)])]
  transfers between devices with their start and end apart: 21 -> 21, of which waited for: 11 -> 9; matrix products, arithmetic and copies ran while one was open for 0% -> 0% of each run, Pallas kernels for 13% -> 13%
where the time goes in v9:
time: 65.8 us; the launch traced here: 65.5 us
  starting transfers between devices  28.4 us (43%)
  Pallas kernels  22.9 us (35%)
  waiting for transfers between devices  13.3 us (20%)
  between operations  0.98 us (1%)
    ppermute x8, starting transfers between devices, to_keys(): lax.ppermute(value, 'keys', [(i, i ^ bits) for i in range(key_devices)])  15.9 us
    ppermute x13, starting transfers between devices, to_heads(): lax.ppermute(value, 'heads', [(i, i ^ bits) for i in range(head_devices)])  12.5 us
    pallas_call x17, Pallas kernels, vmem_call(): pl.pallas_call(body, out_shape=outs, in_specs=[smem_spec] * len(scalars)...  12.2 us
    pallas_call x1, Pallas kernels, main_scores(): pl.pallas_call(body, grid=(blocks // many,), out_shape=(pltpu.VMEM((block...  10.6 us
    ppermute x13, waiting for transfers between devices, to_heads(): lax.ppermute(value, 'heads', [(i, i ^ bits) for i in range(head_devices)])  8.6 us
    ppermute x8, waiting for transfers between devices, to_keys(): lax.ppermute(value, 'keys', [(i, i ^ bits) for i in range(key_devices)])  4.68 us
  transfers between devices with their start and end apart: 21, of which 9 were waited for; matrix products, arithmetic and copies ran while one was open for 0% of the time, Pallas kernels for 13%

profile of v9, /device:TPU:0, one launch (start us, length us, event | category | flops | bytes accessed | tf_op | source)
XLA Modules:
  0.0 65.5 jit_solution(11861989644844307084)
XLA Ops:
  0.7 10.6 %main_scores.1 = (f32[8,2048,256]{2,1,0:T(8,128)S(1)}, f32[8,16,256]{2,1,0:T(8,128)S(1)}, f32[8,256]{1,0:T(8,128)S(1)}) custom-call(s32[1,128]{1,0:T(1,128)} %bitcast.4, bf16[16,576,128]{2,1,0:T(8,128)(2,1)} %bitcast.5, bf16[576,2048]{1,0:T(8,128)(2,1)} %bitcast.6), custom_call_target="tpu_custom_call" | custom-call | tf_op jit(solution)/shard_map/main_scores/pallas_call | solution.py:215
  11.3 3.1 %collective-permute-start = (f32[8,256]{1,0:T(8,128)S(1)}, f32[8,256]{1,0:T(8,128)S(1)}, u32[]{:S(2)}, u32[]{:S(2)}) collective-permute-start(f32[8,256]{1,0:T(8,128)S(1)} %get-tuple-element.50._.left_ref), channel_id=1, source_target_pairs={{0,1},{1,0},{2,3},{3,2},{4,5},{5,4},{6,7},{7,6},{8,9},{9,8},{10,11... | collective-permute-start | bytes 24584 | tf_op jit(solution)/shard_map/ppermute | solution.py:550
  14.4 2.1 %index_forward.1 = (f32[16,2048]{1,0:T(8,128)S(1)}, f32[16,128]{1,0:T(8,128)S(1)}, f32[1040,128]{1,0:T(8,128)S(1)}) custom-call(s32[128]{0:T(128)S(1)} %copy-done.3, bf16[16,64,128]{2,1,0:T(8,128)(2,1)S(1)} %copy-done.1, bf16[2048,128]{1,0:T(8,128)(2,1)S(1)} %copy-done, f32[16,64]{1,0:T(8,128)S(1)} %copy-done.2, f32[8,256]{1,0:T(8,128)S(1)} %get-tuple-element.50._.left_ref), custom_call_target="tpu_custom_call" | custom-call | tf_op jit(solution)/shard_map/index_forward/pallas_call | solution.py:40
  16.6 2.7 %collective-permute-start.1 = (f32[24,256]{1,0:T(8,128)S(1)}, f32[24,256]{1,0:T(8,128)S(1)}, u32[]{:S(2)}, u32[]{:S(2)}) collective-permute-start(f32[24,256]{1,0:T(8,128)S(1)} %join_first.1.left_ref), channel_id=1, source_target_pairs={{0,2},{1,3},{2,0},{3,1},{4,6},{5,7},{6,4},{7,5},{8,10},{9,11},{10,... | collective-permute-start | bytes 73736 | tf_op jit(solution)/shard_map/ppermute | solution.py:550
  19.2 2.1 %collective-permute-done.1.right_ref = f32[24,256]{1,0:T(8,128)S(1)} collective-permute-done((f32[24,256]{1,0:T(8,128)S(1)}, f32[24,256]{1,0:T(8,128)S(1)}, u32[]{:S(2)}, u32[]{:S(2)}) %collective-permute-start.1) | collective-permute-done | bytes 24608 | tf_op jit(solution)/shard_map/ppermute | solution.py:550
  21.4 1.4 %head_sum.1 = (f32[4,16,2048]{2,1,0:T(8,128)S(1)}, f32[4,16,2048]{2,1,0:T(8,128)S(1)}) custom-call(f32[8,2048,256]{2,1,0:T(8,128)S(1)} %get-tuple-element.54.prob_ref, f32[8,16,256]{2,1,0:T(8,128)S(1)} %get-tuple-element.55.top_ref, f32[8,256]{1,0:T(8,128)S(1)} %get-tuple-element.56.stat_ref), custom_call_target="tpu_custom_call" | custom-call | flops 1000000000 | tf_op jit(solution)/shard_map/head_sum/pallas_call | solution.py:40
  23.4 1.4 %collective-permute-done.4.right_ref = f32[4,16,2048]{2,1,0:T(8,128)S(1)} collective-permute-done((f32[4,16,2048]{2,1,0:T(8,128)S(1)}, f32[4,16,2048]{2,1,0:T(8,128)S(1)}, u32[]{:S(2)}, u32[]{:S(2)}) %collective-permute-start.4) | collective-permute-done | bytes 524320 | tf_op jit(solution)/shard_map/ppermute | solution.py:553
  24.8 2.5 %collective-permute-start.5 = (f32[16,2048]{1,0:T(8,128)S(1)}, f32[16,2048]{1,0:T(8,128)S(1)}, u32[]{:S(2)}, u32[]{:S(2)}) collective-permute-start(f32[16,2048]{1,0:T(8,128)S(1)} %get-tuple-element.70), channel_id=1, source_target_pairs={{0,24},{4,28},{8,16},{12,20},{16,8},{20,12},{24,0},{28,4},{1,25},{... | collective-permute-start | bytes 393224 | tf_op jit(solution)/shard_map/ppermute | solution.py:553
  27.8 0.5 collective-permute-start.7
  28.4 1.5 %collective-permute-start.2 = (f32[16,128]{1,0:T(8,128)S(1)}, f32[16,128]{1,0:T(8,128)S(1)}, u32[]{:S(2)}, u32[]{:S(2)}) collective-permute-start(f32[16,128]{1,0:T(8,128)S(1)} %get-tuple-element.59.lse_ref), channel_id=1, source_target_pairs={{0,1},{1,0},{2,3},{3,2},{4,5},{5,4},{6,7},{7,6},{8,9},{9,8},{10,11... | collective-permute-start | bytes 24584 | tf_op jit(solution)/shard_map/ppermute | solution.py:550
  29.9 2.4 %index_signs.1 = (bf16[4,256,2048]{2,1,0:T(8,128)(2,1)S(1)}, bf16[4,128,256]{2,1,0:T(8,128)(2,1)S(1)}, f32[16,128]{1,0:T(8,128)S(1)}) custom-call(f32[16]{0:T(128)S(1)} %copy-done.4, bf16[16,64,128]{2,1,0:T(8,128)(2,1)S(1)} %copy-done.1, bf16[2048,128]{1,0:T(8,128)(2,1)S(1)} %copy-done, f32[16,64]{1,0:T(8,128)S(1)} %copy-done.2), custom_call_target="tpu_custom_call" | custom-call | tf_op jit(solution)/shard_map/index_signs/pallas_call | solution.py:40
  32.5 1.7 %other_signs.1 = (bf16[1024,1024]{1,0:T(8,128)(2,1)S(1)}, bf16[128,1024]{1,0:T(8,128)(2,1)S(1)}) custom-call(f32[1040,128]{1,0:T(8,128)S(1)} %collective-permute-done.3.pack_ref, bf16[2048,128]{1,0:T(8,128)(2,1)S(1)} %copy-done), custom_call_target="tpu_custom_call" | custom-call | tf_op jit(solution)/shard_map/other_signs/pallas_call | solution.py:40
  34.2 0.9 %query_part.1 = (f32[2,256,128]{2,1,0:T(8,128)S(1)}, bf16[512,2048]{1,0:T(8,128)(2,1)S(1)}, f32[4,4,2048]{2,1,0:T(4,128)S(1)}, f32[16,1024]{1,0:T(8,128)S(1)}) custom-call(f32[16,2048]{1,0:T(8,128)S(1)} %get-tuple-element.62.base_ref, f32[16,128]{1,0:T(8,128)S(1)} %get-tuple-element.61.kl_ref, bf16[4,256,2048]{2,1,0:T(8,128)(2,1)S(1)} %get-tuple-element.66.gate_ref, ...), custom_call_target="tpu_custom_call" | custom-call | tf_op jit(solution)/shard_map/query_part/pallas_call | solution.py:40
  35.2 1.6 %collective-permute-start.8 = (f32[2,256,128]{2,1,0:T(8,128)S(1)}, f32[2,256,128]{2,1,0:T(8,128)S(1)}, u32[]{:S(2)}, u32[]{:S(2)}) collective-permute-start(f32[2,256,128]{2,1,0:T(8,128)S(1)} %get-tuple-element.75), channel_id=1, source_target_pairs={{0,1},{1,0},{2,3},{3,2},{4,5},{5,4},{6,7},{7,6},{8,9},{9,8},{10,11... | collective-permute-start | bytes 786440 | tf_op jit(solution)/shard_map/ppermute | solution.py:550
  36.7 0.7 %query_rest.1 = (f32[2,256,128]{2,1,0:T(8,128)S(1)}, bf16[512,2048]{1,0:T(8,128)(2,1)S(1)}) custom-call(f32[4,4,2048]{2,1,0:T(4,128)S(1)} %get-tuple-element.73.delta_ref, bf16[4,256,2048]{2,1,0:T(8,128)(2,1)S(1)} %get-tuple-element.66.gate_ref, bf16[2048,128]{1,0:T(8,128)(2,1)S(1)} %copy-done), custom_call_target="tpu_custom_call" | custom-call | tf_op jit(solution)/shard_map/query_rest/pallas_call | solution.py:40
  38.0 1.2 %key_part.1 = (f32[256,128]{1,0:T(8,128)S(1)}, f32[256,128]{1,0:T(8,128)S(1)}, f32[256,128]{1,0:T(8,128)S(1)}, f32[256,128]{1,0:T(8,128)S(1)}) custom-call(bf16[512,2048]{1,0:T(8,128)(2,1)S(1)} %get-tuple-element.77.odd_ref, bf16[512,2048]{1,0:T(8,128)(2,1)S(1)} %get-tuple-element.78.even_ref, bf16[4,128,256]{2,1,0:T(8,128)(2,1)S(1)} %get-tuple-element.79.wiq_ref, ...), custom_call_target="tpu_custom_call" | custom-call | tf_op jit(solution)/shard_map/key_part/pallas_call | solution.py:40
  39.2 1.5 %collective-permute-start.10 = (f32[256,128]{1,0:T(8,128)S(1)}, f32[256,128]{1,0:T(8,128)S(1)}, u32[]{:S(2)}, u32[]{:S(2)}) collective-permute-start(f32[256,128]{1,0:T(8,128)S(1)} %get-tuple-element.84), channel_id=1, source_target_pairs={{0,16},{4,20},{8,24},{12,28},{16,0},{20,4},{24,8},{28,12},{1,17},{... | collective-permute-start | bytes 393224 | tf_op jit(solution)/shard_map/ppermute | solution.py:553
  40.7 1.5 %collective-permute-start.11 = (f32[256,128]{1,0:T(8,128)S(1)}, f32[256,128]{1,0:T(8,128)S(1)}, u32[]{:S(2)}, u32[]{:S(2)}) collective-permute-start(f32[256,128]{1,0:T(8,128)S(1)} %get-tuple-element.85), channel_id=1, source_target_pairs={{0,24},{4,28},{8,16},{12,20},{16,8},{20,12},{24,0},{28,4},{1,25},{... | collective-permute-start | bytes 393224 | tf_op jit(solution)/shard_map/ppermute | solution.py:553
  42.2 0.5 collective-permute-start.12
  42.7 0.7 %collective-permute-done.8.right_ref = f32[2,256,128]{2,1,0:T(8,128)S(1)} collective-permute-done((f32[2,256,128]{2,1,0:T(8,128)S(1)}, f32[2,256,128]{2,1,0:T(8,128)S(1)}, u32[]{:S(2)}, u32[]{:S(2)}) %collective-permute-start.8) | collective-permute-done | bytes 262176 | tf_op jit(solution)/shard_map/ppermute | solution.py:550
  43.4 2.7 %collective-permute-start.13 = (f32[1,256,128]{2,1,0:T(8,128)S(1)}, f32[1,256,128]{2,1,0:T(8,128)S(1)}, u32[]{:S(2)}, u32[]{:S(2)}) collective-permute-start(f32[1,256,128]{2,1,0:T(8,128)S(1)} %get-tuple-element.89), channel_id=1, source_target_pairs={{0,2},{1,3},{2,0},{3,1},{4,6},{5,7},{6,4},{7,5},{8,10},{9,11},{10,... | collective-permute-start | bytes 393224 | tf_op jit(solution)/shard_map/ppermute | solution.py:550
  46.1 1.2 %collective-permute-done.10.refs_1_ = f32[256,128]{1,0:T(8,128)S(1)} collective-permute-done((f32[256,128]{1,0:T(8,128)S(1)}, f32[256,128]{1,0:T(8,128)S(1)}, u32[]{:S(2)}, u32[]{:S(2)}) %collective-permute-start.10) | collective-permute-done | bytes 131104 | tf_op jit(solution)/shard_map/ppermute | solution.py:553
  47.3 0.7 %collective-permute-done.11.refs_2_ = f32[256,128]{1,0:T(8,128)S(1)} collective-permute-done((f32[256,128]{1,0:T(8,128)S(1)}, f32[256,128]{1,0:T(8,128)S(1)}, u32[]{:S(2)}, u32[]{:S(2)}) %collective-permute-start.11) | collective-permute-done | bytes 131104 | tf_op jit(solution)/shard_map/ppermute | solution.py:553
  47.9 0.9 %collective-permute-done.12.refs_3_ = f32[256,128]{1,0:T(8,128)S(1)} collective-permute-done((f32[256,128]{1,0:T(8,128)S(1)}, f32[256,128]{1,0:T(8,128)S(1)}, u32[]{:S(2)}, u32[]{:S(2)}) %collective-permute-start.12) | collective-permute-done | bytes 131104 | tf_op jit(solution)/shard_map/ppermute | solution.py:553
  48.9 1.5 %collective-permute-start.18 = (f32[272,128]{1,0:T(8,128)S(1)}, f32[272,128]{1,0:T(8,128)S(1)}, u32[]{:S(2)}, u32[]{:S(2)}) collective-permute-start(f32[272,128]{1,0:T(8,128)S(1)} %get-tuple-element.93), channel_id=1, source_target_pairs={{0,16},{4,20},{8,24},{12,28},{16,0},{20,4},{24,8},{28,12},{1,17},{... | collective-permute-start | bytes 417800 | tf_op jit(solution)/shard_map/ppermute | solution.py:553
  50.3 1.3 %collective-permute-start.17 = (f32[272,128]{1,0:T(8,128)S(1)}, f32[272,128]{1,0:T(8,128)S(1)}, u32[]{:S(2)}, u32[]{:S(2)}) collective-permute-start(f32[272,128]{1,0:T(8,128)S(1)} %get-tuple-element.93), channel_id=1, source_target_pairs={{0,8},{4,12},{8,0},{12,4},{16,24},{20,28},{24,16},{28,20},{1,9},{5... | collective-permute-start | bytes 417800 | tf_op jit(solution)/shard_map/ppermute | solution.py:553
  51.8 2.9 %collective-permute-start.16 = (f32[264,128]{1,0:T(8,128)S(1)}, f32[264,128]{1,0:T(8,128)S(1)}, u32[]{:S(2)}, u32[]{:S(2)}) collective-permute-start(f32[264,128]{1,0:T(8,128)S(1)} %own_rows.1.refs_0_), channel_id=1, source_target_pairs={{0,2},{1,3},{2,0},{3,1},{4,6},{5,7},{6,4},{7,5},{8,10},{9,11},{10,... | collective-permute-start | bytes 405512 | tf_op jit(solution)/shard_map/ppermute | solution.py:550
  54.7 1.0 %collective-permute-start.15 = (f32[264,128]{1,0:T(8,128)S(1)}, f32[264,128]{1,0:T(8,128)S(1)}, u32[]{:S(2)}, u32[]{:S(2)}) collective-permute-start(f32[264,128]{1,0:T(8,128)S(1)} %own_rows.1.refs_0_), channel_id=1, source_target_pairs={{0,1},{1,0},{2,3},{3,2},{4,5},{5,4},{6,7},{7,6},{8,9},{9,8},{10,11... | collective-permute-start | bytes 405512 | tf_op jit(solution)/shard_map/ppermute | solution.py:550
  56.3 2.0 %collective-permute-start.19 = (f32[256,128]{1,0:T(8,128)S(1)}, f32[256,128]{1,0:T(8,128)S(1)}, u32[]{:S(2)}, u32[]{:S(2)}) collective-permute-start(f32[256,128]{1,0:T(8,128)S(1)} %get-tuple-element.92.refs_0_), channel_id=1, source_target_pairs={{0,24},{4,28},{8,16},{12,20},{16,8},{20,12},{24,0},{28,4},{1,25},{... | collective-permute-start | bytes 393224 | tf_op jit(solution)/shard_map/ppermute | solution.py:553
  58.2 3.9 %collective-permute-done.19.refs_3_ = f32[256,128]{1,0:T(8,128)S(1)} collective-permute-done((f32[256,128]{1,0:T(8,128)S(1)}, f32[256,128]{1,0:T(8,128)S(1)}, u32[]{:S(2)}, u32[]{:S(2)}) %collective-permute-start.19) | collective-permute-done | bytes 131104 | tf_op jit(solution)/shard_map/ppermute | solution.py:553
  62.3 1.9 %collective-permute-done.16.refs_3_ = f32[264,128]{1,0:T(8,128)S(1)} collective-permute-done((f32[264,128]{1,0:T(8,128)S(1)}, f32[264,128]{1,0:T(8,128)S(1)}, u32[]{:S(2)}, u32[]{:S(2)}) %collective-permute-start.16) | collective-permute-done | bytes 135200 | tf_op jit(solution)/shard_map/ppermute | solution.py:550
  64.2 1.2 %place_all.1 = (f32[1024,128]{1,0:T(8,128)}, f32[2048,128]{1,0:T(8,128)}, f32[16,64]{1,0:T(8,128)}) custom-call(f32[16,64]{1,0:T(8,128)S(1)} %gather_weights.1.weight_ref, f32[1024,128]{1,0:T(8,128)S(1)} %stack_chips.1.mine_ref, f32[1024,128]{1,0:T(8,128)S(1)} %collective-permute-done.20.other_ref, f32[264,128]{1,0:T(8,128)S(1)} %own_rows.1.refs_0_, ...), custom_call_target="tpu_custom_call" | custom-call | tf_op jit(solution)/shard_map/place_all/pallas_call | solution.py:40
  (38 shorter events, 2.8 us)
Async XLA Ops:
  0.6 13.8 %copy-start = (bf16[2048,128]{1,0:T(8,128)(2,1)S(1)}, bf16[2048,128]{1,0:T(8,128)(2,1)}, u32[]{:S(2)}) copy-start(bf16[2048,128]{1,0:T(8,128)(2,1)} %keys_ref.9) | copy-start | bytes 1572868
  0.6 13.7 %copy-start.1 = (bf16[16,64,128]{2,1,0:T(8,128)(2,1)S(1)}, bf16[16,64,128]{2,1,0:T(8,128)(2,1)}, u32[]{:S(2)}) copy-start(bf16[16,64,128]{2,1,0:T(8,128)(2,1)} %query_ref.3) | copy-start | bytes 786436
  0.7 13.7 %copy-start.2 = (f32[16,64]{1,0:T(8,128)S(1)}, f32[16,64]{1,0:T(8,128)}, u32[]{:S(2)}) copy-start(f32[16,64]{1,0:T(8,128)} %weight_ref.5) | copy-start | bytes 12292
  0.7 13.7 %copy-start.3 = (s32[128]{0:T(128)S(1)}, s32[128]{0:T(128)}, u32[]{:S(2)}) copy-start(s32[128]{0:T(128)} %pos_ref.1) | copy-start | bytes 1540
  11.3 5.2 %collective-permute-start = (f32[8,256]{1,0:T(8,128)S(1)}, f32[8,256]{1,0:T(8,128)S(1)}, u32[]{:S(2)}, u32[]{:S(2)}) collective-permute-start(f32[8,256]{1,0:T(8,128)S(1)} %get-tuple-element.50._.left_ref), channel_id=1, source_target_pairs={{0,1},{1,0},{2,3},{3,2},{4,5},{5,4},{6,7},{7,6},{8,9},{9,8},{10,11... | collective-permute-start | bytes 24584 | tf_op jit(solution)/shard_map/ppermute | solution.py:550
  16.6 4.8 %collective-permute-start.1 = (f32[24,256]{1,0:T(8,128)S(1)}, f32[24,256]{1,0:T(8,128)S(1)}, u32[]{:S(2)}, u32[]{:S(2)}) collective-permute-start(f32[24,256]{1,0:T(8,128)S(1)} %join_first.1.left_ref), channel_id=1, source_target_pairs={{0,2},{1,3},{2,0},{3,1},{4,6},{5,7},{6,4},{7,5},{8,10},{9,11},{10,... | collective-permute-start | bytes 73736 | tf_op jit(solution)/shard_map/ppermute | solution.py:550
  21.4 8.5 %copy-start.4 = (f32[16]{0:T(128)S(1)}, f32[16]{0:T(128)}, u32[]{:S(2)}) copy-start(f32[16]{0:T(128)} %kl_ref.1) | copy-start | bytes 196
  22.8 2.0 %collective-permute-start.4 = (f32[4,16,2048]{2,1,0:T(8,128)S(1)}, f32[4,16,2048]{2,1,0:T(8,128)S(1)}, u32[]{:S(2)}, u32[]{:S(2)}) collective-permute-start(f32[4,16,2048]{2,1,0:T(8,128)S(1)} %get-tuple-element.68), channel_id=1, source_target_pairs={{0,4},{4,0},{8,12},{12,8},{16,20},{20,16},{24,28},{28,24},{1,5},{5... | collective-permute-start | bytes 1572872 | tf_op jit(solution)/shard_map/ppermute | solution.py:553
  22.9 9.6 %collective-permute-start.3 = (f32[1040,128]{1,0:T(8,128)S(1)}, f32[1040,128]{1,0:T(8,128)S(1)}, u32[]{:S(2)}, u32[]{:S(2)}) collective-permute-start(f32[1040,128]{1,0:T(8,128)S(1)} %get-tuple-element.63), channel_id=1, source_target_pairs={{0,4},{4,0},{8,12},{12,8},{16,20},{20,16},{24,28},{28,24},{1,5},{5... | collective-permute-start | bytes 1597448 | tf_op jit(solution)/shard_map/ppermute | solution.py:553
  24.8 9.4 %collective-permute-start.5 = (f32[16,2048]{1,0:T(8,128)S(1)}, f32[16,2048]{1,0:T(8,128)S(1)}, u32[]{:S(2)}, u32[]{:S(2)}) collective-permute-start(f32[16,2048]{1,0:T(8,128)S(1)} %get-tuple-element.70), channel_id=1, source_target_pairs={{0,24},{4,28},{8,16},{12,20},{16,8},{20,12},{24,0},{28,4},{1,25},{... | collective-permute-start | bytes 393224 | tf_op jit(solution)/shard_map/ppermute | solution.py:553
  27.3 6.8 %collective-permute-start.6 = (f32[16,2048]{1,0:T(8,128)S(1)}, f32[16,2048]{1,0:T(8,128)S(1)}, u32[]{:S(2)}, u32[]{:S(2)}) collective-permute-start(f32[16,2048]{1,0:T(8,128)S(1)} %get-tuple-element.71), channel_id=1, source_target_pairs={{0,16},{4,20},{8,24},{12,28},{16,0},{20,4},{24,8},{28,12},{1,17},{... | collective-permute-start | bytes 393224 | tf_op jit(solution)/shard_map/ppermute | solution.py:553
  27.8 6.4 %collective-permute-start.7 = (f32[16,2048]{1,0:T(8,128)S(1)}, f32[16,2048]{1,0:T(8,128)S(1)}, u32[]{:S(2)}, u32[]{:S(2)}) collective-permute-start(f32[16,2048]{1,0:T(8,128)S(1)} %get-tuple-element.72), channel_id=1, source_target_pairs={{0,8},{4,12},{8,0},{12,4},{16,24},{20,28},{24,16},{28,20},{1,9},{5... | collective-permute-start | bytes 393224 | tf_op jit(solution)/shard_map/ppermute | solution.py:553
  28.4 3.9 %collective-permute-start.2 = (f32[16,128]{1,0:T(8,128)S(1)}, f32[16,128]{1,0:T(8,128)S(1)}, u32[]{:S(2)}, u32[]{:S(2)}) collective-permute-start(f32[16,128]{1,0:T(8,128)S(1)} %get-tuple-element.59.lse_ref), channel_id=1, source_target_pairs={{0,1},{1,0},{2,3},{3,2},{4,5},{5,4},{6,7},{7,6},{8,9},{9,8},{10,11... | collective-permute-start | bytes 24584 | tf_op jit(solution)/shard_map/ppermute | solution.py:550
  35.2 8.2 %collective-permute-start.8 = (f32[2,256,128]{2,1,0:T(8,128)S(1)}, f32[2,256,128]{2,1,0:T(8,128)S(1)}, u32[]{:S(2)}, u32[]{:S(2)}) collective-permute-start(f32[2,256,128]{2,1,0:T(8,128)S(1)} %get-tuple-element.75), channel_id=1, source_target_pairs={{0,1},{1,0},{2,3},{3,2},{4,5},{5,4},{6,7},{7,6},{8,9},{9,8},{10,11... | collective-permute-start | bytes 786440 | tf_op jit(solution)/shard_map/ppermute | solution.py:550
  36.7 1.3 %collective-permute-start.9 = (f32[16,1024]{1,0:T(8,128)S(1)}, f32[16,1024]{1,0:T(8,128)S(1)}, u32[]{:S(2)}, u32[]{:S(2)}) collective-permute-start(f32[16,1024]{1,0:T(8,128)S(1)} %get-tuple-element.80), channel_id=1, source_target_pairs={{0,4},{4,0},{8,12},{12,8},{16,20},{20,16},{24,28},{28,24},{1,5},{5... | collective-permute-start | bytes 196616 | tf_op jit(solution)/shard_map/ppermute | solution.py:553
  39.2 8.1 %collective-permute-start.10 = (f32[256,128]{1,0:T(8,128)S(1)}, f32[256,128]{1,0:T(8,128)S(1)}, u32[]{:S(2)}, u32[]{:S(2)}) collective-permute-start(f32[256,128]{1,0:T(8,128)S(1)} %get-tuple-element.84), channel_id=1, source_target_pairs={{0,16},{4,20},{8,24},{12,28},{16,0},{20,4},{24,8},{28,12},{1,17},{... | collective-permute-start | bytes 393224 | tf_op jit(solution)/shard_map/ppermute | solution.py:553
  40.7 7.3 %collective-permute-start.11 = (f32[256,128]{1,0:T(8,128)S(1)}, f32[256,128]{1,0:T(8,128)S(1)}, u32[]{:S(2)}, u32[]{:S(2)}) collective-permute-start(f32[256,128]{1,0:T(8,128)S(1)} %get-tuple-element.85), channel_id=1, source_target_pairs={{0,24},{4,28},{8,16},{12,20},{16,8},{20,12},{24,0},{28,4},{1,25},{... | collective-permute-start | bytes 393224 | tf_op jit(solution)/shard_map/ppermute | solution.py:553
  42.2 6.6 %collective-permute-start.12 = (f32[256,128]{1,0:T(8,128)S(1)}, f32[256,128]{1,0:T(8,128)S(1)}, u32[]{:S(2)}, u32[]{:S(2)}) collective-permute-start(f32[256,128]{1,0:T(8,128)S(1)} %get-tuple-element.86), channel_id=1, source_target_pairs={{0,8},{4,12},{8,0},{12,4},{16,24},{20,28},{24,16},{28,20},{1,9},{5... | collective-permute-start | bytes 393224 | tf_op jit(solution)/shard_map/ppermute | solution.py:553
  43.4 8.3 %collective-permute-start.13 = (f32[1,256,128]{2,1,0:T(8,128)S(1)}, f32[1,256,128]{2,1,0:T(8,128)S(1)}, u32[]{:S(2)}, u32[]{:S(2)}) collective-permute-start(f32[1,256,128]{2,1,0:T(8,128)S(1)} %get-tuple-element.89), channel_id=1, source_target_pairs={{0,2},{1,3},{2,0},{3,1},{4,6},{5,7},{6,4},{7,5},{8,10},{9,11},{10,... | collective-permute-start | bytes 393224 | tf_op jit(solution)/shard_map/ppermute | solution.py:550
  48.9 7.4 %collective-permute-start.18 = (f32[272,128]{1,0:T(8,128)S(1)}, f32[272,128]{1,0:T(8,128)S(1)}, u32[]{:S(2)}, u32[]{:S(2)}) collective-permute-start(f32[272,128]{1,0:T(8,128)S(1)} %get-tuple-element.93), channel_id=1, source_target_pairs={{0,16},{4,20},{8,24},{12,28},{16,0},{20,4},{24,8},{28,12},{1,17},{... | collective-permute-start | bytes 417800 | tf_op jit(solution)/shard_map/ppermute | solution.py:553
  50.3 7.9 %collective-permute-start.17 = (f32[272,128]{1,0:T(8,128)S(1)}, f32[272,128]{1,0:T(8,128)S(1)}, u32[]{:S(2)}, u32[]{:S(2)}) collective-permute-start(f32[272,128]{1,0:T(8,128)S(1)} %get-tuple-element.93), channel_id=1, source_target_pairs={{0,8},{4,12},{8,0},{12,4},{16,24},{20,28},{24,16},{28,20},{1,9},{5... | collective-permute-start | bytes 417800 | tf_op jit(solution)/shard_map/ppermute | solution.py:553
  51.8 12.3 %collective-permute-start.16 = (f32[264,128]{1,0:T(8,128)S(1)}, f32[264,128]{1,0:T(8,128)S(1)}, u32[]{:S(2)}, u32[]{:S(2)}) collective-permute-start(f32[264,128]{1,0:T(8,128)S(1)} %own_rows.1.refs_0_), channel_id=1, source_target_pairs={{0,2},{1,3},{2,0},{3,1},{4,6},{5,7},{6,4},{7,5},{8,10},{9,11},{10,... | collective-permute-start | bytes 405512 | tf_op jit(solution)/shard_map/ppermute | solution.py:550
  54.7 9.4 %collective-permute-start.15 = (f32[264,128]{1,0:T(8,128)S(1)}, f32[264,128]{1,0:T(8,128)S(1)}, u32[]{:S(2)}, u32[]{:S(2)}) collective-permute-start(f32[264,128]{1,0:T(8,128)S(1)} %own_rows.1.refs_0_), channel_id=1, source_target_pairs={{0,1},{1,0},{2,3},{3,2},{4,5},{5,4},{6,7},{7,6},{8,9},{9,8},{10,11... | collective-permute-start | bytes 405512 | tf_op jit(solution)/shard_map/ppermute | solution.py:550
  55.7 8.4 %collective-permute-start.14 = (f32[264,128]{1,0:T(8,128)S(1)}, f32[264,128]{1,0:T(8,128)S(1)}, u32[]{:S(2)}, u32[]{:S(2)}) collective-permute-start(f32[264,128]{1,0:T(8,128)S(1)} %own_rows.1.refs_0_), channel_id=1, source_target_pairs={{0,3},{1,2},{2,1},{3,0},{4,7},{5,6},{6,5},{7,4},{8,11},{9,10},{10,... | collective-permute-start | bytes 405512 | tf_op jit(solution)/shard_map/ppermute | solution.py:550
  56.3 5.9 %collective-permute-start.19 = (f32[256,128]{1,0:T(8,128)S(1)}, f32[256,128]{1,0:T(8,128)S(1)}, u32[]{:S(2)}, u32[]{:S(2)}) collective-permute-start(f32[256,128]{1,0:T(8,128)S(1)} %get-tuple-element.92.refs_0_), channel_id=1, source_target_pairs={{0,24},{4,28},{8,16},{12,20},{16,8},{20,12},{24,0},{28,4},{1,25},{... | collective-permute-start | bytes 393224 | tf_op jit(solution)/shard_map/ppermute | solution.py:553
  62.2 2.0 %collective-permute-start.20 = (f32[1024,128]{1,0:T(8,128)S(1)}, f32[1024,128]{1,0:T(8,128)S(1)}, u32[]{:S(2)}, u32[]{:S(2)}) collective-permute-start(f32[1024,128]{1,0:T(8,128)S(1)} %stack_chips.1.mine_ref), channel_id=1, source_target_pairs={{0,4},{4,0},{8,12},{12,8},{16,20},{20,16},{24,28},{28,24},{1,5},{5... | collective-permute-start | bytes 1572872 | tf_op jit(solution)/shard_map/ppermute | solution.py:553
